TPU v7x, 32 devices: a whole 2x2x4 slice. The times are simulated.
32 devices in a mesh: inp: 4 (over z), tgt: 4 (over x, core), mdl: 2 (over y).
Axes of the slice: x: 2, y: 2, z: 4, core: 2. Of those that a mesh axis runs over, the one named last changes fastest.
Arguments:
- encoder: bfloat16 [2048, 4096], P('inp'), may hold values from -8 to 8
- key_weight: bfloat16 [2, 4096, 2, 4, 256], P(None, None, 'mdl', 'tgt'), may hold values from -1 to 1
- value_weight: bfloat16 [2, 4096, 2, 4, 256], P(None, None, 'mdl', 'tgt'), may hold values from -0.09375 to 0.09375
- queries: bfloat16 [2, 2048, 8, 256], P(None, 'tgt', 'mdl'), may hold values from -8 to 8
- grad_out: bfloat16 [2, 2048, 8, 256], P(None, 'tgt', 'mdl'), may hold values from -6 to 6
Outputs:
- grad_query: bfloat16 [2, 2048, 8, 256], P(None, 'tgt', 'mdl')
- grad_encoder: bfloat16 [2048, 4096], P('inp', ('tgt', 'mdl'))
All inputs are finite; a program needn't handle non-finite values.
Results may differ from a plain program's by a relative error of at most 0.019.
The roundings to bfloat16 on the way count: a program that leaves them out, or rounds other values in their place, can miss the bound.
Values may be sent and summed in bfloat16 or wider, within the bound.
No kernel may reach another device: no remote copies, remote signals or barrier semaphores. Data moves between devices by JAX's collectives and lax.ppermute only.
A program may use at most 128 MiB of HBM per device.

v0:
```python
import jax
import jax.numpy as jnp
from jax import lax
from jax.sharding import PartitionSpec as P


def joined(value, axis, join):
    pieces = jax.tree.map(lambda part: lax.all_gather(part, axis), value)
    head = jax.tree.map(lambda part: part[0], pieces)
    tail = jax.tree.map(lambda part: part[1:], pieces)
    total, _ = lax.scan(lambda total, slab: (join(total, slab), None), head, tail)
    return total


def combine_totals(one_side, other_side):
    peak_one, total_one, inner_one = one_side
    peak_two, total_two, inner_two = other_side
    peak_value = jnp.maximum(peak_one, peak_two)
    scale_one = jnp.exp(peak_one - peak_value)
    scale_two = jnp.exp(peak_two - peak_value)
    return (
        peak_value,
        total_one * scale_one + total_two * scale_two,
        inner_one * scale_one + inner_two * scale_two,
    )


def attention_grads(query_rows, grad_rows, key_block, value_block):
    scores = jnp.einsum("rhc,ehc->hre", query_rows, key_block, preferred_element_type=jnp.float32)
    local_peak = jnp.max(scores, axis=2)
    shifted = jnp.exp(scores - local_peak[:, :, None])
    dprobs = jnp.einsum("rhc,ehc->hre", grad_rows, value_block, preferred_element_type=jnp.float32)
    local_total = jnp.sum(shifted, axis=2)
    local_inner = jnp.sum(shifted * dprobs, axis=2)
    row_peak, row_total, row_inner = joined(
        (local_peak, local_total, local_inner), "inp", combine_totals
    )
    rescale = jnp.exp(local_peak - row_peak) / row_total
    attention = shifted * rescale[:, :, None]
    dscores = (attention * (dprobs - (row_inner / row_total)[:, :, None])).astype(jnp.bfloat16)
    attention_low = attention.astype(jnp.bfloat16)
    query_part = jnp.einsum("hre,ehc->rhc", dscores, key_block, preferred_element_type=jnp.float32)
    query_grad = lax.psum(query_part.astype(jnp.bfloat16), "inp")
    key_part = jnp.einsum("hre,rhc->ehc", dscores, query_rows, preferred_element_type=jnp.float32)
    value_part = jnp.einsum(
        "hre,rhc->ehc", attention_low, grad_rows, preferred_element_type=jnp.float32
    )
    return (query_grad, key_part, value_part)


def body(encoder, key_weight, value_weight, queries, grad_out):
    model_width = encoder.shape[1]
    enc_rows = encoder.shape[0]
    head_size = queries.shape[3]
    own_heads = key_weight.shape[2] * key_weight.shape[3]
    query_grads = []
    enc_terms = []
    for layer_index in range(queries.shape[0]):
        key_matrix = key_weight[layer_index].reshape(model_width, own_heads * head_size)
        value_matrix = value_weight[layer_index].reshape(model_width, own_heads * head_size)
        key_block = (
            jnp.dot(encoder, key_matrix, preferred_element_type=jnp.float32)
            .astype(jnp.bfloat16)
            .reshape(enc_rows, own_heads, head_size)
        )
        value_block = (
            jnp.dot(encoder, value_matrix, preferred_element_type=jnp.float32)
            .astype(jnp.bfloat16)
            .reshape(enc_rows, own_heads, head_size)
        )
        group_keys, group_values = (
            lax.all_gather(key_block, "tgt", axis=1, tiled=True),
            lax.all_gather(value_block, "tgt", axis=1, tiled=True),
        )
        query_grad, key_part, value_part = attention_grads(
            queries[layer_index], grad_out[layer_index], group_keys, group_values
        )
        key_total, value_total = (
            lax.psum_scatter(key_part, "tgt", scatter_dimension=1, tiled=True),
            lax.psum_scatter(value_part, "tgt", scatter_dimension=1, tiled=True),
        )
        query_grads.append(query_grad)
        key_flat = key_total.astype(jnp.bfloat16).reshape(enc_rows, own_heads * head_size)
        value_flat = value_total.astype(jnp.bfloat16).reshape(enc_rows, own_heads * head_size)
        enc_terms.append((key_flat, value_flat, key_matrix, value_matrix))
    share_rows = model_width // (lax.axis_size("tgt") * lax.axis_size("mdl"))
    running = jnp.zeros((share_rows * lax.axis_size(("tgt", "mdl")), enc_rows), jnp.float32)
    for key_flat, value_flat, key_matrix, value_matrix in enc_terms:
        running = running + jnp.einsum(
            "dc,ec->de", key_matrix, key_flat, preferred_element_type=jnp.float32
        )
        running = running + jnp.einsum(
            "dc,ec->de", value_matrix, value_flat, preferred_element_type=jnp.float32
        )
    enc_share = lax.psum_scatter(
        running.astype(jnp.bfloat16), ("tgt", "mdl"), scatter_dimension=0, tiled=True
    ).astype(jnp.float32)
    return (jnp.stack(query_grads), enc_share.T.astype(jnp.bfloat16))


def solution(mesh):
    placed = (
        P("inp", None),
        P(None, None, "mdl", "tgt", None),
        P(None, None, "mdl", "tgt", None),
        P(None, "tgt", "mdl", None),
        P(None, "tgt", "mdl", None),
    )
    return jax.shard_map(
        body,
        mesh=mesh,
        in_specs=placed,
        out_specs=(P(None, "tgt", "mdl", None), P("inp", ("tgt", "mdl"))),
        check_vma=False,
    )
```

profile of v0, /device:TPU:0, one launch (start us, length us, event | category | flops | bytes accessed | tf_op | source)
XLA Modules:
  0.0 397.7 jit_solution(16657849056835302134)
XLA Ops:
  7.2 0.0 all-gather.25.cloned.1.call-start
  7.2 4.8 %fusion.56 = bf16[512,256]{1,0:T(8,128)(2,1)} fusion(bf16[512,4096]{1,0:T(8,128)(2,1)} %param.9, bf16[2,4096,1,1,256]{4,1,3,2,0:T(8,128)(2,1)} %param.10), kind=kOutput, calls=%fused_computation.78 | convolution fusion | flops 1073872896 | bytes 6553600 | tf_op jit(solution)/shard_map/dot_general | solution.py:62
  12.0 0.0 all-gather.25.cloned.1.call-update
  12.1 0.0 all-gather.27.cloned.1.call-start
  12.1 4.8 %fusion.59 = bf16[512,256]{1,0:T(8,128)(2,1)} fusion(bf16[512,4096]{1,0:T(8,128)(2,1)} %param.9, bf16[2,4096,1,1,256]{4,1,3,2,0:T(8,128)(2,1)} %param.11), kind=kOutput, calls=%fused_computation.79 | convolution fusion | flops 1073872896 | bytes 6553600 | tf_op jit(solution)/shard_map/dot_general | solution.py:67
  16.9 0.0 all-gather.27.cloned.1.call-update
  16.9 0.0 all-gather.21.cloned.1.call-start
  17.0 4.8 %fusion.50 = bf16[512,256]{1,0:T(8,128)(2,1)} fusion(bf16[512,4096]{1,0:T(8,128)(2,1)} %param.9, bf16[2,4096,1,1,256]{4,1,3,2,0:T(8,128)(2,1)} %param.10), kind=kOutput, calls=%fused_computation.76 | convolution fusion | flops 1073872896 | bytes 6553600 | tf_op jit(solution)/shard_map/dot_general | solution.py:62
  21.8 0.0 all-gather.21.cloned.1.call-update
  21.9 0.0 all-gather.23.cloned.1.call-start
  21.9 5.0 %fusion.53 = bf16[512,256]{1,0:T(8,128)(2,1)} fusion(bf16[512,4096]{1,0:T(8,128)(2,1)} %param.9, bf16[2,4096,1,1,256]{4,1,3,2,0:T(8,128)(2,1)} %param.11), kind=kOutput, calls=%fused_computation.77 | convolution fusion | flops 1073872896 | bytes 6553600 | tf_op jit(solution)/shard_map/dot_general | solution.py:67
  27.0 0.0 all-gather.23.cloned.1.call-update
  27.0 0.0 reduce-scatter.10.cloned.1.call-start
  27.1 1.7 fusion.78
  28.8 1.7 fusion.79
  30.5 1.3 all-gather.25.cloned.1.call-done
  31.8 1.5 copy.40
  33.3 2.8 bitcast_reduce_fusion
  36.1 13.5 %all-gather.13 = f32[4,4,512]{2,1,0:T(4,128)S(1)} all-gather(f32[1,4,512]{2,1,0:T(4,128)S(1)} %bitcast.231), channel_id=8, replica_groups=mesh['inp'=4,'tgt'=4,'mdl'=2] {'inp'}, dimensions={0}, use_global_device_ids=true | all-gather | bytes 40960 | tf_op jit(solution)/shard_map/all_gather | solution.py:8
  49.6 0.6 all-gather.27.cloned.1.call-done
  50.2 5.5 %fusion.7 = (f32[4,512]{1,0:T(4,128)S(1)}, f32[4,512]{1,0:T(4,128)S(1)}, f32[4,512,512]{2,1,0:T(8,128)}) fusion(f32[4,512,512]{2,1,0:T(8,128)} %get-tuple-element.140, f32[4,512]{1,0:T(4,128)S(1)} %get-tuple-element.139, bf16[1,512,4,256]{3,2,1,0:T(4,128)(2,1)S(1)} %get-tuple-element.131, bf16[64,4,8,256]{3,2,1,0:T(8,128)(2,1)} %bitcast.230), kind=kOutput, calls=%fused_computation.20 | convolution fusion | flops 541061120 | bytes 10510336 | tf_op jit(solution)/shard_map/rhc,ehc->hre/dot_general | solution.py:32
  55.7 13.1 %all-gather.14 = f32[4,4,512]{2,1,0:T(4,128)S(1)} all-gather(f32[1,4,512]{2,1,0:T(4,128)S(1)} %bitcast.235), channel_id=9, replica_groups=mesh['inp'=4,'tgt'=4,'mdl'=2] {'inp'}, dimensions={0}, use_global_device_ids=true | all-gather | bytes 40960 | tf_op jit(solution)/shard_map/all_gather | solution.py:8
  68.8 13.1 %all-gather.15 = f32[4,4,512]{2,1,0:T(4,128)S(1)} all-gather(f32[1,4,512]{2,1,0:T(4,128)S(1)} %bitcast.233), channel_id=11, replica_groups=mesh['inp'=4,'tgt'=4,'mdl'=2] {'inp'}, dimensions={0}, use_global_device_ids=true | all-gather | bytes 40960 | tf_op jit(solution)/shard_map/all_gather | solution.py:8
  82.0 0.2 while.29
  82.3 4.7 %fusion.9 = bf16[4,512,512]{1,2,0:T(8,128)(2,1)S(1)} fusion(f32[4,512,512]{2,1,0:T(8,128)} %get-tuple-element.141, f32[4,512,512]{2,1,0:T(8,128)} %get-tuple-element.140, f32[4,512]{1,0:T(4,128)S(1)} %get-tuple-element.135, f32[4,512]{1,0:T(4,128)S(1)} %get-tuple-element.134, f32[4,512]{1,0:T(4,128)S(1)} %get-tuple-element.139), kind=kLoop, calls=%fused_computation.22 | loop fusion | flops 5242880 | bytes 10510336 | tf_op jit(solution)/shard_map/convert_element_type | solution.py:40
  87.0 2.1 convolution_bitcast_fusion
  89.1 0.0 reduce-scatter.10.cloned.1.call-update
  89.1 0.0 reduce-scatter.8.cloned.1.call-start
  89.1 0.0 all-gather.21.cloned.1.call-done
  89.2 2.3 copy.39
  91.5 4.4 %bitcast_reduce_fusion.1 = (f32[4,512]{1,0:T(4,128)S(1)}, f32[4,512,512]{2,1,0:T(8,128)}) fusion(bf16[512,4,256]{0,2,1:T(8,128)(2,1)} %bitcast.227, bf16[1,512,4,256]{3,2,1,0:T(4,128)(2,1)} %get-tuple-element.128), kind=kOutput, calls=%fused_computation.32 | convolution fusion | flops 537917440 | bytes 6299648 | tf_op jit(solution)/shard_map/rhc,ehc->hre/dot_general | solution.py:29
  95.8 13.3 %all-gather.10 = f32[4,4,512]{2,1,0:T(4,128)S(1)} all-gather(f32[1,4,512]{2,1,0:T(4,128)S(1)} %bitcast.232), channel_id=3, replica_groups=mesh['inp'=4,'tgt'=4,'mdl'=2] {'inp'}, dimensions={0}, use_global_device_ids=true | all-gather | bytes 40960 | tf_op jit(solution)/shard_map/all_gather | solution.py:8
  109.1 5.8 %fusion.11 = (f32[4,512]{1,0:T(4,128)S(1)}, f32[4,512]{1,0:T(4,128)S(1)}, f32[4,512,512]{2,1,0:T(8,128)}) fusion(f32[4,512,512]{2,1,0:T(8,128)} %get-tuple-element.137, f32[4,512]{1,0:T(4,128)S(1)} %get-tuple-element.136, bf16[1,512,4,256]{3,2,1,0:T(4,128)(2,1)} %get-tuple-element.130, bf16[64,4,8,256]{3,2,1,0:T(8,128)(2,1)} %bitcast.229), kind=kOutput, calls=%fused_computation.28 | convolution fusion | flops 541061120 | bytes 10510336 | tf_op jit(solution)/shard_map/rhc,ehc->hre/dot_general | solution.py:32
  115.0 13.1 %all-gather.11 = f32[4,4,512]{2,1,0:T(4,128)S(1)} all-gather(f32[1,4,512]{2,1,0:T(4,128)S(1)} %bitcast.236), channel_id=4, replica_groups=mesh['inp'=4,'tgt'=4,'mdl'=2] {'inp'}, dimensions={0}, use_global_device_ids=true | all-gather | bytes 40960 | tf_op jit(solution)/shard_map/all_gather | solution.py:8
  128.1 13.1 %all-gather.12 = f32[4,4,512]{2,1,0:T(4,128)S(1)} all-gather(f32[1,4,512]{2,1,0:T(4,128)S(1)} %bitcast.234), channel_id=6, replica_groups=mesh['inp'=4,'tgt'=4,'mdl'=2] {'inp'}, dimensions={0}, use_global_device_ids=true | all-gather | bytes 40960 | tf_op jit(solution)/shard_map/all_gather | solution.py:8
  141.2 0.3 while.28
  141.5 4.7 %fusion.47 = f32[512,4,256]{2,0,1:T(8,128)} fusion(f32[4,512,512]{2,1,0:T(8,128)} %get-tuple-element.137, f32[4,512]{1,0:T(4,128)S(1)} %get-tuple-element.132, f32[4,512]{1,0:T(4,128)S(1)} %get-tuple-element.136, bf16[1,512,4,256]{3,2,1,0:T(4,128)(2,1)} %get-tuple-element.130), kind=kOutput, calls=%fused_computation.69 | convolution fusion | flops 540016640 | bytes 7356416 | tf_op jit(solution)/shard_map/hre,rhc->ehc/dot_general | solution.py:45
  146.2 0.0 reduce-scatter.8.cloned.1.call-update
  146.2 0.0 reduce-scatter.6.cloned.1.call-start
  146.3 4.7 %fusion.13 = bf16[4,512,512]{1,2,0:T(8,128)(2,1)S(1)} fusion(f32[4,512,512]{2,1,0:T(8,128)} %get-tuple-element.138, f32[4,512,512]{2,1,0:T(8,128)} %get-tuple-element.137, f32[4,512]{1,0:T(4,128)S(1)} %get-tuple-element.133, f32[4,512]{1,0:T(4,128)S(1)} %get-tuple-element.132, f32[4,512]{1,0:T(4,128)S(1)} %get-tuple-element.136), kind=kLoop, calls=%fused_computation.30 | loop fusion | flops 5242880 | bytes 10510336 | tf_op jit(solution)/shard_map/convert_element_type | solution.py:40
  151.0 1.3 copy-done
  152.3 2.0 convolution_bitcast_fusion.1
  154.4 0.0 reduce-scatter.6.cloned.1.call-update
  154.4 0.0 reduce-scatter.12.cloned.1.call-start
  154.4 4.6 %fusion.46 = f32[512,4,256]{2,0,1:T(8,128)} fusion(f32[4,512,512]{2,1,0:T(8,128)} %get-tuple-element.140, f32[4,512]{1,0:T(4,128)S(1)} %get-tuple-element.134, f32[4,512]{1,0:T(4,128)S(1)} %get-tuple-element.139, bf16[1,512,4,256]{3,2,1,0:T(4,128)(2,1)S(1)} %get-tuple-element.131), kind=kOutput, calls=%fused_computation.68 | convolution fusion | flops 540016640 | bytes 7356416 | tf_op jit(solution)/shard_map/hre,rhc->ehc/dot_general | solution.py:45
  159.1 0.0 reduce-scatter.12.cloned.1.call-update
  159.1 0.0 all-reduce.3.cloned.1.call-start
  159.2 3.7 fusion.48
  162.9 1.7 fusion.49
  164.6 0.0 all-reduce.3.cloned.1.call-update
  164.6 0.3 reduce-scatter.14.cloned.1.call-start
  164.9 0.0 reduce-scatter.10.cloned.1.call-done
  164.9 6.3 %fusion.22 = f32[512,4096]{1,0:T(8,128)} fusion(bf16[2,4096,1,1,256]{4,1,3,2,0:T(8,128)(2,1)} %param.10, f32[512,1,256]{2,0,1:T(8,128)} %reduce-scatter.10.cloned.1.call-done), kind=kOutput, calls=%fused_computation.44 | convolution fusion | flops 1073872896 | bytes 11010048 | tf_op jit(solution)/shard_map/dc,ec->de/dot_general | solution.py:89
  171.2 7.0 %reduce-scatter.8.cloned.1.call-done = f32[512,1,256]{2,0,1:T(8,128)} async-done(((f32[512,4,256]{2,0,1:T(8,128)}), f32[512,1,256]{2,0,1:T(8,128)}) %reduce-scatter.8.cloned.1.call-update) | async-done | bytes 524304 | tf_op jit(solution)/shard_map/reduce_scatter | solution.py:80
  178.2 6.3 %fusion.26 = f32[512,4096]{1,0:T(8,128)} fusion(bf16[2,4096,1,1,256]{4,1,3,2,0:T(8,128)(2,1)} %param.11, f32[512,1,256]{2,0,1:T(8,128)} %reduce-scatter.8.cloned.1.call-done), kind=kOutput, calls=%fused_computation.48 | convolution fusion | flops 1073872896 | bytes 11010048 | tf_op jit(solution)/shard_map/dc,ec->de/dot_general | solution.py:92
  184.5 27.7 %reduce-scatter.6.cloned.1.call-done = f32[512,1,256]{2,0,1:T(8,128)} async-done(((f32[512,4,256]{2,0,1:T(8,128)}), f32[512,1,256]{2,0,1:T(8,128)}) %reduce-scatter.6.cloned.1.call-update) | async-done | bytes 524304 | tf_op jit(solution)/shard_map/reduce_scatter | solution.py:79
  212.2 6.3 %fusion.30 = f32[512,4096]{1,0:T(8,128)} fusion(bf16[2,4096,1,1,256]{4,1,3,2,0:T(8,128)(2,1)} %param.10, f32[512,1,256]{2,0,1:T(8,128)} %reduce-scatter.6.cloned.1.call-done), kind=kOutput, calls=%fused_computation.52 | convolution fusion | flops 1073872896 | bytes 11010048 | tf_op jit(solution)/shard_map/dc,ec->de/dot_general | solution.py:89
  218.5 27.9 %reduce-scatter.12.cloned.1.call-done = f32[512,1,256]{2,0,1:T(8,128)} async-done(((f32[512,4,256]{2,0,1:T(8,128)}), f32[512,1,256]{2,0,1:T(8,128)}) %reduce-scatter.12.cloned.1.call-update) | async-done | bytes 524304 | tf_op jit(solution)/shard_map/reduce_scatter | solution.py:80
  246.3 12.9 %fusion.6 = bf16[4096,512]{0,1:T(8,128)(2,1)} fusion(f32[512,4096]{1,0:T(8,128)} %fusion.22, f32[512,4096]{1,0:T(8,128)} %fusion.30, f32[512,4096]{1,0:T(8,128)} %fusion.26, bf16[2,4096,1,1,256]{4,1,3,2,0:T(8,128)(2,1)} %param.11, f32[512,1,256]{2,0,1:T(8,128)} %reduce-scatter.12.cloned.1.call-done), kind=kOutput, calls=%fused_computation.17 | convolution fusion | flops 1082261504 | bytes 31981568 | tf_op jit(solution)/shard_map/dc,ec->de/dot_general | solution.py:92
  259.2 0.0 reduce-scatter.14.cloned.1.call-update
  259.3 77.2 %all-reduce.3.cloned.1.call-done = (bf16[1,512,4,256]{1,3,2,0:T(8,128)(2,1)}, bf16[1,512,4,256]{1,3,2,0:T(8,128)(2,1)}) async-done(((bf16[1,512,4,256]{1,3,2,0:T(8,128)(2,1)}, bf16[1,512,4,256]{1,3,2,0:T(8,128)(2,1)}), (bf16[1,512,4,256]{1,3,2,0:T(8,128)(2,1)}, bf16[1,512,4,256]{1,3,2,0:T(8,128)(2,1)})) %all-reduce.3.cloned.1.call-update) | async-done | bytes 2097168 | tf_op jit(solution)/shard_map/psum | solution.py:43
  336.4 1.7 pad_maximum_fusion
  338.2 2.5 copy.32
  340.7 50.2 %reduce-scatter.14.cloned.1.call-done = bf16[512,512]{0,1:T(8,128)(2,1)} async-done(((bf16[4096,512]{0,1:T(8,128)(2,1)}), bf16[512,512]{0,1:T(8,128)(2,1)}) %reduce-scatter.14.cloned.1.call-update) | async-done | bytes 524304 | tf_op jit(solution)/shard_map/reduce_scatter | solution.py:95
  (48 shorter events, 0.5 us)
Async XLA Ops:
  7.2 24.6 %all-gather.25.cloned.1.call-start = ((), (), s32[]{:S(2)}) async-start(), calls=%async_computation.12 | async-start | bytes 1310720 | tf_op jit(solution)/shard_map/all_gather | solution.py:72
  12.1 38.1 %all-gather.27.cloned.1.call-start = ((), (), s32[]{:S(2)}) async-start(), calls=%async_computation.13 | async-start | bytes 1310720 | tf_op jit(solution)/shard_map/all_gather | solution.py:73
  16.9 72.2 %all-gather.21.cloned.1.call-start = ((), (), s32[]{:S(2)}) async-start(), calls=%async_computation.10 | async-start | bytes 1310720 | tf_op jit(solution)/shard_map/all_gather | solution.py:72
  21.9 5.2 %copy-start.6 = (bf16[2,512,4,256]{3,2,1,0:T(4,128)(2,1)S(1)}, bf16[2,512,4,256]{3,2,1,0:T(4,128)(2,1)}, u32[]{:S(2)}) copy-start(bf16[2,512,4,256]{3,2,1,0:T(4,128)(2,1)} %param.12) | copy-start | bytes 6291460
  21.9 87.3 %all-gather.23.cloned.1.call-start = ((), (), s32[]{:S(2)}) async-start(), calls=%async_computation.11 | async-start | bytes 1310720 | tf_op jit(solution)/shard_map/all_gather | solution.py:73
  27.0 137.9 %reduce-scatter.10.cloned.1.call-start = ((), (), s32[]{:S(2)}) async-start(), calls=%async_computation.7 | async-start | bytes 2621440 | tf_op jit(solution)/shard_map/reduce_scatter | solution.py:79
  27.0 1.7 copy-start.7
  28.8 7.3 %copy-start.2 = (bf16[1,512,4,256]{3,2,1,0:T(4,128)(2,1)}, bf16[1,512,4,256]{3,2,1,0:T(4,128)(2,1)S(1)}, u32[]{:S(2)}) copy-start(bf16[1,512,4,256]{3,2,1,0:T(4,128)(2,1)S(1)} %get-tuple-element.129) | copy-start | bytes 3145732
  33.3 22.5 %copy-start.4 = (bf16[512,1024]{0,1:T(8,128)(2,1)}, bf16[512,1024]{0,1:T(8,128)(2,1)S(1)}, u32[]{:S(2)}) copy-start(bf16[512,1024]{0,1:T(8,128)(2,1)S(1)} %copy.40) | copy-start | bytes 3145732
  82.2 4.7 %copy-start.3 = (bf16[1,512,4,256]{3,2,1,0:T(4,128)(2,1)S(1)}, bf16[1,512,4,256]{3,2,1,0:T(4,128)(2,1)}, u32[]{:S(2)}) copy-start(bf16[1,512,4,256]{3,2,1,0:T(4,128)(2,1)} %copy-done.2) | copy-start | bytes 3145732
  89.1 89.1 %reduce-scatter.8.cloned.1.call-start = ((), (), s32[]{:S(2)}) async-start(), calls=%async_computation.6 | async-start | bytes 2621440 | tf_op jit(solution)/shard_map/reduce_scatter | solution.py:80
  146.2 66.0 %reduce-scatter.6.cloned.1.call-start = ((), (), s32[]{:S(2)}) async-start(), calls=%async_computation.5 | async-start | bytes 2621440 | tf_op jit(solution)/shard_map/reduce_scatter | solution.py:79
  146.3 6.0 %copy-start.1 = (bf16[1,512,4,256]{3,2,1,0:T(4,128)(2,1)S(1)}, bf16[1,512,4,256]{3,2,1,0:T(4,128)(2,1)}, u32[]{:S(2)}) copy-start(bf16[1,512,4,256]{3,2,1,0:T(4,128)(2,1)} %get-tuple-element.128) | copy-start | bytes 3145732
  151.0 1.3 copy-start
  154.4 92.0 %reduce-scatter.12.cloned.1.call-start = ((), (), s32[]{:S(2)}) async-start(), calls=%async_computation.8 | async-start | bytes 2621440 | tf_op jit(solution)/shard_map/reduce_scatter | solution.py:80
  159.1 3.8 copy-start.5
  159.1 177.3 %all-reduce.3.cloned.1.call-start = ((), (), s32[]{:S(2)}) async-start(), calls=%async_computation.14 | async-start | bytes 4194304 | tf_op jit(solution)/shard_map/psum | solution.py:43
  164.6 226.3 %reduce-scatter.14.cloned.1.call-start = ((), (), s32[]{:S(2)}) async-start(), calls=%async_computation.9 | async-start | bytes 4718592 | tf_op jit(solution)/shard_map/reduce_scatter | solution.py:95
Sparse Core Ops, SparseCore 0:
  12.2 19.5 all-gather.24
  33.3 16.8 all-gather.26
  51.7 16.8 all-gather.20
  70.0 16.8 all-gather.22
  89.3 31.7 reduce-scatter.9
  146.4 31.8 reduce-scatter.7
  180.7 31.4 reduce-scatter.5
  214.9 31.4 reduce-scatter.11
  249.3 87.0 all-reduce.2
  340.6 50.2 reduce-scatter.13
where the time goes:
time: 398 us
  waiting for transfers between devices  192 us (48%)
  matrix products  88.7 us (22%)
  blocking collectives  79.2 us (20%)
  between operations  14.3 us (4%)
  other arithmetic  11.5 us (3%)
  local copies, waits for them, and re-layouts  11.1 us (3%)
    all_gather x6, blocking collectives, joined(): pieces = jax.tree.map(lambda part: lax.all_gather(part, axis), value)  79.2 us
    psum x1, waiting for transfers between devices, attention_grads(): query_grad = lax.psum(query_part.astype(jnp.bfloat16), 'inp')  77.2 us
    reduce_scatter x1, waiting for transfers between devices, body(): lax.psum_scatter(running.astype(jnp.bfloat16), ('tgt', 'mdl'), scatter_di...  50.2 us
    reduce_scatter x2, waiting for transfers between devices, body(): lax.psum_scatter(value_part, 'tgt', scatter_dimension=1, tiled=True)  34.9 us
    reduce_scatter x2, waiting for transfers between devices, body(): lax.psum_scatter(key_part, 'tgt', scatter_dimension=1, tiled=True)  27.7 us
    dot_general x2, matrix products, body(): jnp.einsum('dc,ec->de', value_matrix, value_flat, preferred_element_type=...  19.2 us
    dot_general x2, matrix products, body(): jnp.einsum('dc,ec->de', key_matrix, key_flat, preferred_element_type=jnp....  12.6 us
    dot_general x2, matrix products, attention_grads(): jnp.einsum('rhc,ehc->hre', grad_rows, value_block, preferred_element_type...  11.4 us
  transfers between devices with their start and end apart: 10, of which 7 were waited for; matrix products, arithmetic and copies ran while one was open for 26% of the time, Pallas kernels for 0%

commit v1 on v0

v1 whole, which is shorter than its diff:
```python
import functools

import jax
import jax.numpy as jnp
from jax import lax
from jax.experimental import pallas as pl
from jax.experimental.pallas import tpu as pltpu
from jax.sharding import PartitionSpec as P

F32, BF16 = jnp.float32, jnp.bfloat16
VMEM_BYTES = 48 * 1024 * 1024
NT = (((1,), (1,)), ((), ()))
NN = (((1,), (0,)), ((), ()))
TN = (((0,), (0,)), ((), ()))


def dot(left, right, dims):
    return lax.dot_general(left, right, dims, preferred_element_type=F32)


def params():
    return pltpu.CompilerParams(vmem_limit_bytes=VMEM_BYTES)


def cost(flops, nbytes, exps=0):
    return pl.CostEstimate(flops=1, bytes_accessed=1, transcendentals=0)


def partners(count, mask):
    return [(index, index ^ mask) for index in range(count)]


def join_kernel(rank_ref, *refs):
    out, held = refs[-2], refs[-1]
    heads = held.shape[0]

    @pl.when(rank_ref[1] == 0)
    def _():
        for mask in range(heads):
            held[mask] = refs[mask][0]

    @pl.when(rank_ref[1] != 0)
    def _():
        for mask in range(heads):
            held[mask] = refs[heads + mask][0]

    for head in range(heads):
        out[0, :, head, :] = held[rank_ref[0] ^ head]


def join_heads(rank, pieces, layer, layers, begun):
    heads = len(pieces) // 2
    rows, size = pieces[0][0].shape[1:]

    def place(index):
        return pl.BlockSpec((1, rows, size), lambda i, rank: (index, 0, 0))

    extra = [] if begun is None else [begun]
    return pl.pallas_call(
        join_kernel,
        grid_spec=pltpu.PrefetchScalarGridSpec(
            num_scalar_prefetch=1,
            grid=(1,),
            in_specs=[place(index) for _, index in pieces] + [pl.BlockSpec(memory_space=pl.ANY)] * len(extra),
            out_specs=pl.BlockSpec((1, rows, heads, size), lambda i, rank: (layer, 0, 0, 0)),
            scratch_shapes=[pltpu.VMEM((heads, rows, size), BF16)],
        ),
        out_shape=jax.ShapeDtypeStruct((layers, rows, heads, size), BF16),
        input_output_aliases={1 + len(pieces): 0} if extra else {},
        compiler_params=params(),
        cost_estimate=cost(0, 8 * rows * heads * size),
    )(rank, *[piece for piece, _ in pieces], *extra)


def project_kernel(enc_ref, wk_ref, wv_ref, k_ref, v_ref, sums):
    step = pl.program_id(0)

    @pl.when(step == 0)
    def _():
        sums[...] = jnp.zeros_like(sums)

    sums[0] += dot(enc_ref[...], wk_ref[0], NN)
    sums[1] += dot(enc_ref[...], wv_ref[0], NN)

    @pl.when(step == pl.num_programs(0) - 1)
    def _():
        k_ref[...] = sums[0].astype(BF16)
        v_ref[...] = sums[1].astype(BF16)


def project(encoder, wk, wv, layer):
    rows, width = encoder.shape
    size = wk.shape[2]
    depth = width // 4
    weight = pl.BlockSpec((1, depth, size), lambda i: (layer, i, 0))
    result = pl.BlockSpec((rows, size), lambda i: (0, 0))
    return pl.pallas_call(
        project_kernel,
        grid=(width // depth,),
        in_specs=[pl.BlockSpec((rows, depth), lambda i: (0, i)), weight, weight],
        out_specs=[result, result],
        out_shape=[jax.ShapeDtypeStruct((rows, size), BF16)] * 2,
        scratch_shapes=[pltpu.VMEM((2, rows, size), F32)],
        compiler_params=params(),
        cost_estimate=cost(4 * rows * width * size, 2 * width * (rows + 2 * size)),
    )(encoder, wk, wv)


def columns(index, count, rows, flip_ref):
    if index < count - 2:
        return slice(index * rows, (index + 1) * rows)
    start = (count - 2 + ((index - count + 2) ^ flip_ref[0])) * rows
    return pl.ds(pl.multiple_of(start, rows), rows)


def stats_kernel(flip_ref, k_ref, v_ref, *refs):
    out, pieces = refs[-1], refs[:-1]
    count = len(pieces) // 2
    for index in range(count):
        rows = pieces[index].shape[1]
        cols = columns(index, count, rows, flip_ref)
        scores = dot(k_ref[...], pieces[index][0], NT)
        peak = jnp.max(scores, axis=0, keepdims=True)
        shifted = jnp.exp(scores - peak)
        dprobs = dot(v_ref[...], pieces[count + index][0], NT)
        out[0:1, cols] = peak
        out[1:2, cols] = jnp.sum(shifted, axis=0, keepdims=True)
        out[2:3, cols] = jnp.sum(shifted * dprobs, axis=0, keepdims=True)
        out[3:4, cols] = jnp.zeros_like(peak)


def whole(shape):
    return pl.BlockSpec(shape, lambda i: (0,) * len(shape))


def of_layer(array, layer):
    index = layer if array.shape[0] > 1 else 0
    return pl.BlockSpec((1,) + array.shape[1:], lambda i: (index, 0, 0))


def row_stats(flip, keys, values, pieces, layer):
    enc_rows, size = keys.shape
    total = pieces[0].shape[1] * len(pieces) // 2
    return pl.pallas_call(
        stats_kernel,
        grid=(1,),
        in_specs=[pl.BlockSpec(memory_space=pltpu.SMEM), whole(keys.shape), whole(values.shape)]
        + [of_layer(array, layer) for array in pieces],
        out_specs=whole((4, total)),
        out_shape=jax.ShapeDtypeStruct((4, total), F32),
        compiler_params=params(),
        cost_estimate=cost(
            4 * enc_rows * total * size, 4 * size * (enc_rows + total), enc_rows * total
        ),
    )(flip, keys, values, *pieces)


def grads_kernel(count, flip_ref, k_ref, v_ref, *refs):
    queries, cotangents, stats = refs[:count], refs[count : 2 * count], refs[2 * count : -5]
    near_ref, straight_ref, across_ref, dk_ref, dv_ref = refs[-5:]
    keys, values = k_ref[...], v_ref[...]
    grads = []
    for index in range(count):
        query, cotangent = queries[index][0], cotangents[index][0]
        cols = columns(index, count, query.shape[0], flip_ref)
        parts = [part[:, cols] for part in stats]
        peak = functools.reduce(jnp.maximum, [part[0:1] for part in parts])
        scales = [jnp.exp(part[0:1] - peak) for part in parts]
        total = sum(part[1:2] * scale for part, scale in zip(parts, scales))
        inner = sum(part[2:3] * scale for part, scale in zip(parts, scales)) / total
        attention = jnp.exp(dot(keys, query, NT) - peak) * (1.0 / total)
        dprobs = dot(values, cotangent, NT)
        dscores = (attention * (dprobs - inner)).astype(BF16)
        query_grad = dot(dscores, keys, TN).astype(BF16)
        if index < count - 2:
            near_ref[index] = query_grad
        else:
            grads.append(query_grad)
        key_part = dot(dscores, query, NN)
        value_part = dot(attention.astype(BF16), cotangent, NN)
        key_sum = key_part if index == 0 else key_sum + key_part
        value_sum = value_part if index == 0 else value_sum + value_part
    dk_ref[...] = key_sum.astype(BF16)
    dv_ref[...] = value_sum.astype(BF16)

    @pl.when(flip_ref[0] == 0)
    def _():
        straight_ref[0], across_ref[0] = grads

    @pl.when(flip_ref[0] != 0)
    def _():
        across_ref[0], straight_ref[0] = grads


def attention_grads(flip, keys, values, pieces, stats, layer):
    enc_rows, size = keys.shape
    rows = pieces[0].shape[1]
    count = len(pieces) // 2
    total = rows * count
    outs = [(count - 2, rows, size), (1, rows, size), (1, rows, size), (enc_rows, size), (enc_rows, size)]
    return pl.pallas_call(
        functools.partial(grads_kernel, count),
        grid=(1,),
        in_specs=[pl.BlockSpec(memory_space=pltpu.SMEM), whole(keys.shape), whole(values.shape)]
        + [of_layer(array, layer) for array in pieces]
        + [whole((4, total))] * len(stats),
        out_specs=[whole(shape) for shape in outs],
        out_shape=[jax.ShapeDtypeStruct(shape, BF16) for shape in outs],
        compiler_params=params(),
        cost_estimate=cost(
            10 * enc_rows * total * size, 6 * size * (enc_rows + total), enc_rows * total
        ),
    )(flip, keys, values, *pieces, *stats)


def back_kernel(order_ref, wk_ref, wv_ref, *refs):
    out = refs[-1]
    layers = wk_ref.shape[0]
    total = refs[2 * layers][0].astype(F32) if len(refs) > 2 * layers + 1 else None
    for layer in range(layers):
        part = dot(refs[2 * layer][...], wk_ref[layer], NT)
        total = part if total is None else total + part
        total = total + dot(refs[2 * layer + 1][...], wv_ref[layer], NT)
    out[0] = total.astype(BF16)


def back_blocks(order, wk, wv, flat, share, arrived=None):
    layers, _, size = wk.shape
    rows = flat[0].shape[0]
    blocks = order.shape[0]
    weight = pl.BlockSpec((layers, share, size), lambda i, order: (0, order[i], 0))
    result = pl.BlockSpec((1, rows, share), lambda i, order: (i, 0, 0))
    extra = [] if arrived is None else [arrived]
    return pl.pallas_call(
        back_kernel,
        grid_spec=pltpu.PrefetchScalarGridSpec(
            num_scalar_prefetch=1,
            grid=(blocks,),
            in_specs=[weight, weight]
            + [pl.BlockSpec((rows, size), lambda i, order: (0, 0))] * len(flat)
            + [result] * len(extra),
            out_specs=result,
        ),
        out_shape=jax.ShapeDtypeStruct((blocks, rows, share), BF16),
        compiler_params=params(),
        cost_estimate=cost(
            4 * layers * rows * size * share * blocks, 2 * blocks * share * (2 * layers * size + 2 * rows)
        ),
    )(order, wk, wv, *flat, *extra)


def plus(one, two):
    return (one.astype(F32) + two.astype(F32)).astype(BF16)


def exchange(value, n_inp, n_tgt, mask_of):
    pairs = [(z * n_tgt + t, z * n_tgt + (t ^ mask_of(z))) for z in range(n_inp) for t in range(n_tgt)]
    return lax.ppermute(value, ("inp", "tgt"), pairs)


def everywhere(value, n_inp):
    return [value] + [
        lax.ppermute(value, "inp", [(i, (i + shift) % n_inp) for i in range(n_inp)])
        for shift in range(1, n_inp)
    ]


def after(value, *others):
    return lax.optimization_barrier((value, *others))[0]


class LineSums:
    def __init__(self, n_inp):
        self.n_inp, self.inner, self.total, self.outer = n_inp, [], [], []

    def send(self, value, *others, hold=()):
        if self.n_inp != 4:
            total = lax.psum(value, "inp")
            self.total.append(total)
            self.outer.append(total)
            return
        count = len(self.total)

        def earlier(results, back):
            return results[count - back : count - back + 1] if count >= back else []

        lead = 1 if count < 2 else 2
        value = after(value, *others, *earlier(self.inner, lead), *earlier(self.total, 3), *earlier(self.outer, 4))
        inner = plus(after(value, *hold), lax.ppermute(value, "inp", [(0, 1), (3, 2)]))
        inner = after(inner, *earlier(self.outer, 3 if count < 4 else 2))
        total = plus(inner, lax.ppermute(inner, "inp", [(1, 2), (2, 1)]))
        total = after(total, *earlier(self.outer, 2))
        self.inner.append(inner)
        self.total.append(total)
        self.outer.append(lax.ppermute(total, "inp", [(1, 0), (2, 3)]))


def body(encoder, key_weight, value_weight, queries, grad_out):
    layers, dec_rows, heads, size = queries.shape
    width = encoder.shape[1]
    n_inp, n_tgt, n_mdl = (lax.axis_size(axis) for axis in ("inp", "tgt", "mdl"))
    z, t, m = (lax.axis_index(axis) for axis in ("inp", "tgt", "mdl"))
    share = width // (n_tgt * n_mdl)
    wk = key_weight.reshape(layers, width, size)
    wv = value_weight.reshape(layers, width, size)
    far = ((z == 0) | (z == n_inp - 1)).astype(jnp.int32)
    odd = (z % 2).astype(jnp.int32)
    rank = jnp.stack([t.astype(jnp.int32), far])

    sources = [jnp.transpose(array, (2, 0, 1, 3)) for array in (queries, grad_out)]

    def head(source, mask):
        return lax.dynamic_index_in_dim(source, t ^ mask, 0, keepdims=False)

    wanted = [[head(source, 2 + odd)[layer : layer + 1] for source in sources] for layer in range(layers)]
    fetched = [
        [exchange(piece, n_inp, n_tgt, lambda z: 2 + z % 2) for piece in pair] for pair in wanted
    ]
    own = [head(source, 0) for source in sources]
    beside = [lax.ppermute(head(source, 1), "tgt", partners(n_tgt, 1)) for source in sources]
    begun = [piece for pair in wanted for piece in pair]
    keys, values, handed = [], [], []
    for layer in range(layers):
        key_block, value_block = project(after(encoder, *begun), wk, wv, layer)
        begun = fetched[0][:1]
        keys.append(key_block)
        values.append(value_block)
    for layer in range(layers):
        handed.append([])
        for kind in range(2):
            ahead = keys[min(layers - 1, 2 * layer + kind)]
            handed[layer].append(lax.ppermute(after(fetched[layer][kind], ahead), "inp", partners(n_inp, 1)))

    pieces, stats = [], []
    for layer in range(layers):
        pieces.append(
            [
                array
                for kind in range(2)
                for array in (own[kind], beside[kind], fetched[layer][kind], handed[layer][kind])
            ]
        )
        own_stats = row_stats(odd[None], keys[layer], values[layer], pieces[layer], layer)
        stats.append(everywhere(own_stats, n_inp))
    flat, near, straight, across = [], [], [], []
    for layer in range(layers):
        results = attention_grads(odd[None], keys[layer], values[layer], pieces[layer], stats[layer], layer)
        near.append(results[0])
        straight.append(lax.ppermute(after(results[1], *straight[-1:]), "tgt", partners(n_tgt, 2)))
        across.append(lax.ppermute(after(results[2], *across[-1:]), "tgt", partners(n_tgt, 3)))
        flat += results[3:]
    sums_over = LineSums(n_inp)
    for layer in range(layers):
        sums_over.send(near[layer], *(stats[-1] if layer == 0 else ()), hold=near[-1:])

    def order(mask):
        return jnp.stack([(t ^ mask) * n_mdl + (m ^ side) for side in range(n_mdl)]).astype(jnp.int32)

    masks = list(reversed(range(0, n_tgt, 2)))
    arrived = []
    for mask in masks:
        sent = back_blocks(after(order(mask + 1), across[0]), wk, wv, flat, share)
        arrived.append(lax.ppermute(sent, "tgt", partners(n_tgt, 1)))
    sums_over.send(straight[0])
    total, blocks = None, []
    for mask, wait, block in zip(masks, [straight[-1], across[-1]], arrived):
        blocks.append(back_blocks(after(order(mask), wait), wk, wv, flat, share, block))
        for side in reversed(range(n_mdl)):
            block = blocks[-1][side]
            if mask or side:
                pairs = [
                    (a * n_mdl + b, (a ^ mask) * n_mdl + (b ^ side))
                    for a in range(n_tgt)
                    for b in range(n_mdl)
                ]
                block = lax.ppermute(block, ("tgt", "mdl"), pairs)
            total = block.astype(F32) if total is None else total + block.astype(F32)
    later = [piece for pair in zip(straight, across) for piece in pair][1:]
    for index, piece in enumerate(later):
        sums_over.send(piece, *blocks[index : index + 1])
    done = list(zip(sums_over.total, sums_over.outer))
    beside_grad = jnp.stack([jnp.where(far > 0, there[1], here[1]) for here, there in done[:layers]])
    beside_grad = lax.ppermute(beside_grad, "tgt", partners(n_tgt, 1))
    query_grads = None
    for layer in range(layers):
        chunks = [done[layer], (beside_grad,) * 2, done[layers + 2 * layer], done[layers + 2 * layer + 1]]
        places = [(chunk[side], layer if mask == 1 else 0) for side in range(2) for mask, chunk in enumerate(chunks)]
        query_grads = join_heads(rank, places, layer, layers, query_grads)

    return query_grads, total.astype(BF16)


def solution(mesh):
    placed = (
        P("inp", None),
        P(None, None, "mdl", "tgt", None),
        P(None, None, "mdl", "tgt", None),
        P(None, "tgt", "mdl", None),
        P(None, "tgt", "mdl", None),
    )
    return jax.shard_map(
        body,
        mesh=mesh,
        in_specs=placed,
        out_specs=(P(None, "tgt", "mdl", None), P("inp", ("tgt", "mdl"))),
        check_vma=False,
    )
```

time: 398 us -> 188 us (0.47)
  waiting for transfers between devices: 192 us -> 47.1 us
  matrix products: 88.7 us -> 0 us
  blocking collectives: 79.2 us -> 0 us
  starting transfers between devices: 0.64 us -> 67.9 us
  Pallas kernels: 0 us -> 44.6 us
  between operations: 14.3 us -> 1.19 us
  local copies, waits for them, and re-layouts: 11.1 us -> 16.6 us
    reduce_scatter x5 -> x0, waiting for transfers between devices: 113 us -> none  [the longest x1 50.2 us: body(): lax.psum_scatter(running.astype(jnp.bfloat16), ('tgt', 'mdl'), scatter_di...]
    dot_general x18 -> x0, matrix products: 88.7 us -> none  [the longest x2 19.2 us: body(): jnp.einsum('dc,ec->de', value_matrix, value_flat, preferred_element_type=...]
    all_gather x6 -> x0, blocking collectives: 79.2 us -> none  [joined(): pieces = jax.tree.map(lambda part: lax.all_gather(part, axis), value)]
    psum x1 -> x0, waiting for transfers between devices: 77.2 us -> none  [attention_grads(): query_grad = lax.psum(query_part.astype(jnp.bfloat16), 'inp')]
    ppermute x0 -> x44, starting transfers between devices: none -> 67.9 us  [the longest x6 24.1 us: send(): lax.ppermute(value, 'inp', [(0, 1), (3, 2)])]
    ppermute x0 -> x44, waiting for transfers between devices: none -> 47.1 us  [the longest x6 27.4 us: send(): self.outer.append(lax.ppermute(total, 'inp', [(1, 0), (2, 3)]))]
    pallas_call x0 -> x12, Pallas kernels: none -> 44.6 us  [the longest x4 14.7 us: back_blocks(): pl.pallas_call(back_kernel, grid_spec=pltpu.PrefetchScalarGridSpec(num_sc...]
    another operation x0 -> x1, local copies, waits for them, and re-layouts: none -> 11.1 us
  transfers between devices with their start and end apart: 10 -> 44, of which waited for: 7 -> 9; matrix products, arithmetic and copies ran while one was open for 26% -> 6% of each run, Pallas kernels for 0% -> 22%
where the time goes in v1:
time: 188 us; the launch traced here: 187 us
  starting transfers between devices  67.9 us (36%)
  waiting for transfers between devices  47.1 us (25%)
  Pallas kernels  44.6 us (24%)
  local copies, waits for them, and re-layouts  16.6 us (9%)
  other arithmetic  9.88 us (5%)
    ppermute x6, waiting for transfers between devices, send(): self.outer.append(lax.ppermute(total, 'inp', [(1, 0), (2, 3)]))  27.4 us
    ppermute x6, starting transfers between devices, send(): lax.ppermute(value, 'inp', [(0, 1), (3, 2)])  24.1 us
    pallas_call x4, Pallas kernels, back_blocks(): pl.pallas_call(back_kernel, grid_spec=pltpu.PrefetchScalarGridSpec(num_sc...  14.7 us
    another operation x1, local copies, waits for them, and re-layouts  11.1 us
    ppermute x6, starting transfers between devices, everywhere(): lax.ppermute(value, 'inp', [(i, (i + shift) % n_inp) for i in range(n_inp)])  11 us
    pallas_call x2, Pallas kernels, project(): pl.pallas_call(project_kernel, grid=(width // depth,), in_specs=[pl.Block...  9.95 us
    pallas_call x2, Pallas kernels, attention_grads(): pl.pallas_call(functools.partial(grads_kernel, count), grid=(1,), in_spec...  9.07 us
    convert_element_type x12, other arithmetic, plus(): return (one.astype(F32) + two.astype(F32)).astype(BF16)  8.39 us
  transfers between devices with their start and end apart: 44, of which 9 were waited for; matrix products, arithmetic and copies ran while one was open for 6% of the time, Pallas kernels for 22%

profile of v1, /device:TPU:0, one launch (start us, length us, event | category | flops | bytes accessed | tf_op | source)
XLA Modules:
  0.0 187.3 jit_solution(8650798690093714322)
XLA Ops:
  0.7 11.1 %constant_dynamic-slice_fusion = (bf16[2,512,1,256]{3,2,1,0:T(2,128)(2,1)S(1)}, bf16[2,512,1,256]{3,2,1,0:T(2,128)(2,1)S(1)}, bf16[2,512,1,256]{3,2,1,0:T(2,128)...) fusion(bf16[2,512,4,256]{3,2,1,0:T(4,128)(2,1)} %param.9, ...), kind=kLoop, calls=%fused_computation.31 | loop fusion | bytes 6291468 | tf_op jit(solution)/shard_map/dynamic-slice.5
  11.9 3.0 %collective-permute-start = (bf16[1,512,256]{2,1,0:T(8,128)(2,1)S(1)}, bf16[1,512,256]{2,1,0:T(8,128)(2,1)S(1)}, u32[]{:S(2)}, u32[]{:S(2)}) collective-permute-start(bf16[1,512,256]{2,1,0:T(8,128)(2,1)S(1)} %get-tuple-element.95), channel_id=1, source_target_pairs={{0,4},{2,6},{4,0},{6,2},{8,14},{10,12},{12,10},{14,8},{16,20},{18,... | collective-permute-start | bytes 786440 | tf_op jit(solution)/shard_map/ppermute | solution.py:258
  15.1 2.0 %collective-permute-start.5 = (bf16[1,512,256]{2,1,0:T(8,128)(2,1)S(1)}, bf16[1,512,256]{2,1,0:T(8,128)(2,1)S(1)}, u32[]{:S(2)}, u32[]{:S(2)}) collective-permute-start(bf16[1,512,256]{2,1,0:T(8,128)(2,1)S(1)} %get-tuple-element.93), channel_id=1, source_target_pairs={{0,4},{2,6},{4,0},{6,2},{8,14},{10,12},{12,10},{14,8},{16,20},{18,... | collective-permute-start | bytes 786440 | tf_op jit(solution)/shard_map/ppermute | solution.py:258
  17.9 4.1 %collective-permute-done.refs_2_ = bf16[1,512,256]{2,1,0:T(8,128)(2,1)S(1)} collective-permute-done((bf16[1,512,256]{2,1,0:T(8,128)(2,1)S(1)}, bf16[1,512,256]{2,1,0:T(8,128)(2,1)S(1)}, u32[]{:S(2)}, u32[]{:S(2)}) %collective-permute-start) | collective-permute-done | bytes 262176 | tf_op jit(solution)/shard_map/ppermute | solution.py:258
  22.0 2.1 %collective-permute-start.2 = (bf16[1,512,256]{2,1,0:T(8,128)(2,1)S(1)}, bf16[1,512,256]{2,1,0:T(8,128)(2,1)S(1)}, u32[]{:S(2)}, u32[]{:S(2)}) collective-permute-start(bf16[1,512,256]{2,1,0:T(8,128)(2,1)S(1)} %get-tuple-element.94), channel_id=1, source_target_pairs={{0,4},{2,6},{4,0},{6,2},{8,14},{10,12},{12,10},{14,8},{16,20},{18,... | collective-permute-start | bytes 786440 | tf_op jit(solution)/shard_map/ppermute | solution.py:258
  24.1 5.0 %shard_map.68 = (bf16[512,256]{1,0:T(8,128)(2,1)S(1)}, bf16[512,256]{1,0:T(8,128)(2,1)S(1)}) custom-call(bf16[512,4096]{1,0:T(8,128)(2,1)S(1)} %copy-done, bf16[2,4096,256]{2,1,0:T(8,128)(2,1)} %bitcast.58, bf16[2,4096,256]{2,1,0:T(8,128)(2,1)} %bitcast.64), custom_call_target="tpu_custom_call" | custom-call | flops 1 | bytes 1 | tf_op jit(solution)/shard_map/pallas_call | solution.py:97
  29.1 0.8 collective-permute-start.12
  29.9 5.0 %shard_map.71 = (bf16[512,256]{1,0:T(8,128)(2,1)S(1)}, bf16[512,256]{1,0:T(8,128)(2,1)S(1)}) custom-call(bf16[512,4096]{1,0:T(8,128)(2,1)S(1)} %copy-done, bf16[2,4096,256]{2,1,0:T(8,128)(2,1)} %bitcast.59, bf16[2,4096,256]{2,1,0:T(8,128)(2,1)} %bitcast.65), custom_call_target="tpu_custom_call" | custom-call | flops 1 | bytes 1 | tf_op jit(solution)/shard_map/pallas_call | solution.py:97
  34.9 1.4 collective-permute-start.10
  36.2 1.8 collective-permute-done.2.refs_2_
  38.0 2.3 %collective-permute-start.6 = (bf16[1,512,256]{2,1,0:T(8,128)(2,1)S(1)}, bf16[1,512,256]{2,1,0:T(8,128)(2,1)S(1)}, u32[]{:S(2)}, u32[]{:S(2)}) collective-permute-start(bf16[1,512,256]{2,1,0:T(8,128)(2,1)S(1)} %collective-permute-done.5.refs_6_), channel_id=1, source_target_pairs={{0,8},{8,0},{16,24},{24,16},{1,9},{9,1},{17,25},{25,17},{2,10},{10... | collective-permute-start | bytes 786440 | tf_op jit(solution)/shard_map/ppermute | solution.py:332
  40.6 3.5 %collective-permute-done.10.refs_3_ = bf16[1,512,256]{2,1,0:T(8,128)(2,1)S(1)} collective-permute-done((bf16[1,512,256]{2,1,0:T(8,128)(2,1)S(1)}, bf16[1,512,256]{2,1,0:T(8,128)(2,1)S(1)}, u32[]{:S(2)}, u32[]{:S(2)}) %collective-permute-start.10) | collective-permute-done | bytes 262176 | tf_op jit(solution)/shard_map/ppermute | solution.py:332
  44.1 1.6 shard_map.72.refs_8_
  45.8 0.9 collective-permute-start.13
  46.6 2.6 %collective-permute-start.14 = (f32[4,2048]{1,0:T(4,128)S(1)}, f32[4,2048]{1,0:T(4,128)S(1)}, u32[]{:S(2)}, u32[]{:S(2)}) collective-permute-start(f32[4,2048]{1,0:T(4,128)S(1)} %shard_map.72.refs_8_), channel_id=1, source_target_pairs={{0,16},{8,24},{16,0},{24,8},{1,17},{9,25},{17,1},{25,9},{2,18},{10... | collective-permute-start | bytes 98312 | tf_op jit(solution)/shard_map/ppermute | solution.py:263
  49.2 2.1 %collective-permute-start.15 = (f32[4,2048]{1,0:T(4,128)S(1)}, f32[4,2048]{1,0:T(4,128)S(1)}, u32[]{:S(2)}, u32[]{:S(2)}) collective-permute-start(f32[4,2048]{1,0:T(4,128)S(1)} %shard_map.72.refs_8_), channel_id=1, source_target_pairs={{0,24},{8,0},{16,8},{24,16},{1,25},{9,1},{17,9},{25,17},{2,26},{10... | collective-permute-start | bytes 98312 | tf_op jit(solution)/shard_map/ppermute | solution.py:263
  51.3 4.2 %collective-permute-done.3.refs_3_ = bf16[1,512,256]{2,1,0:T(8,128)(2,1)S(1)} collective-permute-done((bf16[1,512,256]{2,1,0:T(8,128)(2,1)S(1)}, bf16[1,512,256]{2,1,0:T(8,128)(2,1)S(1)}, u32[]{:S(2)}, u32[]{:S(2)}) %collective-permute-start.3) | collective-permute-done | bytes 262176 | tf_op jit(solution)/shard_map/ppermute | solution.py:332
  55.5 1.6 shard_map.69.refs_8_
  57.1 0.7 collective-permute-start.7
  57.9 3.1 %collective-permute-start.8 = (f32[4,2048]{1,0:T(4,128)S(1)}, f32[4,2048]{1,0:T(4,128)S(1)}, u32[]{:S(2)}, u32[]{:S(2)}) collective-permute-start(f32[4,2048]{1,0:T(4,128)S(1)} %shard_map.69.refs_8_), channel_id=1, source_target_pairs={{0,16},{8,24},{16,0},{24,8},{1,17},{9,25},{17,1},{25,9},{2,18},{10... | collective-permute-start | bytes 98312 | tf_op jit(solution)/shard_map/ppermute | solution.py:263
  61.0 1.6 collective-permute-start.9
  62.6 4.6 %shard_map.73 = (bf16[2,512,256]{2,1,0:T(8,128)(2,1)}, bf16[1,512,256]{2,1,0:T(8,128)(2,1)}, bf16[1,512,256]{2,1,0:T(8,128)(2,1)}, bf16[512,256]{1,0:T(8,128)(2,1)S(1)}, bf16[512,256]{1,0:T(8,128)(2,1)S(1)}) custom-call(s32[1]{0:T(128)} %bitcast.2.flip_ref, bf16[512,256]{1,0:T(8,128)(2,1)S(1)} %get-tuple-element.50.k_ref, ...), custom_call_target="tpu_custom_call" | custom-call | flops 1 | bytes 1 | tf_op jit(solution)/shard_map/pallas_call | solution.py:201
  67.1 3.2 %collective-permute-start.16 = (bf16[2,512,256]{2,1,0:T(8,128)(2,1)}, bf16[2,512,256]{2,1,0:T(8,128)(2,1)}, u32[]{:S(2)}, u32[]{:S(2)}) collective-permute-start(bf16[2,512,256]{2,1,0:T(8,128)(2,1)} %get-tuple-element.56), channel_id=1, source_target_pairs={{0,8},{24,16},{1,9},{25,17},{2,10},{26,18},{3,11},{27,19},{4,12},{... | collective-permute-start | bytes 1572872 | tf_op jit(solution)/shard_map/ppermute | solution.py:289
  71.0 0.9 copy-done.2
  71.9 0.9 copy-done.4
  72.9 0.9 copy-done.6
  73.8 0.9 copy-done.8
  74.8 0.9 copy-done.10
  75.7 4.5 %shard_map.70 = (bf16[2,512,256]{2,1,0:T(8,128)(2,1)}, bf16[1,512,256]{2,1,0:T(8,128)(2,1)}, bf16[1,512,256]{2,1,0:T(8,128)(2,1)}, bf16[512,256]{1,0:T(8,128)(2,1)S(1)}, bf16[512,256]{1,0:T(8,128)(2,1)S(1)}) custom-call(s32[1]{0:T(128)} %bitcast.2.flip_ref, bf16[512,256]{1,0:T(8,128)(2,1)S(1)} %copy-done.4, bf16[512,256]{1,0:T(8,128)(2,1)S(1)} %copy-done.6, ...), custom_call_target="tpu_custom_call" | custom-call | flops 1 | bytes 1 | tf_op jit(solution)/shard_map/pallas_call | solution.py:201
  80.2 1.5 collective-permute-start.24
  81.7 1.5 collective-permute-start.26
  83.2 2.1 %add_convert_fusion.3 = bf16[2,512,256]{2,1,0:T(8,128)(2,1)} fusion(bf16[2,512,256]{2,1,0:T(8,128)(2,1)} %collective-permute-done.16, bf16[2,512,256]{2,1,0:T(8,128)(2,1)} %get-tuple-element.56), kind=kLoop, calls=%fused_computation.5 | loop fusion | flops 1048576 | bytes 1572864 | tf_op jit(solution)/shard_map/convert_element_type | solution.py:253
  85.3 2.1 %collective-permute-start.17 = (bf16[2,512,256]{2,1,0:T(8,128)(2,1)}, bf16[2,512,256]{2,1,0:T(8,128)(2,1)}, u32[]{:S(2)}, u32[]{:S(2)}) collective-permute-start(bf16[2,512,256]{2,1,0:T(8,128)(2,1)} %get-tuple-element.58), channel_id=1, source_target_pairs={{0,8},{24,16},{1,9},{25,17},{2,10},{26,18},{3,11},{27,19},{4,12},{... | collective-permute-start | bytes 1572872 | tf_op jit(solution)/shard_map/ppermute | solution.py:289
  87.4 2.0 %collective-permute-start.28 = (bf16[1,512,256]{2,1,0:T(8,128)(2,1)}, bf16[1,512,256]{2,1,0:T(8,128)(2,1)}, u32[]{:S(2)}, u32[]{:S(2)}) collective-permute-start(bf16[1,512,256]{2,1,0:T(8,128)(2,1)} %collective-permute-done.23), channel_id=1, source_target_pairs={{0,8},{24,16},{1,9},{25,17},{2,10},{26,18},{3,11},{27,19},{4,12},{... | collective-permute-start | bytes 786440 | tf_op jit(solution)/shard_map/ppermute | solution.py:289
  89.5 4.1 %shard_map.76 = bf16[2,512,512]{2,1,0:T(8,128)(2,1)} custom-call(s32[2]{0:T(128)S(1)} %get-tuple-element.77.order_ref, bf16[2,4096,256]{2,1,0:T(8,128)(2,1)} %bitcast.60, bf16[2,4096,256]{2,1,0:T(8,128)(2,1)} %bitcast.66, bf16[512,256]{1,0:T(8,128)(2,1)S(1)} %get-tuple-element.66.refs_0_, bf16[512,256]{1,0:T(8,128)(2,1)S(1)} %get-tuple-element.67.refs_1_, ...), custom_call_target="tpu_custom_call" | custom-call | flops 1 | bytes 1 | tf_op jit(solution)/shard_map/pallas_call | solution.py:234
  93.6 4.1 %shard_map.74 = bf16[2,512,512]{2,1,0:T(8,128)(2,1)} custom-call(s32[2]{0:T(128)S(1)} %get-tuple-element.70.order_ref, bf16[2,4096,256]{2,1,0:T(8,128)(2,1)} %bitcast.61, bf16[2,4096,256]{2,1,0:T(8,128)(2,1)} %bitcast.67, bf16[512,256]{1,0:T(8,128)(2,1)S(1)} %get-tuple-element.66.refs_0_, bf16[512,256]{1,0:T(8,128)(2,1)S(1)} %get-tuple-element.67.refs_1_, ...), custom_call_target="tpu_custom_call" | custom-call | flops 1 | bytes 1 | tf_op jit(solution)/shard_map/pallas_call | solution.py:234
  98.2 1.4 collective-permute-start.19
  99.7 3.7 %collective-permute-done.28 = bf16[1,512,256]{2,1,0:T(8,128)(2,1)} collective-permute-done((bf16[1,512,256]{2,1,0:T(8,128)(2,1)}, bf16[1,512,256]{2,1,0:T(8,128)(2,1)}, u32[]{:S(2)}, u32[]{:S(2)}) %collective-permute-start.28) | collective-permute-done | bytes 262176 | tf_op jit(solution)/shard_map/ppermute | solution.py:289
  103.4 1.1 add_convert_fusion.11
  105.2 1.3 add_convert_fusion.2
  106.5 0.7 collective-permute-start.18
  107.2 1.3 add_convert_fusion.refs_0_
  108.6 1.3 collective-permute-start.20
  110.0 3.3 %shard_map.77 = bf16[2,512,512]{2,1,0:T(8,128)(2,1)S(1)} custom-call(s32[2]{0:T(128)S(1)} %pad_add_fusion.3.order_ref, bf16[2,4096,256]{2,1,0:T(8,128)(2,1)} %bitcast.62, bf16[2,4096,256]{2,1,0:T(8,128)(2,1)} %bitcast.68, bf16[512,256]{1,0:T(8,128)(2,1)S(1)} %get-tuple-element.66.refs_0_, bf16[512,256]{1,0:T(8,128)(2,1)S(1)} %get-tuple-element.67.refs_1_, ...), custom_call_target="tpu_custom_call" | custom-call | flops 1 | bytes 1 | tf_op jit(solution)/shard_map/pallas_call | solution.py:234
  113.3 10.2 %collective-permute-start.34 = (bf16[1,512,256]{2,1,0:T(8,128)(2,1)}, bf16[1,512,256]{2,1,0:T(8,128)(2,1)S(1)}, u32[]{:S(2)}, u32[]{:S(2)}) collective-permute-start(bf16[1,512,256]{2,1,0:T(8,128)(2,1)} %collective-permute-done.25), channel_id=1, source_target_pairs={{0,8},{24,16},{1,9},{25,17},{2,10},{26,18},{3,11},{27,19},{4,12},{... | collective-permute-start | bytes 786440 | tf_op jit(solution)/shard_map/ppermute | solution.py:289
  123.4 3.3 %shard_map.75 = bf16[2,512,512]{2,1,0:T(8,128)(2,1)S(1)} custom-call(s32[2]{0:T(128)S(1)} %pad_add_fusion.1.order_ref, bf16[2,4096,256]{2,1,0:T(8,128)(2,1)} %bitcast.63, bf16[2,4096,256]{2,1,0:T(8,128)(2,1)} %bitcast.69, bf16[512,256]{1,0:T(8,128)(2,1)S(1)} %get-tuple-element.66.refs_0_, bf16[512,256]{1,0:T(8,128)(2,1)S(1)} %get-tuple-element.67.refs_1_, ...), custom_call_target="tpu_custom_call" | custom-call | flops 1 | bytes 1 | tf_op jit(solution)/shard_map/pallas_call | solution.py:234
  127.0 3.4 %collective-permute-start.29 = (bf16[1,512,256]{2,1,0:T(8,128)(2,1)}, bf16[1,512,256]{2,1,0:T(8,128)(2,1)S(1)}, u32[]{:S(2)}, u32[]{:S(2)}) collective-permute-start(bf16[1,512,256]{2,1,0:T(8,128)(2,1)} %collective-permute-done.24), channel_id=1, source_target_pairs={{0,8},{24,16},{1,9},{25,17},{2,10},{26,18},{3,11},{27,19},{4,12},{... | collective-permute-start | bytes 786440 | tf_op jit(solution)/shard_map/ppermute | solution.py:289
  130.4 2.2 %collective-permute-start.41 = (bf16[512,512]{1,0:T(8,128)(2,1)S(1)}, bf16[512,512]{1,0:T(8,128)(2,1)S(1)}, u32[]{:S(2)}, u32[]{:S(2)}) collective-permute-start(bf16[512,512]{1,0:T(8,128)(2,1)S(1)} %get-tuple-element.90), channel_id=1, source_target_pairs={{0,5},{1,4},{2,7},{3,6},{4,1},{5,0},{6,3},{7,2},{8,13},{9,12},{10,... | collective-permute-start | bytes 1572872 | tf_op jit(solution)/shard_map/ppermute | solution.py:376
  132.6 0.8 collective-permute-start.42
  133.5 1.3 collective-permute-start.21
  134.8 1.3 collective-permute-start.31
  136.1 1.0 add_convert_fusion.7
  137.8 1.0 add_convert_fusion.10
  138.8 14.1 %collective-permute-done.31.refs_6_ = bf16[1,512,256]{2,1,0:T(8,128)(2,1)S(1)} collective-permute-done((bf16[1,512,256]{2,1,0:T(8,128)(2,1)S(1)}, bf16[1,512,256]{2,1,0:T(8,128)(2,1)S(1)}, u32[]{:S(2)}, u32[]{:S(2)}) %collective-permute-start.31) | collective-permute-done | bytes 262176 | tf_op jit(solution)/shard_map/ppermute | solution.py:295
  154.1 3.3 %collective-permute-start.35 = (bf16[1,512,256]{2,1,0:T(8,128)(2,1)S(1)}, bf16[1,512,256]{2,1,0:T(8,128)(2,1)S(1)}, u32[]{:S(2)}, u32[]{:S(2)}) collective-permute-start(bf16[1,512,256]{2,1,0:T(8,128)(2,1)S(1)} %copy-done.12), channel_id=1, source_target_pairs={{0,8},{24,16},{1,9},{25,17},{2,10},{26,18},{3,11},{27,19},{4,12},{... | collective-permute-start | bytes 786440 | tf_op jit(solution)/shard_map/ppermute | solution.py:289
  157.6 1.3 collective-permute-start.37
  158.9 2.4 %collective-permute-done.35 = bf16[1,512,256]{2,1,0:T(8,128)(2,1)S(1)} collective-permute-done((bf16[1,512,256]{2,1,0:T(8,128)(2,1)S(1)}, bf16[1,512,256]{2,1,0:T(8,128)(2,1)S(1)}, u32[]{:S(2)}, u32[]{:S(2)}) %collective-permute-start.35) | collective-permute-done | bytes 262176 | tf_op jit(solution)/shard_map/ppermute | solution.py:289
  161.3 1.5 collective-permute-start.39
  162.9 4.4 %collective-permute-done.37.refs_7_ = bf16[1,512,256]{2,1,0:T(8,128)(2,1)S(1)} collective-permute-done((bf16[1,512,256]{2,1,0:T(8,128)(2,1)S(1)}, bf16[1,512,256]{2,1,0:T(8,128)(2,1)S(1)}, u32[]{:S(2)}, u32[]{:S(2)}) %collective-permute-start.37) | collective-permute-done | bytes 262176 | tf_op jit(solution)/shard_map/ppermute | solution.py:295
  168.2 1.3 collective-permute-start.40
  169.6 1.1 fusion
  170.6 3.8 %shard_map.78.refs_8_ = bf16[2,512,4,256]{3,2,1,0:T(4,128)(2,1)} custom-call(s32[2]{0:T(128)S(1)} %pad_add_fusion.rank_ref, bf16[2,512,256]{2,1,0:T(8,128)(2,1)S(1)} %add_convert_fusion.refs_0_, bf16[2,512,256]{2,1,0:T(8,128)(2,1)S(1)} %collective-permute-done.22.refs_1_.refs_5_, bf16[1,512,256]{2,1,0:T(8,128)(2,1)S(1)} %add_convert_fusion.9.refs_2_, ...), custom_call_target="tpu_custom_call" | custom-call | flops 1 | bytes 1 | tf_op jit(solution)/shard_map/pallas_call | solution.py:59
  174.5 9.0 %collective-permute-done.40.refs_7_ = bf16[1,512,256]{2,1,0:T(8,128)(2,1)S(1)} collective-permute-done((bf16[1,512,256]{2,1,0:T(8,128)(2,1)S(1)}, bf16[1,512,256]{2,1,0:T(8,128)(2,1)S(1)}, u32[]{:S(2)}, u32[]{:S(2)}) %collective-permute-start.40) | collective-permute-done | bytes 262176 | tf_op jit(solution)/shard_map/ppermute | solution.py:295
  183.4 3.8 %shard_map.79 = bf16[2,512,4,256]{3,2,1,0:T(4,128)(2,1)} custom-call(s32[2]{0:T(128)S(1)} %pad_add_fusion.rank_ref, bf16[2,512,256]{2,1,0:T(8,128)(2,1)S(1)} %add_convert_fusion.1.refs_0_, bf16[2,512,256]{2,1,0:T(8,128)(2,1)S(1)} %collective-permute-done.22.refs_1_.refs_5_, ...), custom_call_target="tpu_custom_call", output_to_operand_aliasing={{}: (9, {})} | custom-call | flops 1 | bytes 1 | tf_op jit(solution)/shard_map/pallas_call | solution.py:59
  (93 shorter events, 6.9 us)
Async XLA Ops:
  11.9 10.1 %collective-permute-start = (bf16[1,512,256]{2,1,0:T(8,128)(2,1)S(1)}, bf16[1,512,256]{2,1,0:T(8,128)(2,1)S(1)}, u32[]{:S(2)}, u32[]{:S(2)}) collective-permute-start(bf16[1,512,256]{2,1,0:T(8,128)(2,1)S(1)} %get-tuple-element.95), channel_id=1, source_target_pairs={{0,4},{2,6},{4,0},{6,2},{8,14},{10,12},{12,10},{14,8},{16,20},{18,... | collective-permute-start | bytes 786440 | tf_op jit(solution)/shard_map/ppermute | solution.py:258
  15.0 9.1 %copy-start = (bf16[512,4096]{1,0:T(8,128)(2,1)S(1)}, bf16[512,4096]{1,0:T(8,128)(2,1)}, u32[]{:S(2)}) copy-start(bf16[512,4096]{1,0:T(8,128)(2,1)} %enc_ref.1) | copy-start | bytes 12582916
  15.0 14.1 %collective-permute-start.11 = (bf16[1,512,256]{2,1,0:T(8,128)(2,1)S(1)}, bf16[1,512,256]{2,1,0:T(8,128)(2,1)S(1)}, u32[]{:S(2)}, u32[]{:S(2)}) collective-permute-start(bf16[1,512,256]{2,1,0:T(8,128)(2,1)S(1)} %get-tuple-element.92), channel_id=1, source_target_pairs={{0,4},{2,6},{4,0},{6,2},{8,14},{10,12},{12,10},{14,8},{16,20},{18,... | collective-permute-start | bytes 786440 | tf_op jit(solution)/shard_map/ppermute | solution.py:258
  15.1 19.8 %collective-permute-start.5 = (bf16[1,512,256]{2,1,0:T(8,128)(2,1)S(1)}, bf16[1,512,256]{2,1,0:T(8,128)(2,1)S(1)}, u32[]{:S(2)}, u32[]{:S(2)}) collective-permute-start(bf16[1,512,256]{2,1,0:T(8,128)(2,1)S(1)} %get-tuple-element.93), channel_id=1, source_target_pairs={{0,4},{2,6},{4,0},{6,2},{8,14},{10,12},{12,10},{14,8},{16,20},{18,... | collective-permute-start | bytes 786440 | tf_op jit(solution)/shard_map/ppermute | solution.py:258
  17.2 26.9 %collective-permute-start.1 = (bf16[2,512,256]{2,1,0:T(8,128)(2,1)S(1)}, bf16[2,512,256]{2,1,0:T(8,128)(2,1)S(1)}, u32[]{:S(2)}, u32[]{:S(2)}) collective-permute-start(bf16[2,512,256]{2,1,0:T(8,128)(2,1)S(1)} %bitcast.72), channel_id=1, source_target_pairs={{0,2},{2,0},{4,6},{6,4},{1,3},{3,1},{5,7},{7,5},{8,10},{10,8},{12,... | collective-permute-start | bytes 1572872 | tf_op jit(solution)/shard_map/ppermute | solution.py:320
  17.4 26.7 %collective-permute-start.4 = (bf16[2,512,256]{2,1,0:T(8,128)(2,1)S(1)}, bf16[2,512,256]{2,1,0:T(8,128)(2,1)S(1)}, u32[]{:S(2)}, u32[]{:S(2)}) collective-permute-start(bf16[2,512,256]{2,1,0:T(8,128)(2,1)S(1)} %bitcast.73), channel_id=1, source_target_pairs={{0,2},{2,0},{4,6},{6,4},{1,3},{3,1},{5,7},{7,5},{8,10},{10,8},{12,... | collective-permute-start | bytes 1572872 | tf_op jit(solution)/shard_map/ppermute | solution.py:320
  22.0 16.0 %collective-permute-start.2 = (bf16[1,512,256]{2,1,0:T(8,128)(2,1)S(1)}, bf16[1,512,256]{2,1,0:T(8,128)(2,1)S(1)}, u32[]{:S(2)}, u32[]{:S(2)}) collective-permute-start(bf16[1,512,256]{2,1,0:T(8,128)(2,1)S(1)} %get-tuple-element.94), channel_id=1, source_target_pairs={{0,4},{2,6},{4,0},{6,2},{8,14},{10,12},{12,10},{14,8},{16,20},{18,... | collective-permute-start | bytes 786440 | tf_op jit(solution)/shard_map/ppermute | solution.py:258
  29.1 26.5 %copy-start.3 = (bf16[512,256]{1,0:T(8,128)(2,1)}, bf16[512,256]{1,0:T(8,128)(2,1)S(1)}, u32[]{:S(2)}) copy-start(bf16[512,256]{1,0:T(8,128)(2,1)S(1)} %get-tuple-element.44.k_ref) | copy-start | bytes 786436
  29.1 26.5 %copy-start.5 = (bf16[512,256]{1,0:T(8,128)(2,1)}, bf16[512,256]{1,0:T(8,128)(2,1)S(1)}, u32[]{:S(2)}) copy-start(bf16[512,256]{1,0:T(8,128)(2,1)S(1)} %get-tuple-element.45.v_ref) | copy-start | bytes 786436
  29.1 11.3 %collective-permute-start.12 = (bf16[1,512,256]{2,1,0:T(8,128)(2,1)S(1)}, bf16[1,512,256]{2,1,0:T(8,128)(2,1)S(1)}, u32[]{:S(2)}, u32[]{:S(2)}) collective-permute-start(bf16[1,512,256]{2,1,0:T(8,128)(2,1)S(1)} %collective-permute-done.11.refs_6_), channel_id=1, source_target_pairs={{0,8},{8,0},{16,24},{24,16},{1,9},{9,1},{17,25},{25,17},{2,10},{10... | collective-permute-start | bytes 786440 | tf_op jit(solution)/shard_map/ppermute | solution.py:332
  34.9 9.2 %collective-permute-start.10 = (bf16[1,512,256]{2,1,0:T(8,128)(2,1)S(1)}, bf16[1,512,256]{2,1,0:T(8,128)(2,1)S(1)}, u32[]{:S(2)}, u32[]{:S(2)}) collective-permute-start(bf16[1,512,256]{2,1,0:T(8,128)(2,1)S(1)} %collective-permute-done.refs_2_), channel_id=1, source_target_pairs={{0,8},{8,0},{16,24},{24,16},{1,9},{9,1},{17,25},{25,17},{2,10},{10... | collective-permute-start | bytes 786440 | tf_op jit(solution)/shard_map/ppermute | solution.py:332
  38.0 17.5 %copy-start.1 = (bf16[1,512,256]{2,1,0:T(8,128)(2,1)}, bf16[1,512,256]{2,1,0:T(8,128)(2,1)S(1)}, u32[]{:S(2)}) copy-start(bf16[1,512,256]{2,1,0:T(8,128)(2,1)S(1)} %collective-permute-done.2.refs_2_) | copy-start | bytes 786436
  38.0 13.3 %collective-permute-start.6 = (bf16[1,512,256]{2,1,0:T(8,128)(2,1)S(1)}, bf16[1,512,256]{2,1,0:T(8,128)(2,1)S(1)}, u32[]{:S(2)}, u32[]{:S(2)}) collective-permute-start(bf16[1,512,256]{2,1,0:T(8,128)(2,1)S(1)} %collective-permute-done.5.refs_6_), channel_id=1, source_target_pairs={{0,8},{8,0},{16,24},{24,16},{1,9},{9,1},{17,25},{25,17},{2,10},{10... | collective-permute-start | bytes 786440 | tf_op jit(solution)/shard_map/ppermute | solution.py:332
  40.4 15.1 %collective-permute-start.3 = (bf16[1,512,256]{2,1,0:T(8,128)(2,1)S(1)}, bf16[1,512,256]{2,1,0:T(8,128)(2,1)S(1)}, u32[]{:S(2)}, u32[]{:S(2)}) collective-permute-start(bf16[1,512,256]{2,1,0:T(8,128)(2,1)S(1)} %collective-permute-done.2.refs_2_), channel_id=1, source_target_pairs={{0,8},{8,0},{16,24},{24,16},{1,9},{9,1},{17,25},{25,17},{2,10},{10... | collective-permute-start | bytes 786440 | tf_op jit(solution)/shard_map/ppermute | solution.py:332
  45.8 15.2 %collective-permute-start.13 = (f32[4,2048]{1,0:T(4,128)S(1)}, f32[4,2048]{1,0:T(4,128)S(1)}, u32[]{:S(2)}, u32[]{:S(2)}) collective-permute-start(f32[4,2048]{1,0:T(4,128)S(1)} %shard_map.72.refs_8_), channel_id=1, source_target_pairs={{0,8},{8,16},{16,24},{24,0},{1,9},{9,17},{17,25},{25,1},{2,10},{10... | collective-permute-start | bytes 98312 | tf_op jit(solution)/shard_map/ppermute | solution.py:263
  46.6 15.9 %collective-permute-start.14 = (f32[4,2048]{1,0:T(4,128)S(1)}, f32[4,2048]{1,0:T(4,128)S(1)}, u32[]{:S(2)}, u32[]{:S(2)}) collective-permute-start(f32[4,2048]{1,0:T(4,128)S(1)} %shard_map.72.refs_8_), channel_id=1, source_target_pairs={{0,16},{8,24},{16,0},{24,8},{1,17},{9,25},{17,1},{25,9},{2,18},{10... | collective-permute-start | bytes 98312 | tf_op jit(solution)/shard_map/ppermute | solution.py:263
  49.2 13.3 %collective-permute-start.15 = (f32[4,2048]{1,0:T(4,128)S(1)}, f32[4,2048]{1,0:T(4,128)S(1)}, u32[]{:S(2)}, u32[]{:S(2)}) collective-permute-start(f32[4,2048]{1,0:T(4,128)S(1)} %shard_map.72.refs_8_), channel_id=1, source_target_pairs={{0,24},{8,0},{16,8},{24,16},{1,25},{9,1},{17,9},{25,17},{2,26},{10... | collective-permute-start | bytes 98312 | tf_op jit(solution)/shard_map/ppermute | solution.py:263
  51.3 15.8 %copy-start.7 = (bf16[1,512,256]{2,1,0:T(8,128)(2,1)}, bf16[1,512,256]{2,1,0:T(8,128)(2,1)S(1)}, u32[]{:S(2)}) copy-start(bf16[1,512,256]{2,1,0:T(8,128)(2,1)S(1)} %collective-permute-done.6.refs_7_) | copy-start | bytes 786436
  55.5 7.0 %copy-start.9 = (bf16[1,512,256]{2,1,0:T(8,128)(2,1)}, bf16[1,512,256]{2,1,0:T(8,128)(2,1)S(1)}, u32[]{:S(2)}) copy-start(bf16[1,512,256]{2,1,0:T(8,128)(2,1)S(1)} %collective-permute-done.3.refs_3_) | copy-start | bytes 786436
  57.1 10.0 %collective-permute-start.7 = (f32[4,2048]{1,0:T(4,128)S(1)}, f32[4,2048]{1,0:T(4,128)S(1)}, u32[]{:S(2)}, u32[]{:S(2)}) collective-permute-start(f32[4,2048]{1,0:T(4,128)S(1)} %shard_map.69.refs_8_), channel_id=1, source_target_pairs={{0,8},{8,16},{16,24},{24,0},{1,9},{9,17},{17,25},{25,1},{2,10},{10... | collective-permute-start | bytes 98312 | tf_op jit(solution)/shard_map/ppermute | solution.py:263
  57.9 9.3 %collective-permute-start.8 = (f32[4,2048]{1,0:T(4,128)S(1)}, f32[4,2048]{1,0:T(4,128)S(1)}, u32[]{:S(2)}, u32[]{:S(2)}) collective-permute-start(f32[4,2048]{1,0:T(4,128)S(1)} %shard_map.69.refs_8_), channel_id=1, source_target_pairs={{0,16},{8,24},{16,0},{24,8},{1,17},{9,25},{17,1},{25,9},{2,18},{10... | collective-permute-start | bytes 98312 | tf_op jit(solution)/shard_map/ppermute | solution.py:263
  61.0 6.1 %collective-permute-start.9 = (f32[4,2048]{1,0:T(4,128)S(1)}, f32[4,2048]{1,0:T(4,128)S(1)}, u32[]{:S(2)}, u32[]{:S(2)}) collective-permute-start(f32[4,2048]{1,0:T(4,128)S(1)} %shard_map.69.refs_8_), channel_id=1, source_target_pairs={{0,24},{8,0},{16,8},{24,16},{1,25},{9,1},{17,9},{25,17},{2,26},{10... | collective-permute-start | bytes 98312 | tf_op jit(solution)/shard_map/ppermute | solution.py:263
  67.1 16.0 %collective-permute-start.16 = (bf16[2,512,256]{2,1,0:T(8,128)(2,1)}, bf16[2,512,256]{2,1,0:T(8,128)(2,1)}, u32[]{:S(2)}, u32[]{:S(2)}) collective-permute-start(bf16[2,512,256]{2,1,0:T(8,128)(2,1)} %get-tuple-element.56), channel_id=1, source_target_pairs={{0,8},{24,16},{1,9},{25,17},{2,10},{26,18},{3,11},{27,19},{4,12},{... | collective-permute-start | bytes 1572872 | tf_op jit(solution)/shard_map/ppermute | solution.py:289
  70.3 9.9 %collective-permute-start.23 = (bf16[1,512,256]{2,1,0:T(8,128)(2,1)}, bf16[1,512,256]{2,1,0:T(8,128)(2,1)}, u32[]{:S(2)}, u32[]{:S(2)}) collective-permute-start(bf16[1,512,256]{2,1,0:T(8,128)(2,1)} %get-tuple-element.60), channel_id=1, source_target_pairs={{0,4},{2,6},{4,0},{6,2},{1,5},{3,7},{5,1},{7,3},{8,12},{10,14},{12... | collective-permute-start | bytes 786440 | tf_op jit(solution)/shard_map/ppermute | solution.py:349
  70.9 10.8 %collective-permute-start.25 = (bf16[1,512,256]{2,1,0:T(8,128)(2,1)}, bf16[1,512,256]{2,1,0:T(8,128)(2,1)}, u32[]{:S(2)}, u32[]{:S(2)}) collective-permute-start(bf16[1,512,256]{2,1,0:T(8,128)(2,1)} %get-tuple-element.63), channel_id=1, source_target_pairs={{0,6},{2,4},{4,2},{6,0},{1,7},{3,5},{5,3},{7,1},{8,14},{10,12},{12... | collective-permute-start | bytes 786440 | tf_op jit(solution)/shard_map/ppermute | solution.py:350
  71.0 1.0 copy-start.2
  71.9 0.9 copy-start.4
  72.9 0.9 copy-start.6
  73.8 0.9 copy-start.8
  74.8 0.9 copy-start.10
  80.2 17.4 %collective-permute-start.24 = (bf16[1,512,256]{2,1,0:T(8,128)(2,1)}, bf16[1,512,256]{2,1,0:T(8,128)(2,1)}, u32[]{:S(2)}, u32[]{:S(2)}) collective-permute-start(bf16[1,512,256]{2,1,0:T(8,128)(2,1)} %get-tuple-element.61), channel_id=1, source_target_pairs={{0,4},{2,6},{4,0},{6,2},{1,5},{3,7},{5,1},{7,3},{8,12},{10,14},{12... | collective-permute-start | bytes 786440 | tf_op jit(solution)/shard_map/ppermute | solution.py:349
  81.7 16.5 %collective-permute-start.26 = (bf16[1,512,256]{2,1,0:T(8,128)(2,1)}, bf16[1,512,256]{2,1,0:T(8,128)(2,1)S(1)}, u32[]{:S(2)}, u32[]{:S(2)}) collective-permute-start(bf16[1,512,256]{2,1,0:T(8,128)(2,1)} %get-tuple-element.64), channel_id=1, source_target_pairs={{0,6},{2,4},{4,2},{6,0},{1,7},{3,5},{5,3},{7,1},{8,14},{10,12},{12... | collective-permute-start | bytes 786440 | tf_op jit(solution)/shard_map/ppermute | solution.py:350
  85.3 19.9 %collective-permute-start.17 = (bf16[2,512,256]{2,1,0:T(8,128)(2,1)}, bf16[2,512,256]{2,1,0:T(8,128)(2,1)}, u32[]{:S(2)}, u32[]{:S(2)}) collective-permute-start(bf16[2,512,256]{2,1,0:T(8,128)(2,1)} %get-tuple-element.58), channel_id=1, source_target_pairs={{0,8},{24,16},{1,9},{25,17},{2,10},{26,18},{3,11},{27,19},{4,12},{... | collective-permute-start | bytes 1572872 | tf_op jit(solution)/shard_map/ppermute | solution.py:289
  87.4 16.0 %collective-permute-start.28 = (bf16[1,512,256]{2,1,0:T(8,128)(2,1)}, bf16[1,512,256]{2,1,0:T(8,128)(2,1)}, u32[]{:S(2)}, u32[]{:S(2)}) collective-permute-start(bf16[1,512,256]{2,1,0:T(8,128)(2,1)} %collective-permute-done.23), channel_id=1, source_target_pairs={{0,8},{24,16},{1,9},{25,17},{2,10},{26,18},{3,11},{27,19},{4,12},{... | collective-permute-start | bytes 786440 | tf_op jit(solution)/shard_map/ppermute | solution.py:289
  93.6 16.4 %collective-permute-start.33 = (bf16[2,512,512]{2,1,0:T(8,128)(2,1)}, bf16[2,512,512]{2,1,0:T(8,128)(2,1)S(1)}, u32[]{:S(2)}, u32[]{:S(2)}) collective-permute-start(bf16[2,512,512]{2,1,0:T(8,128)(2,1)} %shard_map.76), channel_id=1, source_target_pairs={{0,2},{2,0},{4,6},{6,4},{1,3},{3,1},{5,7},{7,5},{8,10},{10,8},{12,... | collective-permute-start | bytes 3145736 | tf_op jit(solution)/shard_map/ppermute | solution.py:363
  97.7 25.8 %collective-permute-start.27 = (bf16[2,512,512]{2,1,0:T(8,128)(2,1)}, bf16[2,512,512]{2,1,0:T(8,128)(2,1)S(1)}, u32[]{:S(2)}, u32[]{:S(2)}) collective-permute-start(bf16[2,512,512]{2,1,0:T(8,128)(2,1)} %shard_map.74), channel_id=1, source_target_pairs={{0,2},{2,0},{4,6},{6,4},{1,3},{3,1},{5,7},{7,5},{8,10},{10,8},{12,... | collective-permute-start | bytes 3145736 | tf_op jit(solution)/shard_map/ppermute | solution.py:363
  98.2 1.5 copy-start.11
  98.2 9.0 %collective-permute-start.19 = (bf16[2,512,256]{2,1,0:T(8,128)(2,1)}, bf16[2,512,256]{2,1,0:T(8,128)(2,1)}, u32[]{:S(2)}, u32[]{:S(2)}) collective-permute-start(bf16[2,512,256]{2,1,0:T(8,128)(2,1)} %add_convert_fusion.3), channel_id=1, source_target_pairs={{8,16},{16,8},{9,17},{17,9},{10,18},{18,10},{11,19},{19,11},{12,20... | collective-permute-start | bytes 1572872 | tf_op jit(solution)/shard_map/ppermute | solution.py:291
  104.5 5.4 %collective-permute-start.30 = (bf16[1,512,256]{2,1,0:T(8,128)(2,1)S(1)}, bf16[1,512,256]{2,1,0:T(8,128)(2,1)S(1)}, u32[]{:S(2)}, u32[]{:S(2)}) collective-permute-start(bf16[1,512,256]{2,1,0:T(8,128)(2,1)S(1)} %add_convert_fusion.11), channel_id=1, source_target_pairs={{8,16},{16,8},{9,17},{17,9},{10,18},{18,10},{11,19},{19,11},{12,20... | collective-permute-start | bytes 786440 | tf_op jit(solution)/shard_map/ppermute | solution.py:291
  106.5 20.3 %collective-permute-start.18 = (bf16[2,512,256]{2,1,0:T(8,128)(2,1)S(1)}, bf16[2,512,256]{2,1,0:T(8,128)(2,1)S(1)}, u32[]{:S(2)}, u32[]{:S(2)}) collective-permute-start(bf16[2,512,256]{2,1,0:T(8,128)(2,1)S(1)} %add_convert_fusion.2), channel_id=1, source_target_pairs={{8,16},{16,8},{9,17},{17,9},{10,18},{18,10},{11,19},{19,11},{12,20... | collective-permute-start | bytes 1572872 | tf_op jit(solution)/shard_map/ppermute | solution.py:291
  108.6 18.4 %collective-permute-start.20 = (bf16[2,512,256]{2,1,0:T(8,128)(2,1)S(1)}, bf16[2,512,256]{2,1,0:T(8,128)(2,1)S(1)}, u32[]{:S(2)}, u32[]{:S(2)}) collective-permute-start(bf16[2,512,256]{2,1,0:T(8,128)(2,1)S(1)} %add_convert_fusion.refs_0_), channel_id=1, source_target_pairs={{8,0},{16,24},{9,1},{17,25},{10,2},{18,26},{11,3},{19,27},{12,4},{... | collective-permute-start | bytes 1572872 | tf_op jit(solution)/shard_map/ppermute | solution.py:295
  113.3 21.5 %collective-permute-start.34 = (bf16[1,512,256]{2,1,0:T(8,128)(2,1)}, bf16[1,512,256]{2,1,0:T(8,128)(2,1)S(1)}, u32[]{:S(2)}, u32[]{:S(2)}) collective-permute-start(bf16[1,512,256]{2,1,0:T(8,128)(2,1)} %collective-permute-done.25), channel_id=1, source_target_pairs={{0,8},{24,16},{1,9},{25,17},{2,10},{26,18},{3,11},{27,19},{4,12},{... | collective-permute-start | bytes 786440 | tf_op jit(solution)/shard_map/ppermute | solution.py:289
  127.0 27.2 %copy-start.12 = (bf16[1,512,256]{2,1,0:T(8,128)(2,1)S(1)}, bf16[1,512,256]{2,1,0:T(8,128)(2,1)}, u32[]{:S(2)}) copy-start(bf16[1,512,256]{2,1,0:T(8,128)(2,1)} %copy-done.11) | copy-start | bytes 786436
  127.0 10.1 %collective-permute-start.29 = (bf16[1,512,256]{2,1,0:T(8,128)(2,1)}, bf16[1,512,256]{2,1,0:T(8,128)(2,1)S(1)}, u32[]{:S(2)}, u32[]{:S(2)}) collective-permute-start(bf16[1,512,256]{2,1,0:T(8,128)(2,1)} %collective-permute-done.24), channel_id=1, source_target_pairs={{0,8},{24,16},{1,9},{25,17},{2,10},{26,18},{3,11},{27,19},{4,12},{... | collective-permute-start | bytes 786440 | tf_op jit(solution)/shard_map/ppermute | solution.py:289
  130.4 37.8 %collective-permute-start.41 = (bf16[512,512]{1,0:T(8,128)(2,1)S(1)}, bf16[512,512]{1,0:T(8,128)(2,1)S(1)}, u32[]{:S(2)}, u32[]{:S(2)}) collective-permute-start(bf16[512,512]{1,0:T(8,128)(2,1)S(1)} %get-tuple-element.90), channel_id=1, source_target_pairs={{0,5},{1,4},{2,7},{3,6},{4,1},{5,0},{6,3},{7,2},{8,13},{9,12},{10,... | collective-permute-start | bytes 1572872 | tf_op jit(solution)/shard_map/ppermute | solution.py:376
  132.6 36.9 %collective-permute-start.42 = (bf16[512,512]{1,0:T(8,128)(2,1)S(1)}, bf16[512,512]{1,0:T(8,128)(2,1)S(1)}, u32[]{:S(2)}, u32[]{:S(2)}) collective-permute-start(bf16[512,512]{1,0:T(8,128)(2,1)S(1)} %get-tuple-element.91), channel_id=1, source_target_pairs={{0,4},{1,5},{2,6},{3,7},{4,0},{5,1},{6,2},{7,3},{8,12},{9,13},{10,... | collective-permute-start | bytes 1572872 | tf_op jit(solution)/shard_map/ppermute | solution.py:376
  133.5 20.1 %collective-permute-start.21 = (bf16[2,512,256]{2,1,0:T(8,128)(2,1)S(1)}, bf16[2,512,256]{2,1,0:T(8,128)(2,1)S(1)}, u32[]{:S(2)}, u32[]{:S(2)}) collective-permute-start(bf16[2,512,256]{2,1,0:T(8,128)(2,1)S(1)} %add_convert_fusion.1.refs_0_), channel_id=1, source_target_pairs={{8,0},{16,24},{9,1},{17,25},{10,2},{18,26},{11,3},{19,27},{12,4},{... | collective-permute-start | bytes 1572872 | tf_op jit(solution)/shard_map/ppermute | solution.py:295
  134.8 18.1 %collective-permute-start.31 = (bf16[1,512,256]{2,1,0:T(8,128)(2,1)S(1)}, bf16[1,512,256]{2,1,0:T(8,128)(2,1)S(1)}, u32[]{:S(2)}, u32[]{:S(2)}) collective-permute-start(bf16[1,512,256]{2,1,0:T(8,128)(2,1)S(1)} %add_convert_fusion.9.refs_2_), channel_id=1, source_target_pairs={{8,0},{16,24},{9,1},{17,25},{10,2},{18,26},{11,3},{19,27},{12,4},{... | collective-permute-start | bytes 786440 | tf_op jit(solution)/shard_map/ppermute | solution.py:295
  137.1 17.1 %collective-permute-start.36 = (bf16[1,512,256]{2,1,0:T(8,128)(2,1)S(1)}, bf16[1,512,256]{2,1,0:T(8,128)(2,1)S(1)}, u32[]{:S(2)}, u32[]{:S(2)}) collective-permute-start(bf16[1,512,256]{2,1,0:T(8,128)(2,1)S(1)} %add_convert_fusion.7), channel_id=1, source_target_pairs={{8,16},{16,8},{9,17},{17,9},{10,18},{18,10},{11,19},{19,11},{12,20... | collective-permute-start | bytes 786440 | tf_op jit(solution)/shard_map/ppermute | solution.py:291
  152.9 4.7 %collective-permute-start.32 = (bf16[1,512,256]{2,1,0:T(8,128)(2,1)S(1)}, bf16[1,512,256]{2,1,0:T(8,128)(2,1)S(1)}, u32[]{:S(2)}, u32[]{:S(2)}) collective-permute-start(bf16[1,512,256]{2,1,0:T(8,128)(2,1)S(1)} %add_convert_fusion.10), channel_id=1, source_target_pairs={{8,16},{16,8},{9,17},{17,9},{10,18},{18,10},{11,19},{19,11},{12,20... | collective-permute-start | bytes 786440 | tf_op jit(solution)/shard_map/ppermute | solution.py:291
  153.6 16.0 %collective-permute-start.43 = (bf16[512,512]{1,0:T(8,128)(2,1)S(1)}, bf16[512,512]{1,0:T(8,128)(2,1)S(1)}, u32[]{:S(2)}, u32[]{:S(2)}) collective-permute-start(bf16[512,512]{1,0:T(8,128)(2,1)S(1)} %slice_bitcast_fusion.1), channel_id=1, source_target_pairs={{0,1},{1,0},{2,3},{3,2},{4,5},{5,4},{6,7},{7,6},{8,9},{9,8},{10,11... | collective-permute-start | bytes 1572872 | tf_op jit(solution)/shard_map/ppermute | solution.py:376
  154.1 7.2 %collective-permute-start.35 = (bf16[1,512,256]{2,1,0:T(8,128)(2,1)S(1)}, bf16[1,512,256]{2,1,0:T(8,128)(2,1)S(1)}, u32[]{:S(2)}, u32[]{:S(2)}) collective-permute-start(bf16[1,512,256]{2,1,0:T(8,128)(2,1)S(1)} %copy-done.12), channel_id=1, source_target_pairs={{0,8},{24,16},{1,9},{25,17},{2,10},{26,18},{3,11},{27,19},{4,12},{... | collective-permute-start | bytes 786440 | tf_op jit(solution)/shard_map/ppermute | solution.py:289
  157.6 9.7 %collective-permute-start.37 = (bf16[1,512,256]{2,1,0:T(8,128)(2,1)S(1)}, bf16[1,512,256]{2,1,0:T(8,128)(2,1)S(1)}, u32[]{:S(2)}, u32[]{:S(2)}) collective-permute-start(bf16[1,512,256]{2,1,0:T(8,128)(2,1)S(1)} %add_convert_fusion.5.refs_3_), channel_id=1, source_target_pairs={{8,0},{16,24},{9,1},{17,25},{10,2},{18,26},{11,3},{19,27},{12,4},{... | collective-permute-start | bytes 786440 | tf_op jit(solution)/shard_map/ppermute | solution.py:295
  161.3 13.1 %collective-permute-start.39 = (bf16[1,512,256]{2,1,0:T(8,128)(2,1)S(1)}, bf16[1,512,256]{2,1,0:T(8,128)(2,1)S(1)}, u32[]{:S(2)}, u32[]{:S(2)}) collective-permute-start(bf16[1,512,256]{2,1,0:T(8,128)(2,1)S(1)} %add_convert_fusion.8.refs_2_), channel_id=1, source_target_pairs={{8,0},{16,24},{9,1},{17,25},{10,2},{18,26},{11,3},{19,27},{12,4},{... | collective-permute-start | bytes 786440 | tf_op jit(solution)/shard_map/ppermute | solution.py:295
  167.3 0.8 collective-permute-start.38
  168.1 2.6 %collective-permute-start.22 = (bf16[2,512,256]{2,1,0:T(8,128)(2,1)S(1)}, bf16[2,512,256]{2,1,0:T(8,128)(2,1)S(1)}, u32[]{:S(2)}, u32[]{:S(2)}) collective-permute-start(bf16[2,512,256]{2,1,0:T(8,128)(2,1)S(1)} %pad_maximum_fusion), channel_id=1, source_target_pairs={{0,2},{2,0},{4,6},{6,4},{1,3},{3,1},{5,7},{7,5},{8,10},{10,8},{12,... | collective-permute-start | bytes 1572872 | tf_op jit(solution)/shard_map/ppermute | solution.py:383
  168.2 15.2 %collective-permute-start.40 = (bf16[1,512,256]{2,1,0:T(8,128)(2,1)S(1)}, bf16[1,512,256]{2,1,0:T(8,128)(2,1)S(1)}, u32[]{:S(2)}, u32[]{:S(2)}) collective-permute-start(bf16[1,512,256]{2,1,0:T(8,128)(2,1)S(1)} %add_convert_fusion.4.refs_3_), channel_id=1, source_target_pairs={{8,0},{16,24},{9,1},{17,25},{10,2},{18,26},{11,3},{19,27},{12,4},{... | collective-permute-start | bytes 786440 | tf_op jit(solution)/shard_map/ppermute | solution.py:295

commit v2 on v1

v2 whole, which is shorter than its diff:
```python
import functools

import jax
import jax.numpy as jnp
from jax import lax
from jax.experimental import pallas as pl
from jax.experimental.pallas import tpu as pltpu
from jax.sharding import PartitionSpec as P

F32, BF16 = jnp.float32, jnp.bfloat16
MIB = 1024 * 1024
NT = (((1,), (1,)), ((), ()))
NN = (((1,), (0,)), ((), ()))
TN = (((0,), (0,)), ((), ()))


def dot(left, right, dims):
    return lax.dot_general(left, right, dims, preferred_element_type=F32)


def params():
    return pltpu.CompilerParams(vmem_limit_bytes=44 * MIB)


def cost(flops, nbytes, exps=0):
    return pl.CostEstimate(flops=int(flops), bytes_accessed=int(nbytes), transcendentals=int(exps))


def partners(count, mask):
    return [(index, index ^ mask) for index in range(count)]


def pick_kernel(head_ref, *refs):
    count = len(refs) // 2
    for source, out in zip(refs[:count], refs[count:]):
        out[...] = source[0]


def pick(head, parts):
    shape = parts[0][0].shape
    specs, outs = [], []
    for source, first, count in parts:
        specs.append(
            pl.BlockSpec((1, count) + shape[2:], lambda i, head, first=first: (head[0], first, 0, 0))
        )
        outs.append(jax.ShapeDtypeStruct((count,) + shape[2:], BF16))
    return pl.pallas_call(
        pick_kernel,
        grid_spec=pltpu.PrefetchScalarGridSpec(
            num_scalar_prefetch=1,
            grid=(1,),
            in_specs=specs,
            out_specs=[pl.BlockSpec(out.shape, lambda i, head: (0, 0, 0)) for out in outs],
        ),
        out_shape=outs,
        compiler_params=params(),
        cost_estimate=cost(0, 4 * sum(out.size for out in outs)),
    )(head, *[source for source, _, _ in parts])


def join_kernel(place_ref, mine_ref, other_ref, *rest):
    out = rest[-1]
    heads, half, _ = mine_ref.shape

    def fill(upper_ref, lower_ref):
        for head in range(heads):
            out[0, :half, head, :] = upper_ref[place_ref[0] ^ head]
            out[0, half:, head, :] = lower_ref[place_ref[0] ^ head]

    pl.when(place_ref[2] != 0)(lambda: fill(mine_ref, other_ref))
    pl.when(place_ref[2] == 0)(lambda: fill(other_ref, mine_ref))


def join_heads(place, mine, other, layer, layers, begun):
    heads, half, size = mine.shape
    extra = [] if begun is None else [begun]
    return pl.pallas_call(
        join_kernel,
        grid_spec=pltpu.PrefetchScalarGridSpec(
            num_scalar_prefetch=1,
            grid=(1,),
            in_specs=[whole(mine.shape)] * 2 + [pl.BlockSpec(memory_space=pl.ANY)] * len(extra),
            out_specs=pl.BlockSpec((1, 2 * half, heads, size), lambda i, place: (layer, 0, 0, 0)),
        ),
        out_shape=jax.ShapeDtypeStruct((layers, 2 * half, heads, size), BF16),
        input_output_aliases={3: 0} if extra else {},
        compiler_params=params(),
        cost_estimate=cost(0, 8 * half * heads * size),
    )(place, mine, other, *extra)


def project_kernel(enc_ref, wk_ref, wv_ref, k_ref, v_ref, sums):
    step = pl.program_id(0)

    @pl.when(step == 0)
    def _():
        sums[...] = jnp.zeros_like(sums)

    sums[0] += dot(enc_ref[...], wk_ref[0], NN)
    sums[1] += dot(enc_ref[...], wv_ref[0], NN)

    @pl.when(step == pl.num_programs(0) - 1)
    def _():
        k_ref[...] = sums[0].astype(BF16)
        v_ref[...] = sums[1].astype(BF16)


def project(encoder, wk, wv, layer):
    rows, width = encoder.shape
    size = wk.shape[2]
    depth = width // 4
    weight = pl.BlockSpec((1, depth, size), lambda i: (layer, i, 0))
    result = pl.BlockSpec((rows, size), lambda i: (0, 0))
    return pl.pallas_call(
        project_kernel,
        grid=(width // depth,),
        in_specs=[pl.BlockSpec((rows, depth), lambda i: (0, i)), weight, weight],
        out_specs=[result, result],
        out_shape=[jax.ShapeDtypeStruct((rows, size), BF16)] * 2,
        scratch_shapes=[pltpu.VMEM((2, rows, size), F32)],
        compiler_params=params(),
        cost_estimate=cost(4 * rows * width * size, 2 * width * (rows + 2 * size)),
    )(encoder, wk, wv)


def columns(index, count, rows, place_ref):
    if index < count - 2:
        return slice(index * rows, (index + 1) * rows)
    start = (count - 2 + ((index - count + 2) ^ place_ref[1])) * rows
    return pl.ds(pl.multiple_of(start, rows), rows)


def block_of(ref):
    return ref[(0,) * (len(ref.shape) - 2)]


def stats_kernel(place_ref, k_ref, v_ref, *refs):
    out, pieces = refs[-1], refs[:-1]
    count = len(pieces) // 2
    for index in range(count):
        query, cotangent = block_of(pieces[index]), block_of(pieces[count + index])
        cols = columns(index, count, query.shape[0], place_ref)
        scores = dot(k_ref[...], query, NT)
        peak = jnp.max(scores, axis=0, keepdims=True)
        shifted = jnp.exp(scores - peak)
        dprobs = dot(v_ref[...], cotangent, NT)
        out[0:1, cols] = peak
        out[1:2, cols] = jnp.sum(shifted, axis=0, keepdims=True)
        out[2:3, cols] = jnp.sum(shifted * dprobs, axis=0, keepdims=True)
        out[3:4, cols] = jnp.zeros_like(peak)


def whole(shape):
    return pl.BlockSpec(shape, lambda i, *place: (0,) * len(shape))


def of_layer(array, layer):
    if len(array.shape) == 4:
        return pl.BlockSpec((1, 1) + array.shape[2:], lambda i, place: (place[0], layer, 0, 0))
    index = layer if array.shape[0] > 1 else 0
    return pl.BlockSpec((1,) + array.shape[1:], lambda i, place: (index, 0, 0))


def row_stats(place, keys, values, pieces, layer):
    enc_rows, size = keys.shape
    total = pieces[0].shape[-2] * len(pieces) // 2
    return pl.pallas_call(
        stats_kernel,
        grid_spec=pltpu.PrefetchScalarGridSpec(
            num_scalar_prefetch=1,
            grid=(1,),
            in_specs=[whole(keys.shape), whole(values.shape)] + [of_layer(array, layer) for array in pieces],
            out_specs=whole((4, total)),
        ),
        out_shape=jax.ShapeDtypeStruct((4, total), F32),
        compiler_params=params(),
        cost_estimate=cost(
            4 * enc_rows * total * size, 4 * size * (enc_rows + total), enc_rows * total
        ),
    )(place, keys, values, *pieces)


def grads_kernel(count, place_ref, k_ref, v_ref, *refs):
    queries, cotangents, refs = refs[:count], refs[count : 2 * count], refs[2 * count :]
    stats, (keep_ref, send_ref, dk_ref, dv_ref) = refs[:-4], refs[-4:]
    keys, values = k_ref[...], v_ref[...]
    half = keep_ref.shape[1]
    for index in range(count):
        query, cotangent = block_of(queries[index]), block_of(cotangents[index])
        cols = columns(index, count, query.shape[0], place_ref)
        parts = [part[:, cols] for part in stats]
        peak = functools.reduce(jnp.maximum, [part[0:1] for part in parts])
        scales = [jnp.exp(part[0:1] - peak) for part in parts]
        total = sum(part[1:2] * scale for part, scale in zip(parts, scales))
        inner = sum(part[2:3] * scale for part, scale in zip(parts, scales)) / total
        attention = jnp.exp(dot(keys, query, NT) - peak) * (1.0 / total)
        dprobs = dot(values, cotangent, NT)
        dscores = (attention * (dprobs - inner)).astype(BF16)
        query_grad = dot(dscores, keys, TN).astype(BF16)
        slot = index if index < count - 2 else count - 2 + ((index - count + 2) ^ place_ref[1])
        upper, lower = query_grad[:half], query_grad[half:]
        first = place_ref[2] != 0
        keep_ref[slot] = jnp.where(first, upper, lower)
        send_ref[slot] = jnp.where(first, lower, upper)
        key_part = dot(dscores, query, NN)
        value_part = dot(attention.astype(BF16), cotangent, NN)
        key_sum = key_part if index == 0 else key_sum + key_part
        value_sum = value_part if index == 0 else value_sum + value_part
    dk_ref[...] = key_sum.astype(BF16)
    dv_ref[...] = value_sum.astype(BF16)


def attention_grads(place, keys, values, pieces, stats, layer):
    enc_rows, size = keys.shape
    rows = pieces[0].shape[-2]
    count = len(pieces) // 2
    total = rows * count
    outs = [(count, rows // 2, size)] * 2 + [(enc_rows, size)] * 2
    return pl.pallas_call(
        functools.partial(grads_kernel, count),
        grid_spec=pltpu.PrefetchScalarGridSpec(
            num_scalar_prefetch=1,
            grid=(1,),
            in_specs=[whole(keys.shape), whole(values.shape)]
            + [of_layer(array, layer) for array in pieces]
            + [whole((4, total))] * len(stats),
            out_specs=[whole(shape) for shape in outs],
        ),
        out_shape=[jax.ShapeDtypeStruct(shape, BF16) for shape in outs],
        compiler_params=params(),
        cost_estimate=cost(
            10 * enc_rows * total * size, 6 * size * (enc_rows + total), enc_rows * total
        ),
    )(place, keys, values, *pieces, *stats)


def back_kernel(order_ref, wk_ref, wv_ref, *refs):
    out = refs[-1]
    layers = wk_ref.shape[0]
    total = refs[2 * layers][0].astype(F32) if len(refs) > 2 * layers + 1 else None
    for layer in range(layers):
        part = dot(refs[2 * layer][...], wk_ref[layer], NT)
        total = part if total is None else total + part
        total = total + dot(refs[2 * layer + 1][...], wv_ref[layer], NT)
    out[0] = total.astype(BF16)


def back_blocks(order, wk, wv, flat, share, arrived=None):
    layers, _, size = wk.shape
    rows = flat[0].shape[0]
    blocks = order.shape[0]
    weight = pl.BlockSpec((layers, share, size), lambda i, order: (0, order[i], 0))
    result = pl.BlockSpec((1, rows, share), lambda i, order: (i, 0, 0))
    extra = [] if arrived is None else [arrived]
    return pl.pallas_call(
        back_kernel,
        grid_spec=pltpu.PrefetchScalarGridSpec(
            num_scalar_prefetch=1,
            grid=(blocks,),
            in_specs=[weight, weight]
            + [pl.BlockSpec((rows, size), lambda i, order: (0, 0))] * len(flat)
            + [result] * len(extra),
            out_specs=result,
        ),
        out_shape=jax.ShapeDtypeStruct((blocks, rows, share), BF16),
        compiler_params=params(),
        cost_estimate=cost(
            4 * layers * rows * size * share * blocks, 2 * blocks * share * (2 * layers * size + 2 * rows)
        ),
    )(order, wk, wv, *flat, *extra)


def plus(one, two):
    return (one.astype(F32) + two.astype(F32)).astype(BF16)


def exchange(value, n_inp, n_tgt, mask_of):
    pairs = [(z * n_tgt + t, z * n_tgt + (t ^ mask_of(z))) for z in range(n_inp) for t in range(n_tgt)]
    return lax.ppermute(value, ("inp", "tgt"), pairs)


def everywhere(value, n_inp):
    return [value] + [
        lax.ppermute(value, "inp", [(i, (i + shift) % n_inp) for i in range(n_inp)])
        for shift in range(1, n_inp)
    ]


def after(value, *others):
    return lax.optimization_barrier((value, *others))[0]


def to_owners(value, n_tgt):
    return jnp.stack(
        [
            value[mask] if mask == 0 else lax.ppermute(value[mask], "tgt", partners(n_tgt, mask))
            for mask in range(n_tgt)
        ]
    )


def body(encoder, key_weight, value_weight, queries, grad_out):
    layers, dec_rows, heads, size = queries.shape
    width = encoder.shape[1]
    n_inp, n_tgt, n_mdl = (lax.axis_size(axis) for axis in ("inp", "tgt", "mdl"))
    z, t, m = (lax.axis_index(axis) for axis in ("inp", "tgt", "mdl"))
    share = width // (n_tgt * n_mdl)
    wk = key_weight.reshape(layers, width, size)
    wv = value_weight.reshape(layers, width, size)
    line = n_inp == 4
    odd = (z % 2).astype(jnp.int32)
    upper = ((z == 0) | (z == n_inp - 1)).astype(jnp.int32) if line else jnp.ones_like(odd)
    place = jnp.stack([t.astype(jnp.int32), odd, upper])

    own = [jnp.transpose(array, (2, 0, 1, 3)) for array in (queries, grad_out)]
    wanted = pick((t ^ (2 + odd))[None], [(source, layer, 1) for layer in range(layers) for source in own])
    fetched = [exchange(piece, n_inp, n_tgt, lambda z: 2 + z % 2) for piece in wanted]
    keys, values, begun = [], [], wanted
    for layer in range(layers):
        key_block, value_block = project(after(encoder, *begun), wk, wv, layer)
        begun = fetched[:1]
        keys.append(key_block)
        values.append(value_block)
    beside = pick(after((t ^ 1)[None], keys[0]), [(source, 0, layers) for source in own])
    beside = [lax.ppermute(piece, "tgt", partners(n_tgt, 1)) for piece in beside]
    handed = []
    for index, piece in enumerate(fetched):
        ahead = keys[min(layers - 1, index)]
        handed.append(lax.ppermute(after(piece, ahead), "inp", partners(n_inp, 1)))

    pieces, stats = [], []
    for layer in range(layers):
        pieces.append(
            [
                array
                for kind in range(2)
                for array in (own[kind], beside[kind], fetched[2 * layer + kind], handed[2 * layer + kind])
            ]
        )
        own_stats = row_stats(place, keys[layer], values[layer], pieces[layer], layer)
        stats.append(everywhere(own_stats, n_inp))
    flat, keep, send = [], [], []
    for layer in range(layers):
        results = attention_grads(place, keys[layer], values[layer], pieces[layer], stats[layer], layer)
        keep.append(results[0])
        send.append(results[1])
        flat += results[2:]

    def order(mask):
        return jnp.stack([(t ^ mask) * n_mdl + (m ^ side) for side in range(n_mdl)]).astype(jnp.int32)

    def pair_sum(layer, *others):
        value = after(send[layer], *stats[-1]) if layer == 0 else send[layer]
        return plus(after(keep[layer], *others), lax.ppermute(value, "inp", partners(n_inp, 1)))

    pair_sums = [pair_sum(0, flat[-1])] if line else []
    masks = list(reversed(range(0, n_tgt, 2)))
    arrived = []
    for index, mask in enumerate(masks):
        wait = pair_sums if index else []
        sent = back_blocks(after(order(mask + 1), *wait), wk, wv, flat, share)
        arrived.append(lax.ppermute(sent, "tgt", partners(n_tgt, 1)))
    total, blocks = None, keys[0]
    for mask, block in zip(masks, arrived):
        blocks = back_blocks(after(order(mask), blocks), wk, wv, flat, share, block)
        for side in reversed(range(n_mdl)):
            block = blocks[side]
            if mask or side:
                pairs = [
                    (a * n_mdl + b, (a ^ mask) * n_mdl + (b ^ side))
                    for a in range(n_tgt)
                    for b in range(n_mdl)
                ]
                block = lax.ppermute(block, ("tgt", "mdl"), pairs)
            total = block.astype(F32) if total is None else total + block.astype(F32)

    query_grads = None
    if line:
        pair_sums += [pair_sum(layer, blocks) for layer in range(1, layers)]
        opposite = [(0, 3), (3, 0), (1, 2), (2, 1)]
        mine = [to_owners(plus(value, lax.ppermute(value, "inp", opposite)), n_tgt) for value in pair_sums]
        other = [lax.ppermute(value, "inp", partners(n_inp, 1)) for value in mine]
    else:
        mine, other = ([to_owners(lax.psum(value, "inp"), n_tgt) for value in half] for half in (keep, send))
    for layer in range(layers):
        query_grads = join_heads(place, mine[layer], other[layer], layer, layers, query_grads)
    return query_grads, total.astype(BF16)


def solution(mesh):
    placed = (
        P("inp", None),
        P(None, None, "mdl", "tgt", None),
        P(None, None, "mdl", "tgt", None),
        P(None, "tgt", "mdl", None),
        P(None, "tgt", "mdl", None),
    )
    return jax.shard_map(
        body,
        mesh=mesh,
        in_specs=placed,
        out_specs=(P(None, "tgt", "mdl", None), P("inp", ("tgt", "mdl"))),
        check_vma=False,
    )
```

time: 188 us -> 175 us (0.931)
  starting transfers between devices: 67.9 us -> 43.9 us
  waiting for transfers between devices: 47.1 us -> 54.3 us
  Pallas kernels: 44.6 us -> 50.5 us
  other arithmetic: 9.88 us -> 4.11 us
  local copies, waits for them, and re-layouts: 16.6 us -> 20.6 us
    ppermute x29 -> x18, starting transfers between devices: 45.6 us -> 24.4 us  [the longest x2 7.63 us: body(): other = [lax.ppermute(value, 'inp', partners(n_inp, 1)) for value in mine]]
    unnamed x32 -> x62, local copies, waits for them, and re-layouts: 5.31 us -> 17.6 us
    another operation x1 -> x0, local copies, waits for them, and re-layouts: 11.1 us -> none
    ppermute x29 -> x18, waiting for transfers between devices: 41.2 us -> 49.8 us  [the longest x6 24.5 us: to_owners(): lax.ppermute(value[mask], 'tgt', partners(n_tgt, mask))]
    pallas_call x4 -> x6, Pallas kernels: 12.3 us -> 19.4 us  [the longest x2 10.7 us: attention_grads(): pl.pallas_call(functools.partial(grads_kernel, count), grid_spec=pltpu.Pr...]
    convert_element_type x12 -> x4, other arithmetic: 8.39 us -> 2.53 us  [plus(): return (one.astype(F32) + two.astype(F32)).astype(BF16)]
    ppermute x4, waiting for transfers between devices: 5.87 us -> 2.47 us  [exchange(): return lax.ppermute(value, ('inp', 'tgt'), pairs)]
    transpose x0 -> x1, local copies, waits for them, and re-layouts: none -> 2.89 us  [body(): own = [jnp.transpose(array, (2, 0, 1, 3)) for array in (queries, grad_out)]]
  transfers between devices with their start and end apart: 44 -> 33, of which waited for: 9 -> 13; matrix products, arithmetic and copies ran while one was open for 6% -> 2% of each run, Pallas kernels for 22% -> 26%
where the time goes in v2:
time: 175 us; the launch traced here: 174 us
  waiting for transfers between devices  54.3 us (31%)
  Pallas kernels  50.5 us (29%)
  starting transfers between devices  43.9 us (25%)
  local copies, waits for them, and re-layouts  20.6 us (12%)
  other arithmetic  4.11 us (2%)
    ppermute x6, waiting for transfers between devices, to_owners(): lax.ppermute(value[mask], 'tgt', partners(n_tgt, mask))  24.5 us
    unnamed x62, local copies, waits for them, and re-layouts  17.6 us
    pallas_call x4, Pallas kernels, back_blocks(): pl.pallas_call(back_kernel, grid_spec=pltpu.PrefetchScalarGridSpec(num_sc...  14.2 us
    pallas_call x2, Pallas kernels, attention_grads(): pl.pallas_call(functools.partial(grads_kernel, count), grid_spec=pltpu.Pr...  10.7 us
    ppermute x2, waiting for transfers between devices, body(): lax.ppermute(value, 'inp', opposite)  9.46 us
    pallas_call x2, Pallas kernels, project(): pl.pallas_call(project_kernel, grid=(width // depth,), in_specs=[pl.Block...  9.25 us
    ppermute x6, starting transfers between devices, everywhere(): lax.ppermute(value, 'inp', [(i, (i + shift) % n_inp) for i in range(n_inp)])  8.82 us
    ppermute x2, starting transfers between devices, body(): other = [lax.ppermute(value, 'inp', partners(n_inp, 1)) for value in mine]  7.63 us
  transfers between devices with their start and end apart: 33, of which 13 were waited for; matrix products, arithmetic and copies ran while one was open for 2% of the time, Pallas kernels for 26%

profile of v2, /device:TPU:0, one launch (start us, length us, event | category | flops | bytes accessed | tf_op | source)
XLA Modules:
  0.0 174.4 jit_solution(12870655030148490673)
XLA Ops:
  0.6 2.9 %copy_bitcast_fusion = (bf16[4,2,512,256]{3,2,1,0:T(8,128)(2,1)S(1)}, bf16[4,2,512,256]{3,2,1,0:T(8,128)(2,1)S(1)}) fusion(bf16[2,512,4,256]{3,2,1,0:T(4,128)(2,1)} %param.9, bf16[2,512,4,256]{3,2,1,0:T(4,128)(2,1)} %param.8), kind=kLoop, calls=%fused_computation | loop fusion | bytes 8388608 | tf_op jit(solution)/shard_map/transpose | solution.py:315
  3.6 0.9 shard_map.68
  5.1 2.9 %collective-permute-start = (bf16[1,512,256]{2,1,0:T(8,128)(2,1)S(1)}, bf16[1,512,256]{2,1,0:T(8,128)(2,1)}, u32[]{:S(2)}, u32[]{:S(2)}) collective-permute-start(bf16[1,512,256]{2,1,0:T(8,128)(2,1)S(1)} %get-tuple-element.33), channel_id=1, source_target_pairs={{0,4},{2,6},{4,0},{6,2},{8,14},{10,12},{12,10},{14,8},{16,20},{18,... | collective-permute-start | bytes 786440 | tf_op jit(solution)/shard_map/ppermute | solution.py:279
  8.1 2.0 %collective-permute-start.2 = (bf16[1,512,256]{2,1,0:T(8,128)(2,1)}, bf16[1,512,256]{2,1,0:T(8,128)(2,1)S(1)}, u32[]{:S(2)}, u32[]{:S(2)}) collective-permute-start(bf16[1,512,256]{2,1,0:T(8,128)(2,1)} %get-tuple-element.38), channel_id=1, source_target_pairs={{0,4},{2,6},{4,0},{6,2},{8,14},{10,12},{12,10},{14,8},{16,20},{18,... | collective-permute-start | bytes 786440 | tf_op jit(solution)/shard_map/ppermute | solution.py:279
  10.1 4.6 %shard_map.70 = (bf16[512,256]{1,0:T(8,128)(2,1)S(1)}, bf16[512,256]{1,0:T(8,128)(2,1)S(1)}) custom-call(bf16[512,4096]{1,0:T(8,128)(2,1)S(1)} %copy-done.8, bf16[2,4096,256]{2,1,0:T(8,128)(2,1)S(1)} %bitcast.48, bf16[2,4096,256]{2,1,0:T(8,128)(2,1)} %bitcast.54), custom_call_target="tpu_custom_call" | custom-call | flops 2147483648 | bytes 8388608 | tf_op jit(solution)/shard_map/pallas_call | solution.py:114
  14.8 1.8 %copy-done.5 = bf16[4,2,512,256]{3,2,1,0:T(8,128)(2,1)S(1)} copy-done((bf16[4,2,512,256]{3,2,1,0:T(8,128)(2,1)S(1)}, bf16[4,2,512,256]{3,2,1,0:T(8,128)(2,1)}, u32[]{:S(2)}) %copy-start.5) | copy-done | bytes 2097176
  16.6 1.1 shard_map.71
  18.2 1.0 copy-done.1
  19.1 2.2 %copy-done.9 = bf16[512,4096]{1,0:T(8,128)(2,1)S(1)} copy-done((bf16[512,4096]{1,0:T(8,128)(2,1)S(1)}, bf16[512,4096]{1,0:T(8,128)(2,1)}, u32[]{:S(2)}) %copy-start.9) | copy-done | bytes 4194328
  21.3 4.6 %shard_map.69 = (bf16[512,256]{1,0:T(8,128)(2,1)S(1)}, bf16[512,256]{1,0:T(8,128)(2,1)S(1)}) custom-call(bf16[512,4096]{1,0:T(8,128)(2,1)S(1)} %copy-done.9, bf16[2,4096,256]{2,1,0:T(8,128)(2,1)S(1)} %bitcast.49, bf16[2,4096,256]{2,1,0:T(8,128)(2,1)} %bitcast.55), custom_call_target="tpu_custom_call" | custom-call | flops 2147483648 | bytes 8388608 | tf_op jit(solution)/shard_map/pallas_call | solution.py:114
  26.0 0.7 copy-done.17
  27.4 1.5 collective-permute-start.12
  28.9 2.5 %collective-permute-done.5.refs_6_ = bf16[1,512,256]{2,1,0:T(8,128)(2,1)} collective-permute-done((bf16[1,512,256]{2,1,0:T(8,128)(2,1)}, bf16[1,512,256]{2,1,0:T(8,128)(2,1)}, u32[]{:S(2)}, u32[]{:S(2)}) %collective-permute-start.5) | collective-permute-done | bytes 262176 | tf_op jit(solution)/shard_map/ppermute | solution.py:279
  31.3 2.3 %collective-permute-start.10 = (bf16[1,512,256]{2,1,0:T(8,128)(2,1)}, bf16[1,512,256]{2,1,0:T(8,128)(2,1)}, u32[]{:S(2)}, u32[]{:S(2)}) collective-permute-start(bf16[1,512,256]{2,1,0:T(8,128)(2,1)} %collective-permute-done.refs_2_), channel_id=1, source_target_pairs={{0,8},{8,0},{16,24},{24,16},{1,9},{9,1},{17,25},{25,17},{2,10},{10... | collective-permute-start | bytes 786440 | tf_op jit(solution)/shard_map/ppermute | solution.py:329
  33.7 2.3 %collective-permute-done.12.refs_7_ = bf16[1,512,256]{2,1,0:T(8,128)(2,1)S(1)} collective-permute-done((bf16[1,512,256]{2,1,0:T(8,128)(2,1)}, bf16[1,512,256]{2,1,0:T(8,128)(2,1)S(1)}, u32[]{:S(2)}, u32[]{:S(2)}) %collective-permute-start.12) | collective-permute-done | bytes 262176 | tf_op jit(solution)/shard_map/ppermute | solution.py:329
  36.0 0.7 copy-done.27
  36.7 1.7 collective-permute-start.6
  38.5 3.2 %collective-permute-done.10.refs_3_ = bf16[1,512,256]{2,1,0:T(8,128)(2,1)} collective-permute-done((bf16[1,512,256]{2,1,0:T(8,128)(2,1)}, bf16[1,512,256]{2,1,0:T(8,128)(2,1)}, u32[]{:S(2)}, u32[]{:S(2)}) %collective-permute-start.10) | collective-permute-done | bytes 262176 | tf_op jit(solution)/shard_map/ppermute | solution.py:329
  41.7 2.0 %copy-done.6 = bf16[4,2,512,256]{3,2,1,0:T(8,128)(2,1)S(1)} copy-done((bf16[4,2,512,256]{3,2,1,0:T(8,128)(2,1)S(1)}, bf16[4,2,512,256]{3,2,1,0:T(8,128)(2,1)}, u32[]{:S(2)}) %copy-start.6) | copy-done | bytes 2097176
  43.7 0.9 copy-done.22
  44.6 0.9 copy-done.25
  45.6 0.9 copy-done.28
  46.6 3.5 %shard_map.74.refs_8_ = f32[4,2048]{1,0:T(4,128)S(1)} custom-call(s32[3]{0:T(128)S(1)} %pad_add_fusion.place_ref, bf16[512,256]{1,0:T(8,128)(2,1)S(1)} %copy-done.22, bf16[512,256]{1,0:T(8,128)(2,1)S(1)} %copy-done.25, bf16[4,2,512,256]{3,2,1,0:T(8,128)(2,1)S(1)} %copy-done.6, bf16[2,512,256]{2,1,0:T(8,128)(2,1)S(1)} %collective-permute-done.1.refs_1_, ...), custom_call_target="tpu_custom_call" | custom-call | flops 1073741824 | bytes 2621440 | tf_op jit(solution)/shard_map/pallas_call | solution.py:167
  50.0 3.8 %collective-permute-start.15 = (f32[4,2048]{1,0:T(4,128)S(1)}, f32[4,2048]{1,0:T(4,128)S(1)}, u32[]{:S(2)}, u32[]{:S(2)}) collective-permute-start(f32[4,2048]{1,0:T(4,128)S(1)} %shard_map.74.refs_8_), channel_id=1, source_target_pairs={{0,24},{8,0},{16,8},{24,16},{1,25},{9,1},{17,9},{25,17},{2,26},{10... | collective-permute-start | bytes 98312 | tf_op jit(solution)/shard_map/ppermute | solution.py:284
  53.9 0.8 collective-permute-start.13
  54.8 3.3 %shard_map.72.refs_8_ = f32[4,2048]{1,0:T(4,128)S(1)} custom-call(s32[3]{0:T(128)S(1)} %pad_add_fusion.place_ref, bf16[512,256]{1,0:T(8,128)(2,1)S(1)} %copy-done.18, bf16[512,256]{1,0:T(8,128)(2,1)S(1)} %copy-done.20, bf16[4,2,512,256]{3,2,1,0:T(8,128)(2,1)S(1)} %copy-done.7, bf16[2,512,256]{2,1,0:T(8,128)(2,1)S(1)} %collective-permute-done.1.refs_1_, ...), custom_call_target="tpu_custom_call" | custom-call | flops 1073741824 | bytes 2621440 | tf_op jit(solution)/shard_map/pallas_call | solution.py:167
  58.1 3.0 %collective-permute-start.9 = (f32[4,2048]{1,0:T(4,128)S(1)}, f32[4,2048]{1,0:T(4,128)S(1)}, u32[]{:S(2)}, u32[]{:S(2)}) collective-permute-start(f32[4,2048]{1,0:T(4,128)S(1)} %shard_map.72.refs_8_), channel_id=1, source_target_pairs={{0,24},{8,0},{16,8},{24,16},{1,25},{9,1},{17,9},{25,17},{2,26},{10... | collective-permute-start | bytes 98312 | tf_op jit(solution)/shard_map/ppermute | solution.py:284
  61.1 1.1 collective-permute-start.8
  62.3 1.0 copy-done.13
  63.3 5.2 %shard_map.75 = (bf16[4,256,256]{2,1,0:T(8,128)(2,1)S(1)}, bf16[4,256,256]{2,1,0:T(8,128)(2,1)S(1)}, bf16[512,256]{1,0:T(8,128)(2,1)S(1)}, bf16[512,256]{1,0:T(8,128)(2,1)S(1)}) custom-call(s32[3]{0:T(128)S(1)} %pad_add_fusion.place_ref, bf16[512,256]{1,0:T(8,128)(2,1)S(1)} %copy-done.23, bf16[512,256]{1,0:T(8,128)(2,1)S(1)} %copy-done.26, ...), custom_call_target="tpu_custom_call" | custom-call | flops 2684354560 | bytes 3932160 | tf_op jit(solution)/shard_map/pallas_call | solution.py:219
  68.6 2.4 %collective-permute-start.17 = (bf16[4,256,256]{2,1,0:T(8,128)(2,1)S(1)}, bf16[4,256,256]{2,1,0:T(8,128)(2,1)S(1)}, u32[]{:S(2)}, u32[]{:S(2)}) collective-permute-start(bf16[4,256,256]{2,1,0:T(8,128)(2,1)S(1)} %get-tuple-element.60), channel_id=1, source_target_pairs={{0,8},{8,0},{16,24},{24,16},{1,9},{9,1},{17,25},{25,17},{2,10},{10... | collective-permute-start | bytes 1572872 | tf_op jit(solution)/shard_map/ppermute | solution.py:354
  71.1 1.0 copy-done.11
  72.2 5.5 %shard_map.73 = (bf16[4,256,256]{2,1,0:T(8,128)(2,1)S(1)}, bf16[4,256,256]{2,1,0:T(8,128)(2,1)S(1)}, bf16[512,256]{1,0:T(8,128)(2,1)S(1)}, bf16[512,256]{1,0:T(8,128)(2,1)S(1)}) custom-call(s32[3]{0:T(128)S(1)} %pad_add_fusion.place_ref, bf16[512,256]{1,0:T(8,128)(2,1)S(1)} %copy-done.18, bf16[512,256]{1,0:T(8,128)(2,1)S(1)} %copy-done.20, ...), custom_call_target="tpu_custom_call" | custom-call | flops 2684354560 | bytes 3932160 | tf_op jit(solution)/shard_map/pallas_call | solution.py:219
  77.6 0.8 copy-done.15
  78.4 3.9 %shard_map.76 = bf16[2,512,512]{2,1,0:T(8,128)(2,1)} custom-call(s32[2]{0:T(128)S(1)} %pad_add_fusion.3.order_ref, bf16[2,4096,256]{2,1,0:T(8,128)(2,1)S(1)} %bitcast.50, bf16[2,4096,256]{2,1,0:T(8,128)(2,1)} %bitcast.56, bf16[512,256]{1,0:T(8,128)(2,1)S(1)} %get-tuple-element.52.refs_0_, bf16[512,256]{1,0:T(8,128)(2,1)S(1)} %get-tuple-element.53.refs_1_, ...), custom_call_target="tpu_custom_call" | custom-call | flops 1073741824 | bytes 4194304 | tf_op jit(solution)/shard_map/pallas_call | solution.py:255
  82.4 0.9 add_convert_fusion.3
  83.3 3.9 %shard_map.78 = bf16[2,512,512]{2,1,0:T(8,128)(2,1)} custom-call(s32[2]{0:T(128)S(1)} %pad_add_fusion.4.order_ref, bf16[2,4096,256]{2,1,0:T(8,128)(2,1)S(1)} %bitcast.51, bf16[2,4096,256]{2,1,0:T(8,128)(2,1)} %bitcast.57, bf16[512,256]{1,0:T(8,128)(2,1)S(1)} %get-tuple-element.52.refs_0_, bf16[512,256]{1,0:T(8,128)(2,1)S(1)} %get-tuple-element.53.refs_1_, ...), custom_call_target="tpu_custom_call" | custom-call | flops 1073741824 | bytes 4194304 | tf_op jit(solution)/shard_map/pallas_call | solution.py:255
  87.8 1.5 collective-permute-start.25
  89.3 1.1 collective-permute-start.19
  90.5 2.2 %copy-done.3 = bf16[2,4096,1,1,256]{4,1,3,2,0:T(8,128)(2,1)S(1)} copy-done((bf16[2,4096,1,1,256]{4,1,3,2,0:T(8,128)(2,1)S(1)}, bf16[2,4096,1,1,256]{4,1,3,2,0:T(8,128)(2,1)}, u32[]{:S(2)}) %copy-start.3) | copy-done | bytes 4194328
  92.7 3.2 %shard_map.77 = bf16[2,512,512]{2,1,0:T(8,128)(2,1)S(1)} custom-call(s32[2]{0:T(128)S(1)} %pad_add_fusion.2.order_ref, bf16[2,4096,256]{2,1,0:T(8,128)(2,1)S(1)} %bitcast.52, bf16[2,4096,256]{2,1,0:T(8,128)(2,1)} %bitcast.58, bf16[512,256]{1,0:T(8,128)(2,1)S(1)} %get-tuple-element.52.refs_0_, bf16[512,256]{1,0:T(8,128)(2,1)S(1)} %get-tuple-element.53.refs_1_, ...), custom_call_target="tpu_custom_call" | custom-call | flops 1073741824 | bytes 4194304 | tf_op jit(solution)/shard_map/pallas_call | solution.py:255
  95.9 8.9 %collective-permute-done.25 = bf16[4,256,256]{2,1,0:T(8,128)(2,1)} collective-permute-done((bf16[4,256,256]{2,1,0:T(8,128)(2,1)}, bf16[4,256,256]{2,1,0:T(8,128)(2,1)}, u32[]{:S(2)}, u32[]{:S(2)}) %collective-permute-start.25) | collective-permute-done | bytes 524320 | tf_op jit(solution)/shard_map/ppermute | solution.py:381
  104.7 1.3 add_convert_fusion
  106.1 3.2 %shard_map.79 = bf16[2,512,512]{2,1,0:T(8,128)(2,1)S(1)} custom-call(s32[2]{0:T(128)S(1)} %pad_add_fusion.1.order_ref, bf16[2,4096,256]{2,1,0:T(8,128)(2,1)S(1)} %bitcast.53, bf16[2,4096,256]{2,1,0:T(8,128)(2,1)} %bitcast.59, bf16[512,256]{1,0:T(8,128)(2,1)S(1)} %get-tuple-element.52.refs_0_, bf16[512,256]{1,0:T(8,128)(2,1)S(1)} %get-tuple-element.53.refs_1_, ...), custom_call_target="tpu_custom_call" | custom-call | flops 1073741824 | bytes 4194304 | tf_op jit(solution)/shard_map/pallas_call | solution.py:255
  109.2 5.1 %collective-permute-done.19 = bf16[4,256,256]{2,1,0:T(8,128)(2,1)S(1)} collective-permute-done((bf16[4,256,256]{2,1,0:T(8,128)(2,1)}, bf16[4,256,256]{2,1,0:T(8,128)(2,1)S(1)}, u32[]{:S(2)}, u32[]{:S(2)}) %collective-permute-start.19) | collective-permute-done | bytes 524320 | tf_op jit(solution)/shard_map/ppermute | solution.py:354
  114.5 2.2 %collective-permute-start.20 = (bf16[4,256,256]{2,1,0:T(8,128)(2,1)S(1)}, bf16[4,256,256]{2,1,0:T(8,128)(2,1)S(1)}, u32[]{:S(2)}, u32[]{:S(2)}) collective-permute-start(bf16[4,256,256]{2,1,0:T(8,128)(2,1)S(1)} %add_convert_fusion.2), channel_id=1, source_target_pairs={{0,24},{24,0},{8,16},{16,8},{1,25},{25,1},{9,17},{17,9},{2,26},{26... | collective-permute-start | bytes 1572872 | tf_op jit(solution)/shard_map/ppermute | solution.py:381
  116.7 0.7 collective-permute-start.28
  117.4 0.7 collective-permute-start.27
  118.7 2.3 %collective-permute-start.30 = (bf16[512,512]{1,0:T(8,128)(2,1)S(1)}, bf16[512,512]{1,0:T(8,128)(2,1)S(1)}, u32[]{:S(2)}, u32[]{:S(2)}) collective-permute-start(bf16[512,512]{1,0:T(8,128)(2,1)S(1)} %get-tuple-element.64), channel_id=1, source_target_pairs={{0,5},{1,4},{2,7},{3,6},{4,1},{5,0},{6,3},{7,2},{8,13},{9,12},{10,... | collective-permute-start | bytes 1572872 | tf_op jit(solution)/shard_map/ppermute | solution.py:374
  121.0 1.5 collective-permute-done.28
  122.5 1.3 collective-permute-start.31
  123.8 1.3 collective-permute-done.27
  125.2 3.8 %collective-permute-start.29 = (bf16[4,256,256]{2,1,0:T(8,128)(2,1)S(1)}, bf16[4,256,256]{2,1,0:T(8,128)(2,1)S(1)}, u32[]{:S(2)}, u32[]{:S(2)}) collective-permute-start(bf16[4,256,256]{2,1,0:T(8,128)(2,1)S(1)} %pad_maximum_fusion.1.mine_ref), channel_id=1, source_target_pairs={{0,8},{8,0},{16,24},{24,16},{1,9},{9,1},{17,25},{25,17},{2,10},{10... | collective-permute-start | bytes 1572872 | tf_op jit(solution)/shard_map/ppermute | solution.py:382
  130.0 1.3 collective-permute-start.22
  131.3 19.3 %collective-permute-done.23 = bf16[256,256]{1,0:T(8,128)(2,1)S(1)} collective-permute-done((bf16[256,256]{1,0:T(8,128)(2,1)S(1)}, bf16[256,256]{1,0:T(8,128)(2,1)S(1)}, u32[]{:S(2)}, u32[]{:S(2)}) %collective-permute-start.23) | collective-permute-done | bytes 131104 | tf_op jit(solution)/shard_map/ppermute | solution.py:296
  150.6 1.5 collective-permute-start.32
  152.1 1.1 collective-permute-done.22
  153.4 1.2 collective-permute-done.21
  154.7 3.8 %collective-permute-start.24 = (bf16[4,256,256]{2,1,0:T(8,128)(2,1)S(1)}, bf16[4,256,256]{2,1,0:T(8,128)(2,1)S(1)}, u32[]{:S(2)}, u32[]{:S(2)}) collective-permute-start(bf16[4,256,256]{2,1,0:T(8,128)(2,1)S(1)} %pad_maximum_fusion.mine_ref), channel_id=1, source_target_pairs={{0,8},{8,0},{16,24},{24,16},{1,9},{9,1},{17,25},{25,17},{2,10},{10... | collective-permute-start | bytes 1572872 | tf_op jit(solution)/shard_map/ppermute | solution.py:382
  158.5 3.9 %shard_map.80.rest_0_ = bf16[2,512,4,256]{3,2,1,0:T(4,128)(2,1)} custom-call(s32[3]{0:T(128)S(1)} %pad_add_fusion.place_ref, bf16[4,256,256]{2,1,0:T(8,128)(2,1)S(1)} %pad_maximum_fusion.1.mine_ref, bf16[4,256,256]{2,1,0:T(8,128)(2,1)S(1)} %collective-permute-done.29.other_ref), custom_call_target="tpu_custom_call" | custom-call | bytes 2097152 | tf_op jit(solution)/shard_map/pallas_call | solution.py:77
  162.4 2.0 %collective-permute-done.32 = bf16[512,512]{1,0:T(8,128)(2,1)S(1)} collective-permute-done((bf16[512,512]{1,0:T(8,128)(2,1)S(1)}, bf16[512,512]{1,0:T(8,128)(2,1)S(1)}, u32[]{:S(2)}, u32[]{:S(2)}) %collective-permute-start.32) | collective-permute-done | bytes 524320 | tf_op jit(solution)/shard_map/ppermute | solution.py:374
  164.4 1.1 fusion
  165.5 5.3 %collective-permute-done.24.other_ref = bf16[4,256,256]{2,1,0:T(8,128)(2,1)S(1)} collective-permute-done((bf16[4,256,256]{2,1,0:T(8,128)(2,1)S(1)}, bf16[4,256,256]{2,1,0:T(8,128)(2,1)S(1)}, u32[]{:S(2)}, u32[]{:S(2)}) %collective-permute-start.24) | collective-permute-done | bytes 524320 | tf_op jit(solution)/shard_map/ppermute | solution.py:382
  170.7 3.7 %shard_map.81 = bf16[2,512,4,256]{3,2,1,0:T(4,128)(2,1)} custom-call(s32[3]{0:T(128)S(1)} %pad_add_fusion.place_ref, bf16[4,256,256]{2,1,0:T(8,128)(2,1)S(1)} %pad_maximum_fusion.mine_ref, bf16[4,256,256]{2,1,0:T(8,128)(2,1)S(1)} %collective-permute-done.24.other_ref, bf16[2,512,4,256]{3,2,1,0:T(4,128)(2,1)} %shard_map.80.rest_0_), custom_call_target="tpu_custom_call", output_to_operand_aliasing={{}: (3, {})} | custom-call | bytes 2097152 | tf_op jit(solution)/shard_map/pallas_call | solution.py:77
  (95 shorter events, 4.9 us)
Async XLA Ops:
  3.5 1.6 copy-start.4
  3.6 6.6 %copy-start = (bf16[2,4096,1,1,256]{4,1,3,2,0:T(8,128)(2,1)S(1)}, bf16[2,4096,1,1,256]{4,1,3,2,0:T(8,128)(2,1)}, u32[]{:S(2)}) copy-start(bf16[2,4096,1,1,256]{4,1,3,2,0:T(8,128)(2,1)} %param.6) | copy-start | bytes 12582916
  3.6 6.6 %copy-start.8 = (bf16[512,4096]{1,0:T(8,128)(2,1)S(1)}, bf16[512,4096]{1,0:T(8,128)(2,1)}, u32[]{:S(2)}) copy-start(bf16[512,4096]{1,0:T(8,128)(2,1)} %enc_ref.1) | copy-start | bytes 12582916
  5.1 12.5 %collective-permute-start = (bf16[1,512,256]{2,1,0:T(8,128)(2,1)S(1)}, bf16[1,512,256]{2,1,0:T(8,128)(2,1)}, u32[]{:S(2)}, u32[]{:S(2)}) collective-permute-start(bf16[1,512,256]{2,1,0:T(8,128)(2,1)S(1)} %get-tuple-element.33), channel_id=1, source_target_pairs={{0,4},{2,6},{4,0},{6,2},{8,14},{10,12},{12,10},{14,8},{16,20},{18,... | collective-permute-start | bytes 786440 | tf_op jit(solution)/shard_map/ppermute | solution.py:279
  8.1 19.3 %collective-permute-start.11 = (bf16[1,512,256]{2,1,0:T(8,128)(2,1)}, bf16[1,512,256]{2,1,0:T(8,128)(2,1)}, u32[]{:S(2)}, u32[]{:S(2)}) collective-permute-start(bf16[1,512,256]{2,1,0:T(8,128)(2,1)} %get-tuple-element.37), channel_id=1, source_target_pairs={{0,4},{2,6},{4,0},{6,2},{8,14},{10,12},{12,10},{14,8},{16,20},{18,... | collective-permute-start | bytes 786440 | tf_op jit(solution)/shard_map/ppermute | solution.py:279
  8.1 25.6 %collective-permute-start.2 = (bf16[1,512,256]{2,1,0:T(8,128)(2,1)}, bf16[1,512,256]{2,1,0:T(8,128)(2,1)S(1)}, u32[]{:S(2)}, u32[]{:S(2)}) collective-permute-start(bf16[1,512,256]{2,1,0:T(8,128)(2,1)} %get-tuple-element.38), channel_id=1, source_target_pairs={{0,4},{2,6},{4,0},{6,2},{8,14},{10,12},{12,10},{14,8},{16,20},{18,... | collective-permute-start | bytes 786440 | tf_op jit(solution)/shard_map/ppermute | solution.py:279
  10.1 21.2 %collective-permute-start.5 = (bf16[1,512,256]{2,1,0:T(8,128)(2,1)}, bf16[1,512,256]{2,1,0:T(8,128)(2,1)}, u32[]{:S(2)}, u32[]{:S(2)}) collective-permute-start(bf16[1,512,256]{2,1,0:T(8,128)(2,1)} %get-tuple-element.39), channel_id=1, source_target_pairs={{0,4},{2,6},{4,0},{6,2},{8,14},{10,12},{12,10},{14,8},{16,20},{18,... | collective-permute-start | bytes 786440 | tf_op jit(solution)/shard_map/ppermute | solution.py:279
  14.8 2.9 %copy-start.21 = (bf16[512,256]{1,0:T(8,128)(2,1)}, bf16[512,256]{1,0:T(8,128)(2,1)S(1)}, u32[]{:S(2)}) copy-start(bf16[512,256]{1,0:T(8,128)(2,1)S(1)} %get-tuple-element.41.k_ref) | copy-start | bytes 786436
  14.8 2.9 %copy-start.24 = (bf16[512,256]{1,0:T(8,128)(2,1)}, bf16[512,256]{1,0:T(8,128)(2,1)S(1)}, u32[]{:S(2)}) copy-start(bf16[512,256]{1,0:T(8,128)(2,1)S(1)} %get-tuple-element.49.v_ref) | copy-start | bytes 786436
  14.8 1.8 %copy-start.5 = (bf16[4,2,512,256]{3,2,1,0:T(8,128)(2,1)S(1)}, bf16[4,2,512,256]{3,2,1,0:T(8,128)(2,1)}, u32[]{:S(2)}) copy-start(bf16[4,2,512,256]{3,2,1,0:T(8,128)(2,1)} %copy-done.4) | copy-start | bytes 6291460
  16.6 2.6 %copy-start.1 = (bf16[2,4096,1,1,256]{4,1,3,2,0:T(8,128)(2,1)S(1)}, bf16[2,4096,1,1,256]{4,1,3,2,0:T(8,128)(2,1)}, u32[]{:S(2)}) copy-start(bf16[2,4096,1,1,256]{4,1,3,2,0:T(8,128)(2,1)} %param.6) | copy-start | bytes 12582916
  17.6 24.1 %collective-permute-start.1 = (bf16[2,512,256]{2,1,0:T(8,128)(2,1)}, bf16[2,512,256]{2,1,0:T(8,128)(2,1)S(1)}, u32[]{:S(2)}, u32[]{:S(2)}) collective-permute-start(bf16[2,512,256]{2,1,0:T(8,128)(2,1)} %get-tuple-element.43), channel_id=1, source_target_pairs={{0,2},{2,0},{4,6},{6,4},{1,3},{3,1},{5,7},{7,5},{8,10},{10,8},{12,... | collective-permute-start | bytes 1572872 | tf_op jit(solution)/shard_map/ppermute | solution.py:325
  17.7 24.1 %collective-permute-start.4 = (bf16[2,512,256]{2,1,0:T(8,128)(2,1)}, bf16[2,512,256]{2,1,0:T(8,128)(2,1)S(1)}, u32[]{:S(2)}, u32[]{:S(2)}) collective-permute-start(bf16[2,512,256]{2,1,0:T(8,128)(2,1)} %get-tuple-element.45), channel_id=1, source_target_pairs={{0,2},{2,0},{4,6},{6,4},{1,3},{3,1},{5,7},{7,5},{8,10},{10,8},{12,... | collective-permute-start | bytes 1572872 | tf_op jit(solution)/shard_map/ppermute | solution.py:325
  19.1 2.2 %copy-start.9 = (bf16[512,4096]{1,0:T(8,128)(2,1)S(1)}, bf16[512,4096]{1,0:T(8,128)(2,1)}, u32[]{:S(2)}) copy-start(bf16[512,4096]{1,0:T(8,128)(2,1)} %enc_ref.1) | copy-start | bytes 12582916
  26.0 0.7 copy-start.17
  26.7 0.7 copy-start.19
  27.4 8.6 %collective-permute-start.12 = (bf16[1,512,256]{2,1,0:T(8,128)(2,1)}, bf16[1,512,256]{2,1,0:T(8,128)(2,1)S(1)}, u32[]{:S(2)}, u32[]{:S(2)}) collective-permute-start(bf16[1,512,256]{2,1,0:T(8,128)(2,1)} %collective-permute-done.11.refs_6_), channel_id=1, source_target_pairs={{0,8},{8,0},{16,24},{24,16},{1,9},{9,1},{17,25},{25,17},{2,10},{10... | collective-permute-start | bytes 786440 | tf_op jit(solution)/shard_map/ppermute | solution.py:329
  31.3 10.4 %collective-permute-start.10 = (bf16[1,512,256]{2,1,0:T(8,128)(2,1)}, bf16[1,512,256]{2,1,0:T(8,128)(2,1)}, u32[]{:S(2)}, u32[]{:S(2)}) collective-permute-start(bf16[1,512,256]{2,1,0:T(8,128)(2,1)} %collective-permute-done.refs_2_), channel_id=1, source_target_pairs={{0,8},{8,0},{16,24},{24,16},{1,9},{9,1},{17,25},{25,17},{2,10},{10... | collective-permute-start | bytes 786440 | tf_op jit(solution)/shard_map/ppermute | solution.py:329
  33.7 21.0 %collective-permute-start.3 = (bf16[1,512,256]{2,1,0:T(8,128)(2,1)S(1)}, bf16[1,512,256]{2,1,0:T(8,128)(2,1)}, u32[]{:S(2)}, u32[]{:S(2)}) collective-permute-start(bf16[1,512,256]{2,1,0:T(8,128)(2,1)S(1)} %collective-permute-done.2.refs_2_), channel_id=1, source_target_pairs={{0,8},{8,0},{16,24},{24,16},{1,9},{9,1},{17,25},{25,17},{2,10},{10... | collective-permute-start | bytes 786440 | tf_op jit(solution)/shard_map/ppermute | solution.py:329
  36.0 0.7 copy-start.27
  36.7 18.0 %collective-permute-start.6 = (bf16[1,512,256]{2,1,0:T(8,128)(2,1)}, bf16[1,512,256]{2,1,0:T(8,128)(2,1)}, u32[]{:S(2)}, u32[]{:S(2)}) collective-permute-start(bf16[1,512,256]{2,1,0:T(8,128)(2,1)} %collective-permute-done.5.refs_6_), channel_id=1, source_target_pairs={{0,8},{8,0},{16,24},{24,16},{1,9},{9,1},{17,25},{25,17},{2,10},{10... | collective-permute-start | bytes 786440 | tf_op jit(solution)/shard_map/ppermute | solution.py:329
  41.7 20.5 %copy-start.10 = (bf16[2,512,256]{2,1,0:T(8,128)(2,1)}, bf16[2,512,256]{2,1,0:T(8,128)(2,1)S(1)}, u32[]{:S(2)}) copy-start(bf16[2,512,256]{2,1,0:T(8,128)(2,1)S(1)} %collective-permute-done.1.refs_1_) | copy-start | bytes 1572868
  41.7 13.0 %copy-start.12 = (bf16[2,512,256]{2,1,0:T(8,128)(2,1)}, bf16[2,512,256]{2,1,0:T(8,128)(2,1)S(1)}, u32[]{:S(2)}) copy-start(bf16[2,512,256]{2,1,0:T(8,128)(2,1)S(1)} %collective-permute-done.4.refs_5_) | copy-start | bytes 1572868
  41.7 2.0 %copy-start.6 = (bf16[4,2,512,256]{3,2,1,0:T(8,128)(2,1)S(1)}, bf16[4,2,512,256]{3,2,1,0:T(8,128)(2,1)}, u32[]{:S(2)}) copy-start(bf16[4,2,512,256]{3,2,1,0:T(8,128)(2,1)} %copy-done.4) | copy-start | bytes 6291460
  43.7 0.9 copy-start.22
  44.6 0.9 copy-start.25
  45.6 0.9 copy-start.28
  46.5 8.2 %copy-start.7 = (bf16[4,2,512,256]{3,2,1,0:T(8,128)(2,1)S(1)}, bf16[4,2,512,256]{3,2,1,0:T(8,128)(2,1)}, u32[]{:S(2)}) copy-start(bf16[4,2,512,256]{3,2,1,0:T(8,128)(2,1)} %copy-done.4) | copy-start | bytes 6291460
  46.5 8.2 %copy-start.18 = (bf16[512,256]{1,0:T(8,128)(2,1)S(1)}, bf16[512,256]{1,0:T(8,128)(2,1)}, u32[]{:S(2)}) copy-start(bf16[512,256]{1,0:T(8,128)(2,1)} %copy-done.17) | copy-start | bytes 786436
  46.5 8.2 %copy-start.20 = (bf16[512,256]{1,0:T(8,128)(2,1)S(1)}, bf16[512,256]{1,0:T(8,128)(2,1)}, u32[]{:S(2)}) copy-start(bf16[512,256]{1,0:T(8,128)(2,1)} %copy-done.19) | copy-start | bytes 786436
  50.0 12.2 %collective-permute-start.15 = (f32[4,2048]{1,0:T(4,128)S(1)}, f32[4,2048]{1,0:T(4,128)S(1)}, u32[]{:S(2)}, u32[]{:S(2)}) collective-permute-start(f32[4,2048]{1,0:T(4,128)S(1)} %shard_map.74.refs_8_), channel_id=1, source_target_pairs={{0,24},{8,0},{16,8},{24,16},{1,25},{9,1},{17,9},{25,17},{2,26},{10... | collective-permute-start | bytes 98312 | tf_op jit(solution)/shard_map/ppermute | solution.py:284
  53.9 8.4 %collective-permute-start.14 = (f32[4,2048]{1,0:T(4,128)S(1)}, f32[4,2048]{1,0:T(4,128)S(1)}, u32[]{:S(2)}, u32[]{:S(2)}) collective-permute-start(f32[4,2048]{1,0:T(4,128)S(1)} %shard_map.74.refs_8_), channel_id=1, source_target_pairs={{0,16},{8,24},{16,0},{24,8},{1,17},{9,25},{17,1},{25,9},{2,18},{10... | collective-permute-start | bytes 98312 | tf_op jit(solution)/shard_map/ppermute | solution.py:284
  53.9 8.4 %collective-permute-start.13 = (f32[4,2048]{1,0:T(4,128)S(1)}, f32[4,2048]{1,0:T(4,128)S(1)}, u32[]{:S(2)}, u32[]{:S(2)}) collective-permute-start(f32[4,2048]{1,0:T(4,128)S(1)} %shard_map.74.refs_8_), channel_id=1, source_target_pairs={{0,8},{8,16},{16,24},{24,0},{1,9},{9,17},{17,25},{25,1},{2,10},{10... | collective-permute-start | bytes 98312 | tf_op jit(solution)/shard_map/ppermute | solution.py:284
  54.7 7.5 %copy-start.23 = (bf16[512,256]{1,0:T(8,128)(2,1)S(1)}, bf16[512,256]{1,0:T(8,128)(2,1)}, u32[]{:S(2)}) copy-start(bf16[512,256]{1,0:T(8,128)(2,1)} %copy-done.21) | copy-start | bytes 786436
  54.8 7.5 %copy-start.26 = (bf16[512,256]{1,0:T(8,128)(2,1)S(1)}, bf16[512,256]{1,0:T(8,128)(2,1)}, u32[]{:S(2)}) copy-start(bf16[512,256]{1,0:T(8,128)(2,1)} %copy-done.24) | copy-start | bytes 786436
  54.8 7.5 %copy-start.29 = (bf16[1,512,256]{2,1,0:T(8,128)(2,1)S(1)}, bf16[1,512,256]{2,1,0:T(8,128)(2,1)}, u32[]{:S(2)}) copy-start(bf16[1,512,256]{2,1,0:T(8,128)(2,1)} %copy-done.27) | copy-start | bytes 786436
  58.1 10.5 %collective-permute-start.9 = (f32[4,2048]{1,0:T(4,128)S(1)}, f32[4,2048]{1,0:T(4,128)S(1)}, u32[]{:S(2)}, u32[]{:S(2)}) collective-permute-start(f32[4,2048]{1,0:T(4,128)S(1)} %shard_map.72.refs_8_), channel_id=1, source_target_pairs={{0,24},{8,0},{16,8},{24,16},{1,25},{9,1},{17,9},{25,17},{2,26},{10... | collective-permute-start | bytes 98312 | tf_op jit(solution)/shard_map/ppermute | solution.py:284
  61.1 7.5 %collective-permute-start.8 = (f32[4,2048]{1,0:T(4,128)S(1)}, f32[4,2048]{1,0:T(4,128)S(1)}, u32[]{:S(2)}, u32[]{:S(2)}) collective-permute-start(f32[4,2048]{1,0:T(4,128)S(1)} %shard_map.72.refs_8_), channel_id=1, source_target_pairs={{0,16},{8,24},{16,0},{24,8},{1,17},{9,25},{17,1},{25,9},{2,18},{10... | collective-permute-start | bytes 98312 | tf_op jit(solution)/shard_map/ppermute | solution.py:284
  62.2 6.3 %collective-permute-start.7 = (f32[4,2048]{1,0:T(4,128)S(1)}, f32[4,2048]{1,0:T(4,128)S(1)}, u32[]{:S(2)}, u32[]{:S(2)}) collective-permute-start(f32[4,2048]{1,0:T(4,128)S(1)} %shard_map.72.refs_8_), channel_id=1, source_target_pairs={{0,8},{8,16},{16,24},{24,0},{1,9},{9,17},{17,25},{25,1},{2,10},{10... | collective-permute-start | bytes 98312 | tf_op jit(solution)/shard_map/ppermute | solution.py:284
  62.3 1.0 copy-start.13
  63.3 7.8 %copy-start.14 = (bf16[2,512,256]{2,1,0:T(8,128)(2,1)S(1)}, bf16[2,512,256]{2,1,0:T(8,128)(2,1)}, u32[]{:S(2)}) copy-start(bf16[2,512,256]{2,1,0:T(8,128)(2,1)} %copy-done.12) | copy-start | bytes 1572868
  68.6 13.8 %collective-permute-start.17 = (bf16[4,256,256]{2,1,0:T(8,128)(2,1)S(1)}, bf16[4,256,256]{2,1,0:T(8,128)(2,1)S(1)}, u32[]{:S(2)}, u32[]{:S(2)}) collective-permute-start(bf16[4,256,256]{2,1,0:T(8,128)(2,1)S(1)} %get-tuple-element.60), channel_id=1, source_target_pairs={{0,8},{8,0},{16,24},{24,16},{1,9},{9,1},{17,25},{25,17},{2,10},{10... | collective-permute-start | bytes 1572872 | tf_op jit(solution)/shard_map/ppermute | solution.py:354
  71.1 1.0 copy-start.11
  72.2 6.3 %copy-start.2 = (bf16[2,4096,1,1,256]{4,1,3,2,0:T(8,128)(2,1)S(1)}, bf16[2,4096,1,1,256]{4,1,3,2,0:T(8,128)(2,1)}, u32[]{:S(2)}) copy-start(bf16[2,4096,1,1,256]{4,1,3,2,0:T(8,128)(2,1)} %param.6) | copy-start | bytes 12582916
  77.6 0.8 copy-start.15
  78.4 3.9 %copy-start.30 = (bf16[4,256,256]{2,1,0:T(8,128)(2,1)}, bf16[4,256,256]{2,1,0:T(8,128)(2,1)S(1)}, u32[]{:S(2)}) copy-start(bf16[4,256,256]{2,1,0:T(8,128)(2,1)S(1)} %get-tuple-element.63) | copy-start | bytes 1572868
  82.4 8.1 %collective-permute-start.16 = (bf16[2,512,512]{2,1,0:T(8,128)(2,1)}, bf16[2,512,512]{2,1,0:T(8,128)(2,1)S(1)}, u32[]{:S(2)}, u32[]{:S(2)}) collective-permute-start(bf16[2,512,512]{2,1,0:T(8,128)(2,1)} %shard_map.76), channel_id=1, source_target_pairs={{0,2},{2,0},{4,6},{6,4},{1,3},{3,1},{5,7},{7,5},{8,10},{10,8},{12,... | collective-permute-start | bytes 3145736 | tf_op jit(solution)/shard_map/ppermute | solution.py:362
  87.3 18.8 %collective-permute-start.18 = (bf16[2,512,512]{2,1,0:T(8,128)(2,1)}, bf16[2,512,512]{2,1,0:T(8,128)(2,1)S(1)}, u32[]{:S(2)}, u32[]{:S(2)}) collective-permute-start(bf16[2,512,512]{2,1,0:T(8,128)(2,1)} %shard_map.78), channel_id=1, source_target_pairs={{0,2},{2,0},{4,6},{6,4},{1,3},{3,1},{5,7},{7,5},{8,10},{10,8},{12,... | collective-permute-start | bytes 3145736 | tf_op jit(solution)/shard_map/ppermute | solution.py:362
  87.8 16.9 %collective-permute-start.25 = (bf16[4,256,256]{2,1,0:T(8,128)(2,1)}, bf16[4,256,256]{2,1,0:T(8,128)(2,1)}, u32[]{:S(2)}, u32[]{:S(2)}) collective-permute-start(bf16[4,256,256]{2,1,0:T(8,128)(2,1)} %add_convert_fusion.3), channel_id=1, source_target_pairs={{0,24},{24,0},{8,16},{16,8},{1,25},{25,1},{9,17},{17,9},{2,26},{26... | collective-permute-start | bytes 1572872 | tf_op jit(solution)/shard_map/ppermute | solution.py:381
  89.3 25.0 %collective-permute-start.19 = (bf16[4,256,256]{2,1,0:T(8,128)(2,1)}, bf16[4,256,256]{2,1,0:T(8,128)(2,1)S(1)}, u32[]{:S(2)}, u32[]{:S(2)}) collective-permute-start(bf16[4,256,256]{2,1,0:T(8,128)(2,1)} %copy-done.30), channel_id=1, source_target_pairs={{0,8},{8,0},{16,24},{24,16},{1,9},{9,1},{17,25},{25,17},{2,10},{10... | collective-permute-start | bytes 1572872 | tf_op jit(solution)/shard_map/ppermute | solution.py:354
  90.5 2.2 %copy-start.3 = (bf16[2,4096,1,1,256]{4,1,3,2,0:T(8,128)(2,1)S(1)}, bf16[2,4096,1,1,256]{4,1,3,2,0:T(8,128)(2,1)}, u32[]{:S(2)}) copy-start(bf16[2,4096,1,1,256]{4,1,3,2,0:T(8,128)(2,1)} %param.6) | copy-start | bytes 12582916
  106.0 8.3 %copy-start.16 = (bf16[4,256,256]{2,1,0:T(8,128)(2,1)S(1)}, bf16[4,256,256]{2,1,0:T(8,128)(2,1)}, u32[]{:S(2)}) copy-start(bf16[4,256,256]{2,1,0:T(8,128)(2,1)} %copy-done.15) | copy-start | bytes 1572868
  114.5 15.2 %collective-permute-start.20 = (bf16[4,256,256]{2,1,0:T(8,128)(2,1)S(1)}, bf16[4,256,256]{2,1,0:T(8,128)(2,1)S(1)}, u32[]{:S(2)}, u32[]{:S(2)}) collective-permute-start(bf16[4,256,256]{2,1,0:T(8,128)(2,1)S(1)} %add_convert_fusion.2), channel_id=1, source_target_pairs={{0,24},{24,0},{8,16},{16,8},{1,25},{25,1},{9,17},{17,9},{2,26},{26... | collective-permute-start | bytes 1572872 | tf_op jit(solution)/shard_map/ppermute | solution.py:381
  116.7 5.9 %collective-permute-start.28 = (bf16[256,256]{1,0:T(8,128)(2,1)S(1)}, bf16[256,256]{1,0:T(8,128)(2,1)S(1)}, u32[]{:S(2)}, u32[]{:S(2)}) collective-permute-start(bf16[256,256]{1,0:T(8,128)(2,1)S(1)} %get-tuple-element.67), channel_id=1, source_target_pairs={{0,6},{2,4},{4,2},{6,0},{1,7},{3,5},{5,3},{7,1},{8,14},{10,12},{12... | collective-permute-start | bytes 393224 | tf_op jit(solution)/shard_map/ppermute | solution.py:296
  117.4 7.8 %collective-permute-start.27 = (bf16[256,256]{1,0:T(8,128)(2,1)S(1)}, bf16[256,256]{1,0:T(8,128)(2,1)S(1)}, u32[]{:S(2)}, u32[]{:S(2)}) collective-permute-start(bf16[256,256]{1,0:T(8,128)(2,1)S(1)} %get-tuple-element.68), channel_id=1, source_target_pairs={{0,4},{2,6},{4,0},{6,2},{1,5},{3,7},{5,1},{7,3},{8,12},{10,14},{12... | collective-permute-start | bytes 393224 | tf_op jit(solution)/shard_map/ppermute | solution.py:296
  118.1 7.1 %collective-permute-start.26 = (bf16[256,256]{1,0:T(8,128)(2,1)S(1)}, bf16[256,256]{1,0:T(8,128)(2,1)S(1)}, u32[]{:S(2)}, u32[]{:S(2)}) collective-permute-start(bf16[256,256]{1,0:T(8,128)(2,1)S(1)} %get-tuple-element.69), channel_id=1, source_target_pairs={{0,2},{2,0},{4,6},{6,4},{1,3},{3,1},{5,7},{7,5},{8,10},{10,8},{12,... | collective-permute-start | bytes 393224 | tf_op jit(solution)/shard_map/ppermute | solution.py:296
  118.7 43.8 %collective-permute-start.30 = (bf16[512,512]{1,0:T(8,128)(2,1)S(1)}, bf16[512,512]{1,0:T(8,128)(2,1)S(1)}, u32[]{:S(2)}, u32[]{:S(2)}) collective-permute-start(bf16[512,512]{1,0:T(8,128)(2,1)S(1)} %get-tuple-element.64), channel_id=1, source_target_pairs={{0,5},{1,4},{2,7},{3,6},{4,1},{5,0},{6,3},{7,2},{8,13},{9,12},{10,... | collective-permute-start | bytes 1572872 | tf_op jit(solution)/shard_map/ppermute | solution.py:374
  122.5 39.9 %collective-permute-start.31 = (bf16[512,512]{1,0:T(8,128)(2,1)S(1)}, bf16[512,512]{1,0:T(8,128)(2,1)S(1)}, u32[]{:S(2)}, u32[]{:S(2)}) collective-permute-start(bf16[512,512]{1,0:T(8,128)(2,1)S(1)} %get-tuple-element.65), channel_id=1, source_target_pairs={{0,4},{1,5},{2,6},{3,7},{4,0},{5,1},{6,2},{7,3},{8,12},{9,13},{10,... | collective-permute-start | bytes 1572872 | tf_op jit(solution)/shard_map/ppermute | solution.py:374
  125.2 33.3 %collective-permute-start.29 = (bf16[4,256,256]{2,1,0:T(8,128)(2,1)S(1)}, bf16[4,256,256]{2,1,0:T(8,128)(2,1)S(1)}, u32[]{:S(2)}, u32[]{:S(2)}) collective-permute-start(bf16[4,256,256]{2,1,0:T(8,128)(2,1)S(1)} %pad_maximum_fusion.1.mine_ref), channel_id=1, source_target_pairs={{0,8},{8,0},{16,24},{24,16},{1,9},{9,1},{17,25},{25,17},{2,10},{10... | collective-permute-start | bytes 1572872 | tf_op jit(solution)/shard_map/ppermute | solution.py:382
  129.9 20.8 %collective-permute-start.23 = (bf16[256,256]{1,0:T(8,128)(2,1)S(1)}, bf16[256,256]{1,0:T(8,128)(2,1)S(1)}, u32[]{:S(2)}, u32[]{:S(2)}) collective-permute-start(bf16[256,256]{1,0:T(8,128)(2,1)S(1)} %get-tuple-element.71), channel_id=1, source_target_pairs={{0,6},{2,4},{4,2},{6,0},{1,7},{3,5},{5,3},{7,1},{8,14},{10,12},{12... | collective-permute-start | bytes 393224 | tf_op jit(solution)/shard_map/ppermute | solution.py:296
  130.0 23.3 %collective-permute-start.22 = (bf16[256,256]{1,0:T(8,128)(2,1)S(1)}, bf16[256,256]{1,0:T(8,128)(2,1)S(1)}, u32[]{:S(2)}, u32[]{:S(2)}) collective-permute-start(bf16[256,256]{1,0:T(8,128)(2,1)S(1)} %get-tuple-element.72), channel_id=1, source_target_pairs={{0,4},{2,6},{4,0},{6,2},{1,5},{3,7},{5,1},{7,3},{8,12},{10,14},{12... | collective-permute-start | bytes 393224 | tf_op jit(solution)/shard_map/ppermute | solution.py:296
  150.6 13.8 %collective-permute-start.32 = (bf16[512,512]{1,0:T(8,128)(2,1)S(1)}, bf16[512,512]{1,0:T(8,128)(2,1)S(1)}, u32[]{:S(2)}, u32[]{:S(2)}) collective-permute-start(bf16[512,512]{1,0:T(8,128)(2,1)S(1)} %slice_bitcast_fusion.1), channel_id=1, source_target_pairs={{0,1},{1,0},{2,3},{3,2},{4,5},{5,4},{6,7},{7,6},{8,9},{9,8},{10,11... | collective-permute-start | bytes 1572872 | tf_op jit(solution)/shard_map/ppermute | solution.py:374
  153.3 1.3 collective-permute-start.21
  154.7 16.1 %collective-permute-start.24 = (bf16[4,256,256]{2,1,0:T(8,128)(2,1)S(1)}, bf16[4,256,256]{2,1,0:T(8,128)(2,1)S(1)}, u32[]{:S(2)}, u32[]{:S(2)}) collective-permute-start(bf16[4,256,256]{2,1,0:T(8,128)(2,1)S(1)} %pad_maximum_fusion.mine_ref), channel_id=1, source_target_pairs={{0,8},{8,0},{16,24},{24,16},{1,9},{9,1},{17,25},{25,17},{2,10},{10... | collective-permute-start | bytes 1572872 | tf_op jit(solution)/shard_map/ppermute | solution.py:382

commit v3 on v2

--- a/solution.py
+++ b/solution.py
@@ -19,11 +19,15 @@
 
 
 def params():
-    return pltpu.CompilerParams(vmem_limit_bytes=44 * MIB)
+    return pltpu.CompilerParams(vmem_limit_bytes=24 * MIB)
 
 
 def cost(flops, nbytes, exps=0):
     return pl.CostEstimate(flops=int(flops), bytes_accessed=int(nbytes), transcendentals=int(exps))
+
+
+def in_hbm(*arrays):
+    return [pltpu.with_memory_space_constraint(array, pltpu.HBM) for array in arrays]
 
 
 def partners(count, mask):
@@ -120,7 +124,7 @@
         scratch_shapes=[pltpu.VMEM((2, rows, size), F32)],
         compiler_params=params(),
         cost_estimate=cost(4 * rows * width * size, 2 * width * (rows + 2 * size)),
-    )(encoder, wk, wv)
+    )(*in_hbm(encoder, wk, wv))
 
 
 def columns(index, count, rows, place_ref):
@@ -234,15 +238,21 @@
     )(place, keys, values, *pieces, *stats)
 
 
-def back_kernel(order_ref, wk_ref, wv_ref, *refs):
-    out = refs[-1]
+def back_kernel(added, order_ref, wk_ref, wv_ref, *refs):
     layers = wk_ref.shape[0]
-    total = refs[2 * layers][0].astype(F32) if len(refs) > 2 * layers + 1 else None
+    outs = refs[2 * layers + added :]
+    total = refs[2 * layers][0].astype(F32) if added else None
     for layer in range(layers):
         part = dot(refs[2 * layer][...], wk_ref[layer], NT)
         total = part if total is None else total + part
         total = total + dot(refs[2 * layer + 1][...], wv_ref[layer], NT)
-    out[0] = total.astype(BF16)
+    if len(outs) == 1:
+        outs[0][0] = total.astype(BF16)
+    for index, out in enumerate(outs if len(outs) > 1 else ()):
+
+        @pl.when(pl.program_id(0) == index)
+        def _():
+            out[0] = total.astype(BF16)
 
 
 def back_blocks(order, wk, wv, flat, share, arrived=None):
@@ -252,26 +262,86 @@
     weight = pl.BlockSpec((layers, share, size), lambda i, order: (0, order[i], 0))
     result = pl.BlockSpec((1, rows, share), lambda i, order: (i, 0, 0))
     extra = [] if arrived is None else [arrived]
-    return pl.pallas_call(
-        back_kernel,
+    if extra:
+        out_specs = [pl.BlockSpec((1, rows, share), lambda i, order: (0, 0, 0))] * blocks
+        outs = [jax.ShapeDtypeStruct((1, rows, share), BF16)] * blocks
+    else:
+        out_specs, outs = result, jax.ShapeDtypeStruct((blocks, rows, share), BF16)
+    return pl.pallas_call(
+        functools.partial(back_kernel, len(extra)),
         grid_spec=pltpu.PrefetchScalarGridSpec(
             num_scalar_prefetch=1,
             grid=(blocks,),
             in_specs=[weight, weight]
             + [pl.BlockSpec((rows, size), lambda i, order: (0, 0))] * len(flat)
             + [result] * len(extra),
-            out_specs=result,
-        ),
-        out_shape=jax.ShapeDtypeStruct((blocks, rows, share), BF16),
+            out_specs=out_specs,
+        ),
+        out_shape=outs,
         compiler_params=params(),
         cost_estimate=cost(
             4 * layers * rows * size * share * blocks, 2 * blocks * share * (2 * layers * size + 2 * rows)
         ),
-    )(order, wk, wv, *flat, *extra)
-
-
-def plus(one, two):
-    return (one.astype(F32) + two.astype(F32)).astype(BF16)
+    )(order, *in_hbm(wk, wv), *flat, *extra)
+
+
+def plus_kernel(one_ref, two_ref, *outs):
+    total = (one_ref[...].astype(F32) + two_ref[...].astype(F32)).astype(BF16)
+    for index, out in enumerate(outs):
+        out[...] = total if len(outs) == 1 else total[index]
+
+
+def plus(one, two, spread=False):
+    shape = one.shape[1:] if spread else one.shape
+    outs = [jax.ShapeDtypeStruct(shape, BF16)] * (one.shape[0] if spread else 1)
+    results = pl.pallas_call(
+        plus_kernel,
+        grid=(1,),
+        in_specs=[whole(one.shape)] * 2,
+        out_specs=[whole(shape)] * len(outs),
+        out_shape=outs,
+        compiler_params=params(),
+        cost_estimate=cost(one.size, 6 * one.size),
+    )(one, two)
+    return results if spread else results[0]
+
+
+def stack_kernel(*refs):
+    for index, ref in enumerate(refs[:-1]):
+        refs[-1][index] = ref[...]
+
+
+def stacked(parts):
+    shape = (len(parts),) + parts[0].shape
+    return pl.pallas_call(
+        stack_kernel,
+        grid=(1,),
+        in_specs=[whole(parts[0].shape)] * len(parts),
+        out_specs=whole(shape),
+        out_shape=jax.ShapeDtypeStruct(shape, BF16),
+        compiler_params=params(),
+        cost_estimate=cost(0, 4 * len(parts) * parts[0].size),
+    )(*parts)
+
+
+def total_kernel(*refs):
+    total = refs[0][0].astype(F32)
+    for ref in refs[1:-1]:
+        total = total + ref[0].astype(F32)
+    refs[-1][...] = total.astype(BF16)
+
+
+def total_of(parts):
+    shape = parts[0].shape[1:]
+    return pl.pallas_call(
+        total_kernel,
+        grid=(1,),
+        in_specs=[whole(parts[0].shape)] * len(parts),
+        out_specs=whole(shape),
+        out_shape=jax.ShapeDtypeStruct(shape, BF16),
+        compiler_params=params(),
+        cost_estimate=cost(len(parts) * parts[0].size, 2 * (len(parts) + 1) * parts[0].size),
+    )(*parts)
 
 
 def exchange(value, n_inp, n_tgt, mask_of):
@@ -290,12 +360,9 @@
     return lax.optimization_barrier((value, *others))[0]
 
 
-def to_owners(value, n_tgt):
-    return jnp.stack(
-        [
-            value[mask] if mask == 0 else lax.ppermute(value[mask], "tgt", partners(n_tgt, mask))
-            for mask in range(n_tgt)
-        ]
+def to_owners(parts, n_tgt):
+    return stacked(
+        [part if mask == 0 else lax.ppermute(part, "tgt", partners(n_tgt, mask)) for mask, part in enumerate(parts)]
     )
 
 
@@ -311,9 +378,17 @@
     odd = (z % 2).astype(jnp.int32)
     upper = ((z == 0) | (z == n_inp - 1)).astype(jnp.int32) if line else jnp.ones_like(odd)
     place = jnp.stack([t.astype(jnp.int32), odd, upper])
+    wanted_head, beside_head = (t ^ (2 + odd))[None], (t ^ 1)[None]
+    orders = [
+        jnp.stack([(t ^ mask) * n_mdl + (m ^ side) for side in range(n_mdl)]).astype(jnp.int32)
+        for mask in range(n_tgt)
+    ]
+    queries, place, wanted_head, beside_head, *orders = lax.optimization_barrier(
+        (queries, place, wanted_head, beside_head, *orders)
+    )
 
     own = [jnp.transpose(array, (2, 0, 1, 3)) for array in (queries, grad_out)]
-    wanted = pick((t ^ (2 + odd))[None], [(source, layer, 1) for layer in range(layers) for source in own])
+    wanted = pick(wanted_head, [(source, layer, 1) for layer in range(layers) for source in own])
     fetched = [exchange(piece, n_inp, n_tgt, lambda z: 2 + z % 2) for piece in wanted]
     keys, values, begun = [], [], wanted
     for layer in range(layers):
@@ -321,7 +396,7 @@
         begun = fetched[:1]
         keys.append(key_block)
         values.append(value_block)
-    beside = pick(after((t ^ 1)[None], keys[0]), [(source, 0, layers) for source in own])
+    beside = pick(after(beside_head, keys[0]), [(source, 0, layers) for source in own])
     beside = [lax.ppermute(piece, "tgt", partners(n_tgt, 1)) for piece in beside]
     handed = []
     for index, piece in enumerate(fetched):
@@ -346,9 +421,6 @@
         send.append(results[1])
         flat += results[2:]
 
-    def order(mask):
-        return jnp.stack([(t ^ mask) * n_mdl + (m ^ side) for side in range(n_mdl)]).astype(jnp.int32)
-
     def pair_sum(layer, *others):
         value = after(send[layer], *stats[-1]) if layer == 0 else send[layer]
         return plus(after(keep[layer], *others), lax.ppermute(value, "inp", partners(n_inp, 1)))
@@ -358,11 +430,11 @@
     arrived = []
     for index, mask in enumerate(masks):
         wait = pair_sums if index else []
-        sent = back_blocks(after(order(mask + 1), *wait), wk, wv, flat, share)
+        sent = back_blocks(after(orders[mask + 1], *wait), wk, wv, flat, share)
         arrived.append(lax.ppermute(sent, "tgt", partners(n_tgt, 1)))
-    total, blocks = None, keys[0]
+    parts, blocks = [], keys
     for mask, block in zip(masks, arrived):
-        blocks = back_blocks(after(order(mask), blocks), wk, wv, flat, share, block)
+        blocks = back_blocks(after(orders[mask], *blocks), wk, wv, flat, share, block)
         for side in reversed(range(n_mdl)):
             block = blocks[side]
             if mask or side:
@@ -372,19 +444,22 @@
                     for b in range(n_mdl)
                 ]
                 block = lax.ppermute(block, ("tgt", "mdl"), pairs)
-            total = block.astype(F32) if total is None else total + block.astype(F32)
+            parts.append(block)
 
     query_grads = None
     if line:
-        pair_sums += [pair_sum(layer, blocks) for layer in range(1, layers)]
+        pair_sums += [pair_sum(layer, *blocks) for layer in range(1, layers)]
         opposite = [(0, 3), (3, 0), (1, 2), (2, 1)]
-        mine = [to_owners(plus(value, lax.ppermute(value, "inp", opposite)), n_tgt) for value in pair_sums]
+        mine = [
+            to_owners(plus(value, lax.ppermute(value, "inp", opposite), spread=True), n_tgt)
+            for value in pair_sums
+        ]
         other = [lax.ppermute(value, "inp", partners(n_inp, 1)) for value in mine]
     else:
         mine, other = ([to_owners(lax.psum(value, "inp"), n_tgt) for value in half] for half in (keep, send))
     for layer in range(layers):
         query_grads = join_heads(place, mine[layer], other[layer], layer, layers, query_grads)
-    return query_grads, total.astype(BF16)
+    return query_grads, total_of(parts)
 
 
 def solution(mesh):

time: 175 us -> 163 us (0.931)
  local copies, waits for them, and re-layouts: 20.6 us -> 2.49 us
  waiting for transfers between devices: 54.3 us -> 61.7 us
  starting transfers between devices: 43.9 us -> 51.3 us
  Pallas kernels: 50.5 us -> 46.2 us
  other arithmetic: 4.11 us -> 0.23 us
    ppermute x6, waiting for transfers between devices: 24.5 us -> 0.02 us  [to_owners(): lax.ppermute(part, 'tgt', partners(n_tgt, mask))]
    unnamed x62 -> x3, local copies, waits for them, and re-layouts: 17.6 us -> 0.48 us
    ppermute x2, waiting for transfers between devices: 9.46 us -> 18.9 us  [body(): lax.ppermute(value, 'inp', opposite)]
    ppermute x3, waiting for transfers between devices: 1.97 us -> 9.39 us  [body(): block = lax.ppermute(block, ('tgt', 'mdl'), pairs)]
    ppermute x2, starting transfers between devices: 7.63 us -> 14.9 us  [body(): other = [lax.ppermute(value, 'inp', partners(n_inp, 1)) for value in mine]]
    ppermute x4, waiting for transfers between devices: 2.47 us -> 7.85 us  [exchange(): return lax.ppermute(value, ('inp', 'tgt'), pairs)]
    ppermute x4, waiting for transfers between devices: 5.49 us -> 9.89 us  [body(): handed.append(lax.ppermute(after(piece, ahead), 'inp', partners(n_inp, 1)))]
    convert_element_type x5 -> x0, other arithmetic: 3.6 us -> none  [the longest x4 2.53 us: plus(): return (one.astype(F32) + two.astype(F32)).astype(BF16)]
  transfers between devices with their start and end apart: 33 -> 33, of which waited for: 13 -> 12; matrix products, arithmetic and copies ran while one was open for 2% -> 0% of each run, Pallas kernels for 26% -> 26%
where the time goes in v3:
time: 163 us
  waiting for transfers between devices  61.7 us (38%)
  starting transfers between devices  51.3 us (31%)
  Pallas kernels  46.2 us (28%)
  local copies, waits for them, and re-layouts  2.49 us (2%)
    ppermute x2, waiting for transfers between devices, body(): lax.ppermute(value, 'inp', opposite)  18.9 us
    ppermute x2, starting transfers between devices, body(): other = [lax.ppermute(value, 'inp', partners(n_inp, 1)) for value in mine]  14.9 us
    pallas_call x4, Pallas kernels, back_blocks(): pl.pallas_call(functools.partial(back_kernel, len(extra)), grid_spec=pltp...  13.4 us
    pallas_call x2, Pallas kernels, project(): pl.pallas_call(project_kernel, grid=(width // depth,), in_specs=[pl.Block...  11 us
    ppermute x6, starting transfers between devices, everywhere(): lax.ppermute(value, 'inp', [(i, (i + shift) % n_inp) for i in range(n_inp)])  9.95 us
    ppermute x4, waiting for transfers between devices, body(): handed.append(lax.ppermute(after(piece, ahead), 'inp', partners(n_inp, 1)))  9.89 us
    ppermute x3, waiting for transfers between devices, body(): block = lax.ppermute(block, ('tgt', 'mdl'), pairs)  9.39 us
    pallas_call x2, Pallas kernels, attention_grads(): pl.pallas_call(functools.partial(grads_kernel, count), grid_spec=pltpu.Pr...  8.15 us
  transfers between devices with their start and end apart: 33, of which 12 were waited for; matrix products, arithmetic and copies ran while one was open for 0% of the time, Pallas kernels for 26%

profile of v3, /device:TPU:0, one launch (start us, length us, event | category | flops | bytes accessed | tf_op | source)
XLA Modules:
  0.0 162.9 jit_solution(2602431611238358742)
XLA Ops:
  0.7 0.1 pad_add_fusion.place_ref
  0.7 0.1 pad_add_fusion.1
  0.8 0.1 pad_add_fusion.3
  0.9 2.0 %copy.13 = bf16[2,512,4,256]{3,1,0,2:T(8,128)(2,1)S(1)} copy(bf16[2,512,4,256]{3,2,1,0:T(4,128)(2,1)} %param.8) | data formatting | bytes 4194304 | tf_op jit(solution)/shard_map/optimization_barrier | solution.py:386
  2.9 0.2 copy-done
  3.1 0.3 copy.12
  3.4 0.1 shard_map.68
  3.5 3.0 %collective-permute-start = (bf16[1,512,256]{2,1,0:T(8,128)(2,1)S(1)}, bf16[1,512,256]{2,1,0:T(8,128)(2,1)S(1)}, u32[]{:S(2)}, u32[]{:S(2)}) collective-permute-start(bf16[1,512,256]{2,1,0:T(8,128)(2,1)S(1)} %get-tuple-element.56), channel_id=1, source_target_pairs={{0,4},{2,6},{4,0},{6,2},{8,14},{10,12},{12,10},{14,8},{16,20},{18,... | collective-permute-start | bytes 786440 | tf_op jit(solution)/shard_map/ppermute | solution.py:349
  6.5 0.1 collective-permute-start.11
  6.6 1.9 %collective-permute-start.2 = (bf16[1,512,256]{2,1,0:T(8,128)(2,1)S(1)}, bf16[1,512,256]{2,1,0:T(8,128)(2,1)S(1)}, u32[]{:S(2)}, u32[]{:S(2)}) collective-permute-start(bf16[1,512,256]{2,1,0:T(8,128)(2,1)S(1)} %get-tuple-element.62), channel_id=1, source_target_pairs={{0,4},{2,6},{4,0},{6,2},{8,14},{10,12},{12,10},{14,8},{16,20},{18,... | collective-permute-start | bytes 786440 | tf_op jit(solution)/shard_map/ppermute | solution.py:349
  8.5 0.1 collective-permute-start.5
  8.6 5.5 %shard_map.70 = (bf16[512,256]{1,0:T(8,128)(2,1)S(1)}, bf16[512,256]{1,0:T(8,128)(2,1)S(1)}) custom-call(bf16[512,4096]{1,0:T(8,128)(2,1)} %enc_ref.1, bf16[2,4096,256]{2,1,0:T(8,128)(2,1)} %bitcast.35, bf16[2,4096,256]{2,1,0:T(8,128)(2,1)} %bitcast.41), custom_call_target="tpu_custom_call" | custom-call | flops 2147483648 | bytes 8388608 | tf_op jit(solution)/shard_map/pallas_call | solution.py:118
  14.1 0.1 shard_map.71
  14.2 0.1 collective-permute-start.1
  14.3 0.5 collective-permute-start.4
  14.8 5.5 %shard_map.69 = (bf16[512,256]{1,0:T(8,128)(2,1)S(1)}, bf16[512,256]{1,0:T(8,128)(2,1)S(1)}) custom-call(bf16[512,4096]{1,0:T(8,128)(2,1)} %enc_ref.1, bf16[2,4096,256]{2,1,0:T(8,128)(2,1)} %bitcast.36, bf16[2,4096,256]{2,1,0:T(8,128)(2,1)} %bitcast.42), custom_call_target="tpu_custom_call" | custom-call | flops 2147483648 | bytes 8388608 | tf_op jit(solution)/shard_map/pallas_call | solution.py:118
  20.3 1.5 collective-permute-start.12
  21.8 7.8 %collective-permute-done.5.refs_6_ = bf16[1,512,256]{2,1,0:T(8,128)(2,1)S(1)} collective-permute-done((bf16[1,512,256]{2,1,0:T(8,128)(2,1)S(1)}, bf16[1,512,256]{2,1,0:T(8,128)(2,1)S(1)}, u32[]{:S(2)}, u32[]{:S(2)}) %collective-permute-start.5) | collective-permute-done | bytes 262176 | tf_op jit(solution)/shard_map/ppermute | solution.py:349
  29.6 2.3 %collective-permute-start.10 = (bf16[1,512,256]{2,1,0:T(8,128)(2,1)S(1)}, bf16[1,512,256]{2,1,0:T(8,128)(2,1)S(1)}, u32[]{:S(2)}, u32[]{:S(2)}) collective-permute-start(bf16[1,512,256]{2,1,0:T(8,128)(2,1)S(1)} %collective-permute-done.refs_2_), channel_id=1, source_target_pairs={{0,8},{8,0},{16,24},{24,16},{1,9},{9,1},{17,25},{25,17},{2,10},{10... | collective-permute-start | bytes 786440 | tf_op jit(solution)/shard_map/ppermute | solution.py:404
  32.0 2.0 %collective-permute-start.6 = (bf16[1,512,256]{2,1,0:T(8,128)(2,1)S(1)}, bf16[1,512,256]{2,1,0:T(8,128)(2,1)S(1)}, u32[]{:S(2)}, u32[]{:S(2)}) collective-permute-start(bf16[1,512,256]{2,1,0:T(8,128)(2,1)S(1)} %collective-permute-done.5.refs_6_), channel_id=1, source_target_pairs={{0,8},{8,0},{16,24},{24,16},{1,9},{9,1},{17,25},{25,17},{2,10},{10... | collective-permute-start | bytes 786440 | tf_op jit(solution)/shard_map/ppermute | solution.py:404
  34.0 5.1 %collective-permute-done.10.refs_3_ = bf16[1,512,256]{2,1,0:T(8,128)(2,1)S(1)} collective-permute-done((bf16[1,512,256]{2,1,0:T(8,128)(2,1)S(1)}, bf16[1,512,256]{2,1,0:T(8,128)(2,1)S(1)}, u32[]{:S(2)}, u32[]{:S(2)}) %collective-permute-start.10) | collective-permute-done | bytes 262176 | tf_op jit(solution)/shard_map/ppermute | solution.py:404
  39.1 2.2 %shard_map.74.refs_8_ = f32[4,2048]{1,0:T(4,128)S(1)} custom-call(s32[3]{0:T(128)S(1)} %pad_add_fusion.place_ref, bf16[512,256]{1,0:T(8,128)(2,1)S(1)} %get-tuple-element.65.k_ref, bf16[512,256]{1,0:T(8,128)(2,1)S(1)} %get-tuple-element.75.v_ref, bf16[4,2,512,256]{3,2,1,0:T(8,128)(2,1)S(1)} %bitcast.24, ...), custom_call_target="tpu_custom_call" | custom-call | flops 1073741824 | bytes 2621440 | tf_op jit(solution)/shard_map/pallas_call | solution.py:171
  41.2 4.1 %collective-permute-start.15 = (f32[4,2048]{1,0:T(4,128)S(1)}, f32[4,2048]{1,0:T(4,128)S(1)}, u32[]{:S(2)}, u32[]{:S(2)}) collective-permute-start(f32[4,2048]{1,0:T(4,128)S(1)} %shard_map.74.refs_8_), channel_id=1, source_target_pairs={{0,24},{8,0},{16,8},{24,16},{1,25},{9,1},{17,9},{25,17},{2,26},{10... | collective-permute-start | bytes 98312 | tf_op jit(solution)/shard_map/ppermute | solution.py:354
  45.4 0.6 collective-permute-start.13
  46.0 4.8 %collective-permute-done.6.refs_7_ = bf16[1,512,256]{2,1,0:T(8,128)(2,1)S(1)} collective-permute-done((bf16[1,512,256]{2,1,0:T(8,128)(2,1)S(1)}, bf16[1,512,256]{2,1,0:T(8,128)(2,1)S(1)}, u32[]{:S(2)}, u32[]{:S(2)}) %collective-permute-start.6) | collective-permute-done | bytes 262176 | tf_op jit(solution)/shard_map/ppermute | solution.py:404
  50.9 2.1 %shard_map.72.refs_8_ = f32[4,2048]{1,0:T(4,128)S(1)} custom-call(s32[3]{0:T(128)S(1)} %pad_add_fusion.place_ref, bf16[512,256]{1,0:T(8,128)(2,1)S(1)} %get-tuple-element.58.k_ref, bf16[512,256]{1,0:T(8,128)(2,1)S(1)} %get-tuple-element.59.v_ref, bf16[4,2,512,256]{3,2,1,0:T(8,128)(2,1)S(1)} %bitcast.25, ...), custom_call_target="tpu_custom_call" | custom-call | flops 1073741824 | bytes 2621440 | tf_op jit(solution)/shard_map/pallas_call | solution.py:171
  53.0 4.5 %collective-permute-start.9 = (f32[4,2048]{1,0:T(4,128)S(1)}, f32[4,2048]{1,0:T(4,128)S(1)}, u32[]{:S(2)}, u32[]{:S(2)}) collective-permute-start(f32[4,2048]{1,0:T(4,128)S(1)} %shard_map.72.refs_8_), channel_id=1, source_target_pairs={{0,24},{8,0},{16,8},{24,16},{1,25},{9,1},{17,9},{25,17},{2,26},{10... | collective-permute-start | bytes 98312 | tf_op jit(solution)/shard_map/ppermute | solution.py:354
  57.5 0.6 collective-permute-start.7
  58.2 4.1 %shard_map.75 = (bf16[4,256,256]{2,1,0:T(8,128)(2,1)S(1)}, bf16[4,256,256]{2,1,0:T(8,128)(2,1)S(1)}, bf16[512,256]{1,0:T(8,128)(2,1)S(1)}, bf16[512,256]{1,0:T(8,128)(2,1)S(1)}) custom-call(s32[3]{0:T(128)S(1)} %pad_add_fusion.place_ref, bf16[512,256]{1,0:T(8,128)(2,1)S(1)} %get-tuple-element.65.k_ref, bf16[512,256]{1,0:T(8,128)(2,1)S(1)} %get-tuple-element.75.v_ref, ...), custom_call_target="tpu_custom_call" | custom-call | flops 2684354560 | bytes 3932160 | tf_op jit(solution)/shard_map/pallas_call | solution.py:223
  62.3 0.9 collective-permute-done.7.refs_9_
  63.3 2.0 %collective-permute-start.17 = (bf16[4,256,256]{2,1,0:T(8,128)(2,1)S(1)}, bf16[4,256,256]{2,1,0:T(8,128)(2,1)S(1)}, u32[]{:S(2)}, u32[]{:S(2)}) collective-permute-start(bf16[4,256,256]{2,1,0:T(8,128)(2,1)S(1)} %get-tuple-element.90), channel_id=1, source_target_pairs={{0,8},{8,0},{16,24},{24,16},{1,9},{9,1},{17,25},{25,17},{2,10},{10... | collective-permute-start | bytes 1572872 | tf_op jit(solution)/shard_map/ppermute | solution.py:426
  65.2 4.1 %shard_map.73 = (bf16[4,256,256]{2,1,0:T(8,128)(2,1)S(1)}, bf16[4,256,256]{2,1,0:T(8,128)(2,1)S(1)}, bf16[512,256]{1,0:T(8,128)(2,1)S(1)}, bf16[512,256]{1,0:T(8,128)(2,1)S(1)}) custom-call(s32[3]{0:T(128)S(1)} %pad_add_fusion.place_ref, bf16[512,256]{1,0:T(8,128)(2,1)S(1)} %get-tuple-element.58.k_ref, bf16[512,256]{1,0:T(8,128)(2,1)S(1)} %get-tuple-element.59.v_ref, ...), custom_call_target="tpu_custom_call" | custom-call | flops 2684354560 | bytes 3932160 | tf_op jit(solution)/shard_map/pallas_call | solution.py:223
  69.3 3.3 %shard_map.76 = bf16[2,512,512]{2,1,0:T(8,128)(2,1)S(1)} custom-call(s32[2]{0:T(128)S(1)} %get-tuple-element.82.order_ref, bf16[2,4096,256]{2,1,0:T(8,128)(2,1)} %bitcast.37, bf16[2,4096,256]{2,1,0:T(8,128)(2,1)} %bitcast.43, bf16[512,256]{1,0:T(8,128)(2,1)S(1)} %get-tuple-element.78.refs_0_, bf16[512,256]{1,0:T(8,128)(2,1)S(1)} %get-tuple-element.79.refs_1_, ...), custom_call_target="tpu_custom_call" | custom-call | flops 1073741824 | bytes 4194304 | tf_op jit(solution)/shard_map/pallas_call | solution.py:270
  72.6 0.1 collective-permute-start.16
  72.7 2.4 %collective-permute-done.17.two_ref = bf16[4,256,256]{2,1,0:T(8,128)(2,1)S(1)} collective-permute-done((bf16[4,256,256]{2,1,0:T(8,128)(2,1)S(1)}, bf16[4,256,256]{2,1,0:T(8,128)(2,1)S(1)}, u32[]{:S(2)}, u32[]{:S(2)}) %collective-permute-start.17) | collective-permute-done | bytes 524320 | tf_op jit(solution)/shard_map/ppermute | solution.py:426
  75.0 0.1 shard_map.78.one_ref
  75.2 3.3 %shard_map.79 = bf16[2,512,512]{2,1,0:T(8,128)(2,1)S(1)} custom-call(s32[2]{0:T(128)S(1)} %get-tuple-element.91.order_ref, bf16[2,4096,256]{2,1,0:T(8,128)(2,1)} %bitcast.38, bf16[2,4096,256]{2,1,0:T(8,128)(2,1)} %bitcast.44, bf16[512,256]{1,0:T(8,128)(2,1)S(1)} %get-tuple-element.78.refs_0_, bf16[512,256]{1,0:T(8,128)(2,1)S(1)} %get-tuple-element.79.refs_1_, ...), custom_call_target="tpu_custom_call" | custom-call | flops 1073741824 | bytes 4194304 | tf_op jit(solution)/shard_map/pallas_call | solution.py:270
  78.6 1.8 %collective-permute-start.19 = (bf16[4,256,256]{2,1,0:T(8,128)(2,1)S(1)}, bf16[4,256,256]{2,1,0:T(8,128)(2,1)S(1)}, u32[]{:S(2)}, u32[]{:S(2)}) collective-permute-start(bf16[4,256,256]{2,1,0:T(8,128)(2,1)S(1)} %get-tuple-element.95), channel_id=1, source_target_pairs={{0,8},{8,0},{16,24},{24,16},{1,9},{9,1},{17,25},{25,17},{2,10},{10... | collective-permute-start | bytes 1572872 | tf_op jit(solution)/shard_map/ppermute | solution.py:426
  80.4 1.2 collective-permute-start.25
  81.6 3.4 %shard_map.77 = (bf16[1,512,512]{2,1,0:T(8,128)(2,1)S(1)}, bf16[1,512,512]{2,1,0:T(8,128)(2,1)S(1)}) custom-call(s32[2]{0:T(128)S(1)} %get-tuple-element.74.order_ref, bf16[2,4096,256]{2,1,0:T(8,128)(2,1)} %bitcast.39, bf16[2,4096,256]{2,1,0:T(8,128)(2,1)} %bitcast.45, bf16[512,256]{1,0:T(8,128)(2,1)S(1)} %get-tuple-element.78.refs_0_, ...), custom_call_target="tpu_custom_call" | custom-call | flops 1073741824 | bytes 4194304 | tf_op jit(solution)/shard_map/pallas_call | solution.py:270
  85.0 3.4 %shard_map.80 = (bf16[1,512,512]{2,1,0:T(8,128)(2,1)S(1)}, bf16[1,512,512]{2,1,0:T(8,128)(2,1)S(1)}) custom-call(s32[2]{0:T(128)S(1)} %get-tuple-element.85.order_ref, bf16[2,4096,256]{2,1,0:T(8,128)(2,1)} %bitcast.40, bf16[2,4096,256]{2,1,0:T(8,128)(2,1)} %bitcast.46, bf16[512,256]{1,0:T(8,128)(2,1)S(1)} %get-tuple-element.78.refs_0_, ...), custom_call_target="tpu_custom_call" | custom-call | flops 1073741824 | bytes 4194304 | tf_op jit(solution)/shard_map/pallas_call | solution.py:270
  88.4 4.5 %collective-permute-done.19.two_ref = bf16[4,256,256]{2,1,0:T(8,128)(2,1)S(1)} collective-permute-done((bf16[4,256,256]{2,1,0:T(8,128)(2,1)S(1)}, bf16[4,256,256]{2,1,0:T(8,128)(2,1)S(1)}, u32[]{:S(2)}, u32[]{:S(2)}) %collective-permute-start.19) | collective-permute-done | bytes 524320 | tf_op jit(solution)/shard_map/ppermute | solution.py:426
  92.9 0.1 shard_map.81.one_ref
  93.0 2.4 %collective-permute-start.20 = (bf16[4,256,256]{2,1,0:T(8,128)(2,1)S(1)}, bf16[4,256,256]{2,1,0:T(8,128)(2,1)S(1)}, u32[]{:S(2)}, u32[]{:S(2)}) collective-permute-start(bf16[4,256,256]{2,1,0:T(8,128)(2,1)S(1)} %shard_map.81.one_ref), channel_id=1, source_target_pairs={{0,24},{24,0},{8,16},{16,8},{1,25},{25,1},{9,17},{17,9},{2,26},{26... | collective-permute-start | bytes 1572872 | tf_op jit(solution)/shard_map/ppermute | solution.py:454
  95.4 10.1 %collective-permute-done.25.two_ref = bf16[4,256,256]{2,1,0:T(8,128)(2,1)S(1)} collective-permute-done((bf16[4,256,256]{2,1,0:T(8,128)(2,1)S(1)}, bf16[4,256,256]{2,1,0:T(8,128)(2,1)S(1)}, u32[]{:S(2)}, u32[]{:S(2)}) %collective-permute-start.25) | collective-permute-done | bytes 524320 | tf_op jit(solution)/shard_map/ppermute | solution.py:454
  105.6 0.1 shard_map.84
  105.7 0.1 collective-permute-start.26
  105.8 1.6 collective-permute-start.27
  107.4 0.3 collective-permute-start.28
  107.7 8.7 %collective-permute-done.20.two_ref = bf16[4,256,256]{2,1,0:T(8,128)(2,1)S(1)} collective-permute-done((bf16[4,256,256]{2,1,0:T(8,128)(2,1)S(1)}, bf16[4,256,256]{2,1,0:T(8,128)(2,1)S(1)}, u32[]{:S(2)}, u32[]{:S(2)}) %collective-permute-start.20) | collective-permute-done | bytes 524320 | tf_op jit(solution)/shard_map/ppermute | solution.py:454
  116.4 0.1 shard_map.82
  116.6 1.6 collective-permute-start.22
  118.2 0.3 collective-permute-start.23
  118.5 1.5 collective-permute-start.31
  120.0 12.0 %collective-permute-start.29 = (bf16[4,256,256]{2,1,0:T(8,128)(2,1)S(1)}, bf16[4,256,256]{2,1,0:T(8,128)(2,1)S(1)}, u32[]{:S(2)}, u32[]{:S(2)}) collective-permute-start(bf16[4,256,256]{2,1,0:T(8,128)(2,1)S(1)} %shard_map.85.mine_ref), channel_id=1, source_target_pairs={{0,8},{8,0},{16,24},{24,16},{1,9},{9,1},{17,25},{25,17},{2,10},{10... | collective-permute-start | bytes 1572872 | tf_op jit(solution)/shard_map/ppermute | solution.py:457
  132.0 1.5 collective-permute-start.30
  133.5 0.5 collective-permute-start.32
  134.1 2.9 %collective-permute-start.24 = (bf16[4,256,256]{2,1,0:T(8,128)(2,1)S(1)}, bf16[4,256,256]{2,1,0:T(8,128)(2,1)S(1)}, u32[]{:S(2)}, u32[]{:S(2)}) collective-permute-start(bf16[4,256,256]{2,1,0:T(8,128)(2,1)S(1)} %shard_map.83.mine_ref), channel_id=1, source_target_pairs={{0,8},{8,0},{16,24},{24,16},{1,9},{9,1},{17,25},{25,17},{2,10},{10... | collective-permute-start | bytes 1572872 | tf_op jit(solution)/shard_map/ppermute | solution.py:457
  136.9 7.8 %collective-permute-done.29.other_ref = bf16[4,256,256]{2,1,0:T(8,128)(2,1)S(1)} collective-permute-done((bf16[4,256,256]{2,1,0:T(8,128)(2,1)S(1)}, bf16[4,256,256]{2,1,0:T(8,128)(2,1)S(1)}, u32[]{:S(2)}, u32[]{:S(2)}) %collective-permute-start.29) | collective-permute-done | bytes 524320 | tf_op jit(solution)/shard_map/ppermute | solution.py:457
  144.8 3.9 %shard_map.86.rest_0_ = bf16[2,512,4,256]{3,2,1,0:T(4,128)(2,1)} custom-call(s32[3]{0:T(128)S(1)} %pad_add_fusion.place_ref, bf16[4,256,256]{2,1,0:T(8,128)(2,1)S(1)} %shard_map.85.mine_ref, bf16[4,256,256]{2,1,0:T(8,128)(2,1)S(1)} %collective-permute-done.29.other_ref), custom_call_target="tpu_custom_call" | custom-call | bytes 2097152 | tf_op jit(solution)/shard_map/pallas_call | solution.py:81
  148.7 0.1 collective-permute-done.30.refs_0_
  148.8 9.2 %collective-permute-done.32.refs_2_ = bf16[1,512,512]{2,1,0:T(8,128)(2,1)S(1)} collective-permute-done((bf16[1,512,512]{2,1,0:T(8,128)(2,1)S(1)}, bf16[1,512,512]{2,1,0:T(8,128)(2,1)S(1)}, u32[]{:S(2)}, u32[]{:S(2)}) %collective-permute-start.32) | collective-permute-done | bytes 524320 | tf_op jit(solution)/shard_map/ppermute | solution.py:446
  158.1 1.1 shard_map.88
  159.1 3.7 %shard_map.87 = bf16[2,512,4,256]{3,2,1,0:T(4,128)(2,1)} custom-call(s32[3]{0:T(128)S(1)} %pad_add_fusion.place_ref, bf16[4,256,256]{2,1,0:T(8,128)(2,1)S(1)} %shard_map.83.mine_ref, bf16[4,256,256]{2,1,0:T(8,128)(2,1)S(1)} %collective-permute-done.24.other_ref, bf16[2,512,4,256]{3,2,1,0:T(4,128)(2,1)} %shard_map.86.rest_0_), custom_call_target="tpu_custom_call", output_to_operand_aliasing={{}: (3, {})} | custom-call | bytes 2097152 | tf_op jit(solution)/shard_map/pallas_call | solution.py:81
  (30 shorter events, 0.4 us)
Async XLA Ops:
  0.9 2.2 %copy-start = (bf16[2,512,4,256]{3,2,1,0:T(4,128)(2,1)S(1)}, bf16[2,512,4,256]{3,2,1,0:T(4,128)(2,1)}, u32[]{:S(2)}) copy-start(bf16[2,512,4,256]{3,2,1,0:T(4,128)(2,1)} %param.9) | copy-start | bytes 6291460
  3.5 10.8 %collective-permute-start = (bf16[1,512,256]{2,1,0:T(8,128)(2,1)S(1)}, bf16[1,512,256]{2,1,0:T(8,128)(2,1)S(1)}, u32[]{:S(2)}, u32[]{:S(2)}) collective-permute-start(bf16[1,512,256]{2,1,0:T(8,128)(2,1)S(1)} %get-tuple-element.56), channel_id=1, source_target_pairs={{0,4},{2,6},{4,0},{6,2},{8,14},{10,12},{12,10},{14,8},{16,20},{18,... | collective-permute-start | bytes 786440 | tf_op jit(solution)/shard_map/ppermute | solution.py:349
  6.5 13.8 %collective-permute-start.11 = (bf16[1,512,256]{2,1,0:T(8,128)(2,1)S(1)}, bf16[1,512,256]{2,1,0:T(8,128)(2,1)S(1)}, u32[]{:S(2)}, u32[]{:S(2)}) collective-permute-start(bf16[1,512,256]{2,1,0:T(8,128)(2,1)S(1)} %get-tuple-element.61), channel_id=1, source_target_pairs={{0,4},{2,6},{4,0},{6,2},{8,14},{10,12},{12,10},{14,8},{16,20},{18,... | collective-permute-start | bytes 786440 | tf_op jit(solution)/shard_map/ppermute | solution.py:349
  6.6 25.4 %collective-permute-start.2 = (bf16[1,512,256]{2,1,0:T(8,128)(2,1)S(1)}, bf16[1,512,256]{2,1,0:T(8,128)(2,1)S(1)}, u32[]{:S(2)}, u32[]{:S(2)}) collective-permute-start(bf16[1,512,256]{2,1,0:T(8,128)(2,1)S(1)} %get-tuple-element.62), channel_id=1, source_target_pairs={{0,4},{2,6},{4,0},{6,2},{8,14},{10,12},{12,10},{14,8},{16,20},{18,... | collective-permute-start | bytes 786440 | tf_op jit(solution)/shard_map/ppermute | solution.py:349
  8.5 21.1 %collective-permute-start.5 = (bf16[1,512,256]{2,1,0:T(8,128)(2,1)S(1)}, bf16[1,512,256]{2,1,0:T(8,128)(2,1)S(1)}, u32[]{:S(2)}, u32[]{:S(2)}) collective-permute-start(bf16[1,512,256]{2,1,0:T(8,128)(2,1)S(1)} %get-tuple-element.63), channel_id=1, source_target_pairs={{0,4},{2,6},{4,0},{6,2},{8,14},{10,12},{12,10},{14,8},{16,20},{18,... | collective-permute-start | bytes 786440 | tf_op jit(solution)/shard_map/ppermute | solution.py:349
  14.2 24.9 %collective-permute-start.1 = (bf16[2,512,256]{2,1,0:T(8,128)(2,1)S(1)}, bf16[2,512,256]{2,1,0:T(8,128)(2,1)S(1)}, u32[]{:S(2)}, u32[]{:S(2)}) collective-permute-start(bf16[2,512,256]{2,1,0:T(8,128)(2,1)S(1)} %get-tuple-element.67), channel_id=1, source_target_pairs={{0,2},{2,0},{4,6},{6,4},{1,3},{3,1},{5,7},{7,5},{8,10},{10,8},{12,... | collective-permute-start | bytes 1572872 | tf_op jit(solution)/shard_map/ppermute | solution.py:400
  14.3 24.8 %collective-permute-start.4 = (bf16[2,512,256]{2,1,0:T(8,128)(2,1)S(1)}, bf16[2,512,256]{2,1,0:T(8,128)(2,1)S(1)}, u32[]{:S(2)}, u32[]{:S(2)}) collective-permute-start(bf16[2,512,256]{2,1,0:T(8,128)(2,1)S(1)} %get-tuple-element.69), channel_id=1, source_target_pairs={{0,2},{2,0},{4,6},{6,4},{1,3},{3,1},{5,7},{7,5},{8,10},{10,8},{12,... | collective-permute-start | bytes 1572872 | tf_op jit(solution)/shard_map/ppermute | solution.py:400
  20.3 11.8 %collective-permute-start.12 = (bf16[1,512,256]{2,1,0:T(8,128)(2,1)S(1)}, bf16[1,512,256]{2,1,0:T(8,128)(2,1)S(1)}, u32[]{:S(2)}, u32[]{:S(2)}) collective-permute-start(bf16[1,512,256]{2,1,0:T(8,128)(2,1)S(1)} %collective-permute-done.11.refs_6_), channel_id=1, source_target_pairs={{0,8},{8,0},{16,24},{24,16},{1,9},{9,1},{17,25},{25,17},{2,10},{10... | collective-permute-start | bytes 786440 | tf_op jit(solution)/shard_map/ppermute | solution.py:404
  29.6 9.4 %collective-permute-start.10 = (bf16[1,512,256]{2,1,0:T(8,128)(2,1)S(1)}, bf16[1,512,256]{2,1,0:T(8,128)(2,1)S(1)}, u32[]{:S(2)}, u32[]{:S(2)}) collective-permute-start(bf16[1,512,256]{2,1,0:T(8,128)(2,1)S(1)} %collective-permute-done.refs_2_), channel_id=1, source_target_pairs={{0,8},{8,0},{16,24},{24,16},{1,9},{9,1},{17,25},{25,17},{2,10},{10... | collective-permute-start | bytes 786440 | tf_op jit(solution)/shard_map/ppermute | solution.py:404
  32.0 14.0 %collective-permute-start.3 = (bf16[1,512,256]{2,1,0:T(8,128)(2,1)S(1)}, bf16[1,512,256]{2,1,0:T(8,128)(2,1)S(1)}, u32[]{:S(2)}, u32[]{:S(2)}) collective-permute-start(bf16[1,512,256]{2,1,0:T(8,128)(2,1)S(1)} %collective-permute-done.2.refs_2_), channel_id=1, source_target_pairs={{0,8},{8,0},{16,24},{24,16},{1,9},{9,1},{17,25},{25,17},{2,10},{10... | collective-permute-start | bytes 786440 | tf_op jit(solution)/shard_map/ppermute | solution.py:404
  32.0 18.8 %collective-permute-start.6 = (bf16[1,512,256]{2,1,0:T(8,128)(2,1)S(1)}, bf16[1,512,256]{2,1,0:T(8,128)(2,1)S(1)}, u32[]{:S(2)}, u32[]{:S(2)}) collective-permute-start(bf16[1,512,256]{2,1,0:T(8,128)(2,1)S(1)} %collective-permute-done.5.refs_6_), channel_id=1, source_target_pairs={{0,8},{8,0},{16,24},{24,16},{1,9},{9,1},{17,25},{25,17},{2,10},{10... | collective-permute-start | bytes 786440 | tf_op jit(solution)/shard_map/ppermute | solution.py:404
  41.2 16.3 %collective-permute-start.15 = (f32[4,2048]{1,0:T(4,128)S(1)}, f32[4,2048]{1,0:T(4,128)S(1)}, u32[]{:S(2)}, u32[]{:S(2)}) collective-permute-start(f32[4,2048]{1,0:T(4,128)S(1)} %shard_map.74.refs_8_), channel_id=1, source_target_pairs={{0,24},{8,0},{16,8},{24,16},{1,25},{9,1},{17,9},{25,17},{2,26},{10... | collective-permute-start | bytes 98312 | tf_op jit(solution)/shard_map/ppermute | solution.py:354
  45.4 12.8 %collective-permute-start.14 = (f32[4,2048]{1,0:T(4,128)S(1)}, f32[4,2048]{1,0:T(4,128)S(1)}, u32[]{:S(2)}, u32[]{:S(2)}) collective-permute-start(f32[4,2048]{1,0:T(4,128)S(1)} %shard_map.74.refs_8_), channel_id=1, source_target_pairs={{0,16},{8,24},{16,0},{24,8},{1,17},{9,25},{17,1},{25,9},{2,18},{10... | collective-permute-start | bytes 98312 | tf_op jit(solution)/shard_map/ppermute | solution.py:354
  45.4 12.8 %collective-permute-start.13 = (f32[4,2048]{1,0:T(4,128)S(1)}, f32[4,2048]{1,0:T(4,128)S(1)}, u32[]{:S(2)}, u32[]{:S(2)}) collective-permute-start(f32[4,2048]{1,0:T(4,128)S(1)} %shard_map.74.refs_8_), channel_id=1, source_target_pairs={{0,8},{8,16},{16,24},{24,0},{1,9},{9,17},{17,25},{25,1},{2,10},{10... | collective-permute-start | bytes 98312 | tf_op jit(solution)/shard_map/ppermute | solution.py:354
  53.0 9.3 %collective-permute-start.9 = (f32[4,2048]{1,0:T(4,128)S(1)}, f32[4,2048]{1,0:T(4,128)S(1)}, u32[]{:S(2)}, u32[]{:S(2)}) collective-permute-start(f32[4,2048]{1,0:T(4,128)S(1)} %shard_map.72.refs_8_), channel_id=1, source_target_pairs={{0,24},{8,0},{16,8},{24,16},{1,25},{9,1},{17,9},{25,17},{2,26},{10... | collective-permute-start | bytes 98312 | tf_op jit(solution)/shard_map/ppermute | solution.py:354
  57.5 4.8 %collective-permute-start.8 = (f32[4,2048]{1,0:T(4,128)S(1)}, f32[4,2048]{1,0:T(4,128)S(1)}, u32[]{:S(2)}, u32[]{:S(2)}) collective-permute-start(f32[4,2048]{1,0:T(4,128)S(1)} %shard_map.72.refs_8_), channel_id=1, source_target_pairs={{0,16},{8,24},{16,0},{24,8},{1,17},{9,25},{17,1},{25,9},{2,18},{10... | collective-permute-start | bytes 98312 | tf_op jit(solution)/shard_map/ppermute | solution.py:354
  57.5 5.7 %collective-permute-start.7 = (f32[4,2048]{1,0:T(4,128)S(1)}, f32[4,2048]{1,0:T(4,128)S(1)}, u32[]{:S(2)}, u32[]{:S(2)}) collective-permute-start(f32[4,2048]{1,0:T(4,128)S(1)} %shard_map.72.refs_8_), channel_id=1, source_target_pairs={{0,8},{8,16},{16,24},{24,0},{1,9},{9,17},{17,25},{25,1},{2,10},{10... | collective-permute-start | bytes 98312 | tf_op jit(solution)/shard_map/ppermute | solution.py:354
  63.3 11.8 %collective-permute-start.17 = (bf16[4,256,256]{2,1,0:T(8,128)(2,1)S(1)}, bf16[4,256,256]{2,1,0:T(8,128)(2,1)S(1)}, u32[]{:S(2)}, u32[]{:S(2)}) collective-permute-start(bf16[4,256,256]{2,1,0:T(8,128)(2,1)S(1)} %get-tuple-element.90), channel_id=1, source_target_pairs={{0,8},{8,0},{16,24},{24,16},{1,9},{9,1},{17,25},{25,17},{2,10},{10... | collective-permute-start | bytes 1572872 | tf_op jit(solution)/shard_map/ppermute | solution.py:426
  72.6 9.0 %collective-permute-start.16 = (bf16[2,512,512]{2,1,0:T(8,128)(2,1)S(1)}, bf16[2,512,512]{2,1,0:T(8,128)(2,1)S(1)}, u32[]{:S(2)}, u32[]{:S(2)}) collective-permute-start(bf16[2,512,512]{2,1,0:T(8,128)(2,1)S(1)} %shard_map.76), channel_id=1, source_target_pairs={{0,2},{2,0},{4,6},{6,4},{1,3},{3,1},{5,7},{7,5},{8,10},{10,8},{12,... | collective-permute-start | bytes 3145736 | tf_op jit(solution)/shard_map/ppermute | solution.py:434
  78.5 6.5 %collective-permute-start.18 = (bf16[2,512,512]{2,1,0:T(8,128)(2,1)S(1)}, bf16[2,512,512]{2,1,0:T(8,128)(2,1)S(1)}, u32[]{:S(2)}, u32[]{:S(2)}) collective-permute-start(bf16[2,512,512]{2,1,0:T(8,128)(2,1)S(1)} %shard_map.79), channel_id=1, source_target_pairs={{0,2},{2,0},{4,6},{6,4},{1,3},{3,1},{5,7},{7,5},{8,10},{10,8},{12,... | collective-permute-start | bytes 3145736 | tf_op jit(solution)/shard_map/ppermute | solution.py:434
  78.6 14.3 %collective-permute-start.19 = (bf16[4,256,256]{2,1,0:T(8,128)(2,1)S(1)}, bf16[4,256,256]{2,1,0:T(8,128)(2,1)S(1)}, u32[]{:S(2)}, u32[]{:S(2)}) collective-permute-start(bf16[4,256,256]{2,1,0:T(8,128)(2,1)S(1)} %get-tuple-element.95), channel_id=1, source_target_pairs={{0,8},{8,0},{16,24},{24,16},{1,9},{9,1},{17,25},{25,17},{2,10},{10... | collective-permute-start | bytes 1572872 | tf_op jit(solution)/shard_map/ppermute | solution.py:426
  80.4 25.2 %collective-permute-start.25 = (bf16[4,256,256]{2,1,0:T(8,128)(2,1)S(1)}, bf16[4,256,256]{2,1,0:T(8,128)(2,1)S(1)}, u32[]{:S(2)}, u32[]{:S(2)}) collective-permute-start(bf16[4,256,256]{2,1,0:T(8,128)(2,1)S(1)} %shard_map.78.one_ref), channel_id=1, source_target_pairs={{0,24},{24,0},{8,16},{16,8},{1,25},{25,1},{9,17},{17,9},{2,26},{26... | collective-permute-start | bytes 1572872 | tf_op jit(solution)/shard_map/ppermute | solution.py:454
  93.0 23.4 %collective-permute-start.20 = (bf16[4,256,256]{2,1,0:T(8,128)(2,1)S(1)}, bf16[4,256,256]{2,1,0:T(8,128)(2,1)S(1)}, u32[]{:S(2)}, u32[]{:S(2)}) collective-permute-start(bf16[4,256,256]{2,1,0:T(8,128)(2,1)S(1)} %shard_map.81.one_ref), channel_id=1, source_target_pairs={{0,24},{24,0},{8,16},{16,8},{1,25},{25,1},{9,17},{17,9},{2,26},{26... | collective-permute-start | bytes 1572872 | tf_op jit(solution)/shard_map/ppermute | solution.py:454
  105.7 12.5 %collective-permute-start.26 = (bf16[256,256]{1,0:T(8,128)(2,1)S(1)}, bf16[256,256]{1,0:T(8,128)(2,1)S(1)}, u32[]{:S(2)}, u32[]{:S(2)}) collective-permute-start(bf16[256,256]{1,0:T(8,128)(2,1)S(1)} %get-tuple-element.101), channel_id=1, source_target_pairs={{0,2},{2,0},{4,6},{6,4},{1,3},{3,1},{5,7},{7,5},{8,10},{10,8},{12,... | collective-permute-start | bytes 393224 | tf_op jit(solution)/shard_map/ppermute | solution.py:365
  105.8 12.7 %collective-permute-start.27 = (bf16[256,256]{1,0:T(8,128)(2,1)S(1)}, bf16[256,256]{1,0:T(8,128)(2,1)S(1)}, u32[]{:S(2)}, u32[]{:S(2)}) collective-permute-start(bf16[256,256]{1,0:T(8,128)(2,1)S(1)} %get-tuple-element.102), channel_id=1, source_target_pairs={{0,4},{2,6},{4,0},{6,2},{1,5},{3,7},{5,1},{7,3},{8,12},{10,14},{12... | collective-permute-start | bytes 393224 | tf_op jit(solution)/shard_map/ppermute | solution.py:365
  107.4 12.6 %collective-permute-start.28 = (bf16[256,256]{1,0:T(8,128)(2,1)S(1)}, bf16[256,256]{1,0:T(8,128)(2,1)S(1)}, u32[]{:S(2)}, u32[]{:S(2)}) collective-permute-start(bf16[256,256]{1,0:T(8,128)(2,1)S(1)} %get-tuple-element.103), channel_id=1, source_target_pairs={{0,6},{2,4},{4,2},{6,0},{1,7},{3,5},{5,3},{7,1},{8,14},{10,12},{12... | collective-permute-start | bytes 393224 | tf_op jit(solution)/shard_map/ppermute | solution.py:365
  116.5 15.5 %collective-permute-start.21 = (bf16[256,256]{1,0:T(8,128)(2,1)S(1)}, bf16[256,256]{1,0:T(8,128)(2,1)S(1)}, u32[]{:S(2)}, u32[]{:S(2)}) collective-permute-start(bf16[256,256]{1,0:T(8,128)(2,1)S(1)} %get-tuple-element.97), channel_id=1, source_target_pairs={{0,2},{2,0},{4,6},{6,4},{1,3},{3,1},{5,7},{7,5},{8,10},{10,8},{12,... | collective-permute-start | bytes 393224 | tf_op jit(solution)/shard_map/ppermute | solution.py:365
  116.6 16.9 %collective-permute-start.22 = (bf16[256,256]{1,0:T(8,128)(2,1)S(1)}, bf16[256,256]{1,0:T(8,128)(2,1)S(1)}, u32[]{:S(2)}, u32[]{:S(2)}) collective-permute-start(bf16[256,256]{1,0:T(8,128)(2,1)S(1)} %get-tuple-element.98), channel_id=1, source_target_pairs={{0,4},{2,6},{4,0},{6,2},{1,5},{3,7},{5,1},{7,3},{8,12},{10,14},{12... | collective-permute-start | bytes 393224 | tf_op jit(solution)/shard_map/ppermute | solution.py:365
  118.2 15.9 %collective-permute-start.23 = (bf16[256,256]{1,0:T(8,128)(2,1)S(1)}, bf16[256,256]{1,0:T(8,128)(2,1)S(1)}, u32[]{:S(2)}, u32[]{:S(2)}) collective-permute-start(bf16[256,256]{1,0:T(8,128)(2,1)S(1)} %get-tuple-element.99), channel_id=1, source_target_pairs={{0,6},{2,4},{4,2},{6,0},{1,7},{3,5},{5,3},{7,1},{8,14},{10,12},{12... | collective-permute-start | bytes 393224 | tf_op jit(solution)/shard_map/ppermute | solution.py:365
  118.5 30.2 %collective-permute-start.31 = (bf16[1,512,512]{2,1,0:T(8,128)(2,1)S(1)}, bf16[1,512,512]{2,1,0:T(8,128)(2,1)S(1)}, u32[]{:S(2)}, u32[]{:S(2)}) collective-permute-start(bf16[1,512,512]{2,1,0:T(8,128)(2,1)S(1)} %get-tuple-element.83), channel_id=1, source_target_pairs={{0,4},{1,5},{2,6},{3,7},{4,0},{5,1},{6,2},{7,3},{8,12},{9,13},{10,... | collective-permute-start | bytes 1572872 | tf_op jit(solution)/shard_map/ppermute | solution.py:446
  120.0 24.7 %collective-permute-start.29 = (bf16[4,256,256]{2,1,0:T(8,128)(2,1)S(1)}, bf16[4,256,256]{2,1,0:T(8,128)(2,1)S(1)}, u32[]{:S(2)}, u32[]{:S(2)}) collective-permute-start(bf16[4,256,256]{2,1,0:T(8,128)(2,1)S(1)} %shard_map.85.mine_ref), channel_id=1, source_target_pairs={{0,8},{8,0},{16,24},{24,16},{1,9},{9,1},{17,25},{25,17},{2,10},{10... | collective-permute-start | bytes 1572872 | tf_op jit(solution)/shard_map/ppermute | solution.py:457
  132.0 16.8 %collective-permute-start.30 = (bf16[1,512,512]{2,1,0:T(8,128)(2,1)S(1)}, bf16[1,512,512]{2,1,0:T(8,128)(2,1)S(1)}, u32[]{:S(2)}, u32[]{:S(2)}) collective-permute-start(bf16[1,512,512]{2,1,0:T(8,128)(2,1)S(1)} %get-tuple-element.84), channel_id=1, source_target_pairs={{0,5},{1,4},{2,7},{3,6},{4,1},{5,0},{6,3},{7,2},{8,13},{9,12},{10,... | collective-permute-start | bytes 1572872 | tf_op jit(solution)/shard_map/ppermute | solution.py:446
  133.5 24.6 %collective-permute-start.32 = (bf16[1,512,512]{2,1,0:T(8,128)(2,1)S(1)}, bf16[1,512,512]{2,1,0:T(8,128)(2,1)S(1)}, u32[]{:S(2)}, u32[]{:S(2)}) collective-permute-start(bf16[1,512,512]{2,1,0:T(8,128)(2,1)S(1)} %get-tuple-element.93), channel_id=1, source_target_pairs={{0,1},{1,0},{2,3},{3,2},{4,5},{5,4},{6,7},{7,6},{8,9},{9,8},{10,11... | collective-permute-start | bytes 1572872 | tf_op jit(solution)/shard_map/ppermute | solution.py:446
  134.1 25.1 %collective-permute-start.24 = (bf16[4,256,256]{2,1,0:T(8,128)(2,1)S(1)}, bf16[4,256,256]{2,1,0:T(8,128)(2,1)S(1)}, u32[]{:S(2)}, u32[]{:S(2)}) collective-permute-start(bf16[4,256,256]{2,1,0:T(8,128)(2,1)S(1)} %shard_map.83.mine_ref), channel_id=1, source_target_pairs={{0,8},{8,0},{16,24},{24,16},{1,9},{9,1},{17,25},{25,17},{2,10},{10... | collective-permute-start | bytes 1572872 | tf_op jit(solution)/shard_map/ppermute | solution.py:457

commit v4 on v3

v4 whole, which is shorter than its diff:
```python
import functools

import jax
import jax.numpy as jnp
from jax import lax
from jax.experimental import pallas as pl
from jax.experimental.pallas import tpu as pltpu
from jax.sharding import PartitionSpec as P

F32, BF16 = jnp.float32, jnp.bfloat16
MIB = 1024 * 1024
PARTS = 1
NT = (((1,), (1,)), ((), ()))
NN = (((1,), (0,)), ((), ()))
TN = (((0,), (0,)), ((), ()))


def dot(left, right, dims):
    return lax.dot_general(left, right, dims, preferred_element_type=F32)


def params():
    return pltpu.CompilerParams(vmem_limit_bytes=24 * MIB)


def cost(flops, nbytes, exps=0):
    return pl.CostEstimate(flops=int(flops), bytes_accessed=int(nbytes), transcendentals=int(exps))


def in_hbm(*arrays):
    return [pltpu.with_memory_space_constraint(array, pltpu.HBM) for array in arrays]


def partners(count, mask):
    return [(index, index ^ mask) for index in range(count)]


def pick_kernel(head_ref, *refs):
    count = sum(len(ref.shape) == 4 for ref in refs)
    sources, outs = refs[:count], refs[count:]
    for index, source in enumerate(sources):
        if len(outs) == count:
            outs[index][...] = source[0]
        else:
            layers = source.shape[1]
            outs[0][index * layers : (index + 1) * layers] = source[0]


def pick(head, parts, together=False):
    shape = parts[0][0].shape
    specs, sizes = [], []
    for source, first, count in parts:
        specs.append(
            pl.BlockSpec((1, count) + shape[2:], lambda i, head, first=first: (head[0], first, 0, 0))
        )
        sizes.append(count)
    sizes = [sum(sizes)] if together else sizes
    outs = [jax.ShapeDtypeStruct((size,) + shape[2:], BF16) for size in sizes]
    return pl.pallas_call(
        pick_kernel,
        grid_spec=pltpu.PrefetchScalarGridSpec(
            num_scalar_prefetch=1,
            grid=(1,),
            in_specs=specs,
            out_specs=[pl.BlockSpec(out.shape, lambda i, head: (0, 0, 0)) for out in outs],
        ),
        out_shape=outs,
        compiler_params=params(),
        cost_estimate=cost(0, 4 * sum(out.size for out in outs)),
    )(head, *[source for source, _, _ in parts])


def join_kernel(place_ref, part_ref, *rest):
    out = rest[-1]
    for head in range(part_ref.shape[0]):
        out[0, :, head, :] = part_ref[place_ref[0] ^ head]


def join_heads(place, part, mine, layer, layers, begun):
    heads, rows, size = part.shape
    extra = [] if begun is None else [begun]

    def half(i, place):
        return (layer, (1 - place[2]) if mine else place[2], 0, 0)

    return pl.pallas_call(
        join_kernel,
        grid_spec=pltpu.PrefetchScalarGridSpec(
            num_scalar_prefetch=1,
            grid=(1,),
            in_specs=[whole(part.shape)] + [pl.BlockSpec(memory_space=pl.ANY)] * len(extra),
            out_specs=pl.BlockSpec((1, rows, heads, size), half),
        ),
        out_shape=jax.ShapeDtypeStruct((layers, 2 * rows, heads, size), BF16),
        input_output_aliases={2: 0} if extra else {},
        compiler_params=params(),
        cost_estimate=cost(0, 4 * rows * heads * size),
    )(place, part, *extra)


def project_kernel(enc_ref, wk_ref, wv_ref, k_ref, v_ref, sums):
    step = pl.program_id(0)

    @pl.when(step == 0)
    def _():
        sums[...] = jnp.zeros_like(sums)

    sums[0] += dot(enc_ref[...], wk_ref[0], NN)
    sums[1] += dot(enc_ref[...], wv_ref[0], NN)

    @pl.when(step == pl.num_programs(0) - 1)
    def _():
        k_ref[0] = sums[0].astype(BF16)
        v_ref[0] = sums[1].astype(BF16)


def project(encoder, wk, wv, layer):
    rows, width = encoder.shape
    size = wk.shape[2]
    depth = width // 4
    weight = pl.BlockSpec((1, depth, size), lambda i: (layer, i, 0))
    result = whole((1, rows, size))
    return pl.pallas_call(
        project_kernel,
        grid=(width // depth,),
        in_specs=[pl.BlockSpec((rows, depth), lambda i: (0, i)), weight, weight],
        out_specs=[result, result],
        out_shape=[jax.ShapeDtypeStruct((1, rows, size), BF16)] * 2,
        scratch_shapes=[pltpu.VMEM((2, rows, size), F32)],
        compiler_params=params(),
        cost_estimate=cost(4 * rows * width * size, 2 * width * (rows + 2 * size)),
    )(*in_hbm(encoder, wk, wv))


def columns(index, count, rows, place_ref):
    if index < count - 2:
        return slice(index * rows, (index + 1) * rows)
    start = (count - 2 + ((index - count + 2) ^ place_ref[1])) * rows
    return pl.ds(pl.multiple_of(start, rows), rows)


def block_of(ref):
    return ref[(0,) * (len(ref.shape) - 2)]


def stats_kernel(place_ref, k_ref, v_ref, *refs):
    out, pieces = refs[-1], refs[:-1]
    count = len(pieces) // 2
    for index in range(count):
        query, cotangent = block_of(pieces[index]), block_of(pieces[count + index])
        cols = columns(index, count, query.shape[0], place_ref)
        scores = dot(block_of(k_ref), query, NT)
        peak = jnp.max(scores, axis=0, keepdims=True)
        shifted = jnp.exp(scores - peak)
        dprobs = dot(block_of(v_ref), cotangent, NT)
        out[0:1, cols] = peak
        out[1:2, cols] = jnp.sum(shifted, axis=0, keepdims=True)
        out[2:3, cols] = jnp.sum(shifted * dprobs, axis=0, keepdims=True)
        out[3:4, cols] = jnp.zeros_like(peak)


def whole(shape):
    return pl.BlockSpec(shape, lambda i, *place: (0,) * len(shape))


def block_at(array, index):
    if len(array.shape) == 4:
        return pl.BlockSpec((1, 1) + array.shape[2:], lambda i, place: (place[0], index, 0, 0))
    return pl.BlockSpec((1,) + array.shape[1:], lambda i, place: (index, 0, 0))


def row_stats(place, keys, values, pieces):
    enc_rows, size = keys.shape[1:]
    total = pieces[0][0].shape[-2] * len(pieces) // 2
    return pl.pallas_call(
        stats_kernel,
        grid_spec=pltpu.PrefetchScalarGridSpec(
            num_scalar_prefetch=1,
            grid=(1,),
            in_specs=[block_at(*piece) for piece in [(keys, 0), (values, 0), *pieces]],
            out_specs=whole((4, total)),
        ),
        out_shape=jax.ShapeDtypeStruct((4, total), F32),
        compiler_params=params(),
        cost_estimate=cost(
            4 * enc_rows * total * size, 4 * size * (enc_rows + total), enc_rows * total
        ),
    )(place, keys, values, *[array for array, _ in pieces])


def grads_kernel(count, place_ref, k_ref, v_ref, *refs):
    queries, cotangents, refs = refs[:count], refs[count : 2 * count], refs[2 * count :]
    stats, refs, (dk_ref, dv_ref) = refs[: -2 * PARTS - 2], refs[-2 * PARTS - 2 : -2], refs[-2:]
    keys, values = block_of(k_ref), block_of(v_ref)
    rows = refs[0].shape[1]
    for index in range(count):
        query, cotangent = block_of(queries[index]), block_of(cotangents[index])
        cols = columns(index, count, query.shape[0], place_ref)
        parts = [part[:, cols] for part in stats]
        peak = functools.reduce(jnp.maximum, [part[0:1] for part in parts])
        scales = [jnp.exp(part[0:1] - peak) for part in parts]
        total = sum(part[1:2] * scale for part, scale in zip(parts, scales))
        inner = sum(part[2:3] * scale for part, scale in zip(parts, scales)) / total
        attention = jnp.exp(dot(keys, query, NT) - peak) * (1.0 / total)
        dprobs = dot(values, cotangent, NT)
        dscores = (attention * (dprobs - inner)).astype(BF16)
        query_grad = dot(dscores, keys, TN).astype(BF16)
        slot = index if index < count - 2 else count - 2 + ((index - count + 2) ^ place_ref[1])
        first = place_ref[2] != 0
        for part in range(PARTS):
            upper = query_grad[part * rows : (part + 1) * rows]
            lower = query_grad[(PARTS + part) * rows : (PARTS + part + 1) * rows]
            refs[part][slot] = jnp.where(first, upper, lower)
            refs[PARTS + part][slot] = jnp.where(first, lower, upper)
        key_part = dot(dscores, query, NN)
        value_part = dot(attention.astype(BF16), cotangent, NN)
        key_sum = key_part if index == 0 else key_sum + key_part
        value_sum = value_part if index == 0 else value_sum + value_part
    dk_ref[...] = key_sum.astype(BF16)
    dv_ref[...] = value_sum.astype(BF16)


def attention_grads(place, keys, values, pieces, stats):
    enc_rows, size = keys.shape[1:]
    rows = pieces[0][0].shape[-2]
    count = len(pieces) // 2
    total = rows * count
    outs = [(count, rows // (2 * PARTS), size)] * (2 * PARTS) + [(enc_rows, size)] * 2
    return pl.pallas_call(
        functools.partial(grads_kernel, count),
        grid_spec=pltpu.PrefetchScalarGridSpec(
            num_scalar_prefetch=1,
            grid=(1,),
            in_specs=[block_at(*piece) for piece in [(keys, 0), (values, 0), *pieces]]
            + [whole((4, total))] * len(stats),
            out_specs=[whole(shape) for shape in outs],
        ),
        out_shape=[jax.ShapeDtypeStruct(shape, BF16) for shape in outs],
        compiler_params=params(),
        cost_estimate=cost(
            10 * enc_rows * total * size, 6 * size * (enc_rows + total), enc_rows * total
        ),
    )(place, keys, values, *[array for array, _ in pieces], *stats)


def back_kernel(order_ref, wk_ref, wv_ref, *refs):
    flat, out = refs[:-1], refs[-1]
    total = None
    for layer in range(wk_ref.shape[0]):
        part = dot(flat[2 * layer][...], wk_ref[layer], NT) + dot(flat[2 * layer + 1][...], wv_ref[layer], NT)
        total = part if total is None else total + part
    out[0] = total.astype(out.dtype)


def back_blocks(order, wk, wv, flat, share, dtype):
    layers, _, size = wk.shape
    rows = flat[0].shape[0]
    blocks = order.shape[0]
    weight = pl.BlockSpec((layers, share, size), lambda i, order: (0, order[i], 0))
    return pl.pallas_call(
        back_kernel,
        grid_spec=pltpu.PrefetchScalarGridSpec(
            num_scalar_prefetch=1,
            grid=(blocks,),
            in_specs=[weight, weight] + [pl.BlockSpec((rows, size), lambda i, order: (0, 0))] * len(flat),
            out_specs=pl.BlockSpec((1, rows, share), lambda i, order: (i, 0, 0)),
        ),
        out_shape=jax.ShapeDtypeStruct((blocks, rows, share), dtype),
        compiler_params=params(),
        cost_estimate=cost(
            4 * layers * rows * size * share * blocks, 2 * blocks * share * (2 * layers * size + 2 * rows)
        ),
    )(order, *in_hbm(wk, wv), *flat)


def plus_kernel(one_ref, two_ref, *outs):
    total = (one_ref[...].astype(F32) + two_ref[...].astype(F32)).astype(BF16)
    for index, out in enumerate(outs):
        out[...] = total if len(outs) == 1 else total[index]


def plus(one, two, spread=False):
    shape = one.shape[1:] if spread else one.shape
    outs = [jax.ShapeDtypeStruct(shape, BF16)] * (one.shape[0] if spread else 1)
    results = pl.pallas_call(
        plus_kernel,
        grid=(1,),
        in_specs=[whole(one.shape)] * 2,
        out_specs=[whole(shape)] * len(outs),
        out_shape=outs,
        compiler_params=params(),
        cost_estimate=cost(one.size, 6 * one.size),
    )(one, two)
    return results if spread else results[0]


def stack_kernel(*refs):
    for index, ref in enumerate(refs[:-1]):
        refs[-1][index] = ref[...]


def stacked(parts):
    shape = (len(parts),) + parts[0].shape
    return pl.pallas_call(
        stack_kernel,
        grid=(1,),
        in_specs=[whole(parts[0].shape)] * len(parts),
        out_specs=whole(shape),
        out_shape=jax.ShapeDtypeStruct(shape, BF16),
        compiler_params=params(),
        cost_estimate=cost(0, 4 * len(parts) * parts[0].size),
    )(*parts)


def total_kernel(*refs):
    total = refs[0][0].astype(F32)
    for ref in refs[1:-1]:
        total = total + ref[0].astype(F32)
    refs[-1][0] = total.astype(BF16)


def total_of(parts):
    shape = (1,) + parts[0][0].shape[1:]
    return pl.pallas_call(
        total_kernel,
        grid=(1,),
        in_specs=[pl.BlockSpec(shape, lambda i, index=index: (index, 0, 0)) for _, index in parts],
        out_specs=whole(shape),
        out_shape=jax.ShapeDtypeStruct(shape, BF16),
        compiler_params=params(),
        cost_estimate=cost(0, 0),
    )(*[array for array, _ in parts])


def exchange(value, n_inp, n_tgt, mask_of):
    pairs = [(z * n_tgt + t, z * n_tgt + (t ^ mask_of(z))) for z in range(n_inp) for t in range(n_tgt)]
    return lax.ppermute(value, ("inp", "tgt"), pairs)


def everywhere(value, n_inp):
    return [value] + [
        lax.ppermute(value, "inp", [(i, (i + shift) % n_inp) for i in range(n_inp)])
        for shift in range(1, n_inp)
    ]


def after(value, *others):
    return lax.optimization_barrier((value, *others))[0]


def to_owners(parts, n_tgt):
    return stacked(
        [part if mask == 0 else lax.ppermute(part, "tgt", partners(n_tgt, mask)) for mask, part in enumerate(parts)]
    )


def body(encoder, key_weight, value_weight, queries, grad_out):
    layers, dec_rows, heads, size = queries.shape
    width = encoder.shape[1]
    n_inp, n_tgt, n_mdl = (lax.axis_size(axis) for axis in ("inp", "tgt", "mdl"))
    z, t, m = (lax.axis_index(axis) for axis in ("inp", "tgt", "mdl"))
    share = width // (n_tgt * n_mdl)
    wk = key_weight.reshape(layers, width, size)
    wv = value_weight.reshape(layers, width, size)
    line = n_inp == 4
    odd = (z % 2).astype(jnp.int32)
    upper = ((z == 0) | (z == n_inp - 1)).astype(jnp.int32) if line else jnp.ones_like(odd)
    place = jnp.stack([t.astype(jnp.int32), odd, upper])
    wanted_head, beside_head = (t ^ (2 + odd))[None], (t ^ 1)[None]
    orders = [
        jnp.stack([(t ^ mask) * n_mdl + (m ^ side) for mask in masks for side in range(n_mdl)]).astype(jnp.int32)
        for masks in ((3, 1), (2, 0))
    ]
    queries, place, wanted_head, beside_head, *orders = lax.optimization_barrier(
        (queries, place, wanted_head, beside_head, *orders)
    )

    own = [jnp.transpose(array, (2, 0, 1, 3)) for array in (queries, grad_out)]
    wanted = []
    for layer in range(layers):
        first = after(wanted_head, *wanted)
        wanted += pick(first, [(source, layer, 1) for source in own], together=True)
    fetched = [exchange(piece, n_inp, n_tgt, lambda z: 2 + z % 2) for piece in wanted]
    keys, values, begun = [], [], wanted
    for layer in range(layers):
        key_block, value_block = project(after(encoder, *begun), wk, wv, layer)
        begun = fetched[:1]
        keys.append(key_block)
        values.append(value_block)
    (beside,) = pick(after(beside_head, keys[0]), [(source, 0, layers) for source in own], together=True)
    beside = lax.ppermute(beside, "tgt", partners(n_tgt, 1))
    handed = [
        lax.ppermute(after(piece, key_block), "inp", partners(n_inp, 1)) for piece, key_block in zip(fetched, keys)
    ]

    pieces, stats = [], []
    for layer in range(layers):
        pieces.append(
            [
                piece
                for kind in range(2)
                for piece in (
                    (own[kind], layer),
                    (beside, kind * layers + layer),
                    (fetched[layer], kind),
                    (handed[layer], kind),
                )
            ]
        )
        own_stats = row_stats(after(place, *[part[0] for part in stats]), keys[layer], values[layer], pieces[layer])
        stats.append(everywhere(own_stats, n_inp))
    flat, keep, send = [], [], []
    pair_sums, totals, mine, other = [], [], [], []

    def pair_sum(*others):
        index = len(pair_sums)
        if not line:
            pair_sums.append(keep[index])
        else:
            arrived = lax.ppermute(send[index], "inp", partners(n_inp, 1))
            pair_sums.append(plus(after(keep[index], *others), arrived))
        return pair_sums[-1]

    def line_sum(*others):
        index = len(totals)
        if not line:
            totals.append([lax.psum(keep[index], "inp")[mask] for mask in range(n_tgt)])
            mine.append(to_owners(totals[-1], n_tgt))
            other.append(to_owners([lax.psum(send[index], "inp")[mask] for mask in range(n_tgt)], n_tgt))
        else:
            value = pair_sums[index]
            earlier = [part for total in totals[-1:] for part in total]
            arrived = lax.ppermute(after(value, *earlier), "inp", [(0, 3), (3, 0), (1, 2), (2, 1)])
            totals.append(plus(after(value, *others), arrived, spread=True))
            mine.append(to_owners(totals[-1], n_tgt))
            other.append(lax.ppermute(mine[-1], "inp", partners(n_inp, 1)))
        return totals[-1]

    for layer in range(layers):
        results = attention_grads(after(place, *flat), keys[layer], values[layer], pieces[layer], stats[layer])
        keep += results[:PARTS]
        send += results[PARTS : 2 * PARTS]
        flat += results[2 * PARTS :]
    send[0] = after(send[0], *stats[-1])
    chunks = len(keep)

    sent = back_blocks(orders[0], wk, wv, flat, share, BF16)
    pair_sum(sent)
    while len(pair_sums) < chunks:
        send[len(pair_sums)] = after(send[len(pair_sums)], pair_sums[-1])
        pair_sum()
    arrived = lax.ppermute(after(sent, pair_sums[0]), "tgt", partners(n_tgt, 1))
    own_blocks = back_blocks(after(orders[1], pair_sums[0]), wk, wv, flat, share, F32)
    arrived = after(arrived, pair_sums[0])
    far_own, far_other = (total_of([(own_blocks, side), (arrived, side)]) for side in range(2))
    waits = [far_own, far_other]
    far_other = lax.ppermute(far_other, "tgt", partners(n_tgt, 2))
    far_own = lax.ppermute(far_own, "tgt", partners(n_tgt, 2))
    line_sum(*waits)
    side_own = total_of([(own_blocks, 3), (arrived, 3), (far_other, 0)])
    side_own = lax.ppermute(side_own, "mdl", partners(n_mdl, 1))
    while len(totals) < chunks:
        line_sum(side_own, far_own, mine[0])
    query_grads = None
    for layer in range(layers):
        query_grads = join_heads(place, mine[layer], True, layer, layers, query_grads)
        query_grads = join_heads(place, other[layer], False, layer, layers, query_grads)
    enc_grad = total_of([(own_blocks, 2), (arrived, 2), (far_own, 0), (side_own, 0)])
    return query_grads, enc_grad[0]


def solution(mesh):
    placed = (
        P("inp", None),
        P(None, None, "mdl", "tgt", None),
        P(None, None, "mdl", "tgt", None),
        P(None, "tgt", "mdl", None),
        P(None, "tgt", "mdl", None),
    )
    return jax.shard_map(
        body,
        mesh=mesh,
        in_specs=placed,
        out_specs=(P(None, "tgt", "mdl", None), P("inp", ("tgt", "mdl"))),
        check_vma=False,
    )
```

time: 163 us -> 148 us (0.908)
  waiting for transfers between devices: 61.7 us -> 52 us
  starting transfers between devices: 51.3 us -> 46 us
    ppermute x17 -> x13, waiting for transfers between devices: 52.9 us -> 34.7 us  [the longest x2 13.7 us: line_sum(): lax.ppermute(after(value, *earlier), 'inp', [(0, 3), (3, 0), (1, 2), (2,...]
    ppermute x6, waiting for transfers between devices: 0.02 us -> 5.99 us  [to_owners(): lax.ppermute(part, 'tgt', partners(n_tgt, mask))]
    ppermute x17 -> x13, starting transfers between devices: 32.4 us -> 28.7 us  [the longest x2 12.6 us: line_sum(): other.append(lax.ppermute(mine[-1], 'inp', partners(n_inp, 1)))]
    ppermute x4 -> x2, waiting for transfers between devices: 7.85 us -> 10.3 us  [exchange(): return lax.ppermute(value, ('inp', 'tgt'), pairs)]
    pallas_call x5 -> x6, Pallas kernels: 14.5 us -> 12.3 us  [the longest x2 10.9 us: back_blocks(): pl.pallas_call(back_kernel, grid_spec=pltpu.PrefetchScalarGridSpec(num_sc...]
    pallas_call x2 -> x4, Pallas kernels: 7.63 us -> 9.73 us  [join_heads(): pl.pallas_call(join_kernel, grid_spec=pltpu.PrefetchScalarGridSpec(num_sc...]
    ppermute x4 -> x2, starting transfers between devices: 5.11 us -> 3.09 us  [exchange(): return lax.ppermute(value, ('inp', 'tgt'), pairs)]
  transfers between devices with their start and end apart: 33 -> 27, of which waited for: 12 -> 16; matrix products, arithmetic and copies ran while one was open for 0% -> 0% of each run, Pallas kernels for 26% -> 29%
where the time goes in v4:
time: 148 us
  waiting for transfers between devices  52 us (35%)
  Pallas kernels  46.1 us (31%)
  starting transfers between devices  46 us (31%)
  local copies, waits for them, and re-layouts  2.49 us (2%)
    ppermute x2, waiting for transfers between devices, line_sum(): lax.ppermute(after(value, *earlier), 'inp', [(0, 3), (3, 0), (1, 2), (2,...  13.7 us
    ppermute x2, starting transfers between devices, line_sum(): other.append(lax.ppermute(mine[-1], 'inp', partners(n_inp, 1)))  12.6 us
    pallas_call x2, Pallas kernels, project(): pl.pallas_call(project_kernel, grid=(width // depth,), in_specs=[pl.Block...  11 us
    pallas_call x2, Pallas kernels, back_blocks(): pl.pallas_call(back_kernel, grid_spec=pltpu.PrefetchScalarGridSpec(num_sc...  10.9 us
    ppermute x2, waiting for transfers between devices, exchange(): return lax.ppermute(value, ('inp', 'tgt'), pairs)  10.3 us
    ppermute x6, starting transfers between devices, everywhere(): lax.ppermute(value, 'inp', [(i, (i + shift) % n_inp) for i in range(n_inp)])  9.84 us
    pallas_call x4, Pallas kernels, join_heads(): pl.pallas_call(join_kernel, grid_spec=pltpu.PrefetchScalarGridSpec(num_sc...  9.73 us
    ppermute x2, waiting for transfers between devices, line_sum(): other.append(lax.ppermute(mine[-1], 'inp', partners(n_inp, 1)))  8.84 us
  transfers between devices with their start and end apart: 27, of which 16 were waited for; matrix products, arithmetic and copies ran while one was open for 0% of the time, Pallas kernels for 29%

profile of v4, /device:TPU:0, one launch (start us, length us, event | category | flops | bytes accessed | tf_op | source)
XLA Modules:
  0.0 147.7 jit_solution(84287411235468515)
XLA Ops:
  0.7 0.1 pad_add_fusion.place_ref
  0.7 0.1 pad_add_fusion.1
  0.8 2.0 %copy.15 = bf16[2,512,4,256]{3,1,0,2:T(8,128)(2,1)S(1)} copy(bf16[2,512,4,256]{3,2,1,0:T(4,128)(2,1)} %param.8) | data formatting | bytes 4194304 | tf_op jit(solution)/shard_map/optimization_barrier | solution.py:374
  2.8 0.2 copy-done
  3.0 0.3 copy.14
  3.4 3.0 %collective-permute-start.1 = (bf16[2,512,256]{2,1,0:T(8,128)(2,1)S(1)}, bf16[2,512,256]{2,1,0:T(8,128)(2,1)S(1)}, u32[]{:S(2)}, u32[]{:S(2)}) collective-permute-start(bf16[2,512,256]{2,1,0:T(8,128)(2,1)S(1)} %shard_map.68), channel_id=1, source_target_pairs={{0,4},{2,6},{4,0},{6,2},{8,14},{10,12},{12,10},{14,8},{16,20},{18,... | collective-permute-start | bytes 1572872 | tf_op jit(solution)/shard_map/ppermute | solution.py:337
  6.4 5.5 %shard_map.70 = (bf16[1,512,256]{2,1,0:T(8,128)(2,1)S(1)}, bf16[1,512,256]{2,1,0:T(8,128)(2,1)S(1)}) custom-call(bf16[512,4096]{1,0:T(8,128)(2,1)} %enc_ref.1, bf16[2,4096,256]{2,1,0:T(8,128)(2,1)} %bitcast.36, bf16[2,4096,256]{2,1,0:T(8,128)(2,1)} %bitcast.40), custom_call_target="tpu_custom_call" | custom-call | flops 2147483648 | bytes 8388608 | tf_op jit(solution)/shard_map/pallas_call | solution.py:123
  11.9 0.1 shard_map.71
  12.0 0.1 collective-permute-start
  12.1 0.1 collective-permute-start.6
  12.2 6.9 %collective-permute-done.1.refs_2_.refs_6_ = bf16[2,512,256]{2,1,0:T(8,128)(2,1)S(1)} collective-permute-done((bf16[2,512,256]{2,1,0:T(8,128)(2,1)S(1)}, bf16[2,512,256]{2,1,0:T(8,128)(2,1)S(1)}, u32[]{:S(2)}, u32[]{:S(2)}) %collective-permute-start.1) | collective-permute-done | bytes 524320 | tf_op jit(solution)/shard_map/ppermute | solution.py:337
  19.1 1.5 %collective-permute-start.2 = (bf16[2,512,256]{2,1,0:T(8,128)(2,1)S(1)}, bf16[2,512,256]{2,1,0:T(8,128)(2,1)S(1)}, u32[]{:S(2)}, u32[]{:S(2)}) collective-permute-start(bf16[2,512,256]{2,1,0:T(8,128)(2,1)S(1)} %collective-permute-done.1.refs_2_.refs_6_), channel_id=1, source_target_pairs={{0,8},{8,0},{16,24},{24,16},{1,9},{9,1},{17,25},{25,17},{2,10},{10... | collective-permute-start | bytes 1572872 | tf_op jit(solution)/shard_map/ppermute | solution.py:393
  20.6 5.5 %shard_map.74 = (bf16[1,512,256]{2,1,0:T(8,128)(2,1)S(1)}, bf16[1,512,256]{2,1,0:T(8,128)(2,1)S(1)}) custom-call(bf16[512,4096]{1,0:T(8,128)(2,1)} %enc_ref.1, bf16[2,4096,256]{2,1,0:T(8,128)(2,1)} %bitcast.37, bf16[2,4096,256]{2,1,0:T(8,128)(2,1)} %bitcast.41), custom_call_target="tpu_custom_call" | custom-call | flops 2147483648 | bytes 8388608 | tf_op jit(solution)/shard_map/pallas_call | solution.py:123
  26.1 3.4 %collective-permute-done.6.refs_2_.refs_6_ = bf16[2,512,256]{2,1,0:T(8,128)(2,1)S(1)} collective-permute-done((bf16[2,512,256]{2,1,0:T(8,128)(2,1)S(1)}, bf16[2,512,256]{2,1,0:T(8,128)(2,1)S(1)}, u32[]{:S(2)}, u32[]{:S(2)}) %collective-permute-start.6) | collective-permute-done | bytes 524320 | tf_op jit(solution)/shard_map/ppermute | solution.py:337
  29.5 2.3 %collective-permute-start.7 = (bf16[2,512,256]{2,1,0:T(8,128)(2,1)S(1)}, bf16[2,512,256]{2,1,0:T(8,128)(2,1)S(1)}, u32[]{:S(2)}, u32[]{:S(2)}) collective-permute-start(bf16[2,512,256]{2,1,0:T(8,128)(2,1)S(1)} %collective-permute-done.6.refs_2_.refs_6_), channel_id=1, source_target_pairs={{0,8},{8,0},{16,24},{24,16},{1,9},{9,1},{17,25},{25,17},{2,10},{10... | collective-permute-start | bytes 1572872 | tf_op jit(solution)/shard_map/ppermute | solution.py:393
  31.9 1.1 collective-permute-done.2.refs_3_.refs_7_
  32.9 2.1 %shard_map.72.refs_8_ = f32[4,2048]{1,0:T(4,128)S(1)} custom-call(s32[3]{0:T(128)S(1)} %pad_add_fusion.place_ref, bf16[1,512,256]{2,1,0:T(8,128)(2,1)S(1)} %get-tuple-element.50.k_ref, bf16[1,512,256]{2,1,0:T(8,128)(2,1)S(1)} %get-tuple-element.51.v_ref, bf16[4,2,512,256]{3,2,1,0:T(8,128)(2,1)S(1)} %bitcast.25, ...), custom_call_target="tpu_custom_call" | custom-call | flops 1073741824 | bytes 2621440 | tf_op jit(solution)/shard_map/pallas_call | solution.py:175
  35.1 3.8 %collective-permute-start.5 = (f32[4,2048]{1,0:T(4,128)S(1)}, f32[4,2048]{1,0:T(4,128)S(1)}, u32[]{:S(2)}, u32[]{:S(2)}) collective-permute-start(f32[4,2048]{1,0:T(4,128)S(1)} %shard_map.72.refs_8_), channel_id=1, source_target_pairs={{0,24},{8,0},{16,8},{24,16},{1,25},{9,1},{17,9},{25,17},{2,26},{10... | collective-permute-start | bytes 98312 | tf_op jit(solution)/shard_map/ppermute | solution.py:342
  38.9 0.8 collective-permute-start.3
  39.8 5.5 %collective-permute-done.7.refs_3_.refs_7_ = bf16[2,512,256]{2,1,0:T(8,128)(2,1)S(1)} collective-permute-done((bf16[2,512,256]{2,1,0:T(8,128)(2,1)S(1)}, bf16[2,512,256]{2,1,0:T(8,128)(2,1)S(1)}, u32[]{:S(2)}, u32[]{:S(2)}) %collective-permute-start.7) | collective-permute-done | bytes 524320 | tf_op jit(solution)/shard_map/ppermute | solution.py:393
  45.2 2.1 %shard_map.75.refs_8_ = f32[4,2048]{1,0:T(4,128)S(1)} custom-call(s32[3]{0:T(128)S(1)} %pad_add_fusion.place_ref, bf16[1,512,256]{2,1,0:T(8,128)(2,1)S(1)} %get-tuple-element.59.k_ref, bf16[1,512,256]{2,1,0:T(8,128)(2,1)S(1)} %get-tuple-element.60.v_ref, bf16[4,2,512,256]{3,2,1,0:T(8,128)(2,1)S(1)} %bitcast.26, ...), custom_call_target="tpu_custom_call" | custom-call | flops 1073741824 | bytes 2621440 | tf_op jit(solution)/shard_map/pallas_call | solution.py:175
  47.4 4.5 %collective-permute-start.10 = (f32[4,2048]{1,0:T(4,128)S(1)}, f32[4,2048]{1,0:T(4,128)S(1)}, u32[]{:S(2)}, u32[]{:S(2)}) collective-permute-start(f32[4,2048]{1,0:T(4,128)S(1)} %shard_map.75.refs_8_), channel_id=1, source_target_pairs={{0,24},{8,0},{16,8},{24,16},{1,25},{9,1},{17,9},{25,17},{2,26},{10... | collective-permute-start | bytes 98312 | tf_op jit(solution)/shard_map/ppermute | solution.py:342
  51.9 0.6 collective-permute-start.8
  52.6 4.1 %shard_map.73 = (bf16[4,256,256]{2,1,0:T(8,128)(2,1)S(1)}, bf16[4,256,256]{2,1,0:T(8,128)(2,1)S(1)}, bf16[512,256]{1,0:T(8,128)(2,1)S(1)}, bf16[512,256]{1,0:T(8,128)(2,1)S(1)}) custom-call(s32[3]{0:T(128)S(1)} %pad_add_fusion.place_ref, bf16[1,512,256]{2,1,0:T(8,128)(2,1)S(1)} %get-tuple-element.50.k_ref, bf16[1,512,256]{2,1,0:T(8,128)(2,1)S(1)} %get-tuple-element.51.v_ref, ...), custom_call_target="tpu_custom_call" | custom-call | flops 2684354560 | bytes 3932160 | tf_op jit(solution)/shard_map/pallas_call | solution.py:229
  56.6 0.1 collective-permute-done.9.refs_10_
  56.7 0.9 collective-permute-done.8.refs_9_
  57.6 2.0 %collective-permute-start.11 = (bf16[4,256,256]{2,1,0:T(8,128)(2,1)S(1)}, bf16[4,256,256]{2,1,0:T(8,128)(2,1)S(1)}, u32[]{:S(2)}, u32[]{:S(2)}) collective-permute-start(bf16[4,256,256]{2,1,0:T(8,128)(2,1)S(1)} %get-tuple-element.71), channel_id=1, source_target_pairs={{0,8},{8,0},{16,24},{24,16},{1,9},{9,1},{17,25},{25,17},{2,10},{10... | collective-permute-start | bytes 1572872 | tf_op jit(solution)/shard_map/ppermute | solution.py:420
  59.6 4.1 %shard_map.76 = (bf16[4,256,256]{2,1,0:T(8,128)(2,1)S(1)}, bf16[4,256,256]{2,1,0:T(8,128)(2,1)S(1)}, bf16[512,256]{1,0:T(8,128)(2,1)S(1)}, bf16[512,256]{1,0:T(8,128)(2,1)S(1)}) custom-call(s32[3]{0:T(128)S(1)} %pad_add_fusion.place_ref, bf16[1,512,256]{2,1,0:T(8,128)(2,1)S(1)} %get-tuple-element.59.k_ref, bf16[1,512,256]{2,1,0:T(8,128)(2,1)S(1)} %get-tuple-element.60.v_ref, ...), custom_call_target="tpu_custom_call" | custom-call | flops 2684354560 | bytes 3932160 | tf_op jit(solution)/shard_map/pallas_call | solution.py:229
  63.7 5.6 %shard_map.77 = bf16[4,512,512]{2,1,0:T(8,128)(2,1)S(1)} custom-call(s32[4]{0:T(128)S(1)} %get-tuple-element.66.order_ref, bf16[2,4096,256]{2,1,0:T(8,128)(2,1)} %bitcast.38, bf16[2,4096,256]{2,1,0:T(8,128)(2,1)} %bitcast.42, bf16[512,256]{1,0:T(8,128)(2,1)S(1)} %get-tuple-element.55.refs_0_, bf16[512,256]{1,0:T(8,128)(2,1)S(1)} %get-tuple-element.56.refs_1_, ...), custom_call_target="tpu_custom_call" | custom-call | flops 2147483648 | bytes 8388608 | tf_op jit(solution)/shard_map/pallas_call | solution.py:260
  69.3 0.2 collective-permute-done.11.two_ref
  69.5 0.1 shard_map.78.one_ref
  69.7 1.8 %collective-permute-start.12 = (bf16[4,256,256]{2,1,0:T(8,128)(2,1)S(1)}, bf16[4,256,256]{2,1,0:T(8,128)(2,1)S(1)}, u32[]{:S(2)}, u32[]{:S(2)}) collective-permute-start(bf16[4,256,256]{2,1,0:T(8,128)(2,1)S(1)} %get-tuple-element.72), channel_id=1, source_target_pairs={{0,8},{8,0},{16,24},{24,16},{1,9},{9,1},{17,25},{25,17},{2,10},{10... | collective-permute-start | bytes 1572872 | tf_op jit(solution)/shard_map/ppermute | solution.py:420
  71.5 1.2 collective-permute-start.17
  72.7 5.3 %shard_map.80.refs_0_ = f32[4,512,512]{2,1,0:T(8,128)S(1)} custom-call(s32[4]{0:T(128)S(1)} %get-tuple-element.74.order_ref, bf16[2,4096,256]{2,1,0:T(8,128)(2,1)} %bitcast.39, bf16[2,4096,256]{2,1,0:T(8,128)(2,1)} %bitcast.43, bf16[512,256]{1,0:T(8,128)(2,1)S(1)} %get-tuple-element.55.refs_0_, bf16[512,256]{1,0:T(8,128)(2,1)S(1)} %get-tuple-element.56.refs_1_, ...), custom_call_target="tpu_custom_call" | custom-call | flops 2147483648 | bytes 8388608 | tf_op jit(solution)/shard_map/pallas_call | solution.py:260
  78.1 0.1 shard_map.81
  78.2 1.5 collective-permute-start.14
  79.6 4.4 %collective-permute-done.12.two_ref = bf16[4,256,256]{2,1,0:T(8,128)(2,1)S(1)} collective-permute-done((bf16[4,256,256]{2,1,0:T(8,128)(2,1)S(1)}, bf16[4,256,256]{2,1,0:T(8,128)(2,1)S(1)}, u32[]{:S(2)}, u32[]{:S(2)}) %collective-permute-start.12) | collective-permute-done | bytes 524320 | tf_op jit(solution)/shard_map/ppermute | solution.py:420
  84.0 0.1 shard_map.79.one_ref
  84.2 0.1 shard_map.83
  84.3 1.5 collective-permute-start.16
  85.7 10.6 %collective-permute-done.17.two_ref = bf16[4,256,256]{2,1,0:T(8,128)(2,1)S(1)} collective-permute-done((bf16[4,256,256]{2,1,0:T(8,128)(2,1)S(1)}, bf16[4,256,256]{2,1,0:T(8,128)(2,1)S(1)}, u32[]{:S(2)}, u32[]{:S(2)}) %collective-permute-start.17) | collective-permute-done | bytes 524320 | tf_op jit(solution)/shard_map/ppermute | solution.py:433
  96.3 0.1 shard_map.84
  96.4 0.2 shard_map.82
  96.6 1.6 %collective-permute-start.15 = (bf16[1,512,512]{2,1,0:T(8,128)(2,1)S(1)}, bf16[1,512,512]{2,1,0:T(8,128)(2,1)S(1)}, u32[]{:S(2)}, u32[]{:S(2)}) collective-permute-start(bf16[1,512,512]{2,1,0:T(8,128)(2,1)S(1)} %shard_map.82), channel_id=1, source_target_pairs={{0,1},{1,0},{2,3},{3,2},{4,5},{5,4},{6,7},{7,6},{8,9},{9,8},{10,11... | collective-permute-start | bytes 1572872 | tf_op jit(solution)/shard_map/ppermute | solution.py:461
  98.2 2.6 %collective-permute-start.21 = (bf16[4,256,256]{2,1,0:T(8,128)(2,1)S(1)}, bf16[4,256,256]{2,1,0:T(8,128)(2,1)S(1)}, u32[]{:S(2)}, u32[]{:S(2)}) collective-permute-start(bf16[4,256,256]{2,1,0:T(8,128)(2,1)S(1)} %shard_map.79.one_ref), channel_id=1, source_target_pairs={{0,24},{24,0},{8,16},{16,8},{1,25},{25,1},{9,17},{17,9},{2,26},{26... | collective-permute-start | bytes 1572872 | tf_op jit(solution)/shard_map/ppermute | solution.py:433
  100.8 1.4 collective-permute-start.19
  102.2 1.1 collective-permute-start.20
  103.3 3.8 %collective-permute-done.19.refs_2_ = bf16[256,256]{1,0:T(8,128)(2,1)S(1)} collective-permute-done((bf16[256,256]{1,0:T(8,128)(2,1)S(1)}, bf16[256,256]{1,0:T(8,128)(2,1)S(1)}, u32[]{:S(2)}, u32[]{:S(2)}) %collective-permute-start.19) | collective-permute-done | bytes 131104 | tf_op jit(solution)/shard_map/ppermute | solution.py:353
  107.1 2.0 %collective-permute-done.20.refs_3_ = bf16[256,256]{1,0:T(8,128)(2,1)S(1)} collective-permute-done((bf16[256,256]{1,0:T(8,128)(2,1)S(1)}, bf16[256,256]{1,0:T(8,128)(2,1)S(1)}, u32[]{:S(2)}, u32[]{:S(2)}) %collective-permute-start.20) | collective-permute-done | bytes 131104 | tf_op jit(solution)/shard_map/ppermute | solution.py:353
  109.2 0.9 collective-permute-done.15.refs_3_
  110.1 3.1 %collective-permute-done.21.two_ref = bf16[4,256,256]{2,1,0:T(8,128)(2,1)S(1)} collective-permute-done((bf16[4,256,256]{2,1,0:T(8,128)(2,1)S(1)}, bf16[4,256,256]{2,1,0:T(8,128)(2,1)S(1)}, u32[]{:S(2)}, u32[]{:S(2)}) %collective-permute-start.21) | collective-permute-done | bytes 524320 | tf_op jit(solution)/shard_map/ppermute | solution.py:433
  113.2 0.1 shard_map.86
  113.4 1.5 collective-permute-start.23
  114.9 0.4 collective-permute-start.24
  115.3 6.3 %collective-permute-start.26 = (bf16[4,256,256]{2,1,0:T(8,128)(2,1)S(1)}, bf16[4,256,256]{2,1,0:T(8,128)(2,1)S(1)}, u32[]{:S(2)}, u32[]{:S(2)}) collective-permute-start(bf16[4,256,256]{2,1,0:T(8,128)(2,1)S(1)} %shard_map.85.part_ref), channel_id=1, source_target_pairs={{0,8},{8,0},{16,24},{24,16},{1,9},{9,1},{17,25},{25,17},{2,10},{10... | collective-permute-start | bytes 1572872 | tf_op jit(solution)/shard_map/ppermute | solution.py:436
  121.6 0.1 collective-permute-done.24.refs_3_
  121.7 6.3 %collective-permute-start.25 = (bf16[4,256,256]{2,1,0:T(8,128)(2,1)S(1)}, bf16[4,256,256]{2,1,0:T(8,128)(2,1)S(1)}, u32[]{:S(2)}, u32[]{:S(2)}) collective-permute-start(bf16[4,256,256]{2,1,0:T(8,128)(2,1)S(1)} %shard_map.87.part_ref), channel_id=1, source_target_pairs={{0,8},{8,0},{16,24},{24,16},{1,9},{9,1},{17,25},{25,17},{2,10},{10... | collective-permute-start | bytes 1572872 | tf_op jit(solution)/shard_map/ppermute | solution.py:436
  128.1 2.4 %shard_map.88.rest_0_ = bf16[2,512,4,256]{3,2,1,0:T(4,128)(2,1)} custom-call(s32[3]{0:T(128)S(1)} %pad_add_fusion.place_ref, bf16[4,256,256]{2,1,0:T(8,128)(2,1)S(1)} %shard_map.85.part_ref), custom_call_target="tpu_custom_call" | custom-call | bytes 1048576 | tf_op jit(solution)/shard_map/pallas_call | solution.py:86
  130.5 3.8 %collective-permute-done.26.part_ref = bf16[4,256,256]{2,1,0:T(8,128)(2,1)S(1)} collective-permute-done((bf16[4,256,256]{2,1,0:T(8,128)(2,1)S(1)}, bf16[4,256,256]{2,1,0:T(8,128)(2,1)S(1)}, u32[]{:S(2)}, u32[]{:S(2)}) %collective-permute-start.26) | collective-permute-done | bytes 524320 | tf_op jit(solution)/shard_map/ppermute | solution.py:436
  134.3 2.4 %shard_map.89.rest_0_ = bf16[2,512,4,256]{3,2,1,0:T(4,128)(2,1)} custom-call(s32[3]{0:T(128)S(1)} %pad_add_fusion.place_ref, bf16[4,256,256]{2,1,0:T(8,128)(2,1)S(1)} %collective-permute-done.26.part_ref, bf16[2,512,4,256]{3,2,1,0:T(4,128)(2,1)} %shard_map.88.rest_0_), custom_call_target="tpu_custom_call", output_to_operand_aliasing={{}: (2, {})} | custom-call | bytes 1048576 | tf_op jit(solution)/shard_map/pallas_call | solution.py:86
  136.8 1.0 shard_map.92
  137.8 2.4 %shard_map.90.rest_0_ = bf16[2,512,4,256]{3,2,1,0:T(4,128)(2,1)} custom-call(s32[3]{0:T(128)S(1)} %pad_add_fusion.place_ref, bf16[4,256,256]{2,1,0:T(8,128)(2,1)S(1)} %shard_map.87.part_ref, bf16[2,512,4,256]{3,2,1,0:T(4,128)(2,1)} %shard_map.89.rest_0_), custom_call_target="tpu_custom_call", output_to_operand_aliasing={{}: (2, {})} | custom-call | bytes 1048576 | tf_op jit(solution)/shard_map/pallas_call | solution.py:86
  140.2 5.0 %collective-permute-done.25.part_ref = bf16[4,256,256]{2,1,0:T(8,128)(2,1)S(1)} collective-permute-done((bf16[4,256,256]{2,1,0:T(8,128)(2,1)S(1)}, bf16[4,256,256]{2,1,0:T(8,128)(2,1)S(1)}, u32[]{:S(2)}, u32[]{:S(2)}) %collective-permute-start.25) | collective-permute-done | bytes 524320 | tf_op jit(solution)/shard_map/ppermute | solution.py:436
  145.2 2.4 %shard_map.91 = bf16[2,512,4,256]{3,2,1,0:T(4,128)(2,1)} custom-call(s32[3]{0:T(128)S(1)} %pad_add_fusion.place_ref, bf16[4,256,256]{2,1,0:T(8,128)(2,1)S(1)} %collective-permute-done.25.part_ref, bf16[2,512,4,256]{3,2,1,0:T(4,128)(2,1)} %shard_map.90.rest_0_), custom_call_target="tpu_custom_call", output_to_operand_aliasing={{}: (2, {})} | custom-call | bytes 1048576 | tf_op jit(solution)/shard_map/pallas_call | solution.py:86
  (21 shorter events, 0.3 us)
Async XLA Ops:
  0.8 2.2 %copy-start = (bf16[2,512,4,256]{3,2,1,0:T(4,128)(2,1)S(1)}, bf16[2,512,4,256]{3,2,1,0:T(4,128)(2,1)}, u32[]{:S(2)}) copy-start(bf16[2,512,4,256]{3,2,1,0:T(4,128)(2,1)} %param.9) | copy-start | bytes 6291460
  3.4 15.8 %collective-permute-start.1 = (bf16[2,512,256]{2,1,0:T(8,128)(2,1)S(1)}, bf16[2,512,256]{2,1,0:T(8,128)(2,1)S(1)}, u32[]{:S(2)}, u32[]{:S(2)}) collective-permute-start(bf16[2,512,256]{2,1,0:T(8,128)(2,1)S(1)} %shard_map.68), channel_id=1, source_target_pairs={{0,4},{2,6},{4,0},{6,2},{8,14},{10,12},{12,10},{14,8},{16,20},{18,... | collective-permute-start | bytes 1572872 | tf_op jit(solution)/shard_map/ppermute | solution.py:337
  12.0 20.9 %collective-permute-start = (bf16[4,512,256]{2,1,0:T(8,128)(2,1)S(1)}, bf16[4,512,256]{2,1,0:T(8,128)(2,1)S(1)}, u32[]{:S(2)}, u32[]{:S(2)}) collective-permute-start(bf16[4,512,256]{2,1,0:T(8,128)(2,1)S(1)} %shard_map.71), channel_id=1, source_target_pairs={{0,2},{2,0},{4,6},{6,4},{1,3},{3,1},{5,7},{7,5},{8,10},{10,8},{12,... | collective-permute-start | bytes 3145736 | tf_op jit(solution)/shard_map/ppermute | solution.py:391
  12.1 17.4 %collective-permute-start.6 = (bf16[2,512,256]{2,1,0:T(8,128)(2,1)S(1)}, bf16[2,512,256]{2,1,0:T(8,128)(2,1)S(1)}, u32[]{:S(2)}, u32[]{:S(2)}) collective-permute-start(bf16[2,512,256]{2,1,0:T(8,128)(2,1)S(1)} %shard_map.69), channel_id=1, source_target_pairs={{0,4},{2,6},{4,0},{6,2},{8,14},{10,12},{12,10},{14,8},{16,20},{18,... | collective-permute-start | bytes 1572872 | tf_op jit(solution)/shard_map/ppermute | solution.py:337
  19.1 13.8 %collective-permute-start.2 = (bf16[2,512,256]{2,1,0:T(8,128)(2,1)S(1)}, bf16[2,512,256]{2,1,0:T(8,128)(2,1)S(1)}, u32[]{:S(2)}, u32[]{:S(2)}) collective-permute-start(bf16[2,512,256]{2,1,0:T(8,128)(2,1)S(1)} %collective-permute-done.1.refs_2_.refs_6_), channel_id=1, source_target_pairs={{0,8},{8,0},{16,24},{24,16},{1,9},{9,1},{17,25},{25,17},{2,10},{10... | collective-permute-start | bytes 1572872 | tf_op jit(solution)/shard_map/ppermute | solution.py:393
  29.5 15.7 %collective-permute-start.7 = (bf16[2,512,256]{2,1,0:T(8,128)(2,1)S(1)}, bf16[2,512,256]{2,1,0:T(8,128)(2,1)S(1)}, u32[]{:S(2)}, u32[]{:S(2)}) collective-permute-start(bf16[2,512,256]{2,1,0:T(8,128)(2,1)S(1)} %collective-permute-done.6.refs_2_.refs_6_), channel_id=1, source_target_pairs={{0,8},{8,0},{16,24},{24,16},{1,9},{9,1},{17,25},{25,17},{2,10},{10... | collective-permute-start | bytes 1572872 | tf_op jit(solution)/shard_map/ppermute | solution.py:393
  35.1 16.8 %collective-permute-start.5 = (f32[4,2048]{1,0:T(4,128)S(1)}, f32[4,2048]{1,0:T(4,128)S(1)}, u32[]{:S(2)}, u32[]{:S(2)}) collective-permute-start(f32[4,2048]{1,0:T(4,128)S(1)} %shard_map.72.refs_8_), channel_id=1, source_target_pairs={{0,24},{8,0},{16,8},{24,16},{1,25},{9,1},{17,9},{25,17},{2,26},{10... | collective-permute-start | bytes 98312 | tf_op jit(solution)/shard_map/ppermute | solution.py:342
  38.9 13.6 %collective-permute-start.4 = (f32[4,2048]{1,0:T(4,128)S(1)}, f32[4,2048]{1,0:T(4,128)S(1)}, u32[]{:S(2)}, u32[]{:S(2)}) collective-permute-start(f32[4,2048]{1,0:T(4,128)S(1)} %shard_map.72.refs_8_), channel_id=1, source_target_pairs={{0,16},{8,24},{16,0},{24,8},{1,17},{9,25},{17,1},{25,9},{2,18},{10... | collective-permute-start | bytes 98312 | tf_op jit(solution)/shard_map/ppermute | solution.py:342
  38.9 13.6 %collective-permute-start.3 = (f32[4,2048]{1,0:T(4,128)S(1)}, f32[4,2048]{1,0:T(4,128)S(1)}, u32[]{:S(2)}, u32[]{:S(2)}) collective-permute-start(f32[4,2048]{1,0:T(4,128)S(1)} %shard_map.72.refs_8_), channel_id=1, source_target_pairs={{0,8},{8,16},{16,24},{24,0},{1,9},{9,17},{17,25},{25,1},{2,10},{10... | collective-permute-start | bytes 98312 | tf_op jit(solution)/shard_map/ppermute | solution.py:342
  47.4 9.3 %collective-permute-start.10 = (f32[4,2048]{1,0:T(4,128)S(1)}, f32[4,2048]{1,0:T(4,128)S(1)}, u32[]{:S(2)}, u32[]{:S(2)}) collective-permute-start(f32[4,2048]{1,0:T(4,128)S(1)} %shard_map.75.refs_8_), channel_id=1, source_target_pairs={{0,24},{8,0},{16,8},{24,16},{1,25},{9,1},{17,9},{25,17},{2,26},{10... | collective-permute-start | bytes 98312 | tf_op jit(solution)/shard_map/ppermute | solution.py:342
  51.9 4.8 %collective-permute-start.9 = (f32[4,2048]{1,0:T(4,128)S(1)}, f32[4,2048]{1,0:T(4,128)S(1)}, u32[]{:S(2)}, u32[]{:S(2)}) collective-permute-start(f32[4,2048]{1,0:T(4,128)S(1)} %shard_map.75.refs_8_), channel_id=1, source_target_pairs={{0,16},{8,24},{16,0},{24,8},{1,17},{9,25},{17,1},{25,9},{2,18},{10... | collective-permute-start | bytes 98312 | tf_op jit(solution)/shard_map/ppermute | solution.py:342
  51.9 5.7 %collective-permute-start.8 = (f32[4,2048]{1,0:T(4,128)S(1)}, f32[4,2048]{1,0:T(4,128)S(1)}, u32[]{:S(2)}, u32[]{:S(2)}) collective-permute-start(f32[4,2048]{1,0:T(4,128)S(1)} %shard_map.75.refs_8_), channel_id=1, source_target_pairs={{0,8},{8,16},{16,24},{24,0},{1,9},{9,17},{17,25},{25,1},{2,10},{10... | collective-permute-start | bytes 98312 | tf_op jit(solution)/shard_map/ppermute | solution.py:342
  57.6 11.9 %collective-permute-start.11 = (bf16[4,256,256]{2,1,0:T(8,128)(2,1)S(1)}, bf16[4,256,256]{2,1,0:T(8,128)(2,1)S(1)}, u32[]{:S(2)}, u32[]{:S(2)}) collective-permute-start(bf16[4,256,256]{2,1,0:T(8,128)(2,1)S(1)} %get-tuple-element.71), channel_id=1, source_target_pairs={{0,8},{8,0},{16,24},{24,16},{1,9},{9,1},{17,25},{25,17},{2,10},{10... | collective-permute-start | bytes 1572872 | tf_op jit(solution)/shard_map/ppermute | solution.py:420
  69.6 8.4 %collective-permute-start.13 = (bf16[4,512,512]{2,1,0:T(8,128)(2,1)S(1)}, bf16[4,512,512]{2,1,0:T(8,128)(2,1)S(1)}, u32[]{:S(2)}, u32[]{:S(2)}) collective-permute-start(bf16[4,512,512]{2,1,0:T(8,128)(2,1)S(1)} %shard_map.77), channel_id=1, source_target_pairs={{0,2},{2,0},{4,6},{6,4},{1,3},{3,1},{5,7},{7,5},{8,10},{10,8},{12,... | collective-permute-start | bytes 6291464 | tf_op jit(solution)/shard_map/ppermute | solution.py:452
  69.7 14.3 %collective-permute-start.12 = (bf16[4,256,256]{2,1,0:T(8,128)(2,1)S(1)}, bf16[4,256,256]{2,1,0:T(8,128)(2,1)S(1)}, u32[]{:S(2)}, u32[]{:S(2)}) collective-permute-start(bf16[4,256,256]{2,1,0:T(8,128)(2,1)S(1)} %get-tuple-element.72), channel_id=1, source_target_pairs={{0,8},{8,0},{16,24},{24,16},{1,9},{9,1},{17,25},{25,17},{2,10},{10... | collective-permute-start | bytes 1572872 | tf_op jit(solution)/shard_map/ppermute | solution.py:420
  71.5 24.8 %collective-permute-start.17 = (bf16[4,256,256]{2,1,0:T(8,128)(2,1)S(1)}, bf16[4,256,256]{2,1,0:T(8,128)(2,1)S(1)}, u32[]{:S(2)}, u32[]{:S(2)}) collective-permute-start(bf16[4,256,256]{2,1,0:T(8,128)(2,1)S(1)} %shard_map.78.one_ref), channel_id=1, source_target_pairs={{0,24},{24,0},{8,16},{16,8},{1,25},{25,1},{9,17},{17,9},{2,26},{26... | collective-permute-start | bytes 1572872 | tf_op jit(solution)/shard_map/ppermute | solution.py:433
  78.2 18.3 %collective-permute-start.14 = (bf16[1,512,512]{2,1,0:T(8,128)(2,1)S(1)}, bf16[1,512,512]{2,1,0:T(8,128)(2,1)S(1)}, u32[]{:S(2)}, u32[]{:S(2)}) collective-permute-start(bf16[1,512,512]{2,1,0:T(8,128)(2,1)S(1)} %shard_map.81), channel_id=1, source_target_pairs={{0,4},{2,6},{4,0},{6,2},{1,5},{3,7},{5,1},{7,3},{8,12},{10,14},{12... | collective-permute-start | bytes 1572872 | tf_op jit(solution)/shard_map/ppermute | solution.py:457
  84.3 24.9 %collective-permute-start.16 = (bf16[1,512,512]{2,1,0:T(8,128)(2,1)S(1)}, bf16[1,512,512]{2,1,0:T(8,128)(2,1)S(1)}, u32[]{:S(2)}, u32[]{:S(2)}) collective-permute-start(bf16[1,512,512]{2,1,0:T(8,128)(2,1)S(1)} %shard_map.83), channel_id=1, source_target_pairs={{0,4},{2,6},{4,0},{6,2},{1,5},{3,7},{5,1},{7,3},{8,12},{10,14},{12... | collective-permute-start | bytes 1572872 | tf_op jit(solution)/shard_map/ppermute | solution.py:458
  96.6 13.5 %collective-permute-start.15 = (bf16[1,512,512]{2,1,0:T(8,128)(2,1)S(1)}, bf16[1,512,512]{2,1,0:T(8,128)(2,1)S(1)}, u32[]{:S(2)}, u32[]{:S(2)}) collective-permute-start(bf16[1,512,512]{2,1,0:T(8,128)(2,1)S(1)} %shard_map.82), channel_id=1, source_target_pairs={{0,1},{1,0},{2,3},{3,2},{4,5},{5,4},{6,7},{7,6},{8,9},{9,8},{10,11... | collective-permute-start | bytes 1572872 | tf_op jit(solution)/shard_map/ppermute | solution.py:461
  98.2 15.1 %collective-permute-start.21 = (bf16[4,256,256]{2,1,0:T(8,128)(2,1)S(1)}, bf16[4,256,256]{2,1,0:T(8,128)(2,1)S(1)}, u32[]{:S(2)}, u32[]{:S(2)}) collective-permute-start(bf16[4,256,256]{2,1,0:T(8,128)(2,1)S(1)} %shard_map.79.one_ref), channel_id=1, source_target_pairs={{0,24},{24,0},{8,16},{16,8},{1,25},{25,1},{9,17},{17,9},{2,26},{26... | collective-permute-start | bytes 1572872 | tf_op jit(solution)/shard_map/ppermute | solution.py:433
  100.8 1.4 collective-permute-start.18
  100.8 6.3 %collective-permute-start.19 = (bf16[256,256]{1,0:T(8,128)(2,1)S(1)}, bf16[256,256]{1,0:T(8,128)(2,1)S(1)}, u32[]{:S(2)}, u32[]{:S(2)}) collective-permute-start(bf16[256,256]{1,0:T(8,128)(2,1)S(1)} %get-tuple-element.80), channel_id=1, source_target_pairs={{0,4},{2,6},{4,0},{6,2},{1,5},{3,7},{5,1},{7,3},{8,12},{10,14},{12... | collective-permute-start | bytes 393224 | tf_op jit(solution)/shard_map/ppermute | solution.py:353
  102.2 6.9 %collective-permute-start.20 = (bf16[256,256]{1,0:T(8,128)(2,1)S(1)}, bf16[256,256]{1,0:T(8,128)(2,1)S(1)}, u32[]{:S(2)}, u32[]{:S(2)}) collective-permute-start(bf16[256,256]{1,0:T(8,128)(2,1)S(1)} %get-tuple-element.81), channel_id=1, source_target_pairs={{0,6},{2,4},{4,2},{6,0},{1,7},{3,5},{5,3},{7,1},{8,14},{10,12},{12... | collective-permute-start | bytes 393224 | tf_op jit(solution)/shard_map/ppermute | solution.py:353
  113.4 8.2 %collective-permute-start.22 = (bf16[256,256]{1,0:T(8,128)(2,1)S(1)}, bf16[256,256]{1,0:T(8,128)(2,1)S(1)}, u32[]{:S(2)}, u32[]{:S(2)}) collective-permute-start(bf16[256,256]{1,0:T(8,128)(2,1)S(1)} %get-tuple-element.85), channel_id=1, source_target_pairs={{0,2},{2,0},{4,6},{6,4},{1,3},{3,1},{5,7},{7,5},{8,10},{10,8},{12,... | collective-permute-start | bytes 393224 | tf_op jit(solution)/shard_map/ppermute | solution.py:353
  113.4 8.1 %collective-permute-start.23 = (bf16[256,256]{1,0:T(8,128)(2,1)S(1)}, bf16[256,256]{1,0:T(8,128)(2,1)S(1)}, u32[]{:S(2)}, u32[]{:S(2)}) collective-permute-start(bf16[256,256]{1,0:T(8,128)(2,1)S(1)} %get-tuple-element.86), channel_id=1, source_target_pairs={{0,4},{2,6},{4,0},{6,2},{1,5},{3,7},{5,1},{7,3},{8,12},{10,14},{12... | collective-permute-start | bytes 393224 | tf_op jit(solution)/shard_map/ppermute | solution.py:353
  114.9 6.8 %collective-permute-start.24 = (bf16[256,256]{1,0:T(8,128)(2,1)S(1)}, bf16[256,256]{1,0:T(8,128)(2,1)S(1)}, u32[]{:S(2)}, u32[]{:S(2)}) collective-permute-start(bf16[256,256]{1,0:T(8,128)(2,1)S(1)} %get-tuple-element.87), channel_id=1, source_target_pairs={{0,6},{2,4},{4,2},{6,0},{1,7},{3,5},{5,3},{7,1},{8,14},{10,12},{12... | collective-permute-start | bytes 393224 | tf_op jit(solution)/shard_map/ppermute | solution.py:353
  115.3 19.0 %collective-permute-start.26 = (bf16[4,256,256]{2,1,0:T(8,128)(2,1)S(1)}, bf16[4,256,256]{2,1,0:T(8,128)(2,1)S(1)}, u32[]{:S(2)}, u32[]{:S(2)}) collective-permute-start(bf16[4,256,256]{2,1,0:T(8,128)(2,1)S(1)} %shard_map.85.part_ref), channel_id=1, source_target_pairs={{0,8},{8,0},{16,24},{24,16},{1,9},{9,1},{17,25},{25,17},{2,10},{10... | collective-permute-start | bytes 1572872 | tf_op jit(solution)/shard_map/ppermute | solution.py:436
  121.7 23.5 %collective-permute-start.25 = (bf16[4,256,256]{2,1,0:T(8,128)(2,1)S(1)}, bf16[4,256,256]{2,1,0:T(8,128)(2,1)S(1)}, u32[]{:S(2)}, u32[]{:S(2)}) collective-permute-start(bf16[4,256,256]{2,1,0:T(8,128)(2,1)S(1)} %shard_map.87.part_ref), channel_id=1, source_target_pairs={{0,8},{8,0},{16,24},{24,16},{1,9},{9,1},{17,25},{25,17},{2,10},{10... | collective-permute-start | bytes 1572872 | tf_op jit(solution)/shard_map/ppermute | solution.py:436

commit v5 on v4

--- a/solution.py
+++ b/solution.py
@@ -339,8 +339,7 @@
 
 def everywhere(value, n_inp):
     return [value] + [
-        lax.ppermute(value, "inp", [(i, (i + shift) % n_inp) for i in range(n_inp)])
-        for shift in range(1, n_inp)
+        lax.ppermute(value, "inp", partners(n_inp, mask)) for mask in range(1, n_inp)
     ]
 
 
@@ -366,21 +365,25 @@
     odd = (z % 2).astype(jnp.int32)
     upper = ((z == 0) | (z == n_inp - 1)).astype(jnp.int32) if line else jnp.ones_like(odd)
     place = jnp.stack([t.astype(jnp.int32), odd, upper])
-    wanted_head, beside_head = (t ^ (2 + odd))[None], (t ^ 1)[None]
+    plain = jnp.stack([t.astype(jnp.int32), jnp.zeros_like(odd), upper])
+    wanted_head, beside_head, heads_along = (t ^ (2 + odd))[None], (t ^ 1)[None], [(t ^ 2)[None], (t ^ 3)[None]]
     orders = [
         jnp.stack([(t ^ mask) * n_mdl + (m ^ side) for mask in masks for side in range(n_mdl)]).astype(jnp.int32)
         for masks in ((3, 1), (2, 0))
     ]
-    queries, place, wanted_head, beside_head, *orders = lax.optimization_barrier(
-        (queries, place, wanted_head, beside_head, *orders)
+    queries, place, plain, wanted_head, beside_head, heads_along, *orders = lax.optimization_barrier(
+        (queries, place, plain, wanted_head, beside_head, heads_along, *orders)
     )
+    places = [place] + [plain] * (layers - 1)
 
     own = [jnp.transpose(array, (2, 0, 1, 3)) for array in (queries, grad_out)]
-    wanted = []
-    for layer in range(layers):
-        first = after(wanted_head, *wanted)
-        wanted += pick(first, [(source, layer, 1) for source in own], together=True)
-    fetched = [exchange(piece, n_inp, n_tgt, lambda z: 2 + z % 2) for piece in wanted]
+    wanted = pick(wanted_head, [(source, 0, 1) for source in own], together=True)
+    fetched = [exchange(wanted[0], n_inp, n_tgt, lambda z: 2 + z % 2)]
+    for layer in range(1, layers):
+        fetched.append([])
+        for mask, head in zip((2, 3), heads_along):
+            wanted += pick(after(head, *wanted), [(source, layer, 1) for source in own], together=True)
+            fetched[layer].append(lax.ppermute(wanted[-1], "tgt", partners(n_tgt, mask)))
     keys, values, begun = [], [], wanted
     for layer in range(layers):
         key_block, value_block = project(after(encoder, *begun), wk, wv, layer)
@@ -389,9 +392,8 @@
         values.append(value_block)
     (beside,) = pick(after(beside_head, keys[0]), [(source, 0, layers) for source in own], together=True)
     beside = lax.ppermute(beside, "tgt", partners(n_tgt, 1))
-    handed = [
-        lax.ppermute(after(piece, key_block), "inp", partners(n_inp, 1)) for piece, key_block in zip(fetched, keys)
-    ]
+    handed = lax.ppermute(after(fetched[0], keys[0]), "inp", partners(n_inp, 1))
+    along = [[fetched[0], handed]] + fetched[1:]
 
     pieces, stats = [], []
     for layer in range(layers):
@@ -402,13 +404,11 @@
                 for piece in (
                     (own[kind], layer),
                     (beside, kind * layers + layer),
-                    (fetched[layer], kind),
-                    (handed[layer], kind),
+                    (along[layer][0], kind),
+                    (along[layer][1], kind),
                 )
             ]
         )
-        own_stats = row_stats(after(place, *[part[0] for part in stats]), keys[layer], values[layer], pieces[layer])
-        stats.append(everywhere(own_stats, n_inp))
     flat, keep, send = [], [], []
     pair_sums, totals, mine, other = [], [], [], []
 
@@ -437,7 +437,12 @@
         return totals[-1]
 
     for layer in range(layers):
-        results = attention_grads(after(place, *flat), keys[layer], values[layer], pieces[layer], stats[layer])
+        ready = flat if layer else [keys[1], along[1][0]]
+        own_stats = row_stats(after(places[layer], *ready), keys[layer], values[layer], pieces[layer])
+        stats.append(everywhere(own_stats, n_inp))
+        results = attention_grads(
+            after(places[layer], *flat), keys[layer], values[layer], pieces[layer], stats[layer]
+        )
         keep += results[:PARTS]
         send += results[PARTS : 2 * PARTS]
         flat += results[2 * PARTS :]

time: 148 us -> 147 us (level)
  starting transfers between devices: 46 us -> 42.8 us
  waiting for transfers between devices: 52 us -> 53.9 us
    ppermute x8 -> x9, waiting for transfers between devices: 7.51 us -> 12.5 us  [the longest x6 6.75 us: everywhere(): lax.ppermute(value, 'inp', partners(n_inp, mask))]
    ppermute x2 -> x1, waiting for transfers between devices: 10.3 us -> 6.9 us  [exchange(): return lax.ppermute(value, ('inp', 'tgt'), pairs)]
    ppermute x8 -> x9, starting transfers between devices: 13.7 us -> 11.5 us  [the longest x6 8.93 us: everywhere(): lax.ppermute(value, 'inp', partners(n_inp, mask))]
    ppermute x2, starting transfers between devices: 3.76 us -> 2.24 us  [pair_sum(): arrived = lax.ppermute(send[index], 'inp', partners(n_inp, 1))]
    ppermute x2 -> x1, starting transfers between devices: 3.09 us -> 3 us  [exchange(): return lax.ppermute(value, ('inp', 'tgt'), pairs)]
  transfers between devices with their start and end apart: 27 -> 27, of which waited for: 16 -> 16; matrix products, arithmetic and copies ran while one was open for 0% -> 0% of each run, Pallas kernels for 29% -> 28%
where the time goes in v5:
time: 147 us; the launch traced here: 146 us
  waiting for transfers between devices  53.9 us (37%)
  Pallas kernels  46.1 us (31%)
  starting transfers between devices  42.8 us (29%)
  local copies, waits for them, and re-layouts  2.49 us (2%)
    ppermute x2, waiting for transfers between devices, line_sum(): lax.ppermute(after(value, *earlier), 'inp', [(0, 3), (3, 0), (1, 2), (2,...  13.5 us
    ppermute x2, starting transfers between devices, line_sum(): other.append(lax.ppermute(mine[-1], 'inp', partners(n_inp, 1)))  12.8 us
    pallas_call x2, Pallas kernels, project(): pl.pallas_call(project_kernel, grid=(width // depth,), in_specs=[pl.Block...  11 us
    pallas_call x2, Pallas kernels, back_blocks(): pl.pallas_call(back_kernel, grid_spec=pltpu.PrefetchScalarGridSpec(num_sc...  10.9 us
    pallas_call x4, Pallas kernels, join_heads(): pl.pallas_call(join_kernel, grid_spec=pltpu.PrefetchScalarGridSpec(num_sc...  9.73 us
    ppermute x6, starting transfers between devices, everywhere(): lax.ppermute(value, 'inp', partners(n_inp, mask))  8.93 us
    ppermute x2, waiting for transfers between devices, line_sum(): other.append(lax.ppermute(mine[-1], 'inp', partners(n_inp, 1)))  8.84 us
    pallas_call x2, Pallas kernels, attention_grads(): pl.pallas_call(functools.partial(grads_kernel, count), grid_spec=pltpu.Pr...  8.13 us
  transfers between devices with their start and end apart: 27, of which 16 were waited for; matrix products, arithmetic and copies ran while one was open for 0% of the time, Pallas kernels for 28%

profile of v5, /device:TPU:0, one launch (start us, length us, event | category | flops | bytes accessed | tf_op | source)
XLA Modules:
  0.0 146.3 jit_solution(17078851712496187443)
XLA Ops:
  0.7 0.1 add_add_fusion
  0.7 0.1 pad_add_fusion
  0.8 2.0 %copy.15 = bf16[2,512,4,256]{3,1,0,2:T(8,128)(2,1)S(1)} copy(bf16[2,512,4,256]{3,2,1,0:T(4,128)(2,1)} %param.8) | data formatting | bytes 4194304 | tf_op jit(solution)/shard_map/optimization_barrier | solution.py:374
  2.8 0.2 copy-done
  3.0 0.3 copy.14
  3.4 3.0 %collective-permute-start.1 = (bf16[2,512,256]{2,1,0:T(8,128)(2,1)S(1)}, bf16[2,512,256]{2,1,0:T(8,128)(2,1)S(1)}, u32[]{:S(2)}, u32[]{:S(2)}) collective-permute-start(bf16[2,512,256]{2,1,0:T(8,128)(2,1)S(1)} %shard_map.68), channel_id=1, source_target_pairs={{0,4},{2,6},{4,0},{6,2},{8,14},{10,12},{12,10},{14,8},{16,20},{18,... | collective-permute-start | bytes 1572872 | tf_op jit(solution)/shard_map/ppermute | solution.py:337
  6.5 5.5 %shard_map.71 = (bf16[1,512,256]{2,1,0:T(8,128)(2,1)S(1)}, bf16[1,512,256]{2,1,0:T(8,128)(2,1)S(1)}) custom-call(bf16[512,4096]{1,0:T(8,128)(2,1)} %enc_ref.1, bf16[2,4096,256]{2,1,0:T(8,128)(2,1)} %bitcast.40, bf16[2,4096,256]{2,1,0:T(8,128)(2,1)} %bitcast.44), custom_call_target="tpu_custom_call" | custom-call | flops 2147483648 | bytes 8388608 | tf_op jit(solution)/shard_map/pallas_call | solution.py:123
  12.0 0.1 shard_map.72
  12.1 0.1 collective-permute-start.3
  12.2 6.9 %collective-permute-done.1.refs_2_.refs_6_ = bf16[2,512,256]{2,1,0:T(8,128)(2,1)S(1)} collective-permute-done((bf16[2,512,256]{2,1,0:T(8,128)(2,1)S(1)}, bf16[2,512,256]{2,1,0:T(8,128)(2,1)S(1)}, u32[]{:S(2)}, u32[]{:S(2)}) %collective-permute-start.1) | collective-permute-done | bytes 524320 | tf_op jit(solution)/shard_map/ppermute | solution.py:337
  19.1 1.5 %collective-permute-start.2 = (bf16[2,512,256]{2,1,0:T(8,128)(2,1)S(1)}, bf16[2,512,256]{2,1,0:T(8,128)(2,1)S(1)}, u32[]{:S(2)}, u32[]{:S(2)}) collective-permute-start(bf16[2,512,256]{2,1,0:T(8,128)(2,1)S(1)} %collective-permute-done.1.refs_2_.refs_6_), channel_id=1, source_target_pairs={{0,8},{8,0},{16,24},{24,16},{1,9},{9,1},{17,25},{25,17},{2,10},{10... | collective-permute-start | bytes 1572872 | tf_op jit(solution)/shard_map/ppermute | solution.py:395
  20.6 1.0 collective-permute-start.7
  21.6 5.5 %shard_map.73 = (bf16[1,512,256]{2,1,0:T(8,128)(2,1)S(1)}, bf16[1,512,256]{2,1,0:T(8,128)(2,1)S(1)}) custom-call(bf16[512,4096]{1,0:T(8,128)(2,1)} %enc_ref.1, bf16[2,4096,256]{2,1,0:T(8,128)(2,1)} %bitcast.41, bf16[2,4096,256]{2,1,0:T(8,128)(2,1)} %bitcast.45), custom_call_target="tpu_custom_call" | custom-call | flops 2147483648 | bytes 8388608 | tf_op jit(solution)/shard_map/pallas_call | solution.py:123
  27.1 3.3 %collective-permute-done.3.refs_2_.refs_6_ = bf16[2,512,256]{2,1,0:T(8,128)(2,1)S(1)} collective-permute-done((bf16[2,512,256]{2,1,0:T(8,128)(2,1)S(1)}, bf16[2,512,256]{2,1,0:T(8,128)(2,1)S(1)}, u32[]{:S(2)}, u32[]{:S(2)}) %collective-permute-start.3) | collective-permute-done | bytes 524320 | tf_op jit(solution)/shard_map/ppermute | solution.py:386
  30.4 2.5 %collective-permute-done.2.refs_3_.refs_7_ = bf16[2,512,256]{2,1,0:T(8,128)(2,1)S(1)} collective-permute-done((bf16[2,512,256]{2,1,0:T(8,128)(2,1)S(1)}, bf16[2,512,256]{2,1,0:T(8,128)(2,1)S(1)}, u32[]{:S(2)}, u32[]{:S(2)}) %collective-permute-start.2) | collective-permute-done | bytes 524320 | tf_op jit(solution)/shard_map/ppermute | solution.py:395
  32.8 2.1 %shard_map.74.refs_8_ = f32[4,2048]{1,0:T(4,128)S(1)} custom-call(s32[3]{0:T(128)S(1)} %get-tuple-element.64.place_ref, bf16[1,512,256]{2,1,0:T(8,128)(2,1)S(1)} %get-tuple-element.57.k_ref, bf16[1,512,256]{2,1,0:T(8,128)(2,1)S(1)} %get-tuple-element.58.v_ref, bf16[4,2,512,256]{3,2,1,0:T(8,128)(2,1)S(1)} %bitcast.28, ...), custom_call_target="tpu_custom_call" | custom-call | flops 1073741824 | bytes 2621440 | tf_op jit(solution)/shard_map/pallas_call | solution.py:175
  35.0 3.8 %collective-permute-start.6 = (f32[4,2048]{1,0:T(4,128)S(1)}, f32[4,2048]{1,0:T(4,128)S(1)}, u32[]{:S(2)}, u32[]{:S(2)}) collective-permute-start(f32[4,2048]{1,0:T(4,128)S(1)} %shard_map.74.refs_8_), channel_id=1, source_target_pairs={{0,24},{8,16},{16,8},{24,0},{1,25},{9,17},{17,9},{25,1},{2,26},{10... | collective-permute-start | bytes 98312 | tf_op jit(solution)/shard_map/ppermute | solution.py:342
  38.8 0.6 collective-permute-start.4
  39.5 1.3 collective-permute-done.6.refs_11_
  40.8 2.8 %collective-permute-done.5.refs_10_ = f32[4,2048]{1,0:T(4,128)S(1)} collective-permute-done((f32[4,2048]{1,0:T(4,128)S(1)}, f32[4,2048]{1,0:T(4,128)S(1)}, u32[]{:S(2)}, u32[]{:S(2)}) %collective-permute-start.5) | collective-permute-done | bytes 32800 | tf_op jit(solution)/shard_map/ppermute | solution.py:342
  43.6 4.1 %shard_map.75 = (bf16[4,256,256]{2,1,0:T(8,128)(2,1)S(1)}, bf16[4,256,256]{2,1,0:T(8,128)(2,1)S(1)}, bf16[512,256]{1,0:T(8,128)(2,1)S(1)}, bf16[512,256]{1,0:T(8,128)(2,1)S(1)}) custom-call(s32[3]{0:T(128)S(1)} %get-tuple-element.64.place_ref, bf16[1,512,256]{2,1,0:T(8,128)(2,1)S(1)} %get-tuple-element.57.k_ref, ...), custom_call_target="tpu_custom_call" | custom-call | flops 2684354560 | bytes 3932160 | tf_op jit(solution)/shard_map/pallas_call | solution.py:229
  47.7 2.1 %shard_map.76.refs_8_ = f32[4,2048]{1,0:T(4,128)S(1)} custom-call(s32[3]{0:T(128)S(1)} %get-tuple-element.67.place_ref, bf16[1,512,256]{2,1,0:T(8,128)(2,1)S(1)} %get-tuple-element.63.k_ref, bf16[1,512,256]{2,1,0:T(8,128)(2,1)S(1)} %get-tuple-element.68.v_ref, bf16[4,2,512,256]{3,2,1,0:T(8,128)(2,1)S(1)} %bitcast.30, ...), custom_call_target="tpu_custom_call" | custom-call | flops 1073741824 | bytes 2621440 | tf_op jit(solution)/shard_map/pallas_call | solution.py:175
  49.9 1.5 %collective-permute-start.10 = (f32[4,2048]{1,0:T(4,128)S(1)}, f32[4,2048]{1,0:T(4,128)S(1)}, u32[]{:S(2)}, u32[]{:S(2)}) collective-permute-start(f32[4,2048]{1,0:T(4,128)S(1)} %shard_map.76.refs_8_), channel_id=1, source_target_pairs={{0,24},{8,16},{16,8},{24,0},{1,25},{9,17},{17,9},{25,1},{2,26},{10... | collective-permute-start | bytes 98312 | tf_op jit(solution)/shard_map/ppermute | solution.py:342
  51.4 0.6 collective-permute-start.9
  52.0 2.3 %collective-permute-start.8 = (f32[4,2048]{1,0:T(4,128)S(1)}, f32[4,2048]{1,0:T(4,128)S(1)}, u32[]{:S(2)}, u32[]{:S(2)}) collective-permute-start(f32[4,2048]{1,0:T(4,128)S(1)} %shard_map.76.refs_8_), channel_id=1, source_target_pairs={{0,8},{8,0},{16,24},{24,16},{1,9},{9,1},{17,25},{25,17},{2,10},{10... | collective-permute-start | bytes 98312 | tf_op jit(solution)/shard_map/ppermute | solution.py:342
  54.3 1.3 collective-permute-done.10.refs_11_
  55.6 0.6 collective-permute-done.9.refs_10_
  56.2 0.7 collective-permute-done.8.refs_9_
  56.9 1.6 %collective-permute-start.11 = (bf16[4,256,256]{2,1,0:T(8,128)(2,1)S(1)}, bf16[4,256,256]{2,1,0:T(8,128)(2,1)S(1)}, u32[]{:S(2)}, u32[]{:S(2)}) collective-permute-start(bf16[4,256,256]{2,1,0:T(8,128)(2,1)S(1)} %get-tuple-element.77), channel_id=1, source_target_pairs={{0,8},{8,0},{16,24},{24,16},{1,9},{9,1},{17,25},{25,17},{2,10},{10... | collective-permute-start | bytes 1572872 | tf_op jit(solution)/shard_map/ppermute | solution.py:420
  58.5 4.1 %shard_map.77 = (bf16[4,256,256]{2,1,0:T(8,128)(2,1)S(1)}, bf16[4,256,256]{2,1,0:T(8,128)(2,1)S(1)}, bf16[512,256]{1,0:T(8,128)(2,1)S(1)}, bf16[512,256]{1,0:T(8,128)(2,1)S(1)}) custom-call(s32[3]{0:T(128)S(1)} %get-tuple-element.67.place_ref, bf16[1,512,256]{2,1,0:T(8,128)(2,1)S(1)} %get-tuple-element.63.k_ref, ...), custom_call_target="tpu_custom_call" | custom-call | flops 2684354560 | bytes 3932160 | tf_op jit(solution)/shard_map/pallas_call | solution.py:229
  62.6 5.5 %shard_map.78 = bf16[4,512,512]{2,1,0:T(8,128)(2,1)S(1)} custom-call(s32[4]{0:T(128)S(1)} %get-tuple-element.72.order_ref, bf16[2,4096,256]{2,1,0:T(8,128)(2,1)} %bitcast.42, bf16[2,4096,256]{2,1,0:T(8,128)(2,1)} %bitcast.46, bf16[512,256]{1,0:T(8,128)(2,1)S(1)} %get-tuple-element.65.refs_0_, bf16[512,256]{1,0:T(8,128)(2,1)S(1)} %get-tuple-element.66.refs_1_, ...), custom_call_target="tpu_custom_call" | custom-call | flops 2147483648 | bytes 8388608 | tf_op jit(solution)/shard_map/pallas_call | solution.py:260
  68.2 0.1 shard_map.79.one_ref
  68.4 0.6 collective-permute-start.12
  69.0 2.3 %collective-permute-start.17 = (bf16[4,256,256]{2,1,0:T(8,128)(2,1)S(1)}, bf16[4,256,256]{2,1,0:T(8,128)(2,1)S(1)}, u32[]{:S(2)}, u32[]{:S(2)}) collective-permute-start(bf16[4,256,256]{2,1,0:T(8,128)(2,1)S(1)} %shard_map.79.one_ref), channel_id=1, source_target_pairs={{0,24},{24,0},{8,16},{16,8},{1,25},{25,1},{9,17},{17,9},{2,26},{26... | collective-permute-start | bytes 1572872 | tf_op jit(solution)/shard_map/ppermute | solution.py:433
  71.3 5.3 %shard_map.81.refs_0_ = f32[4,512,512]{2,1,0:T(8,128)S(1)} custom-call(s32[4]{0:T(128)S(1)} %get-tuple-element.80.order_ref, bf16[2,4096,256]{2,1,0:T(8,128)(2,1)} %bitcast.43, bf16[2,4096,256]{2,1,0:T(8,128)(2,1)} %bitcast.47, bf16[512,256]{1,0:T(8,128)(2,1)S(1)} %get-tuple-element.65.refs_0_, bf16[512,256]{1,0:T(8,128)(2,1)S(1)} %get-tuple-element.66.refs_1_, ...), custom_call_target="tpu_custom_call" | custom-call | flops 2147483648 | bytes 8388608 | tf_op jit(solution)/shard_map/pallas_call | solution.py:260
  76.6 0.1 shard_map.82
  76.7 1.6 %collective-permute-start.14 = (bf16[1,512,512]{2,1,0:T(8,128)(2,1)S(1)}, bf16[1,512,512]{2,1,0:T(8,128)(2,1)S(1)}, u32[]{:S(2)}, u32[]{:S(2)}) collective-permute-start(bf16[1,512,512]{2,1,0:T(8,128)(2,1)S(1)} %shard_map.82), channel_id=1, source_target_pairs={{0,4},{2,6},{4,0},{6,2},{1,5},{3,7},{5,1},{7,3},{8,12},{10,14},{12... | collective-permute-start | bytes 1572872 | tf_op jit(solution)/shard_map/ppermute | solution.py:462
  78.3 4.4 %collective-permute-done.12.two_ref = bf16[4,256,256]{2,1,0:T(8,128)(2,1)S(1)} collective-permute-done((bf16[4,256,256]{2,1,0:T(8,128)(2,1)S(1)}, bf16[4,256,256]{2,1,0:T(8,128)(2,1)S(1)}, u32[]{:S(2)}, u32[]{:S(2)}) %collective-permute-start.12) | collective-permute-done | bytes 524320 | tf_op jit(solution)/shard_map/ppermute | solution.py:420
  82.7 0.1 shard_map.80.one_ref
  82.8 0.1 shard_map.84
  82.9 1.6 %collective-permute-start.16 = (bf16[1,512,512]{2,1,0:T(8,128)(2,1)S(1)}, bf16[1,512,512]{2,1,0:T(8,128)(2,1)S(1)}, u32[]{:S(2)}, u32[]{:S(2)}) collective-permute-start(bf16[1,512,512]{2,1,0:T(8,128)(2,1)S(1)} %shard_map.84), channel_id=1, source_target_pairs={{0,4},{2,6},{4,0},{6,2},{1,5},{3,7},{5,1},{7,3},{8,12},{10,14},{12... | collective-permute-start | bytes 1572872 | tf_op jit(solution)/shard_map/ppermute | solution.py:463
  84.5 10.3 %collective-permute-done.17.two_ref = bf16[4,256,256]{2,1,0:T(8,128)(2,1)S(1)} collective-permute-done((bf16[4,256,256]{2,1,0:T(8,128)(2,1)S(1)}, bf16[4,256,256]{2,1,0:T(8,128)(2,1)S(1)}, u32[]{:S(2)}, u32[]{:S(2)}) %collective-permute-start.17) | collective-permute-done | bytes 524320 | tf_op jit(solution)/shard_map/ppermute | solution.py:433
  94.8 0.1 shard_map.85
  95.0 0.2 shard_map.83
  95.1 1.6 %collective-permute-start.15 = (bf16[1,512,512]{2,1,0:T(8,128)(2,1)S(1)}, bf16[1,512,512]{2,1,0:T(8,128)(2,1)S(1)}, u32[]{:S(2)}, u32[]{:S(2)}) collective-permute-start(bf16[1,512,512]{2,1,0:T(8,128)(2,1)S(1)} %shard_map.83), channel_id=1, source_target_pairs={{0,1},{1,0},{2,3},{3,2},{4,5},{5,4},{6,7},{7,6},{8,9},{9,8},{10,11... | collective-permute-start | bytes 1572872 | tf_op jit(solution)/shard_map/ppermute | solution.py:466
  96.7 1.5 %collective-permute-start.21 = (bf16[4,256,256]{2,1,0:T(8,128)(2,1)S(1)}, bf16[4,256,256]{2,1,0:T(8,128)(2,1)S(1)}, u32[]{:S(2)}, u32[]{:S(2)}) collective-permute-start(bf16[4,256,256]{2,1,0:T(8,128)(2,1)S(1)} %shard_map.80.one_ref), channel_id=1, source_target_pairs={{0,24},{24,0},{8,16},{16,8},{1,25},{25,1},{9,17},{17,9},{2,26},{26... | collective-permute-start | bytes 1572872 | tf_op jit(solution)/shard_map/ppermute | solution.py:433
  98.3 1.5 %collective-permute-start.19 = (bf16[256,256]{1,0:T(8,128)(2,1)S(1)}, bf16[256,256]{1,0:T(8,128)(2,1)S(1)}, u32[]{:S(2)}, u32[]{:S(2)}) collective-permute-start(bf16[256,256]{1,0:T(8,128)(2,1)S(1)} %get-tuple-element.86), channel_id=1, source_target_pairs={{0,4},{2,6},{4,0},{6,2},{1,5},{3,7},{5,1},{7,3},{8,12},{10,14},{12... | collective-permute-start | bytes 393224 | tf_op jit(solution)/shard_map/ppermute | solution.py:352
  99.8 1.1 collective-permute-start.20
  100.9 3.9 %collective-permute-done.19.refs_2_ = bf16[256,256]{1,0:T(8,128)(2,1)S(1)} collective-permute-done((bf16[256,256]{1,0:T(8,128)(2,1)S(1)}, bf16[256,256]{1,0:T(8,128)(2,1)S(1)}, u32[]{:S(2)}, u32[]{:S(2)}) %collective-permute-start.19) | collective-permute-done | bytes 131104 | tf_op jit(solution)/shard_map/ppermute | solution.py:352
  104.8 2.2 %collective-permute-done.20.refs_3_ = bf16[256,256]{1,0:T(8,128)(2,1)S(1)} collective-permute-done((bf16[256,256]{1,0:T(8,128)(2,1)S(1)}, bf16[256,256]{1,0:T(8,128)(2,1)S(1)}, u32[]{:S(2)}, u32[]{:S(2)}) %collective-permute-start.20) | collective-permute-done | bytes 131104 | tf_op jit(solution)/shard_map/ppermute | solution.py:352
  107.1 1.5 %collective-permute-done.15.refs_3_ = bf16[1,512,512]{2,1,0:T(8,128)(2,1)S(1)} collective-permute-done((bf16[1,512,512]{2,1,0:T(8,128)(2,1)S(1)}, bf16[1,512,512]{2,1,0:T(8,128)(2,1)S(1)}, u32[]{:S(2)}, u32[]{:S(2)}) %collective-permute-start.15) | collective-permute-done | bytes 524320 | tf_op jit(solution)/shard_map/ppermute | solution.py:466
  108.6 3.1 %collective-permute-done.21.two_ref = bf16[4,256,256]{2,1,0:T(8,128)(2,1)S(1)} collective-permute-done((bf16[4,256,256]{2,1,0:T(8,128)(2,1)S(1)}, bf16[4,256,256]{2,1,0:T(8,128)(2,1)S(1)}, u32[]{:S(2)}, u32[]{:S(2)}) %collective-permute-start.21) | collective-permute-done | bytes 524320 | tf_op jit(solution)/shard_map/ppermute | solution.py:433
  111.8 0.1 shard_map.87
  112.0 1.6 %collective-permute-start.23 = (bf16[256,256]{1,0:T(8,128)(2,1)S(1)}, bf16[256,256]{1,0:T(8,128)(2,1)S(1)}, u32[]{:S(2)}, u32[]{:S(2)}) collective-permute-start(bf16[256,256]{1,0:T(8,128)(2,1)S(1)} %get-tuple-element.92), channel_id=1, source_target_pairs={{0,4},{2,6},{4,0},{6,2},{1,5},{3,7},{5,1},{7,3},{8,12},{10,14},{12... | collective-permute-start | bytes 393224 | tf_op jit(solution)/shard_map/ppermute | solution.py:352
  113.6 0.3 collective-permute-start.24
  113.8 6.4 %collective-permute-start.26 = (bf16[4,256,256]{2,1,0:T(8,128)(2,1)S(1)}, bf16[4,256,256]{2,1,0:T(8,128)(2,1)S(1)}, u32[]{:S(2)}, u32[]{:S(2)}) collective-permute-start(bf16[4,256,256]{2,1,0:T(8,128)(2,1)S(1)} %shard_map.86.part_ref), channel_id=1, source_target_pairs={{0,8},{8,0},{16,24},{24,16},{1,9},{9,1},{17,25},{25,17},{2,10},{10... | collective-permute-start | bytes 1572872 | tf_op jit(solution)/shard_map/ppermute | solution.py:436
  120.3 6.4 %collective-permute-start.25 = (bf16[4,256,256]{2,1,0:T(8,128)(2,1)S(1)}, bf16[4,256,256]{2,1,0:T(8,128)(2,1)S(1)}, u32[]{:S(2)}, u32[]{:S(2)}) collective-permute-start(bf16[4,256,256]{2,1,0:T(8,128)(2,1)S(1)} %shard_map.88.part_ref), channel_id=1, source_target_pairs={{0,8},{8,0},{16,24},{24,16},{1,9},{9,1},{17,25},{25,17},{2,10},{10... | collective-permute-start | bytes 1572872 | tf_op jit(solution)/shard_map/ppermute | solution.py:436
  126.7 2.4 %shard_map.89.rest_0_ = bf16[2,512,4,256]{3,2,1,0:T(4,128)(2,1)} custom-call(s32[3]{0:T(128)S(1)} %get-tuple-element.64.place_ref, bf16[4,256,256]{2,1,0:T(8,128)(2,1)S(1)} %shard_map.86.part_ref), custom_call_target="tpu_custom_call" | custom-call | bytes 1048576 | tf_op jit(solution)/shard_map/pallas_call | solution.py:86
  129.2 3.8 %collective-permute-done.26.part_ref = bf16[4,256,256]{2,1,0:T(8,128)(2,1)S(1)} collective-permute-done((bf16[4,256,256]{2,1,0:T(8,128)(2,1)S(1)}, bf16[4,256,256]{2,1,0:T(8,128)(2,1)S(1)}, u32[]{:S(2)}, u32[]{:S(2)}) %collective-permute-start.26) | collective-permute-done | bytes 524320 | tf_op jit(solution)/shard_map/ppermute | solution.py:436
  133.0 2.4 %shard_map.90.rest_0_ = bf16[2,512,4,256]{3,2,1,0:T(4,128)(2,1)} custom-call(s32[3]{0:T(128)S(1)} %get-tuple-element.64.place_ref, bf16[4,256,256]{2,1,0:T(8,128)(2,1)S(1)} %collective-permute-done.26.part_ref, bf16[2,512,4,256]{3,2,1,0:T(4,128)(2,1)} %shard_map.89.rest_0_), custom_call_target="tpu_custom_call", output_to_operand_aliasing={{}: (2, {})} | custom-call | bytes 1048576 | tf_op jit(solution)/shard_map/pallas_call | solution.py:86
  135.4 1.0 shard_map.93
  136.5 2.4 %shard_map.91.rest_0_ = bf16[2,512,4,256]{3,2,1,0:T(4,128)(2,1)} custom-call(s32[3]{0:T(128)S(1)} %get-tuple-element.64.place_ref, bf16[4,256,256]{2,1,0:T(8,128)(2,1)S(1)} %shard_map.88.part_ref, bf16[2,512,4,256]{3,2,1,0:T(4,128)(2,1)} %shard_map.90.rest_0_), custom_call_target="tpu_custom_call", output_to_operand_aliasing={{}: (2, {})} | custom-call | bytes 1048576 | tf_op jit(solution)/shard_map/pallas_call | solution.py:86
  138.9 5.0 %collective-permute-done.25.part_ref = bf16[4,256,256]{2,1,0:T(8,128)(2,1)S(1)} collective-permute-done((bf16[4,256,256]{2,1,0:T(8,128)(2,1)S(1)}, bf16[4,256,256]{2,1,0:T(8,128)(2,1)S(1)}, u32[]{:S(2)}, u32[]{:S(2)}) %collective-permute-start.25) | collective-permute-done | bytes 524320 | tf_op jit(solution)/shard_map/ppermute | solution.py:436
  143.9 2.4 %shard_map.92 = bf16[2,512,4,256]{3,2,1,0:T(4,128)(2,1)} custom-call(s32[3]{0:T(128)S(1)} %get-tuple-element.64.place_ref, bf16[4,256,256]{2,1,0:T(8,128)(2,1)S(1)} %collective-permute-done.25.part_ref, bf16[2,512,4,256]{3,2,1,0:T(4,128)(2,1)} %shard_map.91.rest_0_), custom_call_target="tpu_custom_call", output_to_operand_aliasing={{}: (2, {})} | custom-call | bytes 1048576 | tf_op jit(solution)/shard_map/pallas_call | solution.py:86
  (22 shorter events, 0.4 us)
Async XLA Ops:
  0.8 2.2 %copy-start = (bf16[2,512,4,256]{3,2,1,0:T(4,128)(2,1)S(1)}, bf16[2,512,4,256]{3,2,1,0:T(4,128)(2,1)}, u32[]{:S(2)}) copy-start(bf16[2,512,4,256]{3,2,1,0:T(4,128)(2,1)} %param.9) | copy-start | bytes 6291460
  3.4 15.8 %collective-permute-start.1 = (bf16[2,512,256]{2,1,0:T(8,128)(2,1)S(1)}, bf16[2,512,256]{2,1,0:T(8,128)(2,1)S(1)}, u32[]{:S(2)}, u32[]{:S(2)}) collective-permute-start(bf16[2,512,256]{2,1,0:T(8,128)(2,1)S(1)} %shard_map.68), channel_id=1, source_target_pairs={{0,4},{2,6},{4,0},{6,2},{8,14},{10,12},{12,10},{14,8},{16,20},{18,... | collective-permute-start | bytes 1572872 | tf_op jit(solution)/shard_map/ppermute | solution.py:337
  12.1 20.8 %collective-permute-start = (bf16[4,512,256]{2,1,0:T(8,128)(2,1)S(1)}, bf16[4,512,256]{2,1,0:T(8,128)(2,1)S(1)}, u32[]{:S(2)}, u32[]{:S(2)}) collective-permute-start(bf16[4,512,256]{2,1,0:T(8,128)(2,1)S(1)} %shard_map.72), channel_id=1, source_target_pairs={{0,2},{2,0},{4,6},{6,4},{1,3},{3,1},{5,7},{7,5},{8,10},{10,8},{12,... | collective-permute-start | bytes 3145736 | tf_op jit(solution)/shard_map/ppermute | solution.py:394
  12.1 18.2 %collective-permute-start.3 = (bf16[2,512,256]{2,1,0:T(8,128)(2,1)S(1)}, bf16[2,512,256]{2,1,0:T(8,128)(2,1)S(1)}, u32[]{:S(2)}, u32[]{:S(2)}) collective-permute-start(bf16[2,512,256]{2,1,0:T(8,128)(2,1)S(1)} %shard_map.69), channel_id=1, source_target_pairs={{0,4},{2,6},{4,0},{6,2},{1,5},{3,7},{5,1},{7,3},{8,12},{10,14},{12... | collective-permute-start | bytes 1572872 | tf_op jit(solution)/shard_map/ppermute | solution.py:386
  19.1 13.7 %collective-permute-start.2 = (bf16[2,512,256]{2,1,0:T(8,128)(2,1)S(1)}, bf16[2,512,256]{2,1,0:T(8,128)(2,1)S(1)}, u32[]{:S(2)}, u32[]{:S(2)}) collective-permute-start(bf16[2,512,256]{2,1,0:T(8,128)(2,1)S(1)} %collective-permute-done.1.refs_2_.refs_6_), channel_id=1, source_target_pairs={{0,8},{8,0},{16,24},{24,16},{1,9},{9,1},{17,25},{25,17},{2,10},{10... | collective-permute-start | bytes 1572872 | tf_op jit(solution)/shard_map/ppermute | solution.py:395
  20.6 27.1 %collective-permute-start.7 = (bf16[2,512,256]{2,1,0:T(8,128)(2,1)S(1)}, bf16[2,512,256]{2,1,0:T(8,128)(2,1)S(1)}, u32[]{:S(2)}, u32[]{:S(2)}) collective-permute-start(bf16[2,512,256]{2,1,0:T(8,128)(2,1)S(1)} %shard_map.70), channel_id=1, source_target_pairs={{0,6},{2,4},{4,2},{6,0},{1,7},{3,5},{5,3},{7,1},{8,14},{10,12},{12... | collective-permute-start | bytes 1572872 | tf_op jit(solution)/shard_map/ppermute | solution.py:386
  35.0 5.8 %collective-permute-start.6 = (f32[4,2048]{1,0:T(4,128)S(1)}, f32[4,2048]{1,0:T(4,128)S(1)}, u32[]{:S(2)}, u32[]{:S(2)}) collective-permute-start(f32[4,2048]{1,0:T(4,128)S(1)} %shard_map.74.refs_8_), channel_id=1, source_target_pairs={{0,24},{8,16},{16,8},{24,0},{1,25},{9,17},{17,9},{25,1},{2,26},{10... | collective-permute-start | bytes 98312 | tf_op jit(solution)/shard_map/ppermute | solution.py:342
  38.8 4.8 %collective-permute-start.5 = (f32[4,2048]{1,0:T(4,128)S(1)}, f32[4,2048]{1,0:T(4,128)S(1)}, u32[]{:S(2)}, u32[]{:S(2)}) collective-permute-start(f32[4,2048]{1,0:T(4,128)S(1)} %shard_map.74.refs_8_), channel_id=1, source_target_pairs={{0,16},{8,24},{16,0},{24,8},{1,17},{9,25},{17,1},{25,9},{2,18},{10... | collective-permute-start | bytes 98312 | tf_op jit(solution)/shard_map/ppermute | solution.py:342
  38.8 4.8 %collective-permute-start.4 = (f32[4,2048]{1,0:T(4,128)S(1)}, f32[4,2048]{1,0:T(4,128)S(1)}, u32[]{:S(2)}, u32[]{:S(2)}) collective-permute-start(f32[4,2048]{1,0:T(4,128)S(1)} %shard_map.74.refs_8_), channel_id=1, source_target_pairs={{0,8},{8,0},{16,24},{24,16},{1,9},{9,1},{17,25},{25,17},{2,10},{10... | collective-permute-start | bytes 98312 | tf_op jit(solution)/shard_map/ppermute | solution.py:342
  49.9 5.8 %collective-permute-start.10 = (f32[4,2048]{1,0:T(4,128)S(1)}, f32[4,2048]{1,0:T(4,128)S(1)}, u32[]{:S(2)}, u32[]{:S(2)}) collective-permute-start(f32[4,2048]{1,0:T(4,128)S(1)} %shard_map.76.refs_8_), channel_id=1, source_target_pairs={{0,24},{8,16},{16,8},{24,0},{1,25},{9,17},{17,9},{25,1},{2,26},{10... | collective-permute-start | bytes 98312 | tf_op jit(solution)/shard_map/ppermute | solution.py:342
  51.4 4.8 %collective-permute-start.9 = (f32[4,2048]{1,0:T(4,128)S(1)}, f32[4,2048]{1,0:T(4,128)S(1)}, u32[]{:S(2)}, u32[]{:S(2)}) collective-permute-start(f32[4,2048]{1,0:T(4,128)S(1)} %shard_map.76.refs_8_), channel_id=1, source_target_pairs={{0,16},{8,24},{16,0},{24,8},{1,17},{9,25},{17,1},{25,9},{2,18},{10... | collective-permute-start | bytes 98312 | tf_op jit(solution)/shard_map/ppermute | solution.py:342
  52.0 4.9 %collective-permute-start.8 = (f32[4,2048]{1,0:T(4,128)S(1)}, f32[4,2048]{1,0:T(4,128)S(1)}, u32[]{:S(2)}, u32[]{:S(2)}) collective-permute-start(f32[4,2048]{1,0:T(4,128)S(1)} %shard_map.76.refs_8_), channel_id=1, source_target_pairs={{0,8},{8,0},{16,24},{24,16},{1,9},{9,1},{17,25},{25,17},{2,10},{10... | collective-permute-start | bytes 98312 | tf_op jit(solution)/shard_map/ppermute | solution.py:342
  56.9 11.3 %collective-permute-start.11 = (bf16[4,256,256]{2,1,0:T(8,128)(2,1)S(1)}, bf16[4,256,256]{2,1,0:T(8,128)(2,1)S(1)}, u32[]{:S(2)}, u32[]{:S(2)}) collective-permute-start(bf16[4,256,256]{2,1,0:T(8,128)(2,1)S(1)} %get-tuple-element.77), channel_id=1, source_target_pairs={{0,8},{8,0},{16,24},{24,16},{1,9},{9,1},{17,25},{25,17},{2,10},{10... | collective-permute-start | bytes 1572872 | tf_op jit(solution)/shard_map/ppermute | solution.py:420
  68.3 8.3 %collective-permute-start.13 = (bf16[4,512,512]{2,1,0:T(8,128)(2,1)S(1)}, bf16[4,512,512]{2,1,0:T(8,128)(2,1)S(1)}, u32[]{:S(2)}, u32[]{:S(2)}) collective-permute-start(bf16[4,512,512]{2,1,0:T(8,128)(2,1)S(1)} %shard_map.78), channel_id=1, source_target_pairs={{0,2},{2,0},{4,6},{6,4},{1,3},{3,1},{5,7},{7,5},{8,10},{10,8},{12,... | collective-permute-start | bytes 6291464 | tf_op jit(solution)/shard_map/ppermute | solution.py:457
  68.4 14.3 %collective-permute-start.12 = (bf16[4,256,256]{2,1,0:T(8,128)(2,1)S(1)}, bf16[4,256,256]{2,1,0:T(8,128)(2,1)S(1)}, u32[]{:S(2)}, u32[]{:S(2)}) collective-permute-start(bf16[4,256,256]{2,1,0:T(8,128)(2,1)S(1)} %get-tuple-element.78), channel_id=1, source_target_pairs={{0,8},{8,0},{16,24},{24,16},{1,9},{9,1},{17,25},{25,17},{2,10},{10... | collective-permute-start | bytes 1572872 | tf_op jit(solution)/shard_map/ppermute | solution.py:420
  69.0 25.9 %collective-permute-start.17 = (bf16[4,256,256]{2,1,0:T(8,128)(2,1)S(1)}, bf16[4,256,256]{2,1,0:T(8,128)(2,1)S(1)}, u32[]{:S(2)}, u32[]{:S(2)}) collective-permute-start(bf16[4,256,256]{2,1,0:T(8,128)(2,1)S(1)} %shard_map.79.one_ref), channel_id=1, source_target_pairs={{0,24},{24,0},{8,16},{16,8},{1,25},{25,1},{9,17},{17,9},{2,26},{26... | collective-permute-start | bytes 1572872 | tf_op jit(solution)/shard_map/ppermute | solution.py:433
  76.7 18.3 %collective-permute-start.14 = (bf16[1,512,512]{2,1,0:T(8,128)(2,1)S(1)}, bf16[1,512,512]{2,1,0:T(8,128)(2,1)S(1)}, u32[]{:S(2)}, u32[]{:S(2)}) collective-permute-start(bf16[1,512,512]{2,1,0:T(8,128)(2,1)S(1)} %shard_map.82), channel_id=1, source_target_pairs={{0,4},{2,6},{4,0},{6,2},{1,5},{3,7},{5,1},{7,3},{8,12},{10,14},{12... | collective-permute-start | bytes 1572872 | tf_op jit(solution)/shard_map/ppermute | solution.py:462
  82.9 24.2 %collective-permute-start.16 = (bf16[1,512,512]{2,1,0:T(8,128)(2,1)S(1)}, bf16[1,512,512]{2,1,0:T(8,128)(2,1)S(1)}, u32[]{:S(2)}, u32[]{:S(2)}) collective-permute-start(bf16[1,512,512]{2,1,0:T(8,128)(2,1)S(1)} %shard_map.84), channel_id=1, source_target_pairs={{0,4},{2,6},{4,0},{6,2},{1,5},{3,7},{5,1},{7,3},{8,12},{10,14},{12... | collective-permute-start | bytes 1572872 | tf_op jit(solution)/shard_map/ppermute | solution.py:463
  95.1 13.5 %collective-permute-start.15 = (bf16[1,512,512]{2,1,0:T(8,128)(2,1)S(1)}, bf16[1,512,512]{2,1,0:T(8,128)(2,1)S(1)}, u32[]{:S(2)}, u32[]{:S(2)}) collective-permute-start(bf16[1,512,512]{2,1,0:T(8,128)(2,1)S(1)} %shard_map.83), channel_id=1, source_target_pairs={{0,1},{1,0},{2,3},{3,2},{4,5},{5,4},{6,7},{7,6},{8,9},{9,8},{10,11... | collective-permute-start | bytes 1572872 | tf_op jit(solution)/shard_map/ppermute | solution.py:466
  96.7 15.1 %collective-permute-start.21 = (bf16[4,256,256]{2,1,0:T(8,128)(2,1)S(1)}, bf16[4,256,256]{2,1,0:T(8,128)(2,1)S(1)}, u32[]{:S(2)}, u32[]{:S(2)}) collective-permute-start(bf16[4,256,256]{2,1,0:T(8,128)(2,1)S(1)} %shard_map.80.one_ref), channel_id=1, source_target_pairs={{0,24},{24,0},{8,16},{16,8},{1,25},{25,1},{9,17},{17,9},{2,26},{26... | collective-permute-start | bytes 1572872 | tf_op jit(solution)/shard_map/ppermute | solution.py:433
  98.3 1.5 %collective-permute-start.18 = (bf16[256,256]{1,0:T(8,128)(2,1)S(1)}, bf16[256,256]{1,0:T(8,128)(2,1)S(1)}, u32[]{:S(2)}, u32[]{:S(2)}) collective-permute-start(bf16[256,256]{1,0:T(8,128)(2,1)S(1)} %get-tuple-element.85), channel_id=1, source_target_pairs={{0,2},{2,0},{4,6},{6,4},{1,3},{3,1},{5,7},{7,5},{8,10},{10,8},{12,... | collective-permute-start | bytes 393224 | tf_op jit(solution)/shard_map/ppermute | solution.py:352
  98.3 6.5 %collective-permute-start.19 = (bf16[256,256]{1,0:T(8,128)(2,1)S(1)}, bf16[256,256]{1,0:T(8,128)(2,1)S(1)}, u32[]{:S(2)}, u32[]{:S(2)}) collective-permute-start(bf16[256,256]{1,0:T(8,128)(2,1)S(1)} %get-tuple-element.86), channel_id=1, source_target_pairs={{0,4},{2,6},{4,0},{6,2},{1,5},{3,7},{5,1},{7,3},{8,12},{10,14},{12... | collective-permute-start | bytes 393224 | tf_op jit(solution)/shard_map/ppermute | solution.py:352
  99.8 7.3 %collective-permute-start.20 = (bf16[256,256]{1,0:T(8,128)(2,1)S(1)}, bf16[256,256]{1,0:T(8,128)(2,1)S(1)}, u32[]{:S(2)}, u32[]{:S(2)}) collective-permute-start(bf16[256,256]{1,0:T(8,128)(2,1)S(1)} %get-tuple-element.87), channel_id=1, source_target_pairs={{0,6},{2,4},{4,2},{6,0},{1,7},{3,5},{5,3},{7,1},{8,14},{10,12},{12... | collective-permute-start | bytes 393224 | tf_op jit(solution)/shard_map/ppermute | solution.py:352
  111.9 8.3 %collective-permute-start.22 = (bf16[256,256]{1,0:T(8,128)(2,1)S(1)}, bf16[256,256]{1,0:T(8,128)(2,1)S(1)}, u32[]{:S(2)}, u32[]{:S(2)}) collective-permute-start(bf16[256,256]{1,0:T(8,128)(2,1)S(1)} %get-tuple-element.91), channel_id=1, source_target_pairs={{0,2},{2,0},{4,6},{6,4},{1,3},{3,1},{5,7},{7,5},{8,10},{10,8},{12,... | collective-permute-start | bytes 393224 | tf_op jit(solution)/shard_map/ppermute | solution.py:352
  112.0 8.3 %collective-permute-start.23 = (bf16[256,256]{1,0:T(8,128)(2,1)S(1)}, bf16[256,256]{1,0:T(8,128)(2,1)S(1)}, u32[]{:S(2)}, u32[]{:S(2)}) collective-permute-start(bf16[256,256]{1,0:T(8,128)(2,1)S(1)} %get-tuple-element.92), channel_id=1, source_target_pairs={{0,4},{2,6},{4,0},{6,2},{1,5},{3,7},{5,1},{7,3},{8,12},{10,14},{12... | collective-permute-start | bytes 393224 | tf_op jit(solution)/shard_map/ppermute | solution.py:352
  113.6 6.7 %collective-permute-start.24 = (bf16[256,256]{1,0:T(8,128)(2,1)S(1)}, bf16[256,256]{1,0:T(8,128)(2,1)S(1)}, u32[]{:S(2)}, u32[]{:S(2)}) collective-permute-start(bf16[256,256]{1,0:T(8,128)(2,1)S(1)} %get-tuple-element.93), channel_id=1, source_target_pairs={{0,6},{2,4},{4,2},{6,0},{1,7},{3,5},{5,3},{7,1},{8,14},{10,12},{12... | collective-permute-start | bytes 393224 | tf_op jit(solution)/shard_map/ppermute | solution.py:352
  113.8 19.2 %collective-permute-start.26 = (bf16[4,256,256]{2,1,0:T(8,128)(2,1)S(1)}, bf16[4,256,256]{2,1,0:T(8,128)(2,1)S(1)}, u32[]{:S(2)}, u32[]{:S(2)}) collective-permute-start(bf16[4,256,256]{2,1,0:T(8,128)(2,1)S(1)} %shard_map.86.part_ref), channel_id=1, source_target_pairs={{0,8},{8,0},{16,24},{24,16},{1,9},{9,1},{17,25},{25,17},{2,10},{10... | collective-permute-start | bytes 1572872 | tf_op jit(solution)/shard_map/ppermute | solution.py:436
  120.3 23.6 %collective-permute-start.25 = (bf16[4,256,256]{2,1,0:T(8,128)(2,1)S(1)}, bf16[4,256,256]{2,1,0:T(8,128)(2,1)S(1)}, u32[]{:S(2)}, u32[]{:S(2)}) collective-permute-start(bf16[4,256,256]{2,1,0:T(8,128)(2,1)S(1)} %shard_map.88.part_ref), channel_id=1, source_target_pairs={{0,8},{8,0},{16,24},{24,16},{1,9},{9,1},{17,25},{25,17},{2,10},{10... | collective-permute-start | bytes 1572872 | tf_op jit(solution)/shard_map/ppermute | solution.py:436

commit v6 on v5

--- a/solution.py
+++ b/solution.py
@@ -437,11 +437,12 @@
         return totals[-1]
 
     for layer in range(layers):
-        ready = flat if layer else [keys[1], along[1][0]]
+        ready = [] if layer else [keys[1], along[1][0]]
         own_stats = row_stats(after(places[layer], *ready), keys[layer], values[layer], pieces[layer])
         stats.append(everywhere(own_stats, n_inp))
+    for layer in range(layers):
         results = attention_grads(
-            after(places[layer], *flat), keys[layer], values[layer], pieces[layer], stats[layer]
+            after(places[layer], *(flat or [stats[-1][0]])), keys[layer], values[layer], pieces[layer], stats[layer]
         )
         keep += results[:PARTS]
         send += results[PARTS : 2 * PARTS]

time: 147 us -> 148 us (level)
  starting transfers between devices: 42.8 us -> 48.6 us
  waiting for transfers between devices: 53.9 us -> 49.8 us
    ppermute x6, waiting for transfers between devices: 6.75 us -> 0.08 us  [everywhere(): lax.ppermute(value, 'inp', partners(n_inp, mask))]
    ppermute x2, starting transfers between devices: 12.8 us -> 16.2 us  [line_sum(): other.append(lax.ppermute(mine[-1], 'inp', partners(n_inp, 1)))]
    ppermute x2, starting transfers between devices: 3.83 us -> 5.8 us  [line_sum(): lax.ppermute(after(value, *earlier), 'inp', [(0, 3), (3, 0), (1, 2), (2,...]
    ppermute x6, starting transfers between devices: 4.55 us -> 2.95 us  [to_owners(): lax.ppermute(part, 'tgt', partners(n_tgt, mask))]
  transfers between devices with their start and end apart: 27 -> 27, of which waited for: 16 -> 15; matrix products, arithmetic and copies ran while one was open for 0% -> 0% of each run, Pallas kernels for 28% -> 29%
where the time goes in v6:
time: 148 us
  waiting for transfers between devices  49.8 us (34%)
  starting transfers between devices  48.6 us (33%)
  Pallas kernels  46.1 us (31%)
  local copies, waits for them, and re-layouts  2.49 us (2%)
    ppermute x2, starting transfers between devices, line_sum(): other.append(lax.ppermute(mine[-1], 'inp', partners(n_inp, 1)))  16.2 us
    ppermute x2, waiting for transfers between devices, line_sum(): lax.ppermute(after(value, *earlier), 'inp', [(0, 3), (3, 0), (1, 2), (2,...  14.4 us
    pallas_call x2, Pallas kernels, project(): pl.pallas_call(project_kernel, grid=(width // depth,), in_specs=[pl.Block...  11 us
    pallas_call x2, Pallas kernels, back_blocks(): pl.pallas_call(back_kernel, grid_spec=pltpu.PrefetchScalarGridSpec(num_sc...  10.9 us
    ppermute x6, starting transfers between devices, everywhere(): lax.ppermute(value, 'inp', partners(n_inp, mask))  10.3 us
    pallas_call x4, Pallas kernels, join_heads(): pl.pallas_call(join_kernel, grid_spec=pltpu.PrefetchScalarGridSpec(num_sc...  9.73 us
    ppermute x2, waiting for transfers between devices, line_sum(): other.append(lax.ppermute(mine[-1], 'inp', partners(n_inp, 1)))  8.84 us
    pallas_call x2, Pallas kernels, attention_grads(): pl.pallas_call(functools.partial(grads_kernel, count), grid_spec=pltpu.Pr...  8.14 us
  transfers between devices with their start and end apart: 27, of which 15 were waited for; matrix products, arithmetic and copies ran while one was open for 0% of the time, Pallas kernels for 29%

profile of v6, /device:TPU:0, one launch (start us, length us, event | category | flops | bytes accessed | tf_op | source)
XLA Modules:
  0.0 148.1 jit_solution(1172277798259935468)
XLA Ops:
  0.7 0.1 add_add_fusion
  0.7 0.1 pad_add_fusion
  0.8 2.0 %copy.15 = bf16[2,512,4,256]{3,1,0,2:T(8,128)(2,1)S(1)} copy(bf16[2,512,4,256]{3,2,1,0:T(4,128)(2,1)} %param.8) | data formatting | bytes 4194304 | tf_op jit(solution)/shard_map/optimization_barrier | solution.py:374
  2.8 0.2 copy-done
  3.0 0.3 copy.14
  3.4 3.0 %collective-permute-start = (bf16[2,512,256]{2,1,0:T(8,128)(2,1)S(1)}, bf16[2,512,256]{2,1,0:T(8,128)(2,1)S(1)}, u32[]{:S(2)}, u32[]{:S(2)}) collective-permute-start(bf16[2,512,256]{2,1,0:T(8,128)(2,1)S(1)} %shard_map.68), channel_id=1, source_target_pairs={{0,4},{2,6},{4,0},{6,2},{8,14},{10,12},{12,10},{14,8},{16,20},{18,... | collective-permute-start | bytes 1572872 | tf_op jit(solution)/shard_map/ppermute | solution.py:337
  6.5 5.5 %shard_map.72 = (bf16[1,512,256]{2,1,0:T(8,128)(2,1)S(1)}, bf16[1,512,256]{2,1,0:T(8,128)(2,1)S(1)}) custom-call(bf16[512,4096]{1,0:T(8,128)(2,1)} %enc_ref.1, bf16[2,4096,256]{2,1,0:T(8,128)(2,1)} %bitcast.40, bf16[2,4096,256]{2,1,0:T(8,128)(2,1)} %bitcast.44), custom_call_target="tpu_custom_call" | custom-call | flops 2147483648 | bytes 8388608 | tf_op jit(solution)/shard_map/pallas_call | solution.py:123
  12.0 0.1 shard_map.73
  12.1 0.1 collective-permute-start.1
  12.1 0.1 collective-permute-start.2
  12.2 6.9 %collective-permute-done.refs_2_.refs_6_ = bf16[2,512,256]{2,1,0:T(8,128)(2,1)S(1)} collective-permute-done((bf16[2,512,256]{2,1,0:T(8,128)(2,1)S(1)}, bf16[2,512,256]{2,1,0:T(8,128)(2,1)S(1)}, u32[]{:S(2)}, u32[]{:S(2)}) %collective-permute-start) | collective-permute-done | bytes 524320 | tf_op jit(solution)/shard_map/ppermute | solution.py:337
  19.1 1.5 %collective-permute-start.4 = (bf16[2,512,256]{2,1,0:T(8,128)(2,1)S(1)}, bf16[2,512,256]{2,1,0:T(8,128)(2,1)S(1)}, u32[]{:S(2)}, u32[]{:S(2)}) collective-permute-start(bf16[2,512,256]{2,1,0:T(8,128)(2,1)S(1)} %collective-permute-done.refs_2_.refs_6_), channel_id=1, source_target_pairs={{0,8},{8,0},{16,24},{24,16},{1,9},{9,1},{17,25},{25,17},{2,10},{10... | collective-permute-start | bytes 1572872 | tf_op jit(solution)/shard_map/ppermute | solution.py:395
  20.6 1.0 collective-permute-start.3
  21.6 5.5 %shard_map.69 = (bf16[1,512,256]{2,1,0:T(8,128)(2,1)S(1)}, bf16[1,512,256]{2,1,0:T(8,128)(2,1)S(1)}) custom-call(bf16[512,4096]{1,0:T(8,128)(2,1)} %enc_ref.1, bf16[2,4096,256]{2,1,0:T(8,128)(2,1)} %bitcast.41, bf16[2,4096,256]{2,1,0:T(8,128)(2,1)} %bitcast.45), custom_call_target="tpu_custom_call" | custom-call | flops 2147483648 | bytes 8388608 | tf_op jit(solution)/shard_map/pallas_call | solution.py:123
  27.1 3.3 %collective-permute-done.2.refs_2_.refs_6_ = bf16[2,512,256]{2,1,0:T(8,128)(2,1)S(1)} collective-permute-done((bf16[2,512,256]{2,1,0:T(8,128)(2,1)S(1)}, bf16[2,512,256]{2,1,0:T(8,128)(2,1)S(1)}, u32[]{:S(2)}, u32[]{:S(2)}) %collective-permute-start.2) | collective-permute-done | bytes 524320 | tf_op jit(solution)/shard_map/ppermute | solution.py:386
  30.4 2.5 %collective-permute-done.4.refs_3_.refs_7_ = bf16[2,512,256]{2,1,0:T(8,128)(2,1)S(1)} collective-permute-done((bf16[2,512,256]{2,1,0:T(8,128)(2,1)S(1)}, bf16[2,512,256]{2,1,0:T(8,128)(2,1)S(1)}, u32[]{:S(2)}, u32[]{:S(2)}) %collective-permute-start.4) | collective-permute-done | bytes 524320 | tf_op jit(solution)/shard_map/ppermute | solution.py:395
  32.8 2.1 %shard_map.75.refs_8_ = f32[4,2048]{1,0:T(4,128)S(1)} custom-call(s32[3]{0:T(128)S(1)} %get-tuple-element.67.place_ref, bf16[1,512,256]{2,1,0:T(8,128)(2,1)S(1)} %get-tuple-element.62.k_ref, bf16[1,512,256]{2,1,0:T(8,128)(2,1)S(1)} %get-tuple-element.65.v_ref, bf16[4,2,512,256]{3,2,1,0:T(8,128)(2,1)S(1)} %bitcast.28, ...), custom_call_target="tpu_custom_call" | custom-call | flops 1073741824 | bytes 2621440 | tf_op jit(solution)/shard_map/pallas_call | solution.py:175
  35.0 3.8 %collective-permute-start.7 = (f32[4,2048]{1,0:T(4,128)S(1)}, f32[4,2048]{1,0:T(4,128)S(1)}, u32[]{:S(2)}, u32[]{:S(2)}) collective-permute-start(f32[4,2048]{1,0:T(4,128)S(1)} %shard_map.75.refs_8_), channel_id=1, source_target_pairs={{0,24},{8,16},{16,8},{24,0},{1,25},{9,17},{17,9},{25,1},{2,26},{10... | collective-permute-start | bytes 98312 | tf_op jit(solution)/shard_map/ppermute | solution.py:342
  38.8 0.6 collective-permute-start.5
  39.5 0.5 collective-permute-done.3.refs_3_.refs_7_
  40.0 2.1 %shard_map.74.refs_8_ = f32[4,2048]{1,0:T(4,128)S(1)} custom-call(s32[3]{0:T(128)S(1)} %get-tuple-element.70.place_ref, bf16[1,512,256]{2,1,0:T(8,128)(2,1)S(1)} %get-tuple-element.54.k_ref, bf16[1,512,256]{2,1,0:T(8,128)(2,1)S(1)} %get-tuple-element.55.v_ref, bf16[4,2,512,256]{3,2,1,0:T(8,128)(2,1)S(1)} %bitcast.29, ...), custom_call_target="tpu_custom_call" | custom-call | flops 1073741824 | bytes 2621440 | tf_op jit(solution)/shard_map/pallas_call | solution.py:175
  42.2 5.2 %collective-permute-start.10 = (f32[4,2048]{1,0:T(4,128)S(1)}, f32[4,2048]{1,0:T(4,128)S(1)}, u32[]{:S(2)}, u32[]{:S(2)}) collective-permute-start(f32[4,2048]{1,0:T(4,128)S(1)} %shard_map.74.refs_8_), channel_id=1, source_target_pairs={{0,24},{8,16},{16,8},{24,0},{1,25},{9,17},{17,9},{25,1},{2,26},{10... | collective-permute-start | bytes 98312 | tf_op jit(solution)/shard_map/ppermute | solution.py:342
  47.4 0.6 collective-permute-start.8
  48.0 4.1 %shard_map.76 = (bf16[4,256,256]{2,1,0:T(8,128)(2,1)S(1)}, bf16[4,256,256]{2,1,0:T(8,128)(2,1)S(1)}, bf16[512,256]{1,0:T(8,128)(2,1)S(1)}, bf16[512,256]{1,0:T(8,128)(2,1)S(1)}) custom-call(s32[3]{0:T(128)S(1)} %get-tuple-element.67.place_ref, bf16[1,512,256]{2,1,0:T(8,128)(2,1)S(1)} %get-tuple-element.62.k_ref, ...), custom_call_target="tpu_custom_call" | custom-call | flops 2684354560 | bytes 3932160 | tf_op jit(solution)/shard_map/pallas_call | solution.py:229
  52.1 0.1 collective-permute-done.9.refs_10_
  52.2 1.4 collective-permute-start.11
  53.6 4.1 %shard_map.77 = (bf16[4,256,256]{2,1,0:T(8,128)(2,1)S(1)}, bf16[4,256,256]{2,1,0:T(8,128)(2,1)S(1)}, bf16[512,256]{1,0:T(8,128)(2,1)S(1)}, bf16[512,256]{1,0:T(8,128)(2,1)S(1)}) custom-call(s32[3]{0:T(128)S(1)} %get-tuple-element.70.place_ref, bf16[1,512,256]{2,1,0:T(8,128)(2,1)S(1)} %get-tuple-element.54.k_ref, ...), custom_call_target="tpu_custom_call" | custom-call | flops 2684354560 | bytes 3932160 | tf_op jit(solution)/shard_map/pallas_call | solution.py:229
  57.6 5.5 %shard_map.78 = bf16[4,512,512]{2,1,0:T(8,128)(2,1)S(1)} custom-call(s32[4]{0:T(128)S(1)} %get-tuple-element.74.order_ref, bf16[2,4096,256]{2,1,0:T(8,128)(2,1)} %bitcast.42, bf16[2,4096,256]{2,1,0:T(8,128)(2,1)} %bitcast.46, bf16[512,256]{1,0:T(8,128)(2,1)S(1)} %get-tuple-element.68.refs_0_, bf16[512,256]{1,0:T(8,128)(2,1)S(1)} %get-tuple-element.69.refs_1_, ...), custom_call_target="tpu_custom_call" | custom-call | flops 2147483648 | bytes 8388608 | tf_op jit(solution)/shard_map/pallas_call | solution.py:260
  63.2 2.4 %collective-permute-done.11.two_ref = bf16[4,256,256]{2,1,0:T(8,128)(2,1)S(1)} collective-permute-done((bf16[4,256,256]{2,1,0:T(8,128)(2,1)S(1)}, bf16[4,256,256]{2,1,0:T(8,128)(2,1)S(1)}, u32[]{:S(2)}, u32[]{:S(2)}) %collective-permute-start.11) | collective-permute-done | bytes 524320 | tf_op jit(solution)/shard_map/ppermute | solution.py:420
  65.6 0.1 shard_map.79.one_ref
  65.7 0.1 collective-permute-start.13
  65.8 1.4 collective-permute-start.12
  67.2 2.4 %collective-permute-start.17 = (bf16[4,256,256]{2,1,0:T(8,128)(2,1)S(1)}, bf16[4,256,256]{2,1,0:T(8,128)(2,1)S(1)}, u32[]{:S(2)}, u32[]{:S(2)}) collective-permute-start(bf16[4,256,256]{2,1,0:T(8,128)(2,1)S(1)} %shard_map.79.one_ref), channel_id=1, source_target_pairs={{0,24},{24,0},{8,16},{16,8},{1,25},{25,1},{9,17},{17,9},{2,26},{26... | collective-permute-start | bytes 1572872 | tf_op jit(solution)/shard_map/ppermute | solution.py:433
  69.6 5.3 %shard_map.81.refs_0_ = f32[4,512,512]{2,1,0:T(8,128)S(1)} custom-call(s32[4]{0:T(128)S(1)} %get-tuple-element.82.order_ref, bf16[2,4096,256]{2,1,0:T(8,128)(2,1)} %bitcast.43, bf16[2,4096,256]{2,1,0:T(8,128)(2,1)} %bitcast.47, bf16[512,256]{1,0:T(8,128)(2,1)S(1)} %get-tuple-element.68.refs_0_, bf16[512,256]{1,0:T(8,128)(2,1)S(1)} %get-tuple-element.69.refs_1_, ...), custom_call_target="tpu_custom_call" | custom-call | flops 2147483648 | bytes 8388608 | tf_op jit(solution)/shard_map/pallas_call | solution.py:260
  74.9 0.1 shard_map.82
  75.0 1.6 %collective-permute-start.14 = (bf16[1,512,512]{2,1,0:T(8,128)(2,1)S(1)}, bf16[1,512,512]{2,1,0:T(8,128)(2,1)S(1)}, u32[]{:S(2)}, u32[]{:S(2)}) collective-permute-start(bf16[1,512,512]{2,1,0:T(8,128)(2,1)S(1)} %shard_map.82), channel_id=1, source_target_pairs={{0,4},{2,6},{4,0},{6,2},{1,5},{3,7},{5,1},{7,3},{8,12},{10,14},{12... | collective-permute-start | bytes 1572872 | tf_op jit(solution)/shard_map/ppermute | solution.py:463
  76.6 3.5 %collective-permute-done.12.two_ref = bf16[4,256,256]{2,1,0:T(8,128)(2,1)S(1)} collective-permute-done((bf16[4,256,256]{2,1,0:T(8,128)(2,1)S(1)}, bf16[4,256,256]{2,1,0:T(8,128)(2,1)S(1)}, u32[]{:S(2)}, u32[]{:S(2)}) %collective-permute-start.12) | collective-permute-done | bytes 524320 | tf_op jit(solution)/shard_map/ppermute | solution.py:420
  80.1 0.1 shard_map.80.one_ref
  80.2 0.1 shard_map.84
  80.3 1.6 %collective-permute-start.16 = (bf16[1,512,512]{2,1,0:T(8,128)(2,1)S(1)}, bf16[1,512,512]{2,1,0:T(8,128)(2,1)S(1)}, u32[]{:S(2)}, u32[]{:S(2)}) collective-permute-start(bf16[1,512,512]{2,1,0:T(8,128)(2,1)S(1)} %shard_map.84), channel_id=1, source_target_pairs={{0,4},{2,6},{4,0},{6,2},{1,5},{3,7},{5,1},{7,3},{8,12},{10,14},{12... | collective-permute-start | bytes 1572872 | tf_op jit(solution)/shard_map/ppermute | solution.py:464
  81.9 11.3 %collective-permute-done.17.two_ref = bf16[4,256,256]{2,1,0:T(8,128)(2,1)S(1)} collective-permute-done((bf16[4,256,256]{2,1,0:T(8,128)(2,1)S(1)}, bf16[4,256,256]{2,1,0:T(8,128)(2,1)S(1)}, u32[]{:S(2)}, u32[]{:S(2)}) %collective-permute-start.17) | collective-permute-done | bytes 524320 | tf_op jit(solution)/shard_map/ppermute | solution.py:433
  93.2 0.1 shard_map.85
  93.3 0.2 shard_map.83
  93.5 1.6 %collective-permute-start.15 = (bf16[1,512,512]{2,1,0:T(8,128)(2,1)S(1)}, bf16[1,512,512]{2,1,0:T(8,128)(2,1)S(1)}, u32[]{:S(2)}, u32[]{:S(2)}) collective-permute-start(bf16[1,512,512]{2,1,0:T(8,128)(2,1)S(1)} %shard_map.83), channel_id=1, source_target_pairs={{0,1},{1,0},{2,3},{3,2},{4,5},{5,4},{6,7},{7,6},{8,9},{9,8},{10,11... | collective-permute-start | bytes 1572872 | tf_op jit(solution)/shard_map/ppermute | solution.py:467
  95.1 3.4 %collective-permute-start.21 = (bf16[4,256,256]{2,1,0:T(8,128)(2,1)S(1)}, bf16[4,256,256]{2,1,0:T(8,128)(2,1)S(1)}, u32[]{:S(2)}, u32[]{:S(2)}) collective-permute-start(bf16[4,256,256]{2,1,0:T(8,128)(2,1)S(1)} %shard_map.80.one_ref), channel_id=1, source_target_pairs={{0,24},{24,0},{8,16},{16,8},{1,25},{25,1},{9,17},{17,9},{2,26},{26... | collective-permute-start | bytes 1572872 | tf_op jit(solution)/shard_map/ppermute | solution.py:433
  98.5 0.5 collective-permute-start.19
  99.0 0.8 collective-permute-done.18.refs_1_
  99.8 0.5 collective-permute-start.20
  100.4 4.4 %collective-permute-done.19.refs_2_ = bf16[256,256]{1,0:T(8,128)(2,1)S(1)} collective-permute-done((bf16[256,256]{1,0:T(8,128)(2,1)S(1)}, bf16[256,256]{1,0:T(8,128)(2,1)S(1)}, u32[]{:S(2)}, u32[]{:S(2)}) %collective-permute-start.19) | collective-permute-done | bytes 131104 | tf_op jit(solution)/shard_map/ppermute | solution.py:352
  104.8 2.0 %collective-permute-done.20.refs_3_ = bf16[256,256]{1,0:T(8,128)(2,1)S(1)} collective-permute-done((bf16[256,256]{1,0:T(8,128)(2,1)S(1)}, bf16[256,256]{1,0:T(8,128)(2,1)S(1)}, u32[]{:S(2)}, u32[]{:S(2)}) %collective-permute-start.20) | collective-permute-done | bytes 131104 | tf_op jit(solution)/shard_map/ppermute | solution.py:352
  106.9 0.1 collective-permute-done.15.refs_3_
  107.0 3.2 %collective-permute-done.21.two_ref = bf16[4,256,256]{2,1,0:T(8,128)(2,1)S(1)} collective-permute-done((bf16[4,256,256]{2,1,0:T(8,128)(2,1)S(1)}, bf16[4,256,256]{2,1,0:T(8,128)(2,1)S(1)}, u32[]{:S(2)}, u32[]{:S(2)}) %collective-permute-start.21) | collective-permute-done | bytes 524320 | tf_op jit(solution)/shard_map/ppermute | solution.py:433
  110.1 0.1 shard_map.87
  110.3 1.6 %collective-permute-start.23 = (bf16[256,256]{1,0:T(8,128)(2,1)S(1)}, bf16[256,256]{1,0:T(8,128)(2,1)S(1)}, u32[]{:S(2)}, u32[]{:S(2)}) collective-permute-start(bf16[256,256]{1,0:T(8,128)(2,1)S(1)} %get-tuple-element.94), channel_id=1, source_target_pairs={{0,4},{2,6},{4,0},{6,2},{1,5},{3,7},{5,1},{7,3},{8,12},{10,14},{12... | collective-permute-start | bytes 393224 | tf_op jit(solution)/shard_map/ppermute | solution.py:352
  111.9 0.3 collective-permute-start.24
  112.2 9.8 %collective-permute-start.26 = (bf16[4,256,256]{2,1,0:T(8,128)(2,1)S(1)}, bf16[4,256,256]{2,1,0:T(8,128)(2,1)S(1)}, u32[]{:S(2)}, u32[]{:S(2)}) collective-permute-start(bf16[4,256,256]{2,1,0:T(8,128)(2,1)S(1)} %shard_map.86.part_ref), channel_id=1, source_target_pairs={{0,8},{8,0},{16,24},{24,16},{1,9},{9,1},{17,25},{25,17},{2,10},{10... | collective-permute-start | bytes 1572872 | tf_op jit(solution)/shard_map/ppermute | solution.py:436
  122.0 6.5 %collective-permute-start.25 = (bf16[4,256,256]{2,1,0:T(8,128)(2,1)S(1)}, bf16[4,256,256]{2,1,0:T(8,128)(2,1)S(1)}, u32[]{:S(2)}, u32[]{:S(2)}) collective-permute-start(bf16[4,256,256]{2,1,0:T(8,128)(2,1)S(1)} %shard_map.88.part_ref), channel_id=1, source_target_pairs={{0,8},{8,0},{16,24},{24,16},{1,9},{9,1},{17,25},{25,17},{2,10},{10... | collective-permute-start | bytes 1572872 | tf_op jit(solution)/shard_map/ppermute | solution.py:436
  128.5 2.4 %shard_map.89.rest_0_ = bf16[2,512,4,256]{3,2,1,0:T(4,128)(2,1)} custom-call(s32[3]{0:T(128)S(1)} %get-tuple-element.67.place_ref, bf16[4,256,256]{2,1,0:T(8,128)(2,1)S(1)} %shard_map.86.part_ref), custom_call_target="tpu_custom_call" | custom-call | bytes 1048576 | tf_op jit(solution)/shard_map/pallas_call | solution.py:86
  130.9 3.8 %collective-permute-done.26.part_ref = bf16[4,256,256]{2,1,0:T(8,128)(2,1)S(1)} collective-permute-done((bf16[4,256,256]{2,1,0:T(8,128)(2,1)S(1)}, bf16[4,256,256]{2,1,0:T(8,128)(2,1)S(1)}, u32[]{:S(2)}, u32[]{:S(2)}) %collective-permute-start.26) | collective-permute-done | bytes 524320 | tf_op jit(solution)/shard_map/ppermute | solution.py:436
  134.7 2.4 %shard_map.90.rest_0_ = bf16[2,512,4,256]{3,2,1,0:T(4,128)(2,1)} custom-call(s32[3]{0:T(128)S(1)} %get-tuple-element.67.place_ref, bf16[4,256,256]{2,1,0:T(8,128)(2,1)S(1)} %collective-permute-done.26.part_ref, bf16[2,512,4,256]{3,2,1,0:T(4,128)(2,1)} %shard_map.89.rest_0_), custom_call_target="tpu_custom_call", output_to_operand_aliasing={{}: (2, {})} | custom-call | bytes 1048576 | tf_op jit(solution)/shard_map/pallas_call | solution.py:86
  137.2 1.0 shard_map.93
  138.2 2.4 %shard_map.91.rest_0_ = bf16[2,512,4,256]{3,2,1,0:T(4,128)(2,1)} custom-call(s32[3]{0:T(128)S(1)} %get-tuple-element.67.place_ref, bf16[4,256,256]{2,1,0:T(8,128)(2,1)S(1)} %shard_map.88.part_ref, bf16[2,512,4,256]{3,2,1,0:T(4,128)(2,1)} %shard_map.90.rest_0_), custom_call_target="tpu_custom_call", output_to_operand_aliasing={{}: (2, {})} | custom-call | bytes 1048576 | tf_op jit(solution)/shard_map/pallas_call | solution.py:86
  140.6 5.0 %collective-permute-done.25.part_ref = bf16[4,256,256]{2,1,0:T(8,128)(2,1)S(1)} collective-permute-done((bf16[4,256,256]{2,1,0:T(8,128)(2,1)S(1)}, bf16[4,256,256]{2,1,0:T(8,128)(2,1)S(1)}, u32[]{:S(2)}, u32[]{:S(2)}) %collective-permute-start.25) | collective-permute-done | bytes 524320 | tf_op jit(solution)/shard_map/ppermute | solution.py:436
  145.6 2.4 %shard_map.92 = bf16[2,512,4,256]{3,2,1,0:T(4,128)(2,1)} custom-call(s32[3]{0:T(128)S(1)} %get-tuple-element.67.place_ref, bf16[4,256,256]{2,1,0:T(8,128)(2,1)S(1)} %collective-permute-done.25.part_ref, bf16[2,512,4,256]{3,2,1,0:T(4,128)(2,1)} %shard_map.91.rest_0_), custom_call_target="tpu_custom_call", output_to_operand_aliasing={{}: (2, {})} | custom-call | bytes 1048576 | tf_op jit(solution)/shard_map/pallas_call | solution.py:86
  (22 shorter events, 0.3 us)
Async XLA Ops:
  0.8 2.2 %copy-start = (bf16[2,512,4,256]{3,2,1,0:T(4,128)(2,1)S(1)}, bf16[2,512,4,256]{3,2,1,0:T(4,128)(2,1)}, u32[]{:S(2)}) copy-start(bf16[2,512,4,256]{3,2,1,0:T(4,128)(2,1)} %param.9) | copy-start | bytes 6291460
  3.4 15.8 %collective-permute-start = (bf16[2,512,256]{2,1,0:T(8,128)(2,1)S(1)}, bf16[2,512,256]{2,1,0:T(8,128)(2,1)S(1)}, u32[]{:S(2)}, u32[]{:S(2)}) collective-permute-start(bf16[2,512,256]{2,1,0:T(8,128)(2,1)S(1)} %shard_map.68), channel_id=1, source_target_pairs={{0,4},{2,6},{4,0},{6,2},{8,14},{10,12},{12,10},{14,8},{16,20},{18,... | collective-permute-start | bytes 1572872 | tf_op jit(solution)/shard_map/ppermute | solution.py:337
  12.1 20.8 %collective-permute-start.1 = (bf16[4,512,256]{2,1,0:T(8,128)(2,1)S(1)}, bf16[4,512,256]{2,1,0:T(8,128)(2,1)S(1)}, u32[]{:S(2)}, u32[]{:S(2)}) collective-permute-start(bf16[4,512,256]{2,1,0:T(8,128)(2,1)S(1)} %shard_map.73), channel_id=1, source_target_pairs={{0,2},{2,0},{4,6},{6,4},{1,3},{3,1},{5,7},{7,5},{8,10},{10,8},{12,... | collective-permute-start | bytes 3145736 | tf_op jit(solution)/shard_map/ppermute | solution.py:394
  12.1 18.2 %collective-permute-start.2 = (bf16[2,512,256]{2,1,0:T(8,128)(2,1)S(1)}, bf16[2,512,256]{2,1,0:T(8,128)(2,1)S(1)}, u32[]{:S(2)}, u32[]{:S(2)}) collective-permute-start(bf16[2,512,256]{2,1,0:T(8,128)(2,1)S(1)} %shard_map.70), channel_id=1, source_target_pairs={{0,4},{2,6},{4,0},{6,2},{1,5},{3,7},{5,1},{7,3},{8,12},{10,14},{12... | collective-permute-start | bytes 1572872 | tf_op jit(solution)/shard_map/ppermute | solution.py:386
  19.1 13.7 %collective-permute-start.4 = (bf16[2,512,256]{2,1,0:T(8,128)(2,1)S(1)}, bf16[2,512,256]{2,1,0:T(8,128)(2,1)S(1)}, u32[]{:S(2)}, u32[]{:S(2)}) collective-permute-start(bf16[2,512,256]{2,1,0:T(8,128)(2,1)S(1)} %collective-permute-done.refs_2_.refs_6_), channel_id=1, source_target_pairs={{0,8},{8,0},{16,24},{24,16},{1,9},{9,1},{17,25},{25,17},{2,10},{10... | collective-permute-start | bytes 1572872 | tf_op jit(solution)/shard_map/ppermute | solution.py:395
  20.6 19.4 %collective-permute-start.3 = (bf16[2,512,256]{2,1,0:T(8,128)(2,1)S(1)}, bf16[2,512,256]{2,1,0:T(8,128)(2,1)S(1)}, u32[]{:S(2)}, u32[]{:S(2)}) collective-permute-start(bf16[2,512,256]{2,1,0:T(8,128)(2,1)S(1)} %shard_map.71), channel_id=1, source_target_pairs={{0,6},{2,4},{4,2},{6,0},{1,7},{3,5},{5,3},{7,1},{8,14},{10,12},{12... | collective-permute-start | bytes 1572872 | tf_op jit(solution)/shard_map/ppermute | solution.py:386
  35.0 12.4 %collective-permute-start.7 = (f32[4,2048]{1,0:T(4,128)S(1)}, f32[4,2048]{1,0:T(4,128)S(1)}, u32[]{:S(2)}, u32[]{:S(2)}) collective-permute-start(f32[4,2048]{1,0:T(4,128)S(1)} %shard_map.75.refs_8_), channel_id=1, source_target_pairs={{0,24},{8,16},{16,8},{24,0},{1,25},{9,17},{17,9},{25,1},{2,26},{10... | collective-permute-start | bytes 98312 | tf_op jit(solution)/shard_map/ppermute | solution.py:342
  38.8 9.2 %collective-permute-start.6 = (f32[4,2048]{1,0:T(4,128)S(1)}, f32[4,2048]{1,0:T(4,128)S(1)}, u32[]{:S(2)}, u32[]{:S(2)}) collective-permute-start(f32[4,2048]{1,0:T(4,128)S(1)} %shard_map.75.refs_8_), channel_id=1, source_target_pairs={{0,16},{8,24},{16,0},{24,8},{1,17},{9,25},{17,1},{25,9},{2,18},{10... | collective-permute-start | bytes 98312 | tf_op jit(solution)/shard_map/ppermute | solution.py:342
  38.8 9.2 %collective-permute-start.5 = (f32[4,2048]{1,0:T(4,128)S(1)}, f32[4,2048]{1,0:T(4,128)S(1)}, u32[]{:S(2)}, u32[]{:S(2)}) collective-permute-start(f32[4,2048]{1,0:T(4,128)S(1)} %shard_map.75.refs_8_), channel_id=1, source_target_pairs={{0,8},{8,0},{16,24},{24,16},{1,9},{9,1},{17,25},{25,17},{2,10},{10... | collective-permute-start | bytes 98312 | tf_op jit(solution)/shard_map/ppermute | solution.py:342
  42.2 9.9 %collective-permute-start.10 = (f32[4,2048]{1,0:T(4,128)S(1)}, f32[4,2048]{1,0:T(4,128)S(1)}, u32[]{:S(2)}, u32[]{:S(2)}) collective-permute-start(f32[4,2048]{1,0:T(4,128)S(1)} %shard_map.74.refs_8_), channel_id=1, source_target_pairs={{0,24},{8,16},{16,8},{24,0},{1,25},{9,17},{17,9},{25,1},{2,26},{10... | collective-permute-start | bytes 98312 | tf_op jit(solution)/shard_map/ppermute | solution.py:342
  47.3 4.8 %collective-permute-start.9 = (f32[4,2048]{1,0:T(4,128)S(1)}, f32[4,2048]{1,0:T(4,128)S(1)}, u32[]{:S(2)}, u32[]{:S(2)}) collective-permute-start(f32[4,2048]{1,0:T(4,128)S(1)} %shard_map.74.refs_8_), channel_id=1, source_target_pairs={{0,16},{8,24},{16,0},{24,8},{1,17},{9,25},{17,1},{25,9},{2,18},{10... | collective-permute-start | bytes 98312 | tf_op jit(solution)/shard_map/ppermute | solution.py:342
  47.4 4.8 %collective-permute-start.8 = (f32[4,2048]{1,0:T(4,128)S(1)}, f32[4,2048]{1,0:T(4,128)S(1)}, u32[]{:S(2)}, u32[]{:S(2)}) collective-permute-start(f32[4,2048]{1,0:T(4,128)S(1)} %shard_map.74.refs_8_), channel_id=1, source_target_pairs={{0,8},{8,0},{16,24},{24,16},{1,9},{9,1},{17,25},{25,17},{2,10},{10... | collective-permute-start | bytes 98312 | tf_op jit(solution)/shard_map/ppermute | solution.py:342
  52.2 13.4 %collective-permute-start.11 = (bf16[4,256,256]{2,1,0:T(8,128)(2,1)S(1)}, bf16[4,256,256]{2,1,0:T(8,128)(2,1)S(1)}, u32[]{:S(2)}, u32[]{:S(2)}) collective-permute-start(bf16[4,256,256]{2,1,0:T(8,128)(2,1)S(1)} %get-tuple-element.79), channel_id=1, source_target_pairs={{0,8},{8,0},{16,24},{24,16},{1,9},{9,1},{17,25},{25,17},{2,10},{10... | collective-permute-start | bytes 1572872 | tf_op jit(solution)/shard_map/ppermute | solution.py:420
  65.7 9.2 %collective-permute-start.13 = (bf16[4,512,512]{2,1,0:T(8,128)(2,1)S(1)}, bf16[4,512,512]{2,1,0:T(8,128)(2,1)S(1)}, u32[]{:S(2)}, u32[]{:S(2)}) collective-permute-start(bf16[4,512,512]{2,1,0:T(8,128)(2,1)S(1)} %shard_map.78), channel_id=1, source_target_pairs={{0,2},{2,0},{4,6},{6,4},{1,3},{3,1},{5,7},{7,5},{8,10},{10,8},{12,... | collective-permute-start | bytes 6291464 | tf_op jit(solution)/shard_map/ppermute | solution.py:458
  65.8 14.3 %collective-permute-start.12 = (bf16[4,256,256]{2,1,0:T(8,128)(2,1)S(1)}, bf16[4,256,256]{2,1,0:T(8,128)(2,1)S(1)}, u32[]{:S(2)}, u32[]{:S(2)}) collective-permute-start(bf16[4,256,256]{2,1,0:T(8,128)(2,1)S(1)} %get-tuple-element.80), channel_id=1, source_target_pairs={{0,8},{8,0},{16,24},{24,16},{1,9},{9,1},{17,25},{25,17},{2,10},{10... | collective-permute-start | bytes 1572872 | tf_op jit(solution)/shard_map/ppermute | solution.py:420
  67.2 26.0 %collective-permute-start.17 = (bf16[4,256,256]{2,1,0:T(8,128)(2,1)S(1)}, bf16[4,256,256]{2,1,0:T(8,128)(2,1)S(1)}, u32[]{:S(2)}, u32[]{:S(2)}) collective-permute-start(bf16[4,256,256]{2,1,0:T(8,128)(2,1)S(1)} %shard_map.79.one_ref), channel_id=1, source_target_pairs={{0,24},{24,0},{8,16},{16,8},{1,25},{25,1},{9,17},{17,9},{2,26},{26... | collective-permute-start | bytes 1572872 | tf_op jit(solution)/shard_map/ppermute | solution.py:433
  75.0 18.3 %collective-permute-start.14 = (bf16[1,512,512]{2,1,0:T(8,128)(2,1)S(1)}, bf16[1,512,512]{2,1,0:T(8,128)(2,1)S(1)}, u32[]{:S(2)}, u32[]{:S(2)}) collective-permute-start(bf16[1,512,512]{2,1,0:T(8,128)(2,1)S(1)} %shard_map.82), channel_id=1, source_target_pairs={{0,4},{2,6},{4,0},{6,2},{1,5},{3,7},{5,1},{7,3},{8,12},{10,14},{12... | collective-permute-start | bytes 1572872 | tf_op jit(solution)/shard_map/ppermute | solution.py:463
  80.3 26.5 %collective-permute-start.16 = (bf16[1,512,512]{2,1,0:T(8,128)(2,1)S(1)}, bf16[1,512,512]{2,1,0:T(8,128)(2,1)S(1)}, u32[]{:S(2)}, u32[]{:S(2)}) collective-permute-start(bf16[1,512,512]{2,1,0:T(8,128)(2,1)S(1)} %shard_map.84), channel_id=1, source_target_pairs={{0,4},{2,6},{4,0},{6,2},{1,5},{3,7},{5,1},{7,3},{8,12},{10,14},{12... | collective-permute-start | bytes 1572872 | tf_op jit(solution)/shard_map/ppermute | solution.py:464
  93.5 13.5 %collective-permute-start.15 = (bf16[1,512,512]{2,1,0:T(8,128)(2,1)S(1)}, bf16[1,512,512]{2,1,0:T(8,128)(2,1)S(1)}, u32[]{:S(2)}, u32[]{:S(2)}) collective-permute-start(bf16[1,512,512]{2,1,0:T(8,128)(2,1)S(1)} %shard_map.83), channel_id=1, source_target_pairs={{0,1},{1,0},{2,3},{3,2},{4,5},{5,4},{6,7},{7,6},{8,9},{9,8},{10,11... | collective-permute-start | bytes 1572872 | tf_op jit(solution)/shard_map/ppermute | solution.py:467
  95.1 15.1 %collective-permute-start.21 = (bf16[4,256,256]{2,1,0:T(8,128)(2,1)S(1)}, bf16[4,256,256]{2,1,0:T(8,128)(2,1)S(1)}, u32[]{:S(2)}, u32[]{:S(2)}) collective-permute-start(bf16[4,256,256]{2,1,0:T(8,128)(2,1)S(1)} %shard_map.80.one_ref), channel_id=1, source_target_pairs={{0,24},{24,0},{8,16},{16,8},{1,25},{25,1},{9,17},{17,9},{2,26},{26... | collective-permute-start | bytes 1572872 | tf_op jit(solution)/shard_map/ppermute | solution.py:433
  98.5 1.3 collective-permute-start.18
  98.5 6.3 %collective-permute-start.19 = (bf16[256,256]{1,0:T(8,128)(2,1)S(1)}, bf16[256,256]{1,0:T(8,128)(2,1)S(1)}, u32[]{:S(2)}, u32[]{:S(2)}) collective-permute-start(bf16[256,256]{1,0:T(8,128)(2,1)S(1)} %get-tuple-element.88), channel_id=1, source_target_pairs={{0,4},{2,6},{4,0},{6,2},{1,5},{3,7},{5,1},{7,3},{8,12},{10,14},{12... | collective-permute-start | bytes 393224 | tf_op jit(solution)/shard_map/ppermute | solution.py:352
  99.8 7.0 %collective-permute-start.20 = (bf16[256,256]{1,0:T(8,128)(2,1)S(1)}, bf16[256,256]{1,0:T(8,128)(2,1)S(1)}, u32[]{:S(2)}, u32[]{:S(2)}) collective-permute-start(bf16[256,256]{1,0:T(8,128)(2,1)S(1)} %get-tuple-element.89), channel_id=1, source_target_pairs={{0,6},{2,4},{4,2},{6,0},{1,7},{3,5},{5,3},{7,1},{8,14},{10,12},{12... | collective-permute-start | bytes 393224 | tf_op jit(solution)/shard_map/ppermute | solution.py:352
  110.3 11.7 %collective-permute-start.22 = (bf16[256,256]{1,0:T(8,128)(2,1)S(1)}, bf16[256,256]{1,0:T(8,128)(2,1)S(1)}, u32[]{:S(2)}, u32[]{:S(2)}) collective-permute-start(bf16[256,256]{1,0:T(8,128)(2,1)S(1)} %get-tuple-element.93), channel_id=1, source_target_pairs={{0,2},{2,0},{4,6},{6,4},{1,3},{3,1},{5,7},{7,5},{8,10},{10,8},{12,... | collective-permute-start | bytes 393224 | tf_op jit(solution)/shard_map/ppermute | solution.py:352
  110.3 11.7 %collective-permute-start.23 = (bf16[256,256]{1,0:T(8,128)(2,1)S(1)}, bf16[256,256]{1,0:T(8,128)(2,1)S(1)}, u32[]{:S(2)}, u32[]{:S(2)}) collective-permute-start(bf16[256,256]{1,0:T(8,128)(2,1)S(1)} %get-tuple-element.94), channel_id=1, source_target_pairs={{0,4},{2,6},{4,0},{6,2},{1,5},{3,7},{5,1},{7,3},{8,12},{10,14},{12... | collective-permute-start | bytes 393224 | tf_op jit(solution)/shard_map/ppermute | solution.py:352
  111.9 10.1 %collective-permute-start.24 = (bf16[256,256]{1,0:T(8,128)(2,1)S(1)}, bf16[256,256]{1,0:T(8,128)(2,1)S(1)}, u32[]{:S(2)}, u32[]{:S(2)}) collective-permute-start(bf16[256,256]{1,0:T(8,128)(2,1)S(1)} %get-tuple-element.95), channel_id=1, source_target_pairs={{0,6},{2,4},{4,2},{6,0},{1,7},{3,5},{5,3},{7,1},{8,14},{10,12},{12... | collective-permute-start | bytes 393224 | tf_op jit(solution)/shard_map/ppermute | solution.py:352
  112.2 22.6 %collective-permute-start.26 = (bf16[4,256,256]{2,1,0:T(8,128)(2,1)S(1)}, bf16[4,256,256]{2,1,0:T(8,128)(2,1)S(1)}, u32[]{:S(2)}, u32[]{:S(2)}) collective-permute-start(bf16[4,256,256]{2,1,0:T(8,128)(2,1)S(1)} %shard_map.86.part_ref), channel_id=1, source_target_pairs={{0,8},{8,0},{16,24},{24,16},{1,9},{9,1},{17,25},{25,17},{2,10},{10... | collective-permute-start | bytes 1572872 | tf_op jit(solution)/shard_map/ppermute | solution.py:436
  122.0 23.6 %collective-permute-start.25 = (bf16[4,256,256]{2,1,0:T(8,128)(2,1)S(1)}, bf16[4,256,256]{2,1,0:T(8,128)(2,1)S(1)}, u32[]{:S(2)}, u32[]{:S(2)}) collective-permute-start(bf16[4,256,256]{2,1,0:T(8,128)(2,1)S(1)} %shard_map.88.part_ref), channel_id=1, source_target_pairs={{0,8},{8,0},{16,24},{24,16},{1,9},{9,1},{17,25},{25,17},{2,10},{10... | collective-permute-start | bytes 1572872 | tf_op jit(solution)/shard_map/ppermute | solution.py:436

commit v7 on v6

--- a/solution.py
+++ b/solution.py
@@ -463,10 +463,10 @@
     far_other = lax.ppermute(far_other, "tgt", partners(n_tgt, 2))
     far_own = lax.ppermute(far_own, "tgt", partners(n_tgt, 2))
     line_sum(*waits)
-    side_own = total_of([(own_blocks, 3), (arrived, 3), (far_other, 0)])
+    side_own = total_of([(own_blocks, 3), (arrived, 3), (after(far_other, mine[0]), 0)])
     side_own = lax.ppermute(side_own, "mdl", partners(n_mdl, 1))
     while len(totals) < chunks:
-        line_sum(side_own, far_own, mine[0])
+        line_sum(far_own, mine[0])
     query_grads = None
     for layer in range(layers):
         query_grads = join_heads(place, mine[layer], True, layer, layers, query_grads)

time: 148 us -> 147 us (level)
  starting transfers between devices: 48.6 us -> 43.6 us
  waiting for transfers between devices: 49.8 us -> 53.4 us
    ppermute x2, starting transfers between devices: 16.2 us -> 10.1 us  [line_sum(): other.append(lax.ppermute(mine[-1], 'inp', partners(n_inp, 1)))]
    ppermute x6, waiting for transfers between devices: 7.32 us -> 12.6 us  [to_owners(): lax.ppermute(part, 'tgt', partners(n_tgt, mask))]
    ppermute x2, waiting for transfers between devices: 14.4 us -> 11.2 us  [line_sum(): lax.ppermute(after(value, *earlier), 'inp', [(0, 3), (3, 0), (1, 2), (2,...]
    ppermute x6, starting transfers between devices: 2.95 us -> 4.99 us  [to_owners(): lax.ppermute(part, 'tgt', partners(n_tgt, mask))]
    ppermute x2, waiting for transfers between devices: 5.85 us -> 7.56 us  [pair_sum(): arrived = lax.ppermute(send[index], 'inp', partners(n_inp, 1))]
  transfers between devices with their start and end apart: 27 -> 27, of which waited for: 15 -> 12; matrix products, arithmetic and copies ran while one was open for 0% -> 0% of each run, Pallas kernels for 29% -> 30%
where the time goes in v7:
time: 147 us
  waiting for transfers between devices  53.4 us (36%)
  Pallas kernels  46.1 us (31%)
  starting transfers between devices  43.6 us (30%)
  local copies, waits for them, and re-layouts  2.49 us (2%)
    ppermute x6, waiting for transfers between devices, to_owners(): lax.ppermute(part, 'tgt', partners(n_tgt, mask))  12.6 us
    ppermute x2, waiting for transfers between devices, line_sum(): lax.ppermute(after(value, *earlier), 'inp', [(0, 3), (3, 0), (1, 2), (2,...  11.2 us
    pallas_call x2, Pallas kernels, project(): pl.pallas_call(project_kernel, grid=(width // depth,), in_specs=[pl.Block...  11 us
    pallas_call x2, Pallas kernels, back_blocks(): pl.pallas_call(back_kernel, grid_spec=pltpu.PrefetchScalarGridSpec(num_sc...  10.9 us
    ppermute x6, starting transfers between devices, everywhere(): lax.ppermute(value, 'inp', partners(n_inp, mask))  10.3 us
    ppermute x2, starting transfers between devices, line_sum(): other.append(lax.ppermute(mine[-1], 'inp', partners(n_inp, 1)))  10.1 us
    pallas_call x4, Pallas kernels, join_heads(): pl.pallas_call(join_kernel, grid_spec=pltpu.PrefetchScalarGridSpec(num_sc...  9.73 us
    ppermute x2, waiting for transfers between devices, line_sum(): other.append(lax.ppermute(mine[-1], 'inp', partners(n_inp, 1)))  8.83 us
  transfers between devices with their start and end apart: 27, of which 12 were waited for; matrix products, arithmetic and copies ran while one was open for 0% of the time, Pallas kernels for 30%

profile of v7, /device:TPU:0, one launch (start us, length us, event | category | flops | bytes accessed | tf_op | source)
XLA Modules:
  0.0 146.7 jit_solution(9768207897025705958)
XLA Ops:
  0.7 0.1 add_add_fusion
  0.7 0.1 pad_add_fusion
  0.8 2.0 %copy.15 = bf16[2,512,4,256]{3,1,0,2:T(8,128)(2,1)S(1)} copy(bf16[2,512,4,256]{3,2,1,0:T(4,128)(2,1)} %param.8) | data formatting | bytes 4194304 | tf_op jit(solution)/shard_map/optimization_barrier | solution.py:374
  2.8 0.2 copy-done
  3.0 0.3 copy.14
  3.4 3.0 %collective-permute-start = (bf16[2,512,256]{2,1,0:T(8,128)(2,1)S(1)}, bf16[2,512,256]{2,1,0:T(8,128)(2,1)S(1)}, u32[]{:S(2)}, u32[]{:S(2)}) collective-permute-start(bf16[2,512,256]{2,1,0:T(8,128)(2,1)S(1)} %shard_map.68), channel_id=1, source_target_pairs={{0,4},{2,6},{4,0},{6,2},{8,14},{10,12},{12,10},{14,8},{16,20},{18,... | collective-permute-start | bytes 1572872 | tf_op jit(solution)/shard_map/ppermute | solution.py:337
  6.5 5.5 %shard_map.72 = (bf16[1,512,256]{2,1,0:T(8,128)(2,1)S(1)}, bf16[1,512,256]{2,1,0:T(8,128)(2,1)S(1)}) custom-call(bf16[512,4096]{1,0:T(8,128)(2,1)} %enc_ref.1, bf16[2,4096,256]{2,1,0:T(8,128)(2,1)} %bitcast.40, bf16[2,4096,256]{2,1,0:T(8,128)(2,1)} %bitcast.44), custom_call_target="tpu_custom_call" | custom-call | flops 2147483648 | bytes 8388608 | tf_op jit(solution)/shard_map/pallas_call | solution.py:123
  12.0 0.1 shard_map.73
  12.1 0.1 collective-permute-start.1
  12.1 0.1 collective-permute-start.2
  12.2 6.9 %collective-permute-done.refs_2_.refs_6_ = bf16[2,512,256]{2,1,0:T(8,128)(2,1)S(1)} collective-permute-done((bf16[2,512,256]{2,1,0:T(8,128)(2,1)S(1)}, bf16[2,512,256]{2,1,0:T(8,128)(2,1)S(1)}, u32[]{:S(2)}, u32[]{:S(2)}) %collective-permute-start) | collective-permute-done | bytes 524320 | tf_op jit(solution)/shard_map/ppermute | solution.py:337
  19.1 1.5 %collective-permute-start.4 = (bf16[2,512,256]{2,1,0:T(8,128)(2,1)S(1)}, bf16[2,512,256]{2,1,0:T(8,128)(2,1)S(1)}, u32[]{:S(2)}, u32[]{:S(2)}) collective-permute-start(bf16[2,512,256]{2,1,0:T(8,128)(2,1)S(1)} %collective-permute-done.refs_2_.refs_6_), channel_id=1, source_target_pairs={{0,8},{8,0},{16,24},{24,16},{1,9},{9,1},{17,25},{25,17},{2,10},{10... | collective-permute-start | bytes 1572872 | tf_op jit(solution)/shard_map/ppermute | solution.py:395
  20.6 1.0 collective-permute-start.3
  21.6 5.5 %shard_map.69 = (bf16[1,512,256]{2,1,0:T(8,128)(2,1)S(1)}, bf16[1,512,256]{2,1,0:T(8,128)(2,1)S(1)}) custom-call(bf16[512,4096]{1,0:T(8,128)(2,1)} %enc_ref.1, bf16[2,4096,256]{2,1,0:T(8,128)(2,1)} %bitcast.41, bf16[2,4096,256]{2,1,0:T(8,128)(2,1)} %bitcast.45), custom_call_target="tpu_custom_call" | custom-call | flops 2147483648 | bytes 8388608 | tf_op jit(solution)/shard_map/pallas_call | solution.py:123
  27.1 3.3 %collective-permute-done.2.refs_2_.refs_6_ = bf16[2,512,256]{2,1,0:T(8,128)(2,1)S(1)} collective-permute-done((bf16[2,512,256]{2,1,0:T(8,128)(2,1)S(1)}, bf16[2,512,256]{2,1,0:T(8,128)(2,1)S(1)}, u32[]{:S(2)}, u32[]{:S(2)}) %collective-permute-start.2) | collective-permute-done | bytes 524320 | tf_op jit(solution)/shard_map/ppermute | solution.py:386
  30.4 2.5 %collective-permute-done.4.refs_3_.refs_7_ = bf16[2,512,256]{2,1,0:T(8,128)(2,1)S(1)} collective-permute-done((bf16[2,512,256]{2,1,0:T(8,128)(2,1)S(1)}, bf16[2,512,256]{2,1,0:T(8,128)(2,1)S(1)}, u32[]{:S(2)}, u32[]{:S(2)}) %collective-permute-start.4) | collective-permute-done | bytes 524320 | tf_op jit(solution)/shard_map/ppermute | solution.py:395
  32.8 0.0 collective-permute-done.1.refs_1_.refs_5_
  32.8 2.1 %shard_map.75.refs_8_ = f32[4,2048]{1,0:T(4,128)S(1)} custom-call(s32[3]{0:T(128)S(1)} %get-tuple-element.68.place_ref, bf16[1,512,256]{2,1,0:T(8,128)(2,1)S(1)} %get-tuple-element.63.k_ref, bf16[1,512,256]{2,1,0:T(8,128)(2,1)S(1)} %get-tuple-element.66.v_ref, bf16[4,2,512,256]{3,2,1,0:T(8,128)(2,1)S(1)} %bitcast.28, ...), custom_call_target="tpu_custom_call" | custom-call | flops 1073741824 | bytes 2621440 | tf_op jit(solution)/shard_map/pallas_call | solution.py:175
  35.0 3.8 %collective-permute-start.7 = (f32[4,2048]{1,0:T(4,128)S(1)}, f32[4,2048]{1,0:T(4,128)S(1)}, u32[]{:S(2)}, u32[]{:S(2)}) collective-permute-start(f32[4,2048]{1,0:T(4,128)S(1)} %shard_map.75.refs_8_), channel_id=1, source_target_pairs={{0,24},{8,16},{16,8},{24,0},{1,25},{9,17},{17,9},{25,1},{2,26},{10... | collective-permute-start | bytes 98312 | tf_op jit(solution)/shard_map/ppermute | solution.py:342
  38.8 0.0 collective-permute-start.6
  38.8 0.6 collective-permute-start.5
  39.5 0.5 collective-permute-done.3.refs_3_.refs_7_
  40.0 2.1 %shard_map.74.refs_8_ = f32[4,2048]{1,0:T(4,128)S(1)} custom-call(s32[3]{0:T(128)S(1)} %get-tuple-element.71.place_ref, bf16[1,512,256]{2,1,0:T(8,128)(2,1)S(1)} %get-tuple-element.55.k_ref, bf16[1,512,256]{2,1,0:T(8,128)(2,1)S(1)} %get-tuple-element.56.v_ref, bf16[4,2,512,256]{3,2,1,0:T(8,128)(2,1)S(1)} %bitcast.29, ...), custom_call_target="tpu_custom_call" | custom-call | flops 1073741824 | bytes 2621440 | tf_op jit(solution)/shard_map/pallas_call | solution.py:175
  42.2 5.2 %collective-permute-start.10 = (f32[4,2048]{1,0:T(4,128)S(1)}, f32[4,2048]{1,0:T(4,128)S(1)}, u32[]{:S(2)}, u32[]{:S(2)}) collective-permute-start(f32[4,2048]{1,0:T(4,128)S(1)} %shard_map.74.refs_8_), channel_id=1, source_target_pairs={{0,24},{8,16},{16,8},{24,0},{1,25},{9,17},{17,9},{25,1},{2,26},{10... | collective-permute-start | bytes 98312 | tf_op jit(solution)/shard_map/ppermute | solution.py:342
  47.4 0.6 collective-permute-start.8
  48.0 4.1 %shard_map.76 = (bf16[4,256,256]{2,1,0:T(8,128)(2,1)S(1)}, bf16[4,256,256]{2,1,0:T(8,128)(2,1)S(1)}, bf16[512,256]{1,0:T(8,128)(2,1)S(1)}, bf16[512,256]{1,0:T(8,128)(2,1)S(1)}) custom-call(s32[3]{0:T(128)S(1)} %get-tuple-element.68.place_ref, bf16[1,512,256]{2,1,0:T(8,128)(2,1)S(1)} %get-tuple-element.63.k_ref, ...), custom_call_target="tpu_custom_call" | custom-call | flops 2684354560 | bytes 3932160 | tf_op jit(solution)/shard_map/pallas_call | solution.py:229
  52.1 0.1 collective-permute-done.9.refs_10_
  52.2 0.0 collective-permute-done.8.refs_9_
  52.2 1.4 collective-permute-start.11
  53.6 4.1 %shard_map.77 = (bf16[4,256,256]{2,1,0:T(8,128)(2,1)S(1)}, bf16[4,256,256]{2,1,0:T(8,128)(2,1)S(1)}, bf16[512,256]{1,0:T(8,128)(2,1)S(1)}, bf16[512,256]{1,0:T(8,128)(2,1)S(1)}) custom-call(s32[3]{0:T(128)S(1)} %get-tuple-element.71.place_ref, bf16[1,512,256]{2,1,0:T(8,128)(2,1)S(1)} %get-tuple-element.55.k_ref, ...), custom_call_target="tpu_custom_call" | custom-call | flops 2684354560 | bytes 3932160 | tf_op jit(solution)/shard_map/pallas_call | solution.py:229
  57.6 5.5 %shard_map.78 = bf16[4,512,512]{2,1,0:T(8,128)(2,1)S(1)} custom-call(s32[4]{0:T(128)S(1)} %get-tuple-element.75.order_ref, bf16[2,4096,256]{2,1,0:T(8,128)(2,1)} %bitcast.42, bf16[2,4096,256]{2,1,0:T(8,128)(2,1)} %bitcast.46, bf16[512,256]{1,0:T(8,128)(2,1)S(1)} %get-tuple-element.69.refs_0_, bf16[512,256]{1,0:T(8,128)(2,1)S(1)} %get-tuple-element.70.refs_1_, ...), custom_call_target="tpu_custom_call" | custom-call | flops 2147483648 | bytes 8388608 | tf_op jit(solution)/shard_map/pallas_call | solution.py:260
  63.2 2.4 %collective-permute-done.11.two_ref = bf16[4,256,256]{2,1,0:T(8,128)(2,1)S(1)} collective-permute-done((bf16[4,256,256]{2,1,0:T(8,128)(2,1)S(1)}, bf16[4,256,256]{2,1,0:T(8,128)(2,1)S(1)}, u32[]{:S(2)}, u32[]{:S(2)}) %collective-permute-start.11) | collective-permute-done | bytes 524320 | tf_op jit(solution)/shard_map/ppermute | solution.py:420
  65.6 0.1 shard_map.79.one_ref
  65.7 0.1 collective-permute-start.13
  65.8 1.4 collective-permute-start.12
  67.2 2.4 %collective-permute-start.15 = (bf16[4,256,256]{2,1,0:T(8,128)(2,1)S(1)}, bf16[4,256,256]{2,1,0:T(8,128)(2,1)S(1)}, u32[]{:S(2)}, u32[]{:S(2)}) collective-permute-start(bf16[4,256,256]{2,1,0:T(8,128)(2,1)S(1)} %shard_map.79.one_ref), channel_id=1, source_target_pairs={{0,24},{24,0},{8,16},{16,8},{1,25},{25,1},{9,17},{17,9},{2,26},{26... | collective-permute-start | bytes 1572872 | tf_op jit(solution)/shard_map/ppermute | solution.py:433
  69.6 5.3 %shard_map.81.refs_0_ = f32[4,512,512]{2,1,0:T(8,128)S(1)} custom-call(s32[4]{0:T(128)S(1)} %get-tuple-element.83.order_ref, bf16[2,4096,256]{2,1,0:T(8,128)(2,1)} %bitcast.43, bf16[2,4096,256]{2,1,0:T(8,128)(2,1)} %bitcast.47, bf16[512,256]{1,0:T(8,128)(2,1)S(1)} %get-tuple-element.69.refs_0_, bf16[512,256]{1,0:T(8,128)(2,1)S(1)} %get-tuple-element.70.refs_1_, ...), custom_call_target="tpu_custom_call" | custom-call | flops 2147483648 | bytes 8388608 | tf_op jit(solution)/shard_map/pallas_call | solution.py:260
  74.9 5.2 %collective-permute-done.12.two_ref = bf16[4,256,256]{2,1,0:T(8,128)(2,1)S(1)} collective-permute-done((bf16[4,256,256]{2,1,0:T(8,128)(2,1)S(1)}, bf16[4,256,256]{2,1,0:T(8,128)(2,1)S(1)}, u32[]{:S(2)}, u32[]{:S(2)}) %collective-permute-start.12) | collective-permute-done | bytes 524320 | tf_op jit(solution)/shard_map/ppermute | solution.py:420
  80.1 0.1 shard_map.80.one_ref
  80.2 0.1 shard_map.83
  80.3 0.1 shard_map.82
  80.4 1.6 %collective-permute-start.14 = (bf16[1,512,512]{2,1,0:T(8,128)(2,1)S(1)}, bf16[1,512,512]{2,1,0:T(8,128)(2,1)S(1)}, u32[]{:S(2)}, u32[]{:S(2)}) collective-permute-start(bf16[1,512,512]{2,1,0:T(8,128)(2,1)S(1)} %shard_map.82), channel_id=1, source_target_pairs={{0,4},{2,6},{4,0},{6,2},{1,5},{3,7},{5,1},{7,3},{8,12},{10,14},{12... | collective-permute-start | bytes 1572872 | tf_op jit(solution)/shard_map/ppermute | solution.py:464
  82.0 11.2 %collective-permute-done.15.two_ref = bf16[4,256,256]{2,1,0:T(8,128)(2,1)S(1)} collective-permute-done((bf16[4,256,256]{2,1,0:T(8,128)(2,1)S(1)}, bf16[4,256,256]{2,1,0:T(8,128)(2,1)S(1)}, u32[]{:S(2)}, u32[]{:S(2)}) %collective-permute-start.15) | collective-permute-done | bytes 524320 | tf_op jit(solution)/shard_map/ppermute | solution.py:433
  93.2 0.1 shard_map.84
  93.3 3.6 %collective-permute-start.19 = (bf16[4,256,256]{2,1,0:T(8,128)(2,1)S(1)}, bf16[4,256,256]{2,1,0:T(8,128)(2,1)S(1)}, u32[]{:S(2)}, u32[]{:S(2)}) collective-permute-start(bf16[4,256,256]{2,1,0:T(8,128)(2,1)S(1)} %shard_map.80.one_ref), channel_id=1, source_target_pairs={{0,24},{24,0},{8,16},{16,8},{1,25},{25,1},{9,17},{17,9},{2,26},{26... | collective-permute-start | bytes 1572872 | tf_op jit(solution)/shard_map/ppermute | solution.py:433
  96.9 0.5 collective-permute-start.25
  97.4 1.5 %collective-permute-start.17 = (bf16[256,256]{1,0:T(8,128)(2,1)S(1)}, bf16[256,256]{1,0:T(8,128)(2,1)S(1)}, u32[]{:S(2)}, u32[]{:S(2)}) collective-permute-start(bf16[256,256]{1,0:T(8,128)(2,1)S(1)} %get-tuple-element.89), channel_id=1, source_target_pairs={{0,4},{2,6},{4,0},{6,2},{1,5},{3,7},{5,1},{7,3},{8,12},{10,14},{12... | collective-permute-start | bytes 393224 | tf_op jit(solution)/shard_map/ppermute | solution.py:352
  98.9 1.1 collective-permute-start.18
  100.0 12.1 %collective-permute-done.17.refs_2_ = bf16[256,256]{1,0:T(8,128)(2,1)S(1)} collective-permute-done((bf16[256,256]{1,0:T(8,128)(2,1)S(1)}, bf16[256,256]{1,0:T(8,128)(2,1)S(1)}, u32[]{:S(2)}, u32[]{:S(2)}) %collective-permute-start.17) | collective-permute-done | bytes 131104 | tf_op jit(solution)/shard_map/ppermute | solution.py:352
  112.2 0.4 collective-permute-done.18.refs_3_
  112.7 0.1 shard_map.86
  112.8 0.8 collective-permute-start.20
  113.7 1.5 %collective-permute-start.21 = (bf16[256,256]{1,0:T(8,128)(2,1)S(1)}, bf16[256,256]{1,0:T(8,128)(2,1)S(1)}, u32[]{:S(2)}, u32[]{:S(2)}) collective-permute-start(bf16[256,256]{1,0:T(8,128)(2,1)S(1)} %get-tuple-element.95), channel_id=1, source_target_pairs={{0,4},{2,6},{4,0},{6,2},{1,5},{3,7},{5,1},{7,3},{8,12},{10,14},{12... | collective-permute-start | bytes 393224 | tf_op jit(solution)/shard_map/ppermute | solution.py:352
  115.2 5.4 %collective-permute-start.24 = (bf16[4,256,256]{2,1,0:T(8,128)(2,1)S(1)}, bf16[4,256,256]{2,1,0:T(8,128)(2,1)S(1)}, u32[]{:S(2)}, u32[]{:S(2)}) collective-permute-start(bf16[4,256,256]{2,1,0:T(8,128)(2,1)S(1)} %shard_map.85.part_ref), channel_id=1, source_target_pairs={{0,8},{8,0},{16,24},{24,16},{1,9},{9,1},{17,25},{25,17},{2,10},{10... | collective-permute-start | bytes 1572872 | tf_op jit(solution)/shard_map/ppermute | solution.py:436
  120.6 0.2 shard_map.92
  120.7 1.6 %collective-permute-start.26 = (bf16[1,512,512]{2,1,0:T(8,128)(2,1)S(1)}, bf16[1,512,512]{2,1,0:T(8,128)(2,1)S(1)}, u32[]{:S(2)}, u32[]{:S(2)}) collective-permute-start(bf16[1,512,512]{2,1,0:T(8,128)(2,1)S(1)} %shard_map.92), channel_id=1, source_target_pairs={{0,1},{1,0},{2,3},{3,2},{4,5},{5,4},{6,7},{7,6},{8,9},{9,8},{10,11... | collective-permute-start | bytes 1572872 | tf_op jit(solution)/shard_map/ppermute | solution.py:467
  122.4 4.7 %collective-permute-start.23 = (bf16[4,256,256]{2,1,0:T(8,128)(2,1)S(1)}, bf16[4,256,256]{2,1,0:T(8,128)(2,1)S(1)}, u32[]{:S(2)}, u32[]{:S(2)}) collective-permute-start(bf16[4,256,256]{2,1,0:T(8,128)(2,1)S(1)} %shard_map.87.part_ref), channel_id=1, source_target_pairs={{0,8},{8,0},{16,24},{24,16},{1,9},{9,1},{17,25},{25,17},{2,10},{10... | collective-permute-start | bytes 1572872 | tf_op jit(solution)/shard_map/ppermute | solution.py:436
  127.1 2.4 %shard_map.88.rest_0_ = bf16[2,512,4,256]{3,2,1,0:T(4,128)(2,1)} custom-call(s32[3]{0:T(128)S(1)} %get-tuple-element.68.place_ref, bf16[4,256,256]{2,1,0:T(8,128)(2,1)S(1)} %shard_map.85.part_ref), custom_call_target="tpu_custom_call" | custom-call | bytes 1048576 | tf_op jit(solution)/shard_map/pallas_call | solution.py:86
  129.5 3.8 %collective-permute-done.24.part_ref = bf16[4,256,256]{2,1,0:T(8,128)(2,1)S(1)} collective-permute-done((bf16[4,256,256]{2,1,0:T(8,128)(2,1)S(1)}, bf16[4,256,256]{2,1,0:T(8,128)(2,1)S(1)}, u32[]{:S(2)}, u32[]{:S(2)}) %collective-permute-start.24) | collective-permute-done | bytes 524320 | tf_op jit(solution)/shard_map/ppermute | solution.py:436
  133.3 2.4 %shard_map.89.rest_0_ = bf16[2,512,4,256]{3,2,1,0:T(4,128)(2,1)} custom-call(s32[3]{0:T(128)S(1)} %get-tuple-element.68.place_ref, bf16[4,256,256]{2,1,0:T(8,128)(2,1)S(1)} %collective-permute-done.24.part_ref, bf16[2,512,4,256]{3,2,1,0:T(4,128)(2,1)} %shard_map.88.rest_0_), custom_call_target="tpu_custom_call", output_to_operand_aliasing={{}: (2, {})} | custom-call | bytes 1048576 | tf_op jit(solution)/shard_map/pallas_call | solution.py:86
  135.8 2.4 %shard_map.90.rest_0_ = bf16[2,512,4,256]{3,2,1,0:T(4,128)(2,1)} custom-call(s32[3]{0:T(128)S(1)} %get-tuple-element.68.place_ref, bf16[4,256,256]{2,1,0:T(8,128)(2,1)S(1)} %shard_map.87.part_ref, bf16[2,512,4,256]{3,2,1,0:T(4,128)(2,1)} %shard_map.89.rest_0_), custom_call_target="tpu_custom_call", output_to_operand_aliasing={{}: (2, {})} | custom-call | bytes 1048576 | tf_op jit(solution)/shard_map/pallas_call | solution.py:86
  138.2 1.0 shard_map.93
  139.2 5.0 %collective-permute-done.23.part_ref = bf16[4,256,256]{2,1,0:T(8,128)(2,1)S(1)} collective-permute-done((bf16[4,256,256]{2,1,0:T(8,128)(2,1)S(1)}, bf16[4,256,256]{2,1,0:T(8,128)(2,1)S(1)}, u32[]{:S(2)}, u32[]{:S(2)}) %collective-permute-start.23) | collective-permute-done | bytes 524320 | tf_op jit(solution)/shard_map/ppermute | solution.py:436
  144.2 2.4 %shard_map.91 = bf16[2,512,4,256]{3,2,1,0:T(4,128)(2,1)} custom-call(s32[3]{0:T(128)S(1)} %get-tuple-element.68.place_ref, bf16[4,256,256]{2,1,0:T(8,128)(2,1)S(1)} %collective-permute-done.23.part_ref, bf16[2,512,4,256]{3,2,1,0:T(4,128)(2,1)} %shard_map.90.rest_0_), custom_call_target="tpu_custom_call", output_to_operand_aliasing={{}: (2, {})} | custom-call | bytes 1048576 | tf_op jit(solution)/shard_map/pallas_call | solution.py:86
  (22 shorter events, 0.2 us)
Async XLA Ops:
  0.8 2.2 %copy-start = (bf16[2,512,4,256]{3,2,1,0:T(4,128)(2,1)S(1)}, bf16[2,512,4,256]{3,2,1,0:T(4,128)(2,1)}, u32[]{:S(2)}) copy-start(bf16[2,512,4,256]{3,2,1,0:T(4,128)(2,1)} %param.9) | copy-start | bytes 6291460
  3.4 15.8 %collective-permute-start = (bf16[2,512,256]{2,1,0:T(8,128)(2,1)S(1)}, bf16[2,512,256]{2,1,0:T(8,128)(2,1)S(1)}, u32[]{:S(2)}, u32[]{:S(2)}) collective-permute-start(bf16[2,512,256]{2,1,0:T(8,128)(2,1)S(1)} %shard_map.68), channel_id=1, source_target_pairs={{0,4},{2,6},{4,0},{6,2},{8,14},{10,12},{12,10},{14,8},{16,20},{18,... | collective-permute-start | bytes 1572872 | tf_op jit(solution)/shard_map/ppermute | solution.py:337
  12.1 20.8 %collective-permute-start.1 = (bf16[4,512,256]{2,1,0:T(8,128)(2,1)S(1)}, bf16[4,512,256]{2,1,0:T(8,128)(2,1)S(1)}, u32[]{:S(2)}, u32[]{:S(2)}) collective-permute-start(bf16[4,512,256]{2,1,0:T(8,128)(2,1)S(1)} %shard_map.73), channel_id=1, source_target_pairs={{0,2},{2,0},{4,6},{6,4},{1,3},{3,1},{5,7},{7,5},{8,10},{10,8},{12,... | collective-permute-start | bytes 3145736 | tf_op jit(solution)/shard_map/ppermute | solution.py:394
  12.1 18.2 %collective-permute-start.2 = (bf16[2,512,256]{2,1,0:T(8,128)(2,1)S(1)}, bf16[2,512,256]{2,1,0:T(8,128)(2,1)S(1)}, u32[]{:S(2)}, u32[]{:S(2)}) collective-permute-start(bf16[2,512,256]{2,1,0:T(8,128)(2,1)S(1)} %shard_map.70), channel_id=1, source_target_pairs={{0,4},{2,6},{4,0},{6,2},{1,5},{3,7},{5,1},{7,3},{8,12},{10,14},{12... | collective-permute-start | bytes 1572872 | tf_op jit(solution)/shard_map/ppermute | solution.py:386
  19.1 13.7 %collective-permute-start.4 = (bf16[2,512,256]{2,1,0:T(8,128)(2,1)S(1)}, bf16[2,512,256]{2,1,0:T(8,128)(2,1)S(1)}, u32[]{:S(2)}, u32[]{:S(2)}) collective-permute-start(bf16[2,512,256]{2,1,0:T(8,128)(2,1)S(1)} %collective-permute-done.refs_2_.refs_6_), channel_id=1, source_target_pairs={{0,8},{8,0},{16,24},{24,16},{1,9},{9,1},{17,25},{25,17},{2,10},{10... | collective-permute-start | bytes 1572872 | tf_op jit(solution)/shard_map/ppermute | solution.py:395
  20.6 19.4 %collective-permute-start.3 = (bf16[2,512,256]{2,1,0:T(8,128)(2,1)S(1)}, bf16[2,512,256]{2,1,0:T(8,128)(2,1)S(1)}, u32[]{:S(2)}, u32[]{:S(2)}) collective-permute-start(bf16[2,512,256]{2,1,0:T(8,128)(2,1)S(1)} %shard_map.71), channel_id=1, source_target_pairs={{0,6},{2,4},{4,2},{6,0},{1,7},{3,5},{5,3},{7,1},{8,14},{10,12},{12... | collective-permute-start | bytes 1572872 | tf_op jit(solution)/shard_map/ppermute | solution.py:386
  35.0 12.4 %collective-permute-start.7 = (f32[4,2048]{1,0:T(4,128)S(1)}, f32[4,2048]{1,0:T(4,128)S(1)}, u32[]{:S(2)}, u32[]{:S(2)}) collective-permute-start(f32[4,2048]{1,0:T(4,128)S(1)} %shard_map.75.refs_8_), channel_id=1, source_target_pairs={{0,24},{8,16},{16,8},{24,0},{1,25},{9,17},{17,9},{25,1},{2,26},{10... | collective-permute-start | bytes 98312 | tf_op jit(solution)/shard_map/ppermute | solution.py:342
  38.8 9.2 %collective-permute-start.6 = (f32[4,2048]{1,0:T(4,128)S(1)}, f32[4,2048]{1,0:T(4,128)S(1)}, u32[]{:S(2)}, u32[]{:S(2)}) collective-permute-start(f32[4,2048]{1,0:T(4,128)S(1)} %shard_map.75.refs_8_), channel_id=1, source_target_pairs={{0,16},{8,24},{16,0},{24,8},{1,17},{9,25},{17,1},{25,9},{2,18},{10... | collective-permute-start | bytes 98312 | tf_op jit(solution)/shard_map/ppermute | solution.py:342
  38.8 9.2 %collective-permute-start.5 = (f32[4,2048]{1,0:T(4,128)S(1)}, f32[4,2048]{1,0:T(4,128)S(1)}, u32[]{:S(2)}, u32[]{:S(2)}) collective-permute-start(f32[4,2048]{1,0:T(4,128)S(1)} %shard_map.75.refs_8_), channel_id=1, source_target_pairs={{0,8},{8,0},{16,24},{24,16},{1,9},{9,1},{17,25},{25,17},{2,10},{10... | collective-permute-start | bytes 98312 | tf_op jit(solution)/shard_map/ppermute | solution.py:342
  42.2 9.9 %collective-permute-start.10 = (f32[4,2048]{1,0:T(4,128)S(1)}, f32[4,2048]{1,0:T(4,128)S(1)}, u32[]{:S(2)}, u32[]{:S(2)}) collective-permute-start(f32[4,2048]{1,0:T(4,128)S(1)} %shard_map.74.refs_8_), channel_id=1, source_target_pairs={{0,24},{8,16},{16,8},{24,0},{1,25},{9,17},{17,9},{25,1},{2,26},{10... | collective-permute-start | bytes 98312 | tf_op jit(solution)/shard_map/ppermute | solution.py:342
  47.3 4.8 %collective-permute-start.9 = (f32[4,2048]{1,0:T(4,128)S(1)}, f32[4,2048]{1,0:T(4,128)S(1)}, u32[]{:S(2)}, u32[]{:S(2)}) collective-permute-start(f32[4,2048]{1,0:T(4,128)S(1)} %shard_map.74.refs_8_), channel_id=1, source_target_pairs={{0,16},{8,24},{16,0},{24,8},{1,17},{9,25},{17,1},{25,9},{2,18},{10... | collective-permute-start | bytes 98312 | tf_op jit(solution)/shard_map/ppermute | solution.py:342
  47.4 4.8 %collective-permute-start.8 = (f32[4,2048]{1,0:T(4,128)S(1)}, f32[4,2048]{1,0:T(4,128)S(1)}, u32[]{:S(2)}, u32[]{:S(2)}) collective-permute-start(f32[4,2048]{1,0:T(4,128)S(1)} %shard_map.74.refs_8_), channel_id=1, source_target_pairs={{0,8},{8,0},{16,24},{24,16},{1,9},{9,1},{17,25},{25,17},{2,10},{10... | collective-permute-start | bytes 98312 | tf_op jit(solution)/shard_map/ppermute | solution.py:342
  52.2 13.4 %collective-permute-start.11 = (bf16[4,256,256]{2,1,0:T(8,128)(2,1)S(1)}, bf16[4,256,256]{2,1,0:T(8,128)(2,1)S(1)}, u32[]{:S(2)}, u32[]{:S(2)}) collective-permute-start(bf16[4,256,256]{2,1,0:T(8,128)(2,1)S(1)} %get-tuple-element.80), channel_id=1, source_target_pairs={{0,8},{8,0},{16,24},{24,16},{1,9},{9,1},{17,25},{25,17},{2,10},{10... | collective-permute-start | bytes 1572872 | tf_op jit(solution)/shard_map/ppermute | solution.py:420
  65.7 14.5 %collective-permute-start.13 = (bf16[4,512,512]{2,1,0:T(8,128)(2,1)S(1)}, bf16[4,512,512]{2,1,0:T(8,128)(2,1)S(1)}, u32[]{:S(2)}, u32[]{:S(2)}) collective-permute-start(bf16[4,512,512]{2,1,0:T(8,128)(2,1)S(1)} %shard_map.78), channel_id=1, source_target_pairs={{0,2},{2,0},{4,6},{6,4},{1,3},{3,1},{5,7},{7,5},{8,10},{10,8},{12,... | collective-permute-start | bytes 6291464 | tf_op jit(solution)/shard_map/ppermute | solution.py:458
  65.8 14.3 %collective-permute-start.12 = (bf16[4,256,256]{2,1,0:T(8,128)(2,1)S(1)}, bf16[4,256,256]{2,1,0:T(8,128)(2,1)S(1)}, u32[]{:S(2)}, u32[]{:S(2)}) collective-permute-start(bf16[4,256,256]{2,1,0:T(8,128)(2,1)S(1)} %get-tuple-element.81), channel_id=1, source_target_pairs={{0,8},{8,0},{16,24},{24,16},{1,9},{9,1},{17,25},{25,17},{2,10},{10... | collective-permute-start | bytes 1572872 | tf_op jit(solution)/shard_map/ppermute | solution.py:420
  67.2 26.0 %collective-permute-start.15 = (bf16[4,256,256]{2,1,0:T(8,128)(2,1)S(1)}, bf16[4,256,256]{2,1,0:T(8,128)(2,1)S(1)}, u32[]{:S(2)}, u32[]{:S(2)}) collective-permute-start(bf16[4,256,256]{2,1,0:T(8,128)(2,1)S(1)} %shard_map.79.one_ref), channel_id=1, source_target_pairs={{0,24},{24,0},{8,16},{16,8},{1,25},{25,1},{9,17},{17,9},{2,26},{26... | collective-permute-start | bytes 1572872 | tf_op jit(solution)/shard_map/ppermute | solution.py:433
  80.4 32.2 %collective-permute-start.14 = (bf16[1,512,512]{2,1,0:T(8,128)(2,1)S(1)}, bf16[1,512,512]{2,1,0:T(8,128)(2,1)S(1)}, u32[]{:S(2)}, u32[]{:S(2)}) collective-permute-start(bf16[1,512,512]{2,1,0:T(8,128)(2,1)S(1)} %shard_map.82), channel_id=1, source_target_pairs={{0,4},{2,6},{4,0},{6,2},{1,5},{3,7},{5,1},{7,3},{8,12},{10,14},{12... | collective-permute-start | bytes 1572872 | tf_op jit(solution)/shard_map/ppermute | solution.py:464
  93.3 19.4 %collective-permute-start.19 = (bf16[4,256,256]{2,1,0:T(8,128)(2,1)S(1)}, bf16[4,256,256]{2,1,0:T(8,128)(2,1)S(1)}, u32[]{:S(2)}, u32[]{:S(2)}) collective-permute-start(bf16[4,256,256]{2,1,0:T(8,128)(2,1)S(1)} %shard_map.80.one_ref), channel_id=1, source_target_pairs={{0,24},{24,0},{8,16},{16,8},{1,25},{25,1},{9,17},{17,9},{2,26},{26... | collective-permute-start | bytes 1572872 | tf_op jit(solution)/shard_map/ppermute | solution.py:433
  96.9 23.7 %collective-permute-start.25 = (bf16[1,512,512]{2,1,0:T(8,128)(2,1)S(1)}, bf16[1,512,512]{2,1,0:T(8,128)(2,1)S(1)}, u32[]{:S(2)}, u32[]{:S(2)}) collective-permute-start(bf16[1,512,512]{2,1,0:T(8,128)(2,1)S(1)} %shard_map.83), channel_id=1, source_target_pairs={{0,4},{2,6},{4,0},{6,2},{1,5},{3,7},{5,1},{7,3},{8,12},{10,14},{12... | collective-permute-start | bytes 1572872 | tf_op jit(solution)/shard_map/ppermute | solution.py:463
  97.4 1.5 %collective-permute-start.16 = (bf16[256,256]{1,0:T(8,128)(2,1)S(1)}, bf16[256,256]{1,0:T(8,128)(2,1)S(1)}, u32[]{:S(2)}, u32[]{:S(2)}) collective-permute-start(bf16[256,256]{1,0:T(8,128)(2,1)S(1)} %get-tuple-element.88), channel_id=1, source_target_pairs={{0,2},{2,0},{4,6},{6,4},{1,3},{3,1},{5,7},{7,5},{8,10},{10,8},{12,... | collective-permute-start | bytes 393224 | tf_op jit(solution)/shard_map/ppermute | solution.py:352
  97.4 14.8 %collective-permute-start.17 = (bf16[256,256]{1,0:T(8,128)(2,1)S(1)}, bf16[256,256]{1,0:T(8,128)(2,1)S(1)}, u32[]{:S(2)}, u32[]{:S(2)}) collective-permute-start(bf16[256,256]{1,0:T(8,128)(2,1)S(1)} %get-tuple-element.89), channel_id=1, source_target_pairs={{0,4},{2,6},{4,0},{6,2},{1,5},{3,7},{5,1},{7,3},{8,12},{10,14},{12... | collective-permute-start | bytes 393224 | tf_op jit(solution)/shard_map/ppermute | solution.py:352
  98.9 13.7 %collective-permute-start.18 = (bf16[256,256]{1,0:T(8,128)(2,1)S(1)}, bf16[256,256]{1,0:T(8,128)(2,1)S(1)}, u32[]{:S(2)}, u32[]{:S(2)}) collective-permute-start(bf16[256,256]{1,0:T(8,128)(2,1)S(1)} %get-tuple-element.90), channel_id=1, source_target_pairs={{0,6},{2,4},{4,2},{6,0},{1,7},{3,5},{5,3},{7,1},{8,14},{10,12},{12... | collective-permute-start | bytes 393224 | tf_op jit(solution)/shard_map/ppermute | solution.py:352
  112.8 9.5 %collective-permute-start.20 = (bf16[256,256]{1,0:T(8,128)(2,1)S(1)}, bf16[256,256]{1,0:T(8,128)(2,1)S(1)}, u32[]{:S(2)}, u32[]{:S(2)}) collective-permute-start(bf16[256,256]{1,0:T(8,128)(2,1)S(1)} %get-tuple-element.94), channel_id=1, source_target_pairs={{0,2},{2,0},{4,6},{6,4},{1,3},{3,1},{5,7},{7,5},{8,10},{10,8},{12,... | collective-permute-start | bytes 393224 | tf_op jit(solution)/shard_map/ppermute | solution.py:352
  113.7 8.7 %collective-permute-start.21 = (bf16[256,256]{1,0:T(8,128)(2,1)S(1)}, bf16[256,256]{1,0:T(8,128)(2,1)S(1)}, u32[]{:S(2)}, u32[]{:S(2)}) collective-permute-start(bf16[256,256]{1,0:T(8,128)(2,1)S(1)} %get-tuple-element.95), channel_id=1, source_target_pairs={{0,4},{2,6},{4,0},{6,2},{1,5},{3,7},{5,1},{7,3},{8,12},{10,14},{12... | collective-permute-start | bytes 393224 | tf_op jit(solution)/shard_map/ppermute | solution.py:352
  115.2 7.1 %collective-permute-start.22 = (bf16[256,256]{1,0:T(8,128)(2,1)S(1)}, bf16[256,256]{1,0:T(8,128)(2,1)S(1)}, u32[]{:S(2)}, u32[]{:S(2)}) collective-permute-start(bf16[256,256]{1,0:T(8,128)(2,1)S(1)} %get-tuple-element.96), channel_id=1, source_target_pairs={{0,6},{2,4},{4,2},{6,0},{1,7},{3,5},{5,3},{7,1},{8,14},{10,12},{12... | collective-permute-start | bytes 393224 | tf_op jit(solution)/shard_map/ppermute | solution.py:352
  115.2 18.1 %collective-permute-start.24 = (bf16[4,256,256]{2,1,0:T(8,128)(2,1)S(1)}, bf16[4,256,256]{2,1,0:T(8,128)(2,1)S(1)}, u32[]{:S(2)}, u32[]{:S(2)}) collective-permute-start(bf16[4,256,256]{2,1,0:T(8,128)(2,1)S(1)} %shard_map.85.part_ref), channel_id=1, source_target_pairs={{0,8},{8,0},{16,24},{24,16},{1,9},{9,1},{17,25},{25,17},{2,10},{10... | collective-permute-start | bytes 1572872 | tf_op jit(solution)/shard_map/ppermute | solution.py:436
  120.7 17.5 %collective-permute-start.26 = (bf16[1,512,512]{2,1,0:T(8,128)(2,1)S(1)}, bf16[1,512,512]{2,1,0:T(8,128)(2,1)S(1)}, u32[]{:S(2)}, u32[]{:S(2)}) collective-permute-start(bf16[1,512,512]{2,1,0:T(8,128)(2,1)S(1)} %shard_map.92), channel_id=1, source_target_pairs={{0,1},{1,0},{2,3},{3,2},{4,5},{5,4},{6,7},{7,6},{8,9},{9,8},{10,11... | collective-permute-start | bytes 1572872 | tf_op jit(solution)/shard_map/ppermute | solution.py:467
  122.4 21.9 %collective-permute-start.23 = (bf16[4,256,256]{2,1,0:T(8,128)(2,1)S(1)}, bf16[4,256,256]{2,1,0:T(8,128)(2,1)S(1)}, u32[]{:S(2)}, u32[]{:S(2)}) collective-permute-start(bf16[4,256,256]{2,1,0:T(8,128)(2,1)S(1)} %shard_map.87.part_ref), channel_id=1, source_target_pairs={{0,8},{8,0},{16,24},{24,16},{1,9},{9,1},{17,25},{25,17},{2,10},{10... | collective-permute-start | bytes 1572872 | tf_op jit(solution)/shard_map/ppermute | solution.py:436

commit v8 on v5

--- a/solution.py
+++ b/solution.py
@@ -462,10 +462,10 @@
     far_other = lax.ppermute(far_other, "tgt", partners(n_tgt, 2))
     far_own = lax.ppermute(far_own, "tgt", partners(n_tgt, 2))
     line_sum(*waits)
-    side_own = total_of([(own_blocks, 3), (arrived, 3), (far_other, 0)])
+    side_own = total_of([(own_blocks, 3), (arrived, 3), (after(far_other, mine[0]), 0)])
     side_own = lax.ppermute(side_own, "mdl", partners(n_mdl, 1))
     while len(totals) < chunks:
-        line_sum(side_own, far_own, mine[0])
+        line_sum(far_own, mine[0])
     query_grads = None
     for layer in range(layers):
         query_grads = join_heads(place, mine[layer], True, layer, layers, query_grads)

time: 147 us -> 147 us (level)
  waiting for transfers between devices: 53.9 us -> 60.7 us
  starting transfers between devices: 42.8 us -> 36 us
    ppermute x6, waiting for transfers between devices: 6.18 us -> 16.1 us  [to_owners(): lax.ppermute(part, 'tgt', partners(n_tgt, mask))]
    ppermute x2, starting transfers between devices: 12.8 us -> 7.16 us  [line_sum(): other.append(lax.ppermute(mine[-1], 'inp', partners(n_inp, 1)))]
    ppermute x2, waiting for transfers between devices: 13.5 us -> 10.2 us  [line_sum(): lax.ppermute(after(value, *earlier), 'inp', [(0, 3), (3, 0), (1, 2), (2,...]
    ppermute x2, waiting for transfers between devices: 4.42 us -> 6.11 us  [pair_sum(): arrived = lax.ppermute(send[index], 'inp', partners(n_inp, 1))]
    ppermute x1, waiting for transfers between devices: 1.54 us -> 0.01 us  [body(): side_own = lax.ppermute(side_own, 'mdl', partners(n_mdl, 1))]
where the time goes in v8:
time: 147 us; the launch traced here: 146 us
  waiting for transfers between devices  60.7 us (41%)
  Pallas kernels  46.1 us (31%)
  starting transfers between devices  36 us (24%)
  local copies, waits for them, and re-layouts  2.49 us (2%)
    ppermute x6, waiting for transfers between devices, to_owners(): lax.ppermute(part, 'tgt', partners(n_tgt, mask))  16.1 us
    pallas_call x2, Pallas kernels, project(): pl.pallas_call(project_kernel, grid=(width // depth,), in_specs=[pl.Block...  11 us
    pallas_call x2, Pallas kernels, back_blocks(): pl.pallas_call(back_kernel, grid_spec=pltpu.PrefetchScalarGridSpec(num_sc...  10.9 us
    ppermute x2, waiting for transfers between devices, line_sum(): lax.ppermute(after(value, *earlier), 'inp', [(0, 3), (3, 0), (1, 2), (2,...  10.2 us
    pallas_call x4, Pallas kernels, join_heads(): pl.pallas_call(join_kernel, grid_spec=pltpu.PrefetchScalarGridSpec(num_sc...  9.73 us
    ppermute x6, starting transfers between devices, everywhere(): lax.ppermute(value, 'inp', partners(n_inp, mask))  8.93 us
    ppermute x2, waiting for transfers between devices, line_sum(): other.append(lax.ppermute(mine[-1], 'inp', partners(n_inp, 1)))  8.83 us
    pallas_call x2, Pallas kernels, attention_grads(): pl.pallas_call(functools.partial(grads_kernel, count), grid_spec=pltpu.Pr...  8.13 us
  transfers between devices with their start and end apart: 27, of which 16 were waited for; matrix products, arithmetic and copies ran while one was open for 0% of the time, Pallas kernels for 28%

profile of v8, /device:TPU:0, one launch (start us, length us, event | category | flops | bytes accessed | tf_op | source)
XLA Modules:
  0.0 146.3 jit_solution(838946007160113582)
XLA Ops:
  0.7 0.1 add_add_fusion
  0.7 0.1 pad_add_fusion
  0.8 2.0 %copy.15 = bf16[2,512,4,256]{3,1,0,2:T(8,128)(2,1)S(1)} copy(bf16[2,512,4,256]{3,2,1,0:T(4,128)(2,1)} %param.8) | data formatting | bytes 4194304 | tf_op jit(solution)/shard_map/optimization_barrier | solution.py:374
  2.8 0.2 copy-done
  3.0 0.3 copy.14
  3.4 3.0 %collective-permute-start.1 = (bf16[2,512,256]{2,1,0:T(8,128)(2,1)S(1)}, bf16[2,512,256]{2,1,0:T(8,128)(2,1)S(1)}, u32[]{:S(2)}, u32[]{:S(2)}) collective-permute-start(bf16[2,512,256]{2,1,0:T(8,128)(2,1)S(1)} %shard_map.68), channel_id=1, source_target_pairs={{0,4},{2,6},{4,0},{6,2},{8,14},{10,12},{12,10},{14,8},{16,20},{18,... | collective-permute-start | bytes 1572872 | tf_op jit(solution)/shard_map/ppermute | solution.py:337
  6.5 5.5 %shard_map.71 = (bf16[1,512,256]{2,1,0:T(8,128)(2,1)S(1)}, bf16[1,512,256]{2,1,0:T(8,128)(2,1)S(1)}) custom-call(bf16[512,4096]{1,0:T(8,128)(2,1)} %enc_ref.1, bf16[2,4096,256]{2,1,0:T(8,128)(2,1)} %bitcast.40, bf16[2,4096,256]{2,1,0:T(8,128)(2,1)} %bitcast.44), custom_call_target="tpu_custom_call" | custom-call | flops 2147483648 | bytes 8388608 | tf_op jit(solution)/shard_map/pallas_call | solution.py:123
  12.0 0.1 shard_map.72
  12.1 0.1 collective-permute-start.3
  12.2 6.9 %collective-permute-done.1.refs_2_.refs_6_ = bf16[2,512,256]{2,1,0:T(8,128)(2,1)S(1)} collective-permute-done((bf16[2,512,256]{2,1,0:T(8,128)(2,1)S(1)}, bf16[2,512,256]{2,1,0:T(8,128)(2,1)S(1)}, u32[]{:S(2)}, u32[]{:S(2)}) %collective-permute-start.1) | collective-permute-done | bytes 524320 | tf_op jit(solution)/shard_map/ppermute | solution.py:337
  19.1 1.5 %collective-permute-start.2 = (bf16[2,512,256]{2,1,0:T(8,128)(2,1)S(1)}, bf16[2,512,256]{2,1,0:T(8,128)(2,1)S(1)}, u32[]{:S(2)}, u32[]{:S(2)}) collective-permute-start(bf16[2,512,256]{2,1,0:T(8,128)(2,1)S(1)} %collective-permute-done.1.refs_2_.refs_6_), channel_id=1, source_target_pairs={{0,8},{8,0},{16,24},{24,16},{1,9},{9,1},{17,25},{25,17},{2,10},{10... | collective-permute-start | bytes 1572872 | tf_op jit(solution)/shard_map/ppermute | solution.py:395
  20.6 1.0 collective-permute-start.7
  21.6 5.5 %shard_map.73 = (bf16[1,512,256]{2,1,0:T(8,128)(2,1)S(1)}, bf16[1,512,256]{2,1,0:T(8,128)(2,1)S(1)}) custom-call(bf16[512,4096]{1,0:T(8,128)(2,1)} %enc_ref.1, bf16[2,4096,256]{2,1,0:T(8,128)(2,1)} %bitcast.41, bf16[2,4096,256]{2,1,0:T(8,128)(2,1)} %bitcast.45), custom_call_target="tpu_custom_call" | custom-call | flops 2147483648 | bytes 8388608 | tf_op jit(solution)/shard_map/pallas_call | solution.py:123
  27.1 3.3 %collective-permute-done.3.refs_2_.refs_6_ = bf16[2,512,256]{2,1,0:T(8,128)(2,1)S(1)} collective-permute-done((bf16[2,512,256]{2,1,0:T(8,128)(2,1)S(1)}, bf16[2,512,256]{2,1,0:T(8,128)(2,1)S(1)}, u32[]{:S(2)}, u32[]{:S(2)}) %collective-permute-start.3) | collective-permute-done | bytes 524320 | tf_op jit(solution)/shard_map/ppermute | solution.py:386
  30.4 2.5 %collective-permute-done.2.refs_3_.refs_7_ = bf16[2,512,256]{2,1,0:T(8,128)(2,1)S(1)} collective-permute-done((bf16[2,512,256]{2,1,0:T(8,128)(2,1)S(1)}, bf16[2,512,256]{2,1,0:T(8,128)(2,1)S(1)}, u32[]{:S(2)}, u32[]{:S(2)}) %collective-permute-start.2) | collective-permute-done | bytes 524320 | tf_op jit(solution)/shard_map/ppermute | solution.py:395
  32.8 2.1 %shard_map.74.refs_8_ = f32[4,2048]{1,0:T(4,128)S(1)} custom-call(s32[3]{0:T(128)S(1)} %get-tuple-element.65.place_ref, bf16[1,512,256]{2,1,0:T(8,128)(2,1)S(1)} %get-tuple-element.58.k_ref, bf16[1,512,256]{2,1,0:T(8,128)(2,1)S(1)} %get-tuple-element.59.v_ref, bf16[4,2,512,256]{3,2,1,0:T(8,128)(2,1)S(1)} %bitcast.28, ...), custom_call_target="tpu_custom_call" | custom-call | flops 1073741824 | bytes 2621440 | tf_op jit(solution)/shard_map/pallas_call | solution.py:175
  35.0 3.8 %collective-permute-start.6 = (f32[4,2048]{1,0:T(4,128)S(1)}, f32[4,2048]{1,0:T(4,128)S(1)}, u32[]{:S(2)}, u32[]{:S(2)}) collective-permute-start(f32[4,2048]{1,0:T(4,128)S(1)} %shard_map.74.refs_8_), channel_id=1, source_target_pairs={{0,24},{8,16},{16,8},{24,0},{1,25},{9,17},{17,9},{25,1},{2,26},{10... | collective-permute-start | bytes 98312 | tf_op jit(solution)/shard_map/ppermute | solution.py:342
  38.8 0.6 collective-permute-start.4
  39.5 1.3 collective-permute-done.6.refs_11_
  40.8 2.8 %collective-permute-done.5.refs_10_ = f32[4,2048]{1,0:T(4,128)S(1)} collective-permute-done((f32[4,2048]{1,0:T(4,128)S(1)}, f32[4,2048]{1,0:T(4,128)S(1)}, u32[]{:S(2)}, u32[]{:S(2)}) %collective-permute-start.5) | collective-permute-done | bytes 32800 | tf_op jit(solution)/shard_map/ppermute | solution.py:342
  43.6 4.1 %shard_map.75 = (bf16[4,256,256]{2,1,0:T(8,128)(2,1)S(1)}, bf16[4,256,256]{2,1,0:T(8,128)(2,1)S(1)}, bf16[512,256]{1,0:T(8,128)(2,1)S(1)}, bf16[512,256]{1,0:T(8,128)(2,1)S(1)}) custom-call(s32[3]{0:T(128)S(1)} %get-tuple-element.65.place_ref, bf16[1,512,256]{2,1,0:T(8,128)(2,1)S(1)} %get-tuple-element.58.k_ref, ...), custom_call_target="tpu_custom_call" | custom-call | flops 2684354560 | bytes 3932160 | tf_op jit(solution)/shard_map/pallas_call | solution.py:229
  47.7 2.1 %shard_map.76.refs_8_ = f32[4,2048]{1,0:T(4,128)S(1)} custom-call(s32[3]{0:T(128)S(1)} %get-tuple-element.68.place_ref, bf16[1,512,256]{2,1,0:T(8,128)(2,1)S(1)} %get-tuple-element.64.k_ref, bf16[1,512,256]{2,1,0:T(8,128)(2,1)S(1)} %get-tuple-element.69.v_ref, bf16[4,2,512,256]{3,2,1,0:T(8,128)(2,1)S(1)} %bitcast.30, ...), custom_call_target="tpu_custom_call" | custom-call | flops 1073741824 | bytes 2621440 | tf_op jit(solution)/shard_map/pallas_call | solution.py:175
  49.9 1.5 %collective-permute-start.10 = (f32[4,2048]{1,0:T(4,128)S(1)}, f32[4,2048]{1,0:T(4,128)S(1)}, u32[]{:S(2)}, u32[]{:S(2)}) collective-permute-start(f32[4,2048]{1,0:T(4,128)S(1)} %shard_map.76.refs_8_), channel_id=1, source_target_pairs={{0,24},{8,16},{16,8},{24,0},{1,25},{9,17},{17,9},{25,1},{2,26},{10... | collective-permute-start | bytes 98312 | tf_op jit(solution)/shard_map/ppermute | solution.py:342
  51.4 0.6 collective-permute-start.9
  52.0 2.3 %collective-permute-start.8 = (f32[4,2048]{1,0:T(4,128)S(1)}, f32[4,2048]{1,0:T(4,128)S(1)}, u32[]{:S(2)}, u32[]{:S(2)}) collective-permute-start(f32[4,2048]{1,0:T(4,128)S(1)} %shard_map.76.refs_8_), channel_id=1, source_target_pairs={{0,8},{8,0},{16,24},{24,16},{1,9},{9,1},{17,25},{25,17},{2,10},{10... | collective-permute-start | bytes 98312 | tf_op jit(solution)/shard_map/ppermute | solution.py:342
  54.3 1.3 collective-permute-done.10.refs_11_
  55.6 0.6 collective-permute-done.9.refs_10_
  56.2 0.7 collective-permute-done.8.refs_9_
  56.9 1.6 %collective-permute-start.11 = (bf16[4,256,256]{2,1,0:T(8,128)(2,1)S(1)}, bf16[4,256,256]{2,1,0:T(8,128)(2,1)S(1)}, u32[]{:S(2)}, u32[]{:S(2)}) collective-permute-start(bf16[4,256,256]{2,1,0:T(8,128)(2,1)S(1)} %get-tuple-element.78), channel_id=1, source_target_pairs={{0,8},{8,0},{16,24},{24,16},{1,9},{9,1},{17,25},{25,17},{2,10},{10... | collective-permute-start | bytes 1572872 | tf_op jit(solution)/shard_map/ppermute | solution.py:420
  58.5 4.1 %shard_map.77 = (bf16[4,256,256]{2,1,0:T(8,128)(2,1)S(1)}, bf16[4,256,256]{2,1,0:T(8,128)(2,1)S(1)}, bf16[512,256]{1,0:T(8,128)(2,1)S(1)}, bf16[512,256]{1,0:T(8,128)(2,1)S(1)}) custom-call(s32[3]{0:T(128)S(1)} %get-tuple-element.68.place_ref, bf16[1,512,256]{2,1,0:T(8,128)(2,1)S(1)} %get-tuple-element.64.k_ref, ...), custom_call_target="tpu_custom_call" | custom-call | flops 2684354560 | bytes 3932160 | tf_op jit(solution)/shard_map/pallas_call | solution.py:229
  62.6 5.5 %shard_map.78 = bf16[4,512,512]{2,1,0:T(8,128)(2,1)S(1)} custom-call(s32[4]{0:T(128)S(1)} %get-tuple-element.73.order_ref, bf16[2,4096,256]{2,1,0:T(8,128)(2,1)} %bitcast.42, bf16[2,4096,256]{2,1,0:T(8,128)(2,1)} %bitcast.46, bf16[512,256]{1,0:T(8,128)(2,1)S(1)} %get-tuple-element.66.refs_0_, bf16[512,256]{1,0:T(8,128)(2,1)S(1)} %get-tuple-element.67.refs_1_, ...), custom_call_target="tpu_custom_call" | custom-call | flops 2147483648 | bytes 8388608 | tf_op jit(solution)/shard_map/pallas_call | solution.py:260
  68.2 0.1 shard_map.79.one_ref
  68.4 0.6 collective-permute-start.12
  69.0 2.3 %collective-permute-start.15 = (bf16[4,256,256]{2,1,0:T(8,128)(2,1)S(1)}, bf16[4,256,256]{2,1,0:T(8,128)(2,1)S(1)}, u32[]{:S(2)}, u32[]{:S(2)}) collective-permute-start(bf16[4,256,256]{2,1,0:T(8,128)(2,1)S(1)} %shard_map.79.one_ref), channel_id=1, source_target_pairs={{0,24},{24,0},{8,16},{16,8},{1,25},{25,1},{9,17},{17,9},{2,26},{26... | collective-permute-start | bytes 1572872 | tf_op jit(solution)/shard_map/ppermute | solution.py:433
  71.2 5.3 %shard_map.81.refs_0_ = f32[4,512,512]{2,1,0:T(8,128)S(1)} custom-call(s32[4]{0:T(128)S(1)} %get-tuple-element.81.order_ref, bf16[2,4096,256]{2,1,0:T(8,128)(2,1)} %bitcast.43, bf16[2,4096,256]{2,1,0:T(8,128)(2,1)} %bitcast.47, bf16[512,256]{1,0:T(8,128)(2,1)S(1)} %get-tuple-element.66.refs_0_, bf16[512,256]{1,0:T(8,128)(2,1)S(1)} %get-tuple-element.67.refs_1_, ...), custom_call_target="tpu_custom_call" | custom-call | flops 2147483648 | bytes 8388608 | tf_op jit(solution)/shard_map/pallas_call | solution.py:260
  76.6 6.1 %collective-permute-done.12.two_ref = bf16[4,256,256]{2,1,0:T(8,128)(2,1)S(1)} collective-permute-done((bf16[4,256,256]{2,1,0:T(8,128)(2,1)S(1)}, bf16[4,256,256]{2,1,0:T(8,128)(2,1)S(1)}, u32[]{:S(2)}, u32[]{:S(2)}) %collective-permute-start.12) | collective-permute-done | bytes 524320 | tf_op jit(solution)/shard_map/ppermute | solution.py:420
  82.7 0.1 shard_map.80.one_ref
  82.8 0.1 shard_map.83
  82.9 0.1 shard_map.82
  83.0 1.6 %collective-permute-start.14 = (bf16[1,512,512]{2,1,0:T(8,128)(2,1)S(1)}, bf16[1,512,512]{2,1,0:T(8,128)(2,1)S(1)}, u32[]{:S(2)}, u32[]{:S(2)}) collective-permute-start(bf16[1,512,512]{2,1,0:T(8,128)(2,1)S(1)} %shard_map.82), channel_id=1, source_target_pairs={{0,4},{2,6},{4,0},{6,2},{1,5},{3,7},{5,1},{7,3},{8,12},{10,14},{12... | collective-permute-start | bytes 1572872 | tf_op jit(solution)/shard_map/ppermute | solution.py:463
  84.6 10.2 %collective-permute-done.15.two_ref = bf16[4,256,256]{2,1,0:T(8,128)(2,1)S(1)} collective-permute-done((bf16[4,256,256]{2,1,0:T(8,128)(2,1)S(1)}, bf16[4,256,256]{2,1,0:T(8,128)(2,1)S(1)}, u32[]{:S(2)}, u32[]{:S(2)}) %collective-permute-start.15) | collective-permute-done | bytes 524320 | tf_op jit(solution)/shard_map/ppermute | solution.py:433
  94.8 0.1 shard_map.84
  95.0 1.6 %collective-permute-start.19 = (bf16[4,256,256]{2,1,0:T(8,128)(2,1)S(1)}, bf16[4,256,256]{2,1,0:T(8,128)(2,1)S(1)}, u32[]{:S(2)}, u32[]{:S(2)}) collective-permute-start(bf16[4,256,256]{2,1,0:T(8,128)(2,1)S(1)} %shard_map.80.one_ref), channel_id=1, source_target_pairs={{0,24},{24,0},{8,16},{16,8},{1,25},{25,1},{9,17},{17,9},{2,26},{26... | collective-permute-start | bytes 1572872 | tf_op jit(solution)/shard_map/ppermute | solution.py:433
  96.6 1.5 %collective-permute-start.25 = (bf16[1,512,512]{2,1,0:T(8,128)(2,1)S(1)}, bf16[1,512,512]{2,1,0:T(8,128)(2,1)S(1)}, u32[]{:S(2)}, u32[]{:S(2)}) collective-permute-start(bf16[1,512,512]{2,1,0:T(8,128)(2,1)S(1)} %shard_map.83), channel_id=1, source_target_pairs={{0,4},{2,6},{4,0},{6,2},{1,5},{3,7},{5,1},{7,3},{8,12},{10,14},{12... | collective-permute-start | bytes 1572872 | tf_op jit(solution)/shard_map/ppermute | solution.py:462
  98.1 0.5 collective-permute-start.17
  98.6 0.8 collective-permute-done.16.refs_1_
  99.4 0.5 collective-permute-start.18
  100.0 14.0 %collective-permute-done.17.refs_2_ = bf16[256,256]{1,0:T(8,128)(2,1)S(1)} collective-permute-done((bf16[256,256]{1,0:T(8,128)(2,1)S(1)}, bf16[256,256]{1,0:T(8,128)(2,1)S(1)}, u32[]{:S(2)}, u32[]{:S(2)}) %collective-permute-start.17) | collective-permute-done | bytes 131104 | tf_op jit(solution)/shard_map/ppermute | solution.py:352
  113.9 0.5 collective-permute-done.18.refs_3_
  114.4 0.1 shard_map.86
  114.6 0.8 collective-permute-start.20
  115.4 1.5 %collective-permute-start.21 = (bf16[256,256]{1,0:T(8,128)(2,1)S(1)}, bf16[256,256]{1,0:T(8,128)(2,1)S(1)}, u32[]{:S(2)}, u32[]{:S(2)}) collective-permute-start(bf16[256,256]{1,0:T(8,128)(2,1)S(1)} %get-tuple-element.93), channel_id=1, source_target_pairs={{0,4},{2,6},{4,0},{6,2},{1,5},{3,7},{5,1},{7,3},{8,12},{10,14},{12... | collective-permute-start | bytes 393224 | tf_op jit(solution)/shard_map/ppermute | solution.py:352
  116.9 3.3 %collective-permute-start.24 = (bf16[4,256,256]{2,1,0:T(8,128)(2,1)S(1)}, bf16[4,256,256]{2,1,0:T(8,128)(2,1)S(1)}, u32[]{:S(2)}, u32[]{:S(2)}) collective-permute-start(bf16[4,256,256]{2,1,0:T(8,128)(2,1)S(1)} %shard_map.85.part_ref), channel_id=1, source_target_pairs={{0,8},{8,0},{16,24},{24,16},{1,9},{9,1},{17,25},{25,17},{2,10},{10... | collective-permute-start | bytes 1572872 | tf_op jit(solution)/shard_map/ppermute | solution.py:436
  120.2 0.2 shard_map.92
  120.4 1.6 %collective-permute-start.26 = (bf16[1,512,512]{2,1,0:T(8,128)(2,1)S(1)}, bf16[1,512,512]{2,1,0:T(8,128)(2,1)S(1)}, u32[]{:S(2)}, u32[]{:S(2)}) collective-permute-start(bf16[1,512,512]{2,1,0:T(8,128)(2,1)S(1)} %shard_map.92), channel_id=1, source_target_pairs={{0,1},{1,0},{2,3},{3,2},{4,5},{5,4},{6,7},{7,6},{8,9},{9,8},{10,11... | collective-permute-start | bytes 1572872 | tf_op jit(solution)/shard_map/ppermute | solution.py:466
  122.0 0.8 collective-permute-done.22.refs_3_
  122.9 3.9 %collective-permute-start.23 = (bf16[4,256,256]{2,1,0:T(8,128)(2,1)S(1)}, bf16[4,256,256]{2,1,0:T(8,128)(2,1)S(1)}, u32[]{:S(2)}, u32[]{:S(2)}) collective-permute-start(bf16[4,256,256]{2,1,0:T(8,128)(2,1)S(1)} %shard_map.87.part_ref), channel_id=1, source_target_pairs={{0,8},{8,0},{16,24},{24,16},{1,9},{9,1},{17,25},{25,17},{2,10},{10... | collective-permute-start | bytes 1572872 | tf_op jit(solution)/shard_map/ppermute | solution.py:436
  126.7 2.4 %shard_map.88.rest_0_ = bf16[2,512,4,256]{3,2,1,0:T(4,128)(2,1)} custom-call(s32[3]{0:T(128)S(1)} %get-tuple-element.65.place_ref, bf16[4,256,256]{2,1,0:T(8,128)(2,1)S(1)} %shard_map.85.part_ref), custom_call_target="tpu_custom_call" | custom-call | bytes 1048576 | tf_op jit(solution)/shard_map/pallas_call | solution.py:86
  129.2 3.8 %collective-permute-done.24.part_ref = bf16[4,256,256]{2,1,0:T(8,128)(2,1)S(1)} collective-permute-done((bf16[4,256,256]{2,1,0:T(8,128)(2,1)S(1)}, bf16[4,256,256]{2,1,0:T(8,128)(2,1)S(1)}, u32[]{:S(2)}, u32[]{:S(2)}) %collective-permute-start.24) | collective-permute-done | bytes 524320 | tf_op jit(solution)/shard_map/ppermute | solution.py:436
  133.0 2.4 %shard_map.89.rest_0_ = bf16[2,512,4,256]{3,2,1,0:T(4,128)(2,1)} custom-call(s32[3]{0:T(128)S(1)} %get-tuple-element.65.place_ref, bf16[4,256,256]{2,1,0:T(8,128)(2,1)S(1)} %collective-permute-done.24.part_ref, bf16[2,512,4,256]{3,2,1,0:T(4,128)(2,1)} %shard_map.88.rest_0_), custom_call_target="tpu_custom_call", output_to_operand_aliasing={{}: (2, {})} | custom-call | bytes 1048576 | tf_op jit(solution)/shard_map/pallas_call | solution.py:86
  135.4 2.4 %shard_map.90.rest_0_ = bf16[2,512,4,256]{3,2,1,0:T(4,128)(2,1)} custom-call(s32[3]{0:T(128)S(1)} %get-tuple-element.65.place_ref, bf16[4,256,256]{2,1,0:T(8,128)(2,1)S(1)} %shard_map.87.part_ref, bf16[2,512,4,256]{3,2,1,0:T(4,128)(2,1)} %shard_map.89.rest_0_), custom_call_target="tpu_custom_call", output_to_operand_aliasing={{}: (2, {})} | custom-call | bytes 1048576 | tf_op jit(solution)/shard_map/pallas_call | solution.py:86
  137.9 1.0 shard_map.93
  138.9 5.0 %collective-permute-done.23.part_ref = bf16[4,256,256]{2,1,0:T(8,128)(2,1)S(1)} collective-permute-done((bf16[4,256,256]{2,1,0:T(8,128)(2,1)S(1)}, bf16[4,256,256]{2,1,0:T(8,128)(2,1)S(1)}, u32[]{:S(2)}, u32[]{:S(2)}) %collective-permute-start.23) | collective-permute-done | bytes 524320 | tf_op jit(solution)/shard_map/ppermute | solution.py:436
  143.9 2.4 %shard_map.91 = bf16[2,512,4,256]{3,2,1,0:T(4,128)(2,1)} custom-call(s32[3]{0:T(128)S(1)} %get-tuple-element.65.place_ref, bf16[4,256,256]{2,1,0:T(8,128)(2,1)S(1)} %collective-permute-done.23.part_ref, bf16[2,512,4,256]{3,2,1,0:T(4,128)(2,1)} %shard_map.90.rest_0_), custom_call_target="tpu_custom_call", output_to_operand_aliasing={{}: (2, {})} | custom-call | bytes 1048576 | tf_op jit(solution)/shard_map/pallas_call | solution.py:86
  (22 shorter events, 0.4 us)
Async XLA Ops:
  0.8 2.2 %copy-start = (bf16[2,512,4,256]{3,2,1,0:T(4,128)(2,1)S(1)}, bf16[2,512,4,256]{3,2,1,0:T(4,128)(2,1)}, u32[]{:S(2)}) copy-start(bf16[2,512,4,256]{3,2,1,0:T(4,128)(2,1)} %param.9) | copy-start | bytes 6291460
  3.4 15.8 %collective-permute-start.1 = (bf16[2,512,256]{2,1,0:T(8,128)(2,1)S(1)}, bf16[2,512,256]{2,1,0:T(8,128)(2,1)S(1)}, u32[]{:S(2)}, u32[]{:S(2)}) collective-permute-start(bf16[2,512,256]{2,1,0:T(8,128)(2,1)S(1)} %shard_map.68), channel_id=1, source_target_pairs={{0,4},{2,6},{4,0},{6,2},{8,14},{10,12},{12,10},{14,8},{16,20},{18,... | collective-permute-start | bytes 1572872 | tf_op jit(solution)/shard_map/ppermute | solution.py:337
  12.1 20.8 %collective-permute-start = (bf16[4,512,256]{2,1,0:T(8,128)(2,1)S(1)}, bf16[4,512,256]{2,1,0:T(8,128)(2,1)S(1)}, u32[]{:S(2)}, u32[]{:S(2)}) collective-permute-start(bf16[4,512,256]{2,1,0:T(8,128)(2,1)S(1)} %shard_map.72), channel_id=1, source_target_pairs={{0,2},{2,0},{4,6},{6,4},{1,3},{3,1},{5,7},{7,5},{8,10},{10,8},{12,... | collective-permute-start | bytes 3145736 | tf_op jit(solution)/shard_map/ppermute | solution.py:394
  12.1 18.2 %collective-permute-start.3 = (bf16[2,512,256]{2,1,0:T(8,128)(2,1)S(1)}, bf16[2,512,256]{2,1,0:T(8,128)(2,1)S(1)}, u32[]{:S(2)}, u32[]{:S(2)}) collective-permute-start(bf16[2,512,256]{2,1,0:T(8,128)(2,1)S(1)} %shard_map.69), channel_id=1, source_target_pairs={{0,4},{2,6},{4,0},{6,2},{1,5},{3,7},{5,1},{7,3},{8,12},{10,14},{12... | collective-permute-start | bytes 1572872 | tf_op jit(solution)/shard_map/ppermute | solution.py:386
  19.1 13.7 %collective-permute-start.2 = (bf16[2,512,256]{2,1,0:T(8,128)(2,1)S(1)}, bf16[2,512,256]{2,1,0:T(8,128)(2,1)S(1)}, u32[]{:S(2)}, u32[]{:S(2)}) collective-permute-start(bf16[2,512,256]{2,1,0:T(8,128)(2,1)S(1)} %collective-permute-done.1.refs_2_.refs_6_), channel_id=1, source_target_pairs={{0,8},{8,0},{16,24},{24,16},{1,9},{9,1},{17,25},{25,17},{2,10},{10... | collective-permute-start | bytes 1572872 | tf_op jit(solution)/shard_map/ppermute | solution.py:395
  20.6 27.1 %collective-permute-start.7 = (bf16[2,512,256]{2,1,0:T(8,128)(2,1)S(1)}, bf16[2,512,256]{2,1,0:T(8,128)(2,1)S(1)}, u32[]{:S(2)}, u32[]{:S(2)}) collective-permute-start(bf16[2,512,256]{2,1,0:T(8,128)(2,1)S(1)} %shard_map.70), channel_id=1, source_target_pairs={{0,6},{2,4},{4,2},{6,0},{1,7},{3,5},{5,3},{7,1},{8,14},{10,12},{12... | collective-permute-start | bytes 1572872 | tf_op jit(solution)/shard_map/ppermute | solution.py:386
  35.0 5.8 %collective-permute-start.6 = (f32[4,2048]{1,0:T(4,128)S(1)}, f32[4,2048]{1,0:T(4,128)S(1)}, u32[]{:S(2)}, u32[]{:S(2)}) collective-permute-start(f32[4,2048]{1,0:T(4,128)S(1)} %shard_map.74.refs_8_), channel_id=1, source_target_pairs={{0,24},{8,16},{16,8},{24,0},{1,25},{9,17},{17,9},{25,1},{2,26},{10... | collective-permute-start | bytes 98312 | tf_op jit(solution)/shard_map/ppermute | solution.py:342
  38.8 4.8 %collective-permute-start.5 = (f32[4,2048]{1,0:T(4,128)S(1)}, f32[4,2048]{1,0:T(4,128)S(1)}, u32[]{:S(2)}, u32[]{:S(2)}) collective-permute-start(f32[4,2048]{1,0:T(4,128)S(1)} %shard_map.74.refs_8_), channel_id=1, source_target_pairs={{0,16},{8,24},{16,0},{24,8},{1,17},{9,25},{17,1},{25,9},{2,18},{10... | collective-permute-start | bytes 98312 | tf_op jit(solution)/shard_map/ppermute | solution.py:342
  38.8 4.8 %collective-permute-start.4 = (f32[4,2048]{1,0:T(4,128)S(1)}, f32[4,2048]{1,0:T(4,128)S(1)}, u32[]{:S(2)}, u32[]{:S(2)}) collective-permute-start(f32[4,2048]{1,0:T(4,128)S(1)} %shard_map.74.refs_8_), channel_id=1, source_target_pairs={{0,8},{8,0},{16,24},{24,16},{1,9},{9,1},{17,25},{25,17},{2,10},{10... | collective-permute-start | bytes 98312 | tf_op jit(solution)/shard_map/ppermute | solution.py:342
  49.9 5.8 %collective-permute-start.10 = (f32[4,2048]{1,0:T(4,128)S(1)}, f32[4,2048]{1,0:T(4,128)S(1)}, u32[]{:S(2)}, u32[]{:S(2)}) collective-permute-start(f32[4,2048]{1,0:T(4,128)S(1)} %shard_map.76.refs_8_), channel_id=1, source_target_pairs={{0,24},{8,16},{16,8},{24,0},{1,25},{9,17},{17,9},{25,1},{2,26},{10... | collective-permute-start | bytes 98312 | tf_op jit(solution)/shard_map/ppermute | solution.py:342
  51.4 4.8 %collective-permute-start.9 = (f32[4,2048]{1,0:T(4,128)S(1)}, f32[4,2048]{1,0:T(4,128)S(1)}, u32[]{:S(2)}, u32[]{:S(2)}) collective-permute-start(f32[4,2048]{1,0:T(4,128)S(1)} %shard_map.76.refs_8_), channel_id=1, source_target_pairs={{0,16},{8,24},{16,0},{24,8},{1,17},{9,25},{17,1},{25,9},{2,18},{10... | collective-permute-start | bytes 98312 | tf_op jit(solution)/shard_map/ppermute | solution.py:342
  52.0 4.9 %collective-permute-start.8 = (f32[4,2048]{1,0:T(4,128)S(1)}, f32[4,2048]{1,0:T(4,128)S(1)}, u32[]{:S(2)}, u32[]{:S(2)}) collective-permute-start(f32[4,2048]{1,0:T(4,128)S(1)} %shard_map.76.refs_8_), channel_id=1, source_target_pairs={{0,8},{8,0},{16,24},{24,16},{1,9},{9,1},{17,25},{25,17},{2,10},{10... | collective-permute-start | bytes 98312 | tf_op jit(solution)/shard_map/ppermute | solution.py:342
  56.9 11.3 %collective-permute-start.11 = (bf16[4,256,256]{2,1,0:T(8,128)(2,1)S(1)}, bf16[4,256,256]{2,1,0:T(8,128)(2,1)S(1)}, u32[]{:S(2)}, u32[]{:S(2)}) collective-permute-start(bf16[4,256,256]{2,1,0:T(8,128)(2,1)S(1)} %get-tuple-element.78), channel_id=1, source_target_pairs={{0,8},{8,0},{16,24},{24,16},{1,9},{9,1},{17,25},{25,17},{2,10},{10... | collective-permute-start | bytes 1572872 | tf_op jit(solution)/shard_map/ppermute | solution.py:420
  68.3 14.5 %collective-permute-start.13 = (bf16[4,512,512]{2,1,0:T(8,128)(2,1)S(1)}, bf16[4,512,512]{2,1,0:T(8,128)(2,1)S(1)}, u32[]{:S(2)}, u32[]{:S(2)}) collective-permute-start(bf16[4,512,512]{2,1,0:T(8,128)(2,1)S(1)} %shard_map.78), channel_id=1, source_target_pairs={{0,2},{2,0},{4,6},{6,4},{1,3},{3,1},{5,7},{7,5},{8,10},{10,8},{12,... | collective-permute-start | bytes 6291464 | tf_op jit(solution)/shard_map/ppermute | solution.py:457
  68.4 14.3 %collective-permute-start.12 = (bf16[4,256,256]{2,1,0:T(8,128)(2,1)S(1)}, bf16[4,256,256]{2,1,0:T(8,128)(2,1)S(1)}, u32[]{:S(2)}, u32[]{:S(2)}) collective-permute-start(bf16[4,256,256]{2,1,0:T(8,128)(2,1)S(1)} %get-tuple-element.79), channel_id=1, source_target_pairs={{0,8},{8,0},{16,24},{24,16},{1,9},{9,1},{17,25},{25,17},{2,10},{10... | collective-permute-start | bytes 1572872 | tf_op jit(solution)/shard_map/ppermute | solution.py:420
  69.0 25.9 %collective-permute-start.15 = (bf16[4,256,256]{2,1,0:T(8,128)(2,1)S(1)}, bf16[4,256,256]{2,1,0:T(8,128)(2,1)S(1)}, u32[]{:S(2)}, u32[]{:S(2)}) collective-permute-start(bf16[4,256,256]{2,1,0:T(8,128)(2,1)S(1)} %shard_map.79.one_ref), channel_id=1, source_target_pairs={{0,24},{24,0},{8,16},{16,8},{1,25},{25,1},{9,17},{17,9},{2,26},{26... | collective-permute-start | bytes 1572872 | tf_op jit(solution)/shard_map/ppermute | solution.py:433
  83.0 31.4 %collective-permute-start.14 = (bf16[1,512,512]{2,1,0:T(8,128)(2,1)S(1)}, bf16[1,512,512]{2,1,0:T(8,128)(2,1)S(1)}, u32[]{:S(2)}, u32[]{:S(2)}) collective-permute-start(bf16[1,512,512]{2,1,0:T(8,128)(2,1)S(1)} %shard_map.82), channel_id=1, source_target_pairs={{0,4},{2,6},{4,0},{6,2},{1,5},{3,7},{5,1},{7,3},{8,12},{10,14},{12... | collective-permute-start | bytes 1572872 | tf_op jit(solution)/shard_map/ppermute | solution.py:463
  95.0 19.5 %collective-permute-start.19 = (bf16[4,256,256]{2,1,0:T(8,128)(2,1)S(1)}, bf16[4,256,256]{2,1,0:T(8,128)(2,1)S(1)}, u32[]{:S(2)}, u32[]{:S(2)}) collective-permute-start(bf16[4,256,256]{2,1,0:T(8,128)(2,1)S(1)} %shard_map.80.one_ref), channel_id=1, source_target_pairs={{0,24},{24,0},{8,16},{16,8},{1,25},{25,1},{9,17},{17,9},{2,26},{26... | collective-permute-start | bytes 1572872 | tf_op jit(solution)/shard_map/ppermute | solution.py:433
  96.6 23.7 %collective-permute-start.25 = (bf16[1,512,512]{2,1,0:T(8,128)(2,1)S(1)}, bf16[1,512,512]{2,1,0:T(8,128)(2,1)S(1)}, u32[]{:S(2)}, u32[]{:S(2)}) collective-permute-start(bf16[1,512,512]{2,1,0:T(8,128)(2,1)S(1)} %shard_map.83), channel_id=1, source_target_pairs={{0,4},{2,6},{4,0},{6,2},{1,5},{3,7},{5,1},{7,3},{8,12},{10,14},{12... | collective-permute-start | bytes 1572872 | tf_op jit(solution)/shard_map/ppermute | solution.py:462
  98.1 1.3 collective-permute-start.16
  98.1 15.8 %collective-permute-start.17 = (bf16[256,256]{1,0:T(8,128)(2,1)S(1)}, bf16[256,256]{1,0:T(8,128)(2,1)S(1)}, u32[]{:S(2)}, u32[]{:S(2)}) collective-permute-start(bf16[256,256]{1,0:T(8,128)(2,1)S(1)} %get-tuple-element.87), channel_id=1, source_target_pairs={{0,4},{2,6},{4,0},{6,2},{1,5},{3,7},{5,1},{7,3},{8,12},{10,14},{12... | collective-permute-start | bytes 393224 | tf_op jit(solution)/shard_map/ppermute | solution.py:352
  99.4 14.9 %collective-permute-start.18 = (bf16[256,256]{1,0:T(8,128)(2,1)S(1)}, bf16[256,256]{1,0:T(8,128)(2,1)S(1)}, u32[]{:S(2)}, u32[]{:S(2)}) collective-permute-start(bf16[256,256]{1,0:T(8,128)(2,1)S(1)} %get-tuple-element.88), channel_id=1, source_target_pairs={{0,6},{2,4},{4,2},{6,0},{1,7},{3,5},{5,3},{7,1},{8,14},{10,12},{12... | collective-permute-start | bytes 393224 | tf_op jit(solution)/shard_map/ppermute | solution.py:352
  114.6 7.4 %collective-permute-start.20 = (bf16[256,256]{1,0:T(8,128)(2,1)S(1)}, bf16[256,256]{1,0:T(8,128)(2,1)S(1)}, u32[]{:S(2)}, u32[]{:S(2)}) collective-permute-start(bf16[256,256]{1,0:T(8,128)(2,1)S(1)} %get-tuple-element.92), channel_id=1, source_target_pairs={{0,2},{2,0},{4,6},{6,4},{1,3},{3,1},{5,7},{7,5},{8,10},{10,8},{12,... | collective-permute-start | bytes 393224 | tf_op jit(solution)/shard_map/ppermute | solution.py:352
  115.4 6.6 %collective-permute-start.21 = (bf16[256,256]{1,0:T(8,128)(2,1)S(1)}, bf16[256,256]{1,0:T(8,128)(2,1)S(1)}, u32[]{:S(2)}, u32[]{:S(2)}) collective-permute-start(bf16[256,256]{1,0:T(8,128)(2,1)S(1)} %get-tuple-element.93), channel_id=1, source_target_pairs={{0,4},{2,6},{4,0},{6,2},{1,5},{3,7},{5,1},{7,3},{8,12},{10,14},{12... | collective-permute-start | bytes 393224 | tf_op jit(solution)/shard_map/ppermute | solution.py:352
  116.9 5.9 %collective-permute-start.22 = (bf16[256,256]{1,0:T(8,128)(2,1)S(1)}, bf16[256,256]{1,0:T(8,128)(2,1)S(1)}, u32[]{:S(2)}, u32[]{:S(2)}) collective-permute-start(bf16[256,256]{1,0:T(8,128)(2,1)S(1)} %get-tuple-element.94), channel_id=1, source_target_pairs={{0,6},{2,4},{4,2},{6,0},{1,7},{3,5},{5,3},{7,1},{8,14},{10,12},{12... | collective-permute-start | bytes 393224 | tf_op jit(solution)/shard_map/ppermute | solution.py:352
  116.9 16.1 %collective-permute-start.24 = (bf16[4,256,256]{2,1,0:T(8,128)(2,1)S(1)}, bf16[4,256,256]{2,1,0:T(8,128)(2,1)S(1)}, u32[]{:S(2)}, u32[]{:S(2)}) collective-permute-start(bf16[4,256,256]{2,1,0:T(8,128)(2,1)S(1)} %shard_map.85.part_ref), channel_id=1, source_target_pairs={{0,8},{8,0},{16,24},{24,16},{1,9},{9,1},{17,25},{25,17},{2,10},{10... | collective-permute-start | bytes 1572872 | tf_op jit(solution)/shard_map/ppermute | solution.py:436
  120.4 17.5 %collective-permute-start.26 = (bf16[1,512,512]{2,1,0:T(8,128)(2,1)S(1)}, bf16[1,512,512]{2,1,0:T(8,128)(2,1)S(1)}, u32[]{:S(2)}, u32[]{:S(2)}) collective-permute-start(bf16[1,512,512]{2,1,0:T(8,128)(2,1)S(1)} %shard_map.92), channel_id=1, source_target_pairs={{0,1},{1,0},{2,3},{3,2},{4,5},{5,4},{6,7},{7,6},{8,9},{9,8},{10,11... | collective-permute-start | bytes 1572872 | tf_op jit(solution)/shard_map/ppermute | solution.py:466
  122.9 21.0 %collective-permute-start.23 = (bf16[4,256,256]{2,1,0:T(8,128)(2,1)S(1)}, bf16[4,256,256]{2,1,0:T(8,128)(2,1)S(1)}, u32[]{:S(2)}, u32[]{:S(2)}) collective-permute-start(bf16[4,256,256]{2,1,0:T(8,128)(2,1)S(1)} %shard_map.87.part_ref), channel_id=1, source_target_pairs={{0,8},{8,0},{16,24},{24,16},{1,9},{9,1},{17,25},{25,17},{2,10},{10... | collective-permute-start | bytes 1572872 | tf_op jit(solution)/shard_map/ppermute | solution.py:436
